TPU v7x, 32 devices: a whole 2x2x4 slice. The times are simulated.
32 devices in a mesh: pole: 4 (over y, x), tile: 8 (over z, core).
Axes of the slice: x: 2, y: 2, z: 4, core: 2. Of those that a mesh axis runs over, the one named last changes fastest.
Arguments:
- state: float32 [3, 128, 2048], P(None, 'tile', 'pole'), may hold values from -6 to 6
- depth: float32 [128, 2048], P('tile', 'pole'), may hold values from 0.5 to 2
- pole_real: float32 [16], P('pole'), may hold values from -1.5 to -0.5
- pole_imag: float32 [16], P('pole'), may hold values from -2 to 2
- pole_weight: float32 [2, 16], P(None, 'pole'), may hold values from -3 to 3
Outputs:
- advanced: float32 [3, 128, 2048], P(None, 'tile', 'pole')
All inputs are finite; a program needn't handle non-finite values.
Results may differ from a plain program's by a relative error of at most 0.00002.
Values sent between devices are 32-bit elements; how exact they have to be, the bound alone decides.
No kernel may reach another device: no remote copies, remote signals or barrier semaphores. Data moves between devices by JAX's collectives and lax.ppermute only.
A program may use at most 64 MiB of HBM per device.

v0:
```python
import jax
import jax.numpy as jnp
from jax import lax
from jax.sharding import PartitionSpec as P

ITERS = 8
DEPTH = 4


coriolis = 0.7
centre = 8.0
half_width = 8.0


def with_halo(block, sides, width):
    for axis, dim in sides:
        count = lax.axis_size(axis)
        forward = [(i, i + 1) for i in range(count - 1)]
        forward.append((count - 1, 0))
        backward = [(target, source) for source, target in forward]
        low = lax.ppermute(
            lax.slice_in_dim(block, block.shape[dim] - width, None, axis=dim), axis, forward
        )
        high = lax.ppermute(lax.slice_in_dim(block, 0, width, axis=dim), axis, backward)
        block = jnp.concatenate([low, block, high], axis=dim)
    return block


def complex_product(left_real, left_imaginary, right_real, right_imaginary):
    return (
        left_real * right_real - left_imaginary * right_imaginary,
        left_real * right_imaginary + left_imaginary * right_real,
    )


def complex_quotient(top_real, top_imaginary, under_real, under_imaginary):
    norm = under_real * under_real + under_imaginary * under_imaginary
    return (
        (top_real * under_real + top_imaginary * under_imaginary) / norm,
        (top_imaginary * under_real - top_real * under_imaginary) / norm,
    )


def chebyshev_table(alpha_real, alpha_imaginary):
    shift_real = alpha_real * alpha_real - alpha_imaginary * alpha_imaginary + coriolis * coriolis
    shift_imaginary = 2.0 * alpha_real * alpha_imaginary
    sigma_real = (shift_real + centre) / half_width
    sigma_imaginary = shift_imaginary / half_width
    unity = jnp.ones_like(sigma_real)
    nought = jnp.zeros_like(sigma_real)
    rho_real, rho_imaginary = complex_quotient(unity, nought, sigma_real, sigma_imaginary)
    table = []
    for index in range(ITERS - 1):
        next_real, next_imaginary = complex_quotient(
            unity, nought, 2.0 * sigma_real - rho_real, 2.0 * sigma_imaginary - rho_imaginary
        )
        keep_real, keep_imaginary = complex_product(
            next_real, next_imaginary, rho_real, rho_imaginary
        )
        table.append(
            (
                keep_real,
                keep_imaginary,
                2.0 * next_real / half_width,
                2.0 * next_imaginary / half_width,
            )
        )
        rho_real, rho_imaginary = (next_real, next_imaginary)
    return (shift_real, shift_imaginary, table)


def advance(entry, search_real, search_imaginary, resid_real, resid_imaginary):
    first_real, first_imaginary = complex_product(entry[0], entry[1], search_real, search_imaginary)
    second_real, second_imaginary = complex_product(entry[2], entry[3], resid_real, resid_imaginary)
    return (first_real + second_real, first_imaginary + second_imaginary)


def row_slope(field):
    return 0.5 * (field[..., 2:, :] - field[..., :-2, :])


def padded_column_slope(field):
    return 0.5 * (field[..., :, 2:] - field[..., :, :-2])


def column_slope(field):
    return 0.5 * (jnp.roll(field, -1, -1) - jnp.roll(field, 1, -1))


def band_stiffness(field, depth_rows):
    east = 0.5 * (depth_rows[:-1] + depth_rows[1:]) * (field[:, 1:] - field[:, :-1])
    inner = field[:, 1:-1]
    depth_inner = depth_rows[1:-1]
    north = 0.5 * (depth_inner + jnp.roll(depth_inner, -1, -1)) * (jnp.roll(inner, -1, -1) - inner)
    return -(east[:, 1:] - east[:, :-1] + north - jnp.roll(north, 1, -1))


def apply_shifted(search_real, search_imaginary, depth_rows, shift_real, shift_imaginary):
    middle_real = search_real[:, 1:-1]
    middle_imaginary = search_imaginary[:, 1:-1]
    image_real = (
        shift_real * middle_real
        - shift_imaginary * middle_imaginary
        + band_stiffness(search_real, depth_rows)
    )
    image_imaginary = (
        shift_real * middle_imaginary
        + shift_imaginary * middle_real
        + band_stiffness(search_imaginary, depth_rows)
    )
    return (image_real, image_imaginary)


def shards(state, depth, pole_real, pole_imag, pole_weight):
    rows = state.shape[1]
    stacked = jnp.concatenate([state, depth[None]], 0)
    padded = with_halo(stacked, (("pole", 2), ("tile", 1)), 1)
    flux_east = padded[3] * padded[1]
    flux_north = padded[3] * padded[2]
    flux_div = row_slope(flux_east)[:, 1:-1] + padded_column_slope(flux_north)[1:-1]
    flux_curl = row_slope(flux_north)[:, 1:-1] - padded_column_slope(flux_east)[1:-1]
    centred = padded[:, 1:-1, 1:-1]
    fields = jnp.stack([centred[0], centred[1], centred[2], flux_div, flux_curl, centred[3]])
    strip = lax.all_gather(fields, "pole", axis=2, tiled=True)
    height = strip[0]
    east_speed = strip[1]
    north_speed = strip[2]
    strip_div = strip[3]
    strip_curl = strip[4]
    strip_depth = strip[5]
    reach = DEPTH
    depth_wide = with_halo(strip_depth, (("tile", 0),), reach)
    alpha_real = pole_real[:, None, None]
    alpha_imaginary = pole_imag[:, None, None]
    shift_real, shift_imaginary, table = chebyshev_table(alpha_real, alpha_imaginary)
    top_real = shift_real * height - alpha_real * strip_div - coriolis * strip_curl
    top_imaginary = shift_imaginary * height - alpha_imaginary * strip_div
    rhs_real, rhs_imaginary = complex_quotient(top_real, top_imaginary, alpha_real, alpha_imaginary)
    resid_real, resid_imaginary = (rhs_real, rhs_imaginary)
    search_real, search_imaginary = complex_quotient(
        rhs_real, rhs_imaginary, shift_real + centre, shift_imaginary
    )
    iterate_real = jnp.zeros_like(rhs_real)
    iterate_imaginary = jnp.zeros_like(rhs_real)
    for block in range(ITERS // reach):
        packed = jnp.stack([resid_real, resid_imaginary, search_real, search_imaginary])
        wide = with_halo(packed, (("tile", 2),), DEPTH)
        resid_real = wide[0]
        resid_imaginary = wide[1]
        search_real = wide[2]
        search_imaginary = wide[3]
        for inner in range(reach):
            index = block * reach + inner
            margin = reach - inner
            iterate_real = iterate_real + search_real[:, margin : margin + rows]
            iterate_imaginary = iterate_imaginary + search_imaginary[:, margin : margin + rows]
            depth_rows = depth_wide[inner : inner + rows + 2 * margin]
            image_real, image_imaginary = apply_shifted(
                search_real, search_imaginary, depth_rows, shift_real, shift_imaginary
            )
            resid_real = resid_real[:, 1:-1] - image_real
            resid_imaginary = resid_imaginary[:, 1:-1] - image_imaginary
            search_real = search_real[:, 1:-1]
            search_imaginary = search_imaginary[:, 1:-1]
            if index < ITERS - 1:
                search_real, search_imaginary = advance(
                    table[index], search_real, search_imaginary, resid_real, resid_imaginary
                )
    weight_real = pole_weight[0][:, None, None]
    weight_imaginary = pole_weight[1][:, None, None]
    scale_real, scale_imaginary = complex_quotient(
        weight_real, weight_imaginary, shift_real, shift_imaginary
    )
    out_height = jnp.sum(weight_real * iterate_real - weight_imaginary * iterate_imaginary, 0)
    wide = with_halo(jnp.stack([iterate_real, iterate_imaginary]), (("tile", 2),), 1)
    push_real = east_speed - row_slope(wide[0])
    push_imaginary = -row_slope(wide[1])
    lift_real = north_speed - column_slope(iterate_real)
    lift_imaginary = -column_slope(iterate_imaginary)
    east_real, east_imaginary = complex_product(
        alpha_real, alpha_imaginary, push_real, push_imaginary
    )
    east_real = east_real + coriolis * lift_real
    east_imaginary = east_imaginary + coriolis * lift_imaginary
    north_real, north_imaginary = complex_product(
        alpha_real, alpha_imaginary, lift_real, lift_imaginary
    )
    north_real = north_real - coriolis * push_real
    north_imaginary = north_imaginary - coriolis * push_imaginary
    out_east = jnp.sum(scale_real * east_real - scale_imaginary * east_imaginary, 0)
    out_north = jnp.sum(scale_real * north_real - scale_imaginary * north_imaginary, 0)
    summed = lax.psum_scatter(
        jnp.stack([out_height, out_east, out_north]), "pole", scatter_dimension=2, tiled=True
    )
    return summed


def solution(mesh):
    return jax.shard_map(
        shards,
        mesh=mesh,
        in_specs=(
            P(None, "tile", "pole"),
            P("tile", "pole"),
            P("pole"),
            P("pole"),
            P(None, "pole"),
        ),
        out_specs=P(None, "tile", "pole"),
        check_vma=False,
    )
```

profile of v0, /device:TPU:0, one launch (start us, length us, event | category | flops | bytes accessed | tf_op | source)
XLA Modules:
  0.0 134.2 jit_solution(10009998595956791551)
XLA Ops:
  6.5 0.9 pad_maximum_fusion.33
  7.4 2.9 %collective-permute-start = (f32[4,16,1]{2,1,0:T(8,128)S(1)}, f32[4,16,1]{2,1,0:T(8,128)S(1)}, u32[]{:S(2)}, u32[]{:S(2)}) collective-permute-start(f32[4,16,1]{2,1,0:T(8,128)S(1)} %get-tuple-element.117), channel_id=1, source_target_pairs={{0,8},{8,16},{16,24},{24,0},{1,9},{9,17},{17,25},{25,1},{2,10},{10... | collective-permute-start | bytes 776 | tf_op jit(solution)/shard_map/ppermute | solution.py:21
  10.4 1.0 collective-permute-start.1
  11.4 0.7 multiply_subtract_fusion.1
  12.2 0.8 add_divide_fusion.2
  12.9 0.3 collective-permute-done
  13.2 1.1 collective-permute-done.1
  14.3 1.0 pad_maximum_fusion.37
  15.3 3.5 %collective-permute-start.3 = (f32[4,1,514]{2,1,0:T(1,128)S(1)}, f32[4,1,514]{2,1,0:T(1,128)S(1)}, u32[]{:S(2)}, u32[]{:S(2)}) collective-permute-start(f32[4,1,514]{2,1,0:T(1,128)S(1)} %get-tuple-element.114), channel_id=1, source_target_pairs={{1,0},{2,1},{3,2},{4,3},{5,4},{6,5},{7,6},{0,7},{9,8},{10,9},{11,1... | collective-permute-start | bytes 24680 | tf_op jit(solution)/shard_map/ppermute | solution.py:24
  18.9 0.8 multiply_add_fusion.16
  19.6 0.6 collective-permute-done.2
  20.2 0.9 fusion.127
  21.2 0.9 maximum_multiply_fusion
  22.3 0.9 pad_maximum_fusion.20
  23.2 12.8 %all_gather.3 = f32[6,16,2048]{2,1,0:T(8,128)S(1)} all-gather(f32[6,16,512]{2,1,0:T(8,128)S(1)} %pad_maximum_fusion.20), channel_id=1, replica_groups=mesh['pole'=4,'tile'=8] {'pole'}, dimensions={2}, use_global_device_ids=true | all-gather | bytes 983040 | tf_op jit(solution)/shard_map/all_gather | solution.py:124
  36.2 3.5 %collective-permute-start.7 = (f32[4,2048]{1,0:T(4,128)S(1)}, f32[4,2048]{1,0:T(4,128)S(1)}, u32[]{:S(2)}, u32[]{:S(2)}) collective-permute-start(f32[4,2048]{1,0:T(4,128)S(1)} %get-tuple-element.75), channel_id=1, source_target_pairs={{1,0},{2,1},{3,2},{4,3},{5,4},{6,5},{7,6},{0,7},{9,8},{10,9},{11,1... | collective-permute-start | bytes 98312 | tf_op jit(solution)/shard_map/ppermute | solution.py:24
  39.9 0.5 add_divide_fusion
  40.4 0.3 pad_maximum_fusion.10
  40.7 3.5 %collective-permute-start.5 = (f32[4,4,4,2048]{3,2,1,0:T(4,128)S(1)}, f32[4,4,4,2048]{3,2,1,0:T(4,128)S(1)}, u32[]{:S(2)}, u32[]{:S(2)}) collective-permute-start(f32[4,4,4,2048]{3,2,1,0:T(4,128)S(1)} %get-tuple-element.58), channel_id=1, source_target_pairs={{1,0},{2,1},{3,2},{4,3},{5,4},{6,5},{7,6},{0,7},{9,8},{10,9},{11,1... | collective-permute-start | bytes 1572872 | tf_op jit(solution)/shard_map/ppermute | solution.py:24
  45.1 11.2 %collective-permute-done.4 = f32[4,4,4,2048]{3,2,1,0:T(4,128)S(1)} collective-permute-done((f32[4,4,4,2048]{3,2,1,0:T(4,128)S(1)}, f32[4,4,4,2048]{3,2,1,0:T(4,128)S(1)}, u32[]{:S(2)}, u32[]{:S(2)}) %collective-permute-start.4) | collective-permute-done | bytes 524320 | tf_op jit(solution)/shard_map/ppermute | solution.py:21
  56.2 0.6 pad_maximum_fusion
  57.1 0.3 slice.1129
  57.4 0.3 slice.1139
  57.9 0.3 fusion.75
  58.4 1.3 add_add_fusion.4
  59.7 0.4 subtract_add_fusion.4
  60.1 0.3 slice.1155
  60.3 0.3 slice.1164
  60.9 0.3 fusion.76
  61.4 1.3 subtract_add_fusion.3
  62.7 0.3 add_add_fusion.3
  63.0 0.3 slice.1189
  63.3 0.3 slice.1180
  63.9 0.3 fusion.79
  64.3 1.2 add_add_fusion.2
  65.5 0.4 subtract_add_fusion.2
  67.0 0.9 add_bitcast_fusion.1
  67.9 0.3 add_bitcast_fusion
  68.2 0.5 pad_maximum_fusion.6
  68.7 3.5 %collective-permute-start.9 = (f32[4,4,4,2048]{3,2,1,0:T(4,128)S(1)}, f32[4,4,4,2048]{3,2,1,0:T(4,128)S(1)}, u32[]{:S(2)}, u32[]{:S(2)}) collective-permute-start(f32[4,4,4,2048]{3,2,1,0:T(4,128)S(1)} %get-tuple-element.56), channel_id=1, source_target_pairs={{1,0},{2,1},{3,2},{4,3},{5,4},{6,5},{7,6},{0,7},{9,8},{10,9},{11,1... | collective-permute-start | bytes 1572872 | tf_op jit(solution)/shard_map/ppermute | solution.py:24
  72.3 10.4 %collective-permute-done.8 = f32[4,4,4,2048]{3,2,1,0:T(4,128)S(1)} collective-permute-done((f32[4,4,4,2048]{3,2,1,0:T(4,128)S(1)}, f32[4,4,4,2048]{3,2,1,0:T(4,128)S(1)}, u32[]{:S(2)}, u32[]{:S(2)}) %collective-permute-start.8) | collective-permute-done | bytes 524320 | tf_op jit(solution)/shard_map/ppermute | solution.py:21
  82.7 0.6 pad_maximum_fusion.1
  83.3 0.3 slice_bitcast_fusion.2
  83.6 0.3 slice.1226
  84.0 0.3 slice.1236
  84.4 0.3 fusion.81
  84.9 1.2 add_add_fusion.1
  86.1 0.4 subtract_add_fusion.1
  86.5 0.3 slice.1248
  87.0 0.3 slice.1257
  87.3 0.3 fusion.82
  87.8 1.3 subtract_add_fusion
  89.1 0.4 add_add_fusion
  89.4 0.3 slice.1278
  90.0 0.3 slice.1269
  90.3 0.4 fusion.152
  90.8 1.1 fusion.10
  91.9 2.0 %subtract_reduce_fusion.2 = (f32[16,2048]{1,0:T(8,128)S(1)}, f32[4,16,2048]{2,1,0:T(8,128)S(1)}, f32[4,16,2048]{2,1,0:T(8,128)S(1)}) fusion(f32[4]{0:T(128)S(1)} %get-tuple-element.148, f32[4]{0:T(128)S(1)} %get-tuple-element.147, f32[4,18,2048]{2,1,0:T(8,128)S(1)} %get-tuple-element.60, f32[4]{0:T(128)S(1)} %get-tuple-element.163, ...), kind=kLoop, calls=%fused_computation.199 | loop fusion | flops 4161536 | bytes 10616928 | tf_op jit(solution)/shard_map/reduce_sum | solution.py:174
  94.6 3.5 %collective-permute-start.11 = (f32[2,4,1,2048]{3,2,1,0:T(1,128)S(1)}, f32[2,4,1,2048]{3,2,1,0:T(1,128)S(1)}, u32[]{:S(2)}, u32[]{:S(2)}) collective-permute-start(f32[2,4,1,2048]{3,2,1,0:T(1,128)S(1)} %get-tuple-element.64), channel_id=1, source_target_pairs={{1,0},{2,1},{3,2},{4,3},{5,4},{6,5},{7,6},{0,7},{9,8},{10,9},{11,1... | collective-permute-start | bytes 196616 | tf_op jit(solution)/shard_map/ppermute | solution.py:24
  98.2 1.9 %collective-permute-done.10 = f32[2,4,1,2048]{3,2,1,0:T(1,128)S(1)} collective-permute-done((f32[2,4,1,2048]{3,2,1,0:T(1,128)S(1)}, f32[2,4,1,2048]{3,2,1,0:T(1,128)S(1)}, u32[]{:S(2)}, u32[]{:S(2)}) %collective-permute-start.10) | collective-permute-done | bytes 65568 | tf_op jit(solution)/shard_map/ppermute | solution.py:21
  100.4 0.6 subtract_reduce_fusion.1
  101.0 0.6 subtract_reduce_fusion
  101.6 0.8 pad_maximum_fusion.11
  102.4 24.9 %reduce-scatter.2.cloned.1.call-done = f32[3,16,512]{2,1,0:T(8,128)} async-done(((f32[3,16,2048]{2,1,0:T(8,128)}), f32[3,16,512]{2,1,0:T(8,128)}) %reduce-scatter.2.cloned.1.call-update) | async-done | bytes 98320 | tf_op jit(solution)/shard_map/reduce_scatter | solution.py:192
  (89 shorter events, 6.3 us)
Async XLA Ops:
  6.5 33.3 %copy-start.1 = (f32[4]{0:T(128)S(1)}, f32[4]{0:T(128)}, u32[]{:S(2)}) copy-start(f32[4]{0:T(128)} %param.7) | copy-start | bytes 52
  6.5 33.3 %copy-start = (f32[4]{0:T(128)S(1)}, f32[4]{0:T(128)}, u32[]{:S(2)}) copy-start(f32[4]{0:T(128)} %param.8) | copy-start | bytes 52
  6.5 120.8 %reduce-scatter.2.cloned.1.call-start = ((), (), s32[]{:S(2)}) async-start(), calls=%async_computation.1 | async-start | bytes 491520 | tf_op jit(solution)/shard_map/reduce_scatter | solution.py:192
  7.4 5.8 %collective-permute-start = (f32[4,16,1]{2,1,0:T(8,128)S(1)}, f32[4,16,1]{2,1,0:T(8,128)S(1)}, u32[]{:S(2)}, u32[]{:S(2)}) collective-permute-start(f32[4,16,1]{2,1,0:T(8,128)S(1)} %get-tuple-element.117), channel_id=1, source_target_pairs={{0,8},{8,16},{16,24},{24,0},{1,9},{9,17},{17,25},{25,1},{2,10},{10... | collective-permute-start | bytes 776 | tf_op jit(solution)/shard_map/ppermute | solution.py:21
  10.4 3.9 %collective-permute-start.1 = (f32[4,16,1]{2,1,0:T(8,128)S(1)}, f32[4,16,1]{2,1,0:T(8,128)S(1)}, u32[]{:S(2)}, u32[]{:S(2)}) collective-permute-start(f32[4,16,1]{2,1,0:T(8,128)S(1)} %get-tuple-element.118), channel_id=1, source_target_pairs={{8,0},{16,8},{24,16},{0,24},{9,1},{17,9},{25,17},{1,25},{10,2},{18... | collective-permute-start | bytes 776 | tf_op jit(solution)/shard_map/ppermute | solution.py:24
  15.3 4.9 %collective-permute-start.2 = (f32[4,1,514]{2,1,0:T(1,128)S(1)}, f32[4,1,514]{2,1,0:T(1,128)S(1)}, u32[]{:S(2)}, u32[]{:S(2)}) collective-permute-start(f32[4,1,514]{2,1,0:T(1,128)S(1)} %get-tuple-element.113), channel_id=1, source_target_pairs={{0,1},{1,2},{2,3},{3,4},{4,5},{5,6},{6,7},{7,0},{8,9},{9,10},{10,1... | collective-permute-start | bytes 24680 | tf_op jit(solution)/shard_map/ppermute | solution.py:21
  15.3 4.9 %collective-permute-start.3 = (f32[4,1,514]{2,1,0:T(1,128)S(1)}, f32[4,1,514]{2,1,0:T(1,128)S(1)}, u32[]{:S(2)}, u32[]{:S(2)}) collective-permute-start(f32[4,1,514]{2,1,0:T(1,128)S(1)} %get-tuple-element.114), channel_id=1, source_target_pairs={{1,0},{2,1},{3,2},{4,3},{5,4},{6,5},{7,6},{0,7},{9,8},{10,9},{11,1... | collective-permute-start | bytes 24680 | tf_op jit(solution)/shard_map/ppermute | solution.py:24
  36.2 8.1 %collective-permute-start.6 = (f32[4,2048]{1,0:T(4,128)S(1)}, f32[4,2048]{1,0:T(4,128)S(1)}, u32[]{:S(2)}, u32[]{:S(2)}) collective-permute-start(f32[4,2048]{1,0:T(4,128)S(1)} %get-tuple-element.74), channel_id=1, source_target_pairs={{0,1},{1,2},{2,3},{3,4},{4,5},{5,6},{6,7},{7,0},{8,9},{9,10},{10,1... | collective-permute-start | bytes 98312 | tf_op jit(solution)/shard_map/ppermute | solution.py:21
  36.2 8.0 %collective-permute-start.7 = (f32[4,2048]{1,0:T(4,128)S(1)}, f32[4,2048]{1,0:T(4,128)S(1)}, u32[]{:S(2)}, u32[]{:S(2)}) collective-permute-start(f32[4,2048]{1,0:T(4,128)S(1)} %get-tuple-element.75), channel_id=1, source_target_pairs={{1,0},{2,1},{3,2},{4,3},{5,4},{6,5},{7,6},{0,7},{9,8},{10,9},{11,1... | collective-permute-start | bytes 98312 | tf_op jit(solution)/shard_map/ppermute | solution.py:24
  40.6 15.6 %collective-permute-start.4 = (f32[4,4,4,2048]{3,2,1,0:T(4,128)S(1)}, f32[4,4,4,2048]{3,2,1,0:T(4,128)S(1)}, u32[]{:S(2)}, u32[]{:S(2)}) collective-permute-start(f32[4,4,4,2048]{3,2,1,0:T(4,128)S(1)} %get-tuple-element.57), channel_id=1, source_target_pairs={{0,1},{1,2},{2,3},{3,4},{4,5},{5,6},{6,7},{7,0},{8,9},{9,10},{10,1... | collective-permute-start | bytes 1572872 | tf_op jit(solution)/shard_map/ppermute | solution.py:21
  40.7 15.5 %collective-permute-start.5 = (f32[4,4,4,2048]{3,2,1,0:T(4,128)S(1)}, f32[4,4,4,2048]{3,2,1,0:T(4,128)S(1)}, u32[]{:S(2)}, u32[]{:S(2)}) collective-permute-start(f32[4,4,4,2048]{3,2,1,0:T(4,128)S(1)} %get-tuple-element.58), channel_id=1, source_target_pairs={{1,0},{2,1},{3,2},{4,3},{5,4},{6,5},{7,6},{0,7},{9,8},{10,9},{11,1... | collective-permute-start | bytes 1572872 | tf_op jit(solution)/shard_map/ppermute | solution.py:24
  67.9 4.4 %copy-start.2 = (f32[2,4]{1,0:T(2,128)S(1)}, f32[2,4]{1,0:T(2,128)}, u32[]{:S(2)}) copy-start(f32[2,4]{1,0:T(2,128)} %param.9) | copy-start | bytes 100
  68.7 14.0 %collective-permute-start.8 = (f32[4,4,4,2048]{3,2,1,0:T(4,128)S(1)}, f32[4,4,4,2048]{3,2,1,0:T(4,128)S(1)}, u32[]{:S(2)}, u32[]{:S(2)}) collective-permute-start(f32[4,4,4,2048]{3,2,1,0:T(4,128)S(1)} %get-tuple-element.55), channel_id=1, source_target_pairs={{0,1},{1,2},{2,3},{3,4},{4,5},{5,6},{6,7},{7,0},{8,9},{9,10},{10,1... | collective-permute-start | bytes 1572872 | tf_op jit(solution)/shard_map/ppermute | solution.py:21
  68.7 14.0 %collective-permute-start.9 = (f32[4,4,4,2048]{3,2,1,0:T(4,128)S(1)}, f32[4,4,4,2048]{3,2,1,0:T(4,128)S(1)}, u32[]{:S(2)}, u32[]{:S(2)}) collective-permute-start(f32[4,4,4,2048]{3,2,1,0:T(4,128)S(1)} %get-tuple-element.56), channel_id=1, source_target_pairs={{1,0},{2,1},{3,2},{4,3},{5,4},{6,5},{7,6},{0,7},{9,8},{10,9},{11,1... | collective-permute-start | bytes 1572872 | tf_op jit(solution)/shard_map/ppermute | solution.py:24
  94.5 5.5 %collective-permute-start.10 = (f32[2,4,1,2048]{3,2,1,0:T(1,128)S(1)}, f32[2,4,1,2048]{3,2,1,0:T(1,128)S(1)}, u32[]{:S(2)}, u32[]{:S(2)}) collective-permute-start(f32[2,4,1,2048]{3,2,1,0:T(1,128)S(1)} %get-tuple-element.63), channel_id=1, source_target_pairs={{0,1},{1,2},{2,3},{3,4},{4,5},{5,6},{6,7},{7,0},{8,9},{9,10},{10,1... | collective-permute-start | bytes 196616 | tf_op jit(solution)/shard_map/ppermute | solution.py:21
  94.6 5.5 %collective-permute-start.11 = (f32[2,4,1,2048]{3,2,1,0:T(1,128)S(1)}, f32[2,4,1,2048]{3,2,1,0:T(1,128)S(1)}, u32[]{:S(2)}, u32[]{:S(2)}) collective-permute-start(f32[2,4,1,2048]{3,2,1,0:T(1,128)S(1)} %get-tuple-element.64), channel_id=1, source_target_pairs={{1,0},{2,1},{3,2},{4,3},{5,4},{6,5},{7,6},{0,7},{9,8},{10,9},{11,1... | collective-permute-start | bytes 196616 | tf_op jit(solution)/shard_map/ppermute | solution.py:24
Sparse Core Ops, SparseCore 0:
  102.6 24.7 reduce-scatter.1
where the time goes:
time: 135 us; the launch traced here: 134 us
  waiting for transfers between devices  50.3 us (37%)
  other arithmetic  28.4 us (21%)
  starting transfers between devices  21.9 us (16%)
  between operations  14.1 us (10%)
  blocking collectives  12.8 us (9%)
  local copies, waits for them, and re-layouts  6.7 us (5%)
    reduce_scatter x1, waiting for transfers between devices, shards(): lax.psum_scatter(jnp.stack([out_height, out_east, out_north]), 'pole', sc...  24.9 us
    ppermute x6, waiting for transfers between devices, with_halo(): lax.ppermute(lax.slice_in_dim(block, block.shape[dim] - width, None, axis...  24.3 us
    ppermute x6, starting transfers between devices, with_halo(): lax.ppermute(lax.slice_in_dim(block, 0, width, axis=dim), axis, backward)  18.7 us
    all_gather x1, blocking collectives, shards(): strip = lax.all_gather(fields, 'pole', axis=2, tiled=True)  12.8 us
    add x10, other arithmetic, advance(): return (first_real + second_real, first_imaginary + second_imaginary)  8.07 us
    slice x28, local copies, waits for them, and re-layouts, band_stiffness(): jnp.roll(inner, -1, -1) - inner  3.83 us
    ppermute x6, starting transfers between devices, with_halo(): lax.ppermute(lax.slice_in_dim(block, block.shape[dim] - width, None, axis...  3.23 us
  transfers between devices with their start and end apart: 13, of which 7 were waited for; matrix products, arithmetic and copies ran while one was open for 3% of the time, Pallas kernels for 0%

commit v1 on v0

v1 whole, which is shorter than its diff:
```python
import functools

import jax
import jax.numpy as jnp
from jax import lax
from jax.experimental import pallas as pl
from jax.experimental.pallas import tpu as pltpu
from jax.sharding import PartitionSpec as P

ITERS = 8
REACH = ITERS + 1
SUB = 8
LANES = 128
SIDE = 32

coriolis = 0.7
centre = 8.0
half_width = 8.0


def pairs(count, phase):
    swap = []
    for i in range(phase, count + phase, 2):
        a, b = i % count, (i + 1) % count
        swap += [(a, b), (b, a)]
    return swap


def swap(block, axis, phase):
    return lax.ppermute(block, axis, pairs(lax.axis_size(axis), phase))


def shift(block, axis, step):
    count = lax.axis_size(axis)
    return lax.ppermute(block, axis, [(i, (i + step) % count) for i in range(count)])


def cmul(a, b):
    return (a[0] * b[0] - a[1] * b[1], a[0] * b[1] + a[1] * b[0])


def cinv(a):
    norm = 1.0 / (a[0] * a[0] + a[1] * a[1])
    return (a[0] * norm, -a[1] * norm)


def cscale(a, factor):
    return (a[0] * factor, a[1] * factor)


def pack_rows_kernel(state, depth, real, imag, weight, near, far, scalars):
    odd = lax.rem(lax.axis_index("tile"), 2) == 1
    rows = depth.shape[0]
    fields = [state.at[0], state.at[1], state.at[2], depth]
    for target, low in ((near, odd), (far, jnp.logical_not(odd))):
        @pl.when(low)
        def _():
            for f, field in enumerate(fields):
                target[f * SUB : (f + 1) * SUB] = field[0:SUB]
                target[4 * SUB + f : 4 * SUB + f + 1] = field[SUB : SUB + 1]

        @pl.when(jnp.logical_not(low))
        def _():
            for f, field in enumerate(fields):
                target[f * SUB : (f + 1) * SUB] = field[rows - SUB : rows]
                target[4 * SUB + f : 4 * SUB + f + 1] = field[rows - SUB - 1 : rows - SUB]

    poles = real.shape[0]
    values = [real[i] for i in range(poles)] + [imag[i] for i in range(poles)]
    values += [weight[0, i] for i in range(poles)] + [weight[1, i] for i in range(poles)]
    for i, value in enumerate(values):
        scalars[i : i + 1] = jnp.full((1, LANES), value, jnp.float32)


def column_block(fields, start):
    lane = lax.broadcasted_iota(jnp.int32, fields[0].shape, 1)
    total = None
    for f, field in enumerate(fields):
        turn = (SIDE * f - start) % LANES
        turned = pltpu.roll(field, turn, 1) if turn else field
        total = turned if total is None else jnp.where(lane < SIDE * f, total, turned)
    return total


def pack_columns_kernel(state, depth, near, far, scalars, first, second):
    odd = lax.rem(lax.axis_index("pole"), 2) == 1
    rows, columns = depth.shape
    own = [state.at[0], state.at[1], state.at[2], depth]

    def edge(side):
        lanes = pl.ds(0, LANES) if side == 0 else pl.ds(columns - LANES, LANES)
        start = 0 if side == 0 else LANES - SIDE
        out = []
        for g in range(rows // SUB):
            out.append(column_block([field[pl.ds(g * SUB, SUB), lanes] for field in own], start))
        for halo in (near, far):
            out.append(
                column_block([halo[pl.ds(f * SUB, SUB), lanes] for f in range(4)], start)
            )
        ext = jnp.concatenate(
            [near[pl.ds(4 * SUB, 4), lanes], far[pl.ds(4 * SUB, 4), lanes]], axis=0
        )
        out.append(pltpu.roll(ext, SIDE, 1) if start else ext)
        return out

    left = edge(0)
    right = edge(1)
    for i, (a, b) in enumerate(zip(left, right)):
        first[pl.ds(i * SUB, SUB)] = jnp.where(odd, a, b)
        second[pl.ds(i * SUB, SUB)] = jnp.where(odd, b, a)
    base = len(left) * SUB
    first[pl.ds(base, scalars.shape[0])] = scalars[...]
    second[pl.ds(base, scalars.shape[0])] = scalars[...]


def strips_of(tiles, west, east):
    lane = lax.broadcasted_iota(jnp.int32, (SUB, LANES), 1)
    up = [pltpu.roll(tile, SIDE, 1) for tile in tiles]
    down = [pltpu.roll(tile, LANES - SIDE, 1) for tile in tiles]
    out = []
    for q in range(len(tiles)):
        out.append(jnp.where(lane < SIDE, up[q - 1] if q else west, up[q]))
        after = down[q + 1] if q + 1 < len(tiles) else east
        out.append(jnp.where(lane < LANES - SIDE, down[q], after))
    return out


def step_kernel(state, depth, near, far, first, second, scalars, others, out, grid, poly, coef, result):
    rows, columns = depth.shape
    groups = rows // SUB
    tiles = columns // LANES
    odd_pole = lax.rem(lax.axis_index("pole"), 2) == 1
    odd_tile = lax.rem(lax.axis_index("tile"), 2) == 1
    own = [state.at[0], state.at[1], state.at[2], depth]

    def sides(index):
        one = first[pl.ds(index * SUB, SUB)]
        two = second[pl.ds(index * SUB, SUB)]
        return jnp.where(odd_pole, one, two), jnp.where(odd_pole, two, one)

    def turned(block, turn):
        return pltpu.roll(block, turn % LANES, 1) if turn % LANES else block

    def lay(block, west, east, f, at, size, stride):
        cut = [block[:, t * LANES : (t + 1) * LANES] for t in range(tiles)]
        strips = strips_of(cut, turned(west, -SIDE * f), turned(east, LANES - SIDE - SIDE * f))
        for s, strip in enumerate(strips):
            grid[pl.Slice(at * SUB + s, size, stride * SUB), :] = strip[0:size]

    for g in range(groups):
        west, east = sides(g)
        for f in range(4):
            block = own[f][pl.ds(g * SUB, SUB), :]
            lay(block, west, east, f, (REACH + g * SUB) * 4 + f, SUB, 4)
    below = REACH + rows
    near_main = jnp.where(odd_tile, 1, below)
    far_main = jnp.where(odd_tile, below, 1)
    near_ext = jnp.where(odd_tile, 0, below + SUB)
    far_ext = jnp.where(odd_tile, below + SUB, 0)
    for i, (halo, main) in enumerate(((near, near_main), (far, far_main))):
        west, east = sides(groups + i)
        for f in range(4):
            lay(halo[pl.ds(f * SUB, SUB), :], west, east, f, main * 4 + f, SUB, 4)
    west, east = sides(groups + 2)
    lay(near[pl.ds(4 * SUB, SUB), :], west, east, 0, near_ext * 4, 4, 1)
    west = pltpu.roll(west, 4, 0)
    east = pltpu.roll(east, 4, 0)
    lay(far[pl.ds(4 * SUB, SUB), :], west, east, 0, far_ext * 4, 4, 1)

    def cell(f, r):
        return grid[pl.ds((r * 4 + f) * SUB, SUB), :]

    def left(x):
        return pltpu.roll(x, 1, 1)

    def right(x):
        return pltpu.roll(x, LANES - 1, 1)

    height = rows + 2 * REACH

    across = {}
    flux_east = {}
    flux_north = {}
    for r in range(height):
        h = cell(3, r)
        flux_east[r] = h * cell(1, r)
        flux_north[r] = h * cell(2, r)
        if r < height - 1:
            across[r] = 0.125 * (h + cell(3, r + 1))
            coef[0, r] = across[r]
        if 1 <= r < height - 1:
            north = 0.125 * (h + right(h))
            south = left(north)
            coef[1, r] = north
            coef[2, r] = south
            coef[3, r] = 2.0 - ((across[r] + across[r - 1]) + (north + south))
        if r >= 2:
            c = r - 1
            east_slope = flux_east[r] - flux_east[r - 2]
            north_slope = right(flux_north[c]) - left(flux_north[c])
            poly[1, 0, c] = 0.5 * (east_slope + north_slope)
            east_slope = flux_north[r] - flux_north[r - 2]
            north_slope = right(flux_east[c]) - left(flux_east[c])
            poly[2, 0, c] = 0.5 * (east_slope - north_slope)
            poly[0, 0, c] = cell(0, c)

    blocks = [scalars[...], first[pl.ds((groups + 3) * SUB, scalars.shape[0])]]
    blocks += [second[pl.ds((groups + 3) * SUB, scalars.shape[0])]]
    blocks += [others[i] for i in range(others.shape[0])]
    poles = scalars.shape[0] // 4
    quantity = []
    for q in range(4):
        cut = [b[q * poles : (q + 1) * poles] for b in blocks]
        quantity.append(jnp.concatenate(cut, axis=0))
    alpha = (quantity[0], quantity[1])
    beta = (quantity[2], quantity[3])
    square = cmul(alpha, alpha)
    shifted = (square[0] + coriolis * coriolis, square[1])
    sigma = ((shifted[0] + centre) / half_width, shifted[1] / half_width)
    rho = [cinv(sigma)]
    for j in range(1, ITERS):
        rho.append(cinv((2.0 * sigma[0] - rho[-1][0], 2.0 * sigma[1] - rho[-1][1])))
    gain = None
    start = []
    for m in range(ITERS):
        if m == 0:
            start.append(cscale(rho[0], 1.0 / half_width))
        else:
            gain = rho[0] if gain is None else cmul(gain, rho[m - 1])
            start.append(cscale(cmul(rho[m], gain), 2.0 / half_width))
    tail = None
    weight = [None] * ITERS
    for m in reversed(range(ITERS)):
        if tail is None:
            weight[m] = start[m]
            tail = (jnp.ones_like(sigma[0]), jnp.zeros_like(sigma[0]))
        else:
            tail = cmul(cmul(rho[m + 1], rho[m]), tail)
            tail = (tail[0] + 1.0, tail[1])
            weight[m] = cmul(start[m], tail)
    inverse_alpha = cinv(alpha)
    inverse_shift = cinv(shifted)
    by_alpha = cmul(beta, inverse_alpha)
    by_shift = cmul(beta, inverse_shift)
    products = {
        "b": beta,
        "b/a": by_alpha,
        "b/s": by_shift,
        "bs/a": cmul(by_alpha, shifted),
        "ba/s": cmul(by_shift, alpha),
        "b/as": cmul(by_alpha, inverse_shift),
    }

    def total(x):
        s = x[0:SUB]
        for i in range(1, x.shape[0] // SUB):
            s = s + x[i * SUB : (i + 1) * SUB]
        for turn in (4, 2, 1):
            s = s + pltpu.roll(s, turn, 0)
        return s

    names = [("bs/a", "b", "b/a"), ("b", "ba/s", "b/s"), ("b/a", "b/s", "b/as")]
    factor = (1.0, -1.0, -coriolis)
    sums = {}
    for name in products:
        for m in range(ITERS):
            w = products[name]
            sums[name, m] = total(w[0] * weight[m][0] - w[1] * weight[m][1])
    push = total(products["ba/s"][0])
    lift = coriolis * total(products["b/s"][0])

    for m in range(ITERS - 1):
        for r in range(m + 2, height - m - 2):
            above, below_, north, south, diag = (
                coef[0, r],
                coef[0, r - 1],
                coef[1, r],
                coef[2, r],
                coef[3, r],
            )
            for f in range(3):
                w = poly[f, m, r]
                value = diag * w + (above * poly[f, m, r + 1] + below_ * poly[f, m, r - 1])
                value = value + (north * right(w) + south * left(w))
                if m == 0:
                    value = 0.5 * value
                else:
                    value = value - poly[f, m - 1, r]
                poly[f, m + 1, r] = value

    sol = {}
    for r in range(REACH - 1, REACH + rows + 1):
        for g in range(3):
            if g == 0 and not REACH <= r < REACH + rows:
                continue
            acc = None
            for f in range(3):
                part = None
                for m in range(ITERS):
                    term = sums[names[g][f], m] * poly[f, m, r]
                    part = term if part is None else part + term
                part = part if f == 0 else factor[f] * part
                acc = part if acc is None else acc + part
            sol[g, r] = acc
    for i in range(rows):
        r = REACH + i
        u, v = cell(1, r), cell(2, r)
        result[0, pl.ds(i * SUB, SUB)] = sol[0, r]
        east = 0.5 * (sol[1, r + 1] - sol[1, r - 1])
        north = 0.5 * (right(sol[2, r]) - left(sol[2, r]))
        result[1, pl.ds(i * SUB, SUB)] = (push * u + lift * v) - (east + coriolis * north)
        east = 0.5 * (sol[2, r + 1] - sol[2, r - 1])
        north = 0.5 * (right(sol[1, r]) - left(sol[1, r]))
        result[2, pl.ds(i * SUB, SUB)] = (push * v - lift * u) + (coriolis * east - north)

    lane = lax.broadcasted_iota(jnp.int32, (SUB, LANES), 1)
    for k in range(3):
        for g in range(groups):
            for t in range(tiles):
                one = result[k, pl.Slice(g * SUB * SUB + 2 * t, SUB, SUB), :]
                two = result[k, pl.Slice(g * SUB * SUB + 2 * t + 1, SUB, SUB), :]
                joined = jnp.where(
                    lane < LANES // 2, pltpu.roll(one, LANES - SIDE, 1), pltpu.roll(two, SIDE, 1)
                )
                out[k, pl.ds(g * SUB, SUB), pl.ds(t * LANES, LANES)] = joined


def shards(state, depth, pole_real, pole_imag, pole_weight):
    rows, columns = depth.shape
    poles = pole_real.shape[0]
    vmem = pl.BlockSpec(memory_space=pltpu.VMEM)
    smem = pl.BlockSpec(memory_space=pltpu.SMEM)
    f32 = jnp.float32
    halo = jax.ShapeDtypeStruct((5 * SUB, columns), f32)
    near, far, scalars = pl.pallas_call(
        pack_rows_kernel,
        out_shape=(halo, halo, jax.ShapeDtypeStruct((4 * poles, LANES), f32)),
        in_specs=[vmem, vmem, smem, smem, smem],
        out_specs=(vmem, vmem, vmem),
        name="pack_rows",
    )(state, depth, pole_real, pole_imag, pole_weight)
    far = swap(far, "tile", 1)
    near = swap(near, "tile", 0)
    count = lax.axis_size("pole")
    others = jnp.stack([shift(scalars, "pole", step) for step in range(2, count - 1)])
    block_rows = (rows // SUB + 3) * SUB + 4 * poles
    block = jax.ShapeDtypeStruct((block_rows, LANES), f32)
    first, second = pl.pallas_call(
        pack_columns_kernel,
        out_shape=(block, block),
        in_specs=[vmem] * 5,
        out_specs=(vmem, vmem),
        name="pack_columns",
    )(state, depth, near, far, scalars)
    first = swap(first, "pole", 0)
    second = swap(second, "pole", 1)
    height = rows + 2 * REACH
    return pl.pallas_call(
        step_kernel,
        out_shape=jax.ShapeDtypeStruct(state.shape, f32),
        in_specs=[vmem] * 8,
        out_specs=vmem,
        scratch_shapes=[
            pltpu.VMEM((height * 4 * SUB, LANES), f32),
            pltpu.VMEM((3, ITERS, height, SUB, LANES), f32),
            pltpu.VMEM((4, height, SUB, LANES), f32),
            pltpu.VMEM((3, rows * SUB, LANES), f32),
        ],
        compiler_params=pltpu.CompilerParams(vmem_limit_bytes=32 * 1024 * 1024),
        name="step",
    )(state, depth, near, far, first, second, scalars, others)


def solution(mesh):
    return jax.shard_map(
        shards,
        mesh=mesh,
        in_specs=(
            P(None, "tile", "pole"),
            P("tile", "pole"),
            P("pole"),
            P("pole"),
            P(None, "pole"),
        ),
        out_specs=P(None, "tile", "pole"),
        check_vma=False,
    )
```

time: 135 us -> 23.4 us (0.17)
  waiting for transfers between devices: 50.3 us -> 5.65 us
  other arithmetic: 28.4 us -> 0 us
  between operations: 14.1 us -> 0.03 us
  starting transfers between devices: 21.9 us -> 8.65 us
  blocking collectives: 12.8 us -> 0 us
  Pallas kernels: 0 us -> 6.39 us
  local copies, waits for them, and re-layouts: 6.7 us -> 2.4 us
    reduce_scatter x1 -> x0, waiting for transfers between devices: 24.9 us -> none  [shards(): lax.psum_scatter(jnp.stack([out_height, out_east, out_north]), 'pole', sc...]
    ppermute x12 -> x5, waiting for transfers between devices: 25.4 us -> 5.65 us  [the longest x1 3.14 us: shift(): lax.ppermute(block, axis, [(i, (i + step) % count) for i in range(count)])]
    ppermute x12 -> x5, starting transfers between devices: 21.9 us -> 8.65 us  [the longest x4 8.15 us: swap(): return lax.ppermute(block, axis, pairs(lax.axis_size(axis), phase))]
    all_gather x1 -> x0, blocking collectives: 12.8 us -> none  [shards(): strip = lax.all_gather(fields, 'pole', axis=2, tiled=True)]
    add x11 -> x0, other arithmetic: 8.83 us -> none  [the longest x10 8.07 us: advance(): return (first_real + second_real, first_imaginary + second_imaginary)]
    pallas_call x0 -> x3, Pallas kernels: none -> 6.39 us  [the longest x1 3.04 us: shards(): pl.pallas_call(step_kernel, out_shape=jax.ShapeDtypeStruct(state.shape, f...]
    slice x52 -> x0, local copies, waits for them, and re-layouts: 6 us -> none  [the longest x28 3.83 us: band_stiffness(): jnp.roll(inner, -1, -1) - inner]
    mul x24 -> x0, other arithmetic: 5.6 us -> none  [the longest x9 2.07 us: band_stiffness(): 0.5 * (depth_inner + jnp.roll(depth_inner, -1, -1))]
  transfers between devices with their start and end apart: 13 -> 5, of which waited for: 7 -> 2; matrix products, arithmetic and copies ran while one was open for 3% -> 0% of each run, Pallas kernels for 0% -> 0%
where the time goes in v1:
time: 23.4 us; the launch traced here: 23.1 us
  starting transfers between devices  8.65 us (37%)
  Pallas kernels  6.39 us (27%)
  waiting for transfers between devices  5.65 us (24%)
  local copies, waits for them, and re-layouts  2.4 us (10%)
    ppermute x4, starting transfers between devices, swap(): return lax.ppermute(block, axis, pairs(lax.axis_size(axis), phase))  8.15 us
    ppermute x1, waiting for transfers between devices, shift(): lax.ppermute(block, axis, [(i, (i + step) % count) for i in range(count)])  3.14 us
    pallas_call x1, Pallas kernels, shards(): pl.pallas_call(step_kernel, out_shape=jax.ShapeDtypeStruct(state.shape, f...  3.04 us
    ppermute x4, waiting for transfers between devices, swap(): return lax.ppermute(block, axis, pairs(lax.axis_size(axis), phase))  2.51 us
    unnamed x14, local copies, waits for them, and re-layouts  2.4 us
    pallas_call x1, Pallas kernels, shards(): pl.pallas_call(pack_columns_kernel, out_shape=(block, block), in_specs=[v...  1.75 us
    pallas_call x1, Pallas kernels, shards(): pl.pallas_call(pack_rows_kernel, out_shape=(halo, halo, jax.ShapeDtypeStr...  1.6 us
    ppermute x1, starting transfers between devices, shift(): lax.ppermute(block, axis, [(i, (i + step) % count) for i in range(count)])  0.51 us
  transfers between devices with their start and end apart: 5, of which 2 were waited for; matrix products, arithmetic and copies ran while one was open for 0% of the time, Pallas kernels for 0%

profile of v1, /device:TPU:0, one launch (start us, length us, event | category | flops | bytes accessed | tf_op | source)
XLA Modules:
  0.0 23.1 jit_solution(14633915803032604360)
XLA Ops:
  0.0 1.6 %pack_rows.1 = (f32[40,512]{1,0:T(8,128)}, f32[40,512]{1,0:T(8,128)}, f32[16,128]{1,0:T(8,128)}) custom-call(f32[3,16,512]{2,1,0:T(8,128)} %state.5, f32[16,512]{1,0:T(8,128)} %depth.5, f32[4]{0:T(128)} %real.1, f32[4]{0:T(128)} %imag.1, f32[2,4]{1,0:T(2,128)} %weight.1), custom_call_target="tpu_custom_call" | custom-call | tf_op jit(solution)/shard_map/pack_rows/pallas_call | solution.py:335
  1.6 0.5 %collective-permute-start = (f32[40,512]{1,0:T(8,128)}, f32[40,512]{1,0:T(8,128)S(1)}, u32[]{:S(2)}, u32[]{:S(2)}) collective-permute-start(f32[40,512]{1,0:T(8,128)} %get-tuple-element.10), channel_id=1, source_target_pairs={{0,1},{1,0},{2,3},{3,2},{4,5},{5,4},{6,7},{7,6},{8,9},{9,8},{10,11... | collective-permute-start | bytes 245768 | tf_op jit(solution)/shard_map/ppermute | solution.py:30
  2.1 4.7 %collective-permute-start.1 = (f32[40,512]{1,0:T(8,128)}, f32[40,512]{1,0:T(8,128)S(1)}, u32[]{:S(2)}, u32[]{:S(2)}) collective-permute-start(f32[40,512]{1,0:T(8,128)} %get-tuple-element.11), channel_id=1, source_target_pairs={{1,2},{2,1},{3,4},{4,3},{5,6},{6,5},{7,0},{0,7},{9,10},{10,9},{11,... | collective-permute-start | bytes 245768 | tf_op jit(solution)/shard_map/ppermute | solution.py:30
  6.8 0.0 collective-permute-done.near
  6.8 0.0 copy-start.1
  6.8 2.5 %collective-permute-done.1.far = f32[40,512]{1,0:T(8,128)S(1)} collective-permute-done((f32[40,512]{1,0:T(8,128)}, f32[40,512]{1,0:T(8,128)S(1)}, u32[]{:S(2)}, u32[]{:S(2)}) %collective-permute-start.1) | collective-permute-done | bytes 81952 | tf_op jit(solution)/shard_map/ppermute | solution.py:30
  9.3 0.0 copy-start.3
  9.3 0.0 copy-done.1
  9.3 0.6 %copy-done.3 = f32[40,512]{1,0:T(8,128)} copy-done((f32[40,512]{1,0:T(8,128)}, f32[40,512]{1,0:T(8,128)S(1)}, u32[]{:S(2)}) %copy-start.3) | copy-done | bytes 81944
  9.9 0.0 copy-start.6
  9.9 0.0 copy-start
  9.9 0.0 copy-start.5
  9.9 1.8 %pack_columns.1 = (f32[56,128]{1,0:T(8,128)}, f32[56,128]{1,0:T(8,128)}) custom-call(f32[3,16,512]{2,1,0:T(8,128)} %state.5, f32[16,512]{1,0:T(8,128)} %depth.5, f32[40,512]{1,0:T(8,128)} %copy-done.1, f32[40,512]{1,0:T(8,128)} %copy-done.3, f32[16,128]{1,0:T(8,128)} %get-tuple-element.12.scalars), custom_call_target="tpu_custom_call" | custom-call | tf_op jit(solution)/shard_map/pack_columns/pallas_call | solution.py:348
  11.7 1.5 %collective-permute-start.2 = (f32[56,128]{1,0:T(8,128)}, f32[56,128]{1,0:T(8,128)S(1)}, u32[]{:S(2)}, u32[]{:S(2)}) collective-permute-start(f32[56,128]{1,0:T(8,128)} %get-tuple-element.13), channel_id=1, source_target_pairs={{0,8},{8,0},{16,24},{24,16},{1,9},{9,1},{17,25},{25,17},{2,10},{10... | collective-permute-start | bytes 86024 | tf_op jit(solution)/shard_map/ppermute | solution.py:30
  13.2 1.5 %collective-permute-start.3 = (f32[56,128]{1,0:T(8,128)}, f32[56,128]{1,0:T(8,128)S(1)}, u32[]{:S(2)}, u32[]{:S(2)}) collective-permute-start(f32[56,128]{1,0:T(8,128)} %get-tuple-element.14), channel_id=1, source_target_pairs={{8,16},{16,8},{24,0},{0,24},{9,17},{17,9},{25,1},{1,25},{10,18},{1... | collective-permute-start | bytes 86024 | tf_op jit(solution)/shard_map/ppermute | solution.py:30
  14.6 0.0 copy-done.6
  14.6 0.5 %collective-permute-start.4 = (f32[16,128]{1,0:T(8,128)S(1)}, f32[16,128]{1,0:T(8,128)S(1)}, u32[]{:S(2)}, u32[]{:S(2)}) collective-permute-start(f32[16,128]{1,0:T(8,128)S(1)} %copy-done.6), channel_id=1, source_target_pairs={{0,16},{8,24},{16,0},{24,8},{1,17},{9,25},{17,1},{25,9},{2,18},{10... | collective-permute-start | bytes 24584 | tf_op jit(solution)/shard_map/ppermute | solution.py:35
  15.2 3.1 %collective-permute-done.4 = f32[16,128]{1,0:T(8,128)S(1)} collective-permute-done((f32[16,128]{1,0:T(8,128)S(1)}, f32[16,128]{1,0:T(8,128)S(1)}, u32[]{:S(2)}, u32[]{:S(2)}) %collective-permute-start.4) | collective-permute-done | bytes 8224 | tf_op jit(solution)/shard_map/ppermute | solution.py:35
  18.3 0.0 collective-permute-done.2.first
  18.3 0.0 collective-permute-done.3.second
  18.3 0.0 copy-done
  18.3 0.0 copy-done.5
  18.3 0.0 copy-start.2
  18.3 0.9 %copy-done.2 = f32[40,512]{1,0:T(8,128)S(1)} copy-done((f32[40,512]{1,0:T(8,128)S(1)}, f32[40,512]{1,0:T(8,128)}, u32[]{:S(2)}) %copy-start.2) | copy-done | bytes 81944
  19.2 0.0 copy-start.4
  19.2 0.9 %copy-done.4 = f32[40,512]{1,0:T(8,128)S(1)} copy-done((f32[40,512]{1,0:T(8,128)S(1)}, f32[40,512]{1,0:T(8,128)}, u32[]{:S(2)}) %copy-start.4) | copy-done | bytes 81944
  20.1 3.0 %step.1 = f32[3,16,512]{2,1,0:T(8,128)} custom-call(f32[3,16,512]{2,1,0:T(8,128)S(1)} %copy-done, f32[16,512]{1,0:T(8,128)S(1)} %copy-done.5, f32[40,512]{1,0:T(8,128)S(1)} %copy-done.2, f32[40,512]{1,0:T(8,128)S(1)} %copy-done.4, f32[56,128]{1,0:T(8,128)S(1)} %collective-permute-done.2.first, f32[56,128]{1,0:T(8,128)S(1)} %collective-permute-done.3.second, ...), custom_call_target="tpu_custom_call" | custom-call | tf_op jit(solution)/shard_map/step/pallas_call | solution.py:358
Async XLA Ops:
  1.6 5.2 %collective-permute-start = (f32[40,512]{1,0:T(8,128)}, f32[40,512]{1,0:T(8,128)S(1)}, u32[]{:S(2)}, u32[]{:S(2)}) collective-permute-start(f32[40,512]{1,0:T(8,128)} %get-tuple-element.10), channel_id=1, source_target_pairs={{0,1},{1,0},{2,3},{3,2},{4,5},{5,4},{6,7},{7,6},{8,9},{9,8},{10,11... | collective-permute-start | bytes 245768 | tf_op jit(solution)/shard_map/ppermute | solution.py:30
  2.1 7.2 %collective-permute-start.1 = (f32[40,512]{1,0:T(8,128)}, f32[40,512]{1,0:T(8,128)S(1)}, u32[]{:S(2)}, u32[]{:S(2)}) collective-permute-start(f32[40,512]{1,0:T(8,128)} %get-tuple-element.11), channel_id=1, source_target_pairs={{1,2},{2,1},{3,4},{4,3},{5,6},{6,5},{7,0},{0,7},{9,10},{10,9},{11,... | collective-permute-start | bytes 245768 | tf_op jit(solution)/shard_map/ppermute | solution.py:30
  6.8 2.5 %copy-start.1 = (f32[40,512]{1,0:T(8,128)}, f32[40,512]{1,0:T(8,128)S(1)}, u32[]{:S(2)}) copy-start(f32[40,512]{1,0:T(8,128)S(1)} %collective-permute-done.near) | copy-start | bytes 245764
  9.3 0.6 %copy-start.3 = (f32[40,512]{1,0:T(8,128)}, f32[40,512]{1,0:T(8,128)S(1)}, u32[]{:S(2)}) copy-start(f32[40,512]{1,0:T(8,128)S(1)} %collective-permute-done.1.far) | copy-start | bytes 245764
  9.9 4.7 %copy-start.6 = (f32[16,128]{1,0:T(8,128)S(1)}, f32[16,128]{1,0:T(8,128)}, u32[]{:S(2)}) copy-start(f32[16,128]{1,0:T(8,128)} %get-tuple-element.12.scalars) | copy-start | bytes 24580
  9.9 8.4 %copy-start = (f32[3,16,512]{2,1,0:T(8,128)S(1)}, f32[3,16,512]{2,1,0:T(8,128)}, u32[]{:S(2)}) copy-start(f32[3,16,512]{2,1,0:T(8,128)} %state.5) | copy-start | bytes 294916
  9.9 8.4 %copy-start.5 = (f32[16,512]{1,0:T(8,128)S(1)}, f32[16,512]{1,0:T(8,128)}, u32[]{:S(2)}) copy-start(f32[16,512]{1,0:T(8,128)} %depth.5) | copy-start | bytes 98308
  11.7 6.6 %collective-permute-start.2 = (f32[56,128]{1,0:T(8,128)}, f32[56,128]{1,0:T(8,128)S(1)}, u32[]{:S(2)}, u32[]{:S(2)}) collective-permute-start(f32[56,128]{1,0:T(8,128)} %get-tuple-element.13), channel_id=1, source_target_pairs={{0,8},{8,0},{16,24},{24,16},{1,9},{9,1},{17,25},{25,17},{2,10},{10... | collective-permute-start | bytes 86024 | tf_op jit(solution)/shard_map/ppermute | solution.py:30
  13.2 5.2 %collective-permute-start.3 = (f32[56,128]{1,0:T(8,128)}, f32[56,128]{1,0:T(8,128)S(1)}, u32[]{:S(2)}, u32[]{:S(2)}) collective-permute-start(f32[56,128]{1,0:T(8,128)} %get-tuple-element.14), channel_id=1, source_target_pairs={{8,16},{16,8},{24,0},{0,24},{9,17},{17,9},{25,1},{1,25},{10,18},{1... | collective-permute-start | bytes 86024 | tf_op jit(solution)/shard_map/ppermute | solution.py:30
  14.6 3.7 %collective-permute-start.4 = (f32[16,128]{1,0:T(8,128)S(1)}, f32[16,128]{1,0:T(8,128)S(1)}, u32[]{:S(2)}, u32[]{:S(2)}) collective-permute-start(f32[16,128]{1,0:T(8,128)S(1)} %copy-done.6), channel_id=1, source_target_pairs={{0,16},{8,24},{16,0},{24,8},{1,17},{9,25},{17,1},{25,9},{2,18},{10... | collective-permute-start | bytes 24584 | tf_op jit(solution)/shard_map/ppermute | solution.py:35
  18.3 0.9 %copy-start.2 = (f32[40,512]{1,0:T(8,128)S(1)}, f32[40,512]{1,0:T(8,128)}, u32[]{:S(2)}) copy-start(f32[40,512]{1,0:T(8,128)} %copy-done.1) | copy-start | bytes 245764
  19.2 0.9 %copy-start.4 = (f32[40,512]{1,0:T(8,128)S(1)}, f32[40,512]{1,0:T(8,128)}, u32[]{:S(2)}) copy-start(f32[40,512]{1,0:T(8,128)} %copy-done.3) | copy-start | bytes 245764

commit v2 on v1

--- a/solution.py
+++ b/solution.py
@@ -11,6 +11,7 @@
 REACH = ITERS + 1
 SUB = 8
 LANES = 128
+GRANT = 16 * 1024 * 1024
 SIDE = 32
 
 coriolis = 0.7
@@ -48,7 +49,7 @@
     return (a[0] * factor, a[1] * factor)
 
 
-def pack_rows_kernel(state, depth, real, imag, weight, near, far, scalars):
+def pack_rows_kernel(state, depth, real, imag, weight, far, near, scalars):
     odd = lax.rem(lax.axis_index("tile"), 2) == 1
     rows = depth.shape[0]
     fields = [state.at[0], state.at[1], state.at[2], depth]
@@ -332,11 +333,12 @@
     smem = pl.BlockSpec(memory_space=pltpu.SMEM)
     f32 = jnp.float32
     halo = jax.ShapeDtypeStruct((5 * SUB, columns), f32)
-    near, far, scalars = pl.pallas_call(
+    far, near, scalars = pl.pallas_call(
         pack_rows_kernel,
         out_shape=(halo, halo, jax.ShapeDtypeStruct((4 * poles, LANES), f32)),
         in_specs=[vmem, vmem, smem, smem, smem],
         out_specs=(vmem, vmem, vmem),
+        compiler_params=pltpu.CompilerParams(vmem_limit_bytes=GRANT),
         name="pack_rows",
     )(state, depth, pole_real, pole_imag, pole_weight)
     far = swap(far, "tile", 1)
@@ -350,6 +352,7 @@
         out_shape=(block, block),
         in_specs=[vmem] * 5,
         out_specs=(vmem, vmem),
+        compiler_params=pltpu.CompilerParams(vmem_limit_bytes=GRANT),
         name="pack_columns",
     )(state, depth, near, far, scalars)
     first = swap(first, "pole", 0)
@@ -366,7 +369,7 @@
             pltpu.VMEM((4, height, SUB, LANES), f32),
             pltpu.VMEM((3, rows * SUB, LANES), f32),
         ],
-        compiler_params=pltpu.CompilerParams(vmem_limit_bytes=32 * 1024 * 1024),
+        compiler_params=pltpu.CompilerParams(vmem_limit_bytes=GRANT),
         name="step",
     )(state, depth, near, far, first, second, scalars, others)
 

time: 23.4 us -> 21.9 us (0.936)
  Pallas kernels: 6.39 us -> 3.72 us
  local copies, waits for them, and re-layouts: 2.4 us -> 3.64 us
    pallas_call x1, Pallas kernels: 1.75 us -> 0.09 us  [shards(): pl.pallas_call(pack_columns_kernel, out_shape=(block, block), in_specs=[v...]
    unnamed x14 -> x10, local copies, waits for them, and re-layouts: 2.4 us -> 3.64 us
    pallas_call x1, Pallas kernels: 1.6 us -> 0.59 us  [shards(): pl.pallas_call(pack_rows_kernel, out_shape=(halo, halo, jax.ShapeDtypeStr...]
where the time goes in v2:
time: 21.9 us; the launch traced here: 21.6 us
  starting transfers between devices  8.78 us (40%)
  waiting for transfers between devices  5.45 us (25%)
  Pallas kernels  3.72 us (17%)
  local copies, waits for them, and re-layouts  3.64 us (17%)
    ppermute x4, starting transfers between devices, swap(): return lax.ppermute(block, axis, pairs(lax.axis_size(axis), phase))  8.28 us
    unnamed x10, local copies, waits for them, and re-layouts  3.64 us
    ppermute x1, waiting for transfers between devices, shift(): lax.ppermute(block, axis, [(i, (i + step) % count) for i in range(count)])  3.14 us
    pallas_call x1, Pallas kernels, shards(): pl.pallas_call(step_kernel, out_shape=jax.ShapeDtypeStruct(state.shape, f...  3.04 us
    ppermute x4, waiting for transfers between devices, swap(): return lax.ppermute(block, axis, pairs(lax.axis_size(axis), phase))  2.3 us
    pallas_call x1, Pallas kernels, shards(): pl.pallas_call(pack_rows_kernel, out_shape=(halo, halo, jax.ShapeDtypeStr...  0.59 us
    ppermute x1, starting transfers between devices, shift(): lax.ppermute(block, axis, [(i, (i + step) % count) for i in range(count)])  0.51 us
  transfers between devices with their start and end apart: 5, of which 2 were waited for; matrix products, arithmetic and copies ran while one was open for 0% of the time, Pallas kernels for 0%

profile of v2, /device:TPU:0, one launch (start us, length us, event | category | flops | bytes accessed | tf_op | source)
XLA Modules:
  0.0 21.6 jit_solution(5421606808683743235)
XLA Ops:
  0.0 0.0 copy-start
  0.0 0.9 %copy-done = f32[3,16,512]{2,1,0:T(8,128)S(1)} copy-done((f32[3,16,512]{2,1,0:T(8,128)S(1)}, f32[3,16,512]{2,1,0:T(8,128)}, u32[]{:S(2)}) %copy-start) | copy-done | bytes 98328
  0.9 0.0 copy-start.1
  0.9 0.8 %copy-done.1 = f32[16,512]{1,0:T(8,128)S(1)} copy-done((f32[16,512]{1,0:T(8,128)S(1)}, f32[16,512]{1,0:T(8,128)}, u32[]{:S(2)}) %copy-start.1) | copy-done | bytes 32792
  1.7 0.0 copy-start.2
  1.7 0.7 %copy-done.2 = f32[2,4]{1,0:T(2,128)S(1)} copy-done((f32[2,4]{1,0:T(2,128)S(1)}, f32[2,4]{1,0:T(2,128)}, u32[]{:S(2)}) %copy-start.2) | copy-done | bytes 56
  2.3 0.0 copy-start.3
  2.3 0.7 %copy-done.3 = f32[4]{0:T(128)S(1)} copy-done((f32[4]{0:T(128)S(1)}, f32[4]{0:T(128)}, u32[]{:S(2)}) %copy-start.3) | copy-done | bytes 40
  3.0 0.0 copy-start.4
  3.0 0.7 %copy-done.4 = f32[4]{0:T(128)S(1)} copy-done((f32[4]{0:T(128)S(1)}, f32[4]{0:T(128)}, u32[]{:S(2)}) %copy-start.4) | copy-done | bytes 40
  3.6 0.6 %pack_rows.1 = (f32[40,512]{1,0:T(8,128)S(1)}, f32[40,512]{1,0:T(8,128)S(1)}, f32[16,128]{1,0:T(8,128)S(1)}) custom-call(f32[3,16,512]{2,1,0:T(8,128)S(1)} %copy-done, f32[16,512]{1,0:T(8,128)S(1)} %copy-done.1, f32[4]{0:T(128)S(1)} %copy-done.3, f32[4]{0:T(128)S(1)} %copy-done.4, f32[2,4]{1,0:T(2,128)S(1)} %copy-done.2), custom_call_target="tpu_custom_call" | custom-call | tf_op jit(solution)/shard_map/pack_rows/pallas_call | solution.py:336
  4.2 0.5 %collective-permute-start = (f32[40,512]{1,0:T(8,128)S(1)}, f32[40,512]{1,0:T(8,128)S(1)}, u32[]{:S(2)}, u32[]{:S(2)}) collective-permute-start(f32[40,512]{1,0:T(8,128)S(1)} %get-tuple-element.10), channel_id=1, source_target_pairs={{0,1},{1,0},{2,3},{3,2},{4,5},{5,4},{6,7},{7,6},{8,9},{9,8},{10,11... | collective-permute-start | bytes 245768 | tf_op jit(solution)/shard_map/ppermute | solution.py:31
  4.8 4.7 %collective-permute-start.1 = (f32[40,512]{1,0:T(8,128)S(1)}, f32[40,512]{1,0:T(8,128)S(1)}, u32[]{:S(2)}, u32[]{:S(2)}) collective-permute-start(f32[40,512]{1,0:T(8,128)S(1)} %get-tuple-element.11), channel_id=1, source_target_pairs={{1,2},{2,1},{3,4},{4,3},{5,6},{6,5},{7,0},{0,7},{9,10},{10,9},{11,... | collective-permute-start | bytes 245768 | tf_op jit(solution)/shard_map/ppermute | solution.py:31
  9.5 0.0 collective-permute-done.near
  9.5 2.3 %collective-permute-done.1.far = f32[40,512]{1,0:T(8,128)S(1)} collective-permute-done((f32[40,512]{1,0:T(8,128)S(1)}, f32[40,512]{1,0:T(8,128)S(1)}, u32[]{:S(2)}, u32[]{:S(2)}) %collective-permute-start.1) | collective-permute-done | bytes 81952 | tf_op jit(solution)/shard_map/ppermute | solution.py:31
  11.8 0.1 pack_columns.1
  11.9 1.6 %collective-permute-start.2 = (f32[56,128]{1,0:T(8,128)S(1)}, f32[56,128]{1,0:T(8,128)S(1)}, u32[]{:S(2)}, u32[]{:S(2)}) collective-permute-start(f32[56,128]{1,0:T(8,128)S(1)} %get-tuple-element.13), channel_id=1, source_target_pairs={{0,8},{8,0},{16,24},{24,16},{1,9},{9,1},{17,25},{25,17},{2,10},{10... | collective-permute-start | bytes 86024 | tf_op jit(solution)/shard_map/ppermute | solution.py:31
  13.4 1.5 %collective-permute-start.3 = (f32[56,128]{1,0:T(8,128)S(1)}, f32[56,128]{1,0:T(8,128)S(1)}, u32[]{:S(2)}, u32[]{:S(2)}) collective-permute-start(f32[56,128]{1,0:T(8,128)S(1)} %get-tuple-element.14), channel_id=1, source_target_pairs={{8,16},{16,8},{24,0},{0,24},{9,17},{17,9},{25,1},{1,25},{10,18},{1... | collective-permute-start | bytes 86024 | tf_op jit(solution)/shard_map/ppermute | solution.py:31
  14.9 0.5 %collective-permute-start.4 = (f32[16,128]{1,0:T(8,128)S(1)}, f32[16,128]{1,0:T(8,128)S(1)}, u32[]{:S(2)}, u32[]{:S(2)}) collective-permute-start(f32[16,128]{1,0:T(8,128)S(1)} %get-tuple-element.12.scalars), channel_id=1, source_target_pairs={{0,16},{8,24},{16,0},{24,8},{1,17},{9,25},{17,1},{25,9},{2,18},{10... | collective-permute-start | bytes 24584 | tf_op jit(solution)/shard_map/ppermute | solution.py:36
  15.4 3.1 %collective-permute-done.4 = f32[16,128]{1,0:T(8,128)S(1)} collective-permute-done((f32[16,128]{1,0:T(8,128)S(1)}, f32[16,128]{1,0:T(8,128)S(1)}, u32[]{:S(2)}, u32[]{:S(2)}) %collective-permute-start.4) | collective-permute-done | bytes 8224 | tf_op jit(solution)/shard_map/ppermute | solution.py:36
  18.6 0.0 collective-permute-done.2.first
  18.6 0.0 collective-permute-done.3.second
  18.6 3.0 %step.1 = f32[3,16,512]{2,1,0:T(8,128)} custom-call(f32[3,16,512]{2,1,0:T(8,128)S(1)} %copy-done, f32[16,512]{1,0:T(8,128)S(1)} %copy-done.1, f32[40,512]{1,0:T(8,128)S(1)} %collective-permute-done.near, f32[40,512]{1,0:T(8,128)S(1)} %collective-permute-done.1.far, f32[56,128]{1,0:T(8,128)S(1)} %collective-permute-done.2.first, ...), custom_call_target="tpu_custom_call" | custom-call | tf_op jit(solution)/shard_map/step/pallas_call | solution.py:361
Async XLA Ops:
  0.0 0.9 %copy-start = (f32[3,16,512]{2,1,0:T(8,128)S(1)}, f32[3,16,512]{2,1,0:T(8,128)}, u32[]{:S(2)}) copy-start(f32[3,16,512]{2,1,0:T(8,128)} %state.5) | copy-start | bytes 294916
  0.9 0.8 %copy-start.1 = (f32[16,512]{1,0:T(8,128)S(1)}, f32[16,512]{1,0:T(8,128)}, u32[]{:S(2)}) copy-start(f32[16,512]{1,0:T(8,128)} %depth.5) | copy-start | bytes 98308
  1.7 0.7 %copy-start.2 = (f32[2,4]{1,0:T(2,128)S(1)}, f32[2,4]{1,0:T(2,128)}, u32[]{:S(2)}) copy-start(f32[2,4]{1,0:T(2,128)} %weight.1) | copy-start | bytes 100
  2.3 0.7 %copy-start.3 = (f32[4]{0:T(128)S(1)}, f32[4]{0:T(128)}, u32[]{:S(2)}) copy-start(f32[4]{0:T(128)} %real.1) | copy-start | bytes 52
  3.0 0.7 %copy-start.4 = (f32[4]{0:T(128)S(1)}, f32[4]{0:T(128)}, u32[]{:S(2)}) copy-start(f32[4]{0:T(128)} %imag.1) | copy-start | bytes 52
  4.2 5.2 %collective-permute-start = (f32[40,512]{1,0:T(8,128)S(1)}, f32[40,512]{1,0:T(8,128)S(1)}, u32[]{:S(2)}, u32[]{:S(2)}) collective-permute-start(f32[40,512]{1,0:T(8,128)S(1)} %get-tuple-element.10), channel_id=1, source_target_pairs={{0,1},{1,0},{2,3},{3,2},{4,5},{5,4},{6,7},{7,6},{8,9},{9,8},{10,11... | collective-permute-start | bytes 245768 | tf_op jit(solution)/shard_map/ppermute | solution.py:31
  4.8 7.0 %collective-permute-start.1 = (f32[40,512]{1,0:T(8,128)S(1)}, f32[40,512]{1,0:T(8,128)S(1)}, u32[]{:S(2)}, u32[]{:S(2)}) collective-permute-start(f32[40,512]{1,0:T(8,128)S(1)} %get-tuple-element.11), channel_id=1, source_target_pairs={{1,2},{2,1},{3,4},{4,3},{5,6},{6,5},{7,0},{0,7},{9,10},{10,9},{11,... | collective-permute-start | bytes 245768 | tf_op jit(solution)/shard_map/ppermute | solution.py:31
  11.9 6.7 %collective-permute-start.2 = (f32[56,128]{1,0:T(8,128)S(1)}, f32[56,128]{1,0:T(8,128)S(1)}, u32[]{:S(2)}, u32[]{:S(2)}) collective-permute-start(f32[56,128]{1,0:T(8,128)S(1)} %get-tuple-element.13), channel_id=1, source_target_pairs={{0,8},{8,0},{16,24},{24,16},{1,9},{9,1},{17,25},{25,17},{2,10},{10... | collective-permute-start | bytes 86024 | tf_op jit(solution)/shard_map/ppermute | solution.py:31
  13.4 5.1 %collective-permute-start.3 = (f32[56,128]{1,0:T(8,128)S(1)}, f32[56,128]{1,0:T(8,128)S(1)}, u32[]{:S(2)}, u32[]{:S(2)}) collective-permute-start(f32[56,128]{1,0:T(8,128)S(1)} %get-tuple-element.14), channel_id=1, source_target_pairs={{8,16},{16,8},{24,0},{0,24},{9,17},{17,9},{25,1},{1,25},{10,18},{1... | collective-permute-start | bytes 86024 | tf_op jit(solution)/shard_map/ppermute | solution.py:31
  14.9 3.7 %collective-permute-start.4 = (f32[16,128]{1,0:T(8,128)S(1)}, f32[16,128]{1,0:T(8,128)S(1)}, u32[]{:S(2)}, u32[]{:S(2)}) collective-permute-start(f32[16,128]{1,0:T(8,128)S(1)} %get-tuple-element.12.scalars), channel_id=1, source_target_pairs={{0,16},{8,24},{16,0},{24,8},{1,17},{9,25},{17,1},{25,9},{2,18},{10... | collective-permute-start | bytes 24584 | tf_op jit(solution)/shard_map/ppermute | solution.py:36

commit v3 on v2

--- a/solution.py
+++ b/solution.py
@@ -1,5 +1,3 @@
-import functools
-
 import jax
 import jax.numpy as jnp
 from jax import lax
@@ -31,11 +29,6 @@
     return lax.ppermute(block, axis, pairs(lax.axis_size(axis), phase))
 
 
-def shift(block, axis, step):
-    count = lax.axis_size(axis)
-    return lax.ppermute(block, axis, [(i, (i + step) % count) for i in range(count)])
-
-
 def cmul(a, b):
     return (a[0] * b[0] - a[1] * b[1], a[0] * b[1] + a[1] * b[0])
 
@@ -49,28 +42,23 @@
     return (a[0] * factor, a[1] * factor)
 
 
-def pack_rows_kernel(state, depth, real, imag, weight, far, near, scalars):
+def pack_rows_kernel(fields, far, near):
     odd = lax.rem(lax.axis_index("tile"), 2) == 1
-    rows = depth.shape[0]
-    fields = [state.at[0], state.at[1], state.at[2], depth]
-    for target, low in ((near, odd), (far, jnp.logical_not(odd))):
+    rows = fields.shape[1]
+    for target, low in ((far, jnp.logical_not(odd)), (near, odd)):
         @pl.when(low)
         def _():
-            for f, field in enumerate(fields):
-                target[f * SUB : (f + 1) * SUB] = field[0:SUB]
-                target[4 * SUB + f : 4 * SUB + f + 1] = field[SUB : SUB + 1]
+            for f in range(4):
+                target[f * SUB : (f + 1) * SUB] = fields[f, 0:SUB]
+                target[4 * SUB + f : 4 * SUB + f + 1] = fields[f, SUB : SUB + 1]
 
         @pl.when(jnp.logical_not(low))
         def _():
-            for f, field in enumerate(fields):
-                target[f * SUB : (f + 1) * SUB] = field[rows - SUB : rows]
-                target[4 * SUB + f : 4 * SUB + f + 1] = field[rows - SUB - 1 : rows - SUB]
-
-    poles = real.shape[0]
-    values = [real[i] for i in range(poles)] + [imag[i] for i in range(poles)]
-    values += [weight[0, i] for i in range(poles)] + [weight[1, i] for i in range(poles)]
-    for i, value in enumerate(values):
-        scalars[i : i + 1] = jnp.full((1, LANES), value, jnp.float32)
+            for f in range(4):
+                target[f * SUB : (f + 1) * SUB] = fields[f, rows - SUB : rows]
+                target[4 * SUB + f : 4 * SUB + f + 1] = fields[f, rows - SUB - 1 : rows - SUB]
+
+        target[4 * SUB + 4 : 5 * SUB] = jnp.zeros((4, target.shape[1]), jnp.float32)
 
 
 def column_block(fields, start):
@@ -83,10 +71,11 @@
     return total
 
 
-def pack_columns_kernel(state, depth, near, far, scalars, first, second):
-    odd = lax.rem(lax.axis_index("pole"), 2) == 1
-    rows, columns = depth.shape
-    own = [state.at[0], state.at[1], state.at[2], depth]
+def pack_columns_kernel(fields, near, far, scalars, blocks):
+    me = lax.axis_index("pole")
+    count = blocks.shape[0]
+    rows, columns = fields.shape[1:]
+    own = [fields.at[f] for f in range(4)]
 
     def edge(side):
         lanes = pl.ds(0, LANES) if side == 0 else pl.ds(columns - LANES, LANES)
@@ -106,12 +95,16 @@
 
     left = edge(0)
     right = edge(1)
-    for i, (a, b) in enumerate(zip(left, right)):
-        first[pl.ds(i * SUB, SUB)] = jnp.where(odd, a, b)
-        second[pl.ds(i * SUB, SUB)] = jnp.where(odd, b, a)
     base = len(left) * SUB
-    first[pl.ds(base, scalars.shape[0])] = scalars[...]
-    second[pl.ds(base, scalars.shape[0])] = scalars[...]
+    for step in range(1, count):
+        there = lax.rem(me + step, count)
+        if step in (1, count - 1):
+            for i, part in enumerate(right if step == 1 else left):
+                blocks[there, pl.ds(i * SUB, SUB)] = part
+        else:
+            blocks[there, pl.ds(0, base)] = jnp.zeros((base, LANES), jnp.float32)
+        blocks[there, pl.ds(base, scalars.shape[0])] = scalars[...]
+    blocks[me] = jnp.zeros(blocks.shape[1:], jnp.float32)
 
 
 def strips_of(tiles, west, east):
@@ -126,18 +119,19 @@
     return out
 
 
-def step_kernel(state, depth, near, far, first, second, scalars, others, out, grid, poly, coef, result):
-    rows, columns = depth.shape
+def step_kernel(fields, near, far, scalars, blocks, out, grid, poly, coef, result):
+    rows, columns = fields.shape[1:]
+    me = lax.axis_index("pole")
+    count = blocks.shape[0]
     groups = rows // SUB
     tiles = columns // LANES
-    odd_pole = lax.rem(lax.axis_index("pole"), 2) == 1
+    after = lax.rem(me + 1, count)
+    before = lax.rem(me + count - 1, count)
     odd_tile = lax.rem(lax.axis_index("tile"), 2) == 1
-    own = [state.at[0], state.at[1], state.at[2], depth]
+    own = [fields.at[f] for f in range(4)]
 
     def sides(index):
-        one = first[pl.ds(index * SUB, SUB)]
-        two = second[pl.ds(index * SUB, SUB)]
-        return jnp.where(odd_pole, one, two), jnp.where(odd_pole, two, one)
+        return blocks[before, pl.ds(index * SUB, SUB)], blocks[after, pl.ds(index * SUB, SUB)]
 
     def turned(block, turn):
         return pltpu.roll(block, turn % LANES, 1) if turn % LANES else block
@@ -205,13 +199,14 @@
             poly[2, 0, c] = 0.5 * (east_slope - north_slope)
             poly[0, 0, c] = cell(0, c)
 
-    blocks = [scalars[...], first[pl.ds((groups + 3) * SUB, scalars.shape[0])]]
-    blocks += [second[pl.ds((groups + 3) * SUB, scalars.shape[0])]]
-    blocks += [others[i] for i in range(others.shape[0])]
+    given = [scalars[...]]
+    for step in range(1, count):
+        there = lax.rem(me + step, count)
+        given.append(blocks[there, pl.ds((groups + 3) * SUB, scalars.shape[0])])
     poles = scalars.shape[0] // 4
     quantity = []
     for q in range(4):
-        cut = [b[q * poles : (q + 1) * poles] for b in blocks]
+        cut = [b[q * poles : (q + 1) * poles] for b in given]
         quantity.append(jnp.concatenate(cut, axis=0))
     alpha = (quantity[0], quantity[1])
     beta = (quantity[2], quantity[3])
@@ -330,38 +325,37 @@
     rows, columns = depth.shape
     poles = pole_real.shape[0]
     vmem = pl.BlockSpec(memory_space=pltpu.VMEM)
-    smem = pl.BlockSpec(memory_space=pltpu.SMEM)
     f32 = jnp.float32
     halo = jax.ShapeDtypeStruct((5 * SUB, columns), f32)
-    far, near, scalars = pl.pallas_call(
+    fields = jnp.concatenate([state, depth[None]])
+    far, near = pl.pallas_call(
         pack_rows_kernel,
-        out_shape=(halo, halo, jax.ShapeDtypeStruct((4 * poles, LANES), f32)),
-        in_specs=[vmem, vmem, smem, smem, smem],
-        out_specs=(vmem, vmem, vmem),
+        out_shape=(halo, halo),
+        in_specs=[vmem],
+        out_specs=(vmem, vmem),
         compiler_params=pltpu.CompilerParams(vmem_limit_bytes=GRANT),
         name="pack_rows",
-    )(state, depth, pole_real, pole_imag, pole_weight)
+    )(fields)
+    scalars = jnp.concatenate([pole_real, pole_imag, pole_weight[0], pole_weight[1]])
+    scalars = jnp.broadcast_to(scalars[:, None], (4 * poles, LANES))
     far = swap(far, "tile", 1)
     near = swap(near, "tile", 0)
     count = lax.axis_size("pole")
-    others = jnp.stack([shift(scalars, "pole", step) for step in range(2, count - 1)])
     block_rows = (rows // SUB + 3) * SUB + 4 * poles
-    block = jax.ShapeDtypeStruct((block_rows, LANES), f32)
-    first, second = pl.pallas_call(
+    blocks = pl.pallas_call(
         pack_columns_kernel,
-        out_shape=(block, block),
-        in_specs=[vmem] * 5,
-        out_specs=(vmem, vmem),
+        out_shape=jax.ShapeDtypeStruct((count, block_rows, LANES), f32),
+        in_specs=[vmem] * 4,
+        out_specs=vmem,
         compiler_params=pltpu.CompilerParams(vmem_limit_bytes=GRANT),
         name="pack_columns",
-    )(state, depth, near, far, scalars)
-    first = swap(first, "pole", 0)
-    second = swap(second, "pole", 1)
+    )(fields, near, far, scalars)
+    blocks = lax.all_to_all(blocks, "pole", 0, 0, tiled=True)
     height = rows + 2 * REACH
     return pl.pallas_call(
         step_kernel,
         out_shape=jax.ShapeDtypeStruct(state.shape, f32),
-        in_specs=[vmem] * 8,
+        in_specs=[vmem] * 5,
         out_specs=vmem,
         scratch_shapes=[
             pltpu.VMEM((height * 4 * SUB, LANES), f32),
@@ -371,7 +365,7 @@
         ],
         compiler_params=pltpu.CompilerParams(vmem_limit_bytes=GRANT),
         name="step",
-    )(state, depth, near, far, first, second, scalars, others)
+    )(fields, near, far, scalars, blocks)
 
 
 def solution(mesh):

time: 21.9 us -> 20.4 us (0.932)
  blocking collectives: 0 us -> 8.49 us
  waiting for transfers between devices: 5.45 us -> 1.54 us
  starting transfers between devices: 8.78 us -> 5.23 us
  local copies, waits for them, and re-layouts: 3.64 us -> 0.74 us
  other arithmetic: 0 us -> 1 us
  Pallas kernels: 3.72 us -> 3.21 us
    all_to_all x0 -> x1, blocking collectives: none -> 8.49 us  [shards(): blocks = lax.all_to_all(blocks, 'pole', 0, 0, tiled=True)]
    ppermute x1 -> x0, waiting for transfers between devices: 3.14 us -> none  [shift(): lax.ppermute(block, axis, [(i, (i + step) % count) for i in range(count)])]
    ppermute x4 -> x2, starting transfers between devices: 8.28 us -> 5.23 us  [swap(): return lax.ppermute(block, axis, pairs(lax.axis_size(axis), phase))]
    unnamed x10 -> x6, local copies, waits for them, and re-layouts: 3.64 us -> 0.67 us
    concatenate x0 -> x2, other arithmetic: none -> 1 us  [the longest x1 0.92 us: shards(): fields = jnp.concatenate([state, depth[None]])]
    ppermute x4 -> x2, waiting for transfers between devices: 2.3 us -> 1.54 us  [swap(): return lax.ppermute(block, axis, pairs(lax.axis_size(axis), phase))]
    pallas_call x2, Pallas kernels: 0.68 us -> 0.13 us  [the longest x1 0.1 us: shards(): pl.pallas_call(pack_columns_kernel, out_shape=jax.ShapeDtypeStruct((count...]
    ppermute x1 -> x0, starting transfers between devices: 0.51 us -> none  [shift(): lax.ppermute(block, axis, [(i, (i + step) % count) for i in range(count)])]
  transfers between devices with their start and end apart: 5 -> 2, of which waited for: 2 -> 1; matrix products, arithmetic and copies ran while one was open for 0% -> 0% of each run, Pallas kernels for 0% -> 0%
where the time goes in v3:
time: 20.4 us; the launch traced here: 20.3 us
  blocking collectives  8.49 us (42%)
  starting transfers between devices  5.23 us (26%)
  Pallas kernels  3.21 us (16%)
  waiting for transfers between devices  1.54 us (8%)
  other arithmetic  1 us (5%)
  local copies, waits for them, and re-layouts  0.74 us (4%)
    all_to_all x1, blocking collectives, shards(): blocks = lax.all_to_all(blocks, 'pole', 0, 0, tiled=True)  8.49 us
    ppermute x2, starting transfers between devices, swap(): return lax.ppermute(block, axis, pairs(lax.axis_size(axis), phase))  5.23 us
    pallas_call x1, Pallas kernels, shards(): pl.pallas_call(step_kernel, out_shape=jax.ShapeDtypeStruct(state.shape, f...  3.08 us
    ppermute x2, waiting for transfers between devices, swap(): return lax.ppermute(block, axis, pairs(lax.axis_size(axis), phase))  1.54 us
    concatenate x1, other arithmetic, shards(): fields = jnp.concatenate([state, depth[None]])  0.92 us
    unnamed x6, local copies, waits for them, and re-layouts  0.67 us
  transfers between devices with their start and end apart: 2, of which 1 were waited for; matrix products, arithmetic and copies ran while one was open for 0% of the time, Pallas kernels for 0%

profile of v3, /device:TPU:0, one launch (start us, length us, event | category | flops | bytes accessed | tf_op | source)
XLA Modules:
  0.0 20.3 jit_solution(14057429734623752855)
XLA Ops:
  0.0 0.9 %pad_maximum_fusion.fields = f32[4,16,512]{2,1,0:T(8,128)S(1)} fusion(f32[1,16,512]{2,1,0:T(8,128)} %bitcast.5, f32[3,16,512]{2,1,0:T(8,128)} %param.5), kind=kLoop, calls=%fused_computation | loop fusion | flops 32768 | bytes 262144 | tf_op jit(solution)/shard_map/concatenate | solution.py:330
  1.0 0.0 copy-start
  1.0 0.5 %collective-permute-start = (f32[40,512]{1,0:T(8,128)S(1)}, f32[40,512]{1,0:T(8,128)S(1)}, u32[]{:S(2)}, u32[]{:S(2)}) collective-permute-start(f32[40,512]{1,0:T(8,128)S(1)} %get-tuple-element.7), channel_id=1, source_target_pairs={{0,1},{1,0},{2,3},{3,2},{4,5},{5,4},{6,7},{7,6},{8,9},{9,8},{10,11... | collective-permute-start | bytes 245768 | tf_op jit(solution)/shard_map/ppermute | solution.py:29
  1.5 4.7 %collective-permute-start.1 = (f32[40,512]{1,0:T(8,128)S(1)}, f32[40,512]{1,0:T(8,128)S(1)}, u32[]{:S(2)}, u32[]{:S(2)}) collective-permute-start(f32[40,512]{1,0:T(8,128)S(1)} %get-tuple-element.8), channel_id=1, source_target_pairs={{1,2},{2,1},{3,4},{4,3},{5,6},{6,5},{7,0},{0,7},{9,10},{10,9},{11,... | collective-permute-start | bytes 245768 | tf_op jit(solution)/shard_map/ppermute | solution.py:29
  6.2 0.0 copy-done
  6.2 0.0 copy-start.1
  6.2 0.0 copy-start.2
  6.2 0.6 %copy-done.1 = f32[4]{0:T(128)S(1)} copy-done((f32[4]{0:T(128)S(1)}, f32[4]{0:T(128)}, u32[]{:S(2)}) %copy-start.1) | copy-done | bytes 40
  6.9 0.0 copy-done.2
  6.9 0.1 pad_maximum_fusion.1
  7.0 0.0 collective-permute-done.near
  7.0 1.5 %collective-permute-done.1.far = f32[40,512]{1,0:T(8,128)S(1)} collective-permute-done((f32[40,512]{1,0:T(8,128)S(1)}, f32[40,512]{1,0:T(8,128)S(1)}, u32[]{:S(2)}, u32[]{:S(2)}) %collective-permute-start.1) | collective-permute-done | bytes 81952 | tf_op jit(solution)/shard_map/ppermute | solution.py:29
  8.5 0.1 broadcast_in_dim.10.scalars
  8.6 0.1 pack_columns.1
  8.7 8.5 %all_to_all.5.blocks = f32[4,56,128]{2,1,0:T(8,128)S(1)} all-to-all(f32[4,56,128]{2,1,0:T(8,128)S(1)} %pack_columns.1), channel_id=1, replica_groups=mesh['pole'=4,'tile'=8] {'pole'}, dimensions={0} | all-to-all | bytes 229376 | tf_op jit(solution)/shard_map/all_to_all | solution.py:353
  17.2 3.1 %step.1 = f32[3,16,512]{2,1,0:T(8,128)} custom-call(f32[4,16,512]{2,1,0:T(8,128)S(1)} %pad_maximum_fusion.fields, f32[40,512]{1,0:T(8,128)S(1)} %collective-permute-done.near, f32[40,512]{1,0:T(8,128)S(1)} %collective-permute-done.1.far, f32[16,128]{1,0:T(8,128)S(1)} %broadcast_in_dim.10.scalars, f32[4,56,128]{2,1,0:T(8,128)S(1)} %all_to_all.5.blocks), custom_call_target="tpu_custom_call" | custom-call | tf_op jit(solution)/shard_map/step/pallas_call | solution.py:355
  (2 shorter events, 0.0 us)
Async XLA Ops:
  1.0 5.2 %copy-start = (f32[2,4]{1,0:T(2,128)S(1)}, f32[2,4]{1,0:T(2,128)}, u32[]{:S(2)}) copy-start(f32[2,4]{1,0:T(2,128)} %param.9) | copy-start | bytes 100
  1.0 6.0 %collective-permute-start = (f32[40,512]{1,0:T(8,128)S(1)}, f32[40,512]{1,0:T(8,128)S(1)}, u32[]{:S(2)}, u32[]{:S(2)}) collective-permute-start(f32[40,512]{1,0:T(8,128)S(1)} %get-tuple-element.7), channel_id=1, source_target_pairs={{0,1},{1,0},{2,3},{3,2},{4,5},{5,4},{6,7},{7,6},{8,9},{9,8},{10,11... | collective-permute-start | bytes 245768 | tf_op jit(solution)/shard_map/ppermute | solution.py:29
  1.5 7.0 %collective-permute-start.1 = (f32[40,512]{1,0:T(8,128)S(1)}, f32[40,512]{1,0:T(8,128)S(1)}, u32[]{:S(2)}, u32[]{:S(2)}) collective-permute-start(f32[40,512]{1,0:T(8,128)S(1)} %get-tuple-element.8), channel_id=1, source_target_pairs={{1,2},{2,1},{3,4},{4,3},{5,6},{6,5},{7,0},{0,7},{9,10},{10,9},{11,... | collective-permute-start | bytes 245768 | tf_op jit(solution)/shard_map/ppermute | solution.py:29
  6.2 0.7 %copy-start.1 = (f32[4]{0:T(128)S(1)}, f32[4]{0:T(128)}, u32[]{:S(2)}) copy-start(f32[4]{0:T(128)} %param.8) | copy-start | bytes 52
  6.2 0.7 %copy-start.2 = (f32[4]{0:T(128)S(1)}, f32[4]{0:T(128)}, u32[]{:S(2)}) copy-start(f32[4]{0:T(128)} %param.7) | copy-start | bytes 52

commit v4 on v1

v4 whole, which is shorter than its diff:
```python
import jax
import jax.numpy as jnp
from jax import lax
from jax.experimental import pallas as pl
from jax.experimental.pallas import tpu as pltpu
from jax.sharding import PartitionSpec as P

ITERS = 8
REACH = ITERS + 1
SUB = 8
LANES = 128
HALF = LANES // 2
SIDE = 32
EDGE = 12
EAST = HALF + EDGE
GRANT = 16 * 1024 * 1024

coriolis = 0.7
centre = 8.0
half_width = 8.0


def pairs(count, phase):
    swap = []
    for i in range(phase, count + phase, 2):
        a, b = i % count, (i + 1) % count
        swap += [(a, b), (b, a)]
    return swap


def swap(block, axis, phase):
    return lax.ppermute(block, axis, pairs(lax.axis_size(axis), phase))


def shift(block, axis, step):
    count = lax.axis_size(axis)
    return lax.ppermute(block, axis, [(i, (i + step) % count) for i in range(count)])


def turn(x, lanes):
    return pltpu.roll(x, lanes % LANES, 1) if lanes % LANES else x


def cmul(a, b):
    return (a[0] * b[0] - a[1] * b[1], a[0] * b[1] + a[1] * b[0])


def cinv(a):
    norm = 1.0 / (a[0] * a[0] + a[1] * a[1])
    return (a[0] * norm, -a[1] * norm)


def cscale(a, factor):
    return (a[0] * factor, a[1] * factor)


def pack_columns_kernel(
    state_west, state_east, depth_west, depth_east, real, imag, weight, first, second, scalars
):
    odd = lax.rem(lax.axis_index("pole"), 2) == 1
    rows = depth_west.shape[0]
    lane = lax.broadcasted_iota(jnp.int32, (SUB, LANES), 1)
    sub = lax.broadcasted_iota(jnp.int32, (SUB, LANES), 0)
    poles = real.shape[0]
    values = [real[i] for i in range(poles)] + [imag[i] for i in range(poles)]
    values += [weight[0, i] for i in range(poles)] + [weight[1, i] for i in range(poles)]
    spread = []
    for g in range(len(values) // SUB):
        block = jnp.full((SUB, LANES), values[g * SUB], jnp.float32)
        for i in range(1, SUB):
            block = jnp.where(sub == i, values[g * SUB + i], block)
        scalars[pl.ds(g * SUB, SUB)] = block
        spread.append(block)
    for g in range(rows // SUB):
        cut = pl.ds(g * SUB, SUB)
        rest = spread[g] if g < len(spread) else jnp.zeros((SUB, LANES), jnp.float32)
        eastward = rest
        westward = rest
        for f in range(4):
            west = depth_west[cut, :] if f == 3 else state_west[f, cut, :]
            east = depth_east[cut, :] if f == 3 else state_east[f, cut, :]
            low, high = EDGE * f, EDGE * (f + 1)
            take = jnp.logical_and(lane >= low, lane < high)
            eastward = jnp.where(take, turn(east, low + EDGE), eastward)
            take = jnp.logical_and(lane >= EAST + low, lane < EAST + high)
            westward = jnp.where(take, turn(west, EAST + low), westward)
        first[cut, :] = jnp.where(odd, westward, eastward)
        second[cut, :] = jnp.where(odd, eastward, westward)


def sides_of(first, second, cut):
    odd = lax.rem(lax.axis_index("pole"), 2) == 1
    lane = lax.broadcasted_iota(jnp.int32, (SUB, LANES), 1)
    from_first = jnp.logical_xor(lane >= HALF, odd)
    return jnp.where(from_first, first[cut, :], second[cut, :])


def pack_rows_kernel(state, depth, first, second, far, near):
    odd = lax.rem(lax.axis_index("tile"), 2) == 1
    rows = depth.shape[0]
    fields = [state.at[0], state.at[1], state.at[2], depth]
    for target, low in ((far, jnp.logical_not(odd)), (near, odd)):
        def fill(main, ext):
            for f in range(4):
                target[f * SUB : (f + 1) * SUB] = fields[f][main : main + SUB]
                target[4 * SUB + f : 4 * SUB + f + 1] = fields[f][ext : ext + 1]
            side = sides_of(first, second, pl.ds(main, SUB))
            base = 4 * SUB + 4
            target[base : base + 4, 0:LANES] = side[0:4]
            target[base : base + 4, LANES : 2 * LANES] = side[4:8]
            group = ext // SUB * SUB
            side = sides_of(first, second, pl.ds(group, SUB))
            target[base : base + 1, 2 * LANES : 3 * LANES] = side[ext - group : ext - group + 1]

        pl.when(low)(lambda: fill(0, SUB))
        pl.when(jnp.logical_not(low))(lambda: fill(rows - SUB, rows - SUB - 1))


def pole_sums_kernel(scalars, first, second, others, sums):
    odd = lax.rem(lax.axis_index("pole"), 2) == 1
    count = scalars.shape[0]
    lane = lax.broadcasted_iota(jnp.int32, (SUB, LANES), 1)
    blocks = [[scalars[pl.ds(g, SUB)] for g in range(0, count, SUB)]]
    for i, message in enumerate((first, second)):
        low = jnp.logical_xor(lane < HALF, odd if i == 0 else jnp.logical_not(odd))
        part = []
        for g in range(0, count, SUB):
            x = message[pl.ds(g, SUB), :]
            part.append(jnp.where(low, x, turn(x, HALF)))
        blocks.append(part)
    for i in range(others.shape[0]):
        blocks.append([others[i, pl.ds(g, SUB)] for g in range(0, count, SUB)])
    poles = count // 4
    quantity = []
    for q in range(4):
        cut = []
        for block in blocks:
            whole = jnp.concatenate(block, axis=0)
            cut.append(whole[q * poles : (q + 1) * poles])
        quantity.append(jnp.concatenate(cut, axis=0))
    alpha = (quantity[0], quantity[1])
    beta = (quantity[2], quantity[3])
    square = cmul(alpha, alpha)
    shifted = (square[0] + coriolis * coriolis, square[1])
    sigma = ((shifted[0] + centre) / half_width, shifted[1] / half_width)
    rho = [cinv(sigma)]
    for j in range(1, ITERS):
        rho.append(cinv((2.0 * sigma[0] - rho[-1][0], 2.0 * sigma[1] - rho[-1][1])))
    gain = None
    start = []
    for m in range(ITERS):
        if m == 0:
            start.append(cscale(rho[0], 1.0 / half_width))
        else:
            gain = rho[0] if gain is None else cmul(gain, rho[m - 1])
            start.append(cscale(cmul(rho[m], gain), 2.0 / half_width))
    tail = None
    weight = [None] * ITERS
    for m in reversed(range(ITERS)):
        if tail is None:
            weight[m] = start[m]
            tail = (jnp.ones_like(sigma[0]), jnp.zeros_like(sigma[0]))
        else:
            tail = cmul(cmul(rho[m + 1], rho[m]), tail)
            tail = (tail[0] + 1.0, tail[1])
            weight[m] = cmul(start[m], tail)
    inverse_alpha = cinv(alpha)
    inverse_shift = cinv(shifted)
    by_alpha = cmul(beta, inverse_alpha)
    by_shift = cmul(beta, inverse_shift)
    products = {
        "b": beta,
        "b/a": by_alpha,
        "b/s": by_shift,
        "bs/a": cmul(by_alpha, shifted),
        "ba/s": cmul(by_shift, alpha),
        "b/as": cmul(by_alpha, inverse_shift),
    }

    def total(x):
        s = x[0:SUB]
        for i in range(1, x.shape[0] // SUB):
            s = s + x[i * SUB : (i + 1) * SUB]
        for step in (4, 2, 1):
            s = s + pltpu.roll(s, step, 0)
        return s

    names = [("bs/a", "b", "b/a"), ("b", "ba/s", "b/s"), ("b/a", "b/s", "b/as")]
    factor = (1.0, -1.0, -coriolis)
    found = {}
    for m in range(ITERS):
        for name, w in products.items():
            found[name, m] = total(w[0] * weight[m][0] - w[1] * weight[m][1])
        for g in range(3):
            for f in range(3):
                value = found[names[g][f], m]
                sums[(g * 3 + f) * ITERS + m] = value if f == 0 else factor[f] * value
    sums[9 * ITERS] = total(products["ba/s"][0])
    sums[9 * ITERS + 1] = coriolis * total(products["b/s"][0])


def strips_of(tiles, side):
    lane = lax.broadcasted_iota(jnp.int32, (SUB, LANES), 1)
    up = [turn(tile, SIDE) for tile in tiles]
    down = [turn(tile, -SIDE) for tile in tiles]
    out = []
    for q in range(len(tiles)):
        out.append(jnp.where(lane < SIDE, up[q - 1] if q else side, up[q]))
        after = down[q + 1] if q + 1 < len(tiles) else side
        out.append(jnp.where(lane < LANES - SIDE, down[q], after))
    return out


def step_kernel(state, depth, far, near, first, second, sums, out, grid, poly, coef, result):
    rows, columns = depth.shape
    groups = rows // SUB
    tiles = columns // LANES
    odd_tile = lax.rem(lax.axis_index("tile"), 2) == 1
    own = [state.at[0], state.at[1], state.at[2], depth]
    lane = lax.broadcasted_iota(jnp.int32, (SUB, LANES), 1)
    sub = lax.broadcasted_iota(jnp.int32, (SUB, LANES), 0)

    def lay(block, side, at, size, stride):
        cut = [block[:, t * LANES : (t + 1) * LANES] for t in range(tiles)]
        for s, strip in enumerate(strips_of(cut, side)):
            grid[pl.Slice(at * SUB + s, size, stride * SUB), :] = strip[0:size]

    def place(side, f):
        return turn(side, SIDE - EDGE - EDGE * f)

    for g in range(groups):
        side = sides_of(first, second, pl.ds(g * SUB, SUB))
        for f in range(4):
            block = own[f][pl.ds(g * SUB, SUB), :]
            lay(block, place(side, f), (REACH + g * SUB) * 4 + f, SUB, 4)
    below = REACH + rows
    near_main = jnp.where(odd_tile, 1, below)
    far_main = jnp.where(odd_tile, below, 1)
    near_ext = jnp.where(odd_tile, 0, below + SUB)
    far_ext = jnp.where(odd_tile, below + SUB, 0)
    base = 4 * SUB + 4
    for halo, main, ext in ((near, near_main, near_ext), (far, far_main, far_ext)):
        side = jnp.concatenate(
            [halo[base : base + 4, 0:LANES], halo[base : base + 4, LANES : 2 * LANES]], axis=0
        )
        for f in range(4):
            lay(halo[pl.ds(f * SUB, SUB), :], place(side, f), main * 4 + f, SUB, 4)
        line = halo[base : base + 1, 2 * LANES : 3 * LANES]
        line = jnp.broadcast_to(line, (SUB, LANES))
        side = place(line, 0)
        for f in range(1, 4):
            side = jnp.where(sub == f, place(line, f), side)
        lay(halo[pl.ds(4 * SUB, SUB), :], side, ext * 4, 4, 1)

    def cell(f, r):
        return grid[pl.ds((r * 4 + f) * SUB, SUB), :]

    def left(x):
        return pltpu.roll(x, 1, 1)

    def right(x):
        return pltpu.roll(x, LANES - 1, 1)

    height = rows + 2 * REACH

    flux_east = [None] * 3
    flux_north = [None] * 3
    depths = [None] * 2
    across = None
    for r in range(height):
        h = cell(3, r)
        flux_east = flux_east[1:] + [h * cell(1, r)]
        flux_north = flux_north[1:] + [h * cell(2, r)]
        depths = depths[1:] + [h]
        if r >= 1:
            before, across = across, 0.125 * (depths[0] + depths[1])
            coef[0, r - 1] = across
        if r >= 2:
            c = r - 1
            north = 0.125 * (depths[0] + right(depths[0]))
            south = left(north)
            coef[1, c] = north
            coef[2, c] = south
            coef[3, c] = 2.0 - ((across + before) + (north + south))
            east_slope = flux_east[2] - flux_east[0]
            north_slope = right(flux_north[1]) - left(flux_north[1])
            poly[1, 0, c] = 0.5 * (east_slope + north_slope)
            east_slope = flux_north[2] - flux_north[0]
            north_slope = right(flux_east[1]) - left(flux_east[1])
            poly[2, 0, c] = 0.5 * (east_slope - north_slope)
            poly[0, 0, c] = cell(0, c)

    for m in range(ITERS - 1):
        low, high = m + 2, height - m - 2
        back = [poly[f, m, low - 1] for f in range(3)]
        here = [poly[f, m, low] for f in range(3)]
        below_ = coef[0, low - 1]
        for r in range(low, high):
            above, north, south, diag = coef[0, r], coef[1, r], coef[2, r], coef[3, r]
            ahead = [poly[f, m, r + 1] for f in range(3)]
            for f in range(3):
                value = diag * here[f] + (above * ahead[f] + below_ * back[f])
                value = value + (north * right(here[f]) + south * left(here[f]))
                value = 0.5 * value if m == 0 else value - poly[f, m - 1, r]
                poly[f, m + 1, r] = value
            back, here, below_ = here, ahead, above

    sol = {}
    block = 6
    for r0 in range(REACH - 1, REACH + rows + 1, block):
        span = range(r0, min(r0 + block, REACH + rows + 1))
        acc = {}
        for f in range(3):
            for m in range(ITERS):
                value = [poly[f, m, r] for r in span]
                for g in range(3):
                    c = sums[(g * 3 + f) * ITERS + m]
                    for r, v in zip(span, value):
                        if g == 0 and not REACH <= r < REACH + rows:
                            continue
                        acc[g, r] = acc[g, r] + c * v if (g, r) in acc else c * v
        sol.update(acc)
    push = sums[9 * ITERS]
    lift = sums[9 * ITERS + 1]
    for i in range(rows):
        r = REACH + i
        u, v = cell(1, r), cell(2, r)
        result[0, pl.ds(i * SUB, SUB)] = sol[0, r]
        east = 0.5 * (sol[1, r + 1] - sol[1, r - 1])
        north = 0.5 * (right(sol[2, r]) - left(sol[2, r]))
        result[1, pl.ds(i * SUB, SUB)] = (push * u + lift * v) - (east + coriolis * north)
        east = 0.5 * (sol[2, r + 1] - sol[2, r - 1])
        north = 0.5 * (right(sol[1, r]) - left(sol[1, r]))
        result[2, pl.ds(i * SUB, SUB)] = (push * v - lift * u) + (coriolis * east - north)

    for k in range(3):
        for g in range(groups):
            for t in range(tiles):
                one = result[k, pl.Slice(g * SUB * SUB + 2 * t, SUB, SUB), :]
                two = result[k, pl.Slice(g * SUB * SUB + 2 * t + 1, SUB, SUB), :]
                joined = jnp.where(lane < HALF, turn(one, -SIDE), turn(two, SIDE))
                out[k, pl.ds(g * SUB, SUB), pl.ds(t * LANES, LANES)] = joined


def shards(state, depth, pole_real, pole_imag, pole_weight):
    rows, columns = depth.shape
    poles = pole_real.shape[0]
    vmem = pl.BlockSpec(memory_space=pltpu.VMEM)
    smem = pl.BlockSpec(memory_space=pltpu.SMEM)
    small = pltpu.CompilerParams(vmem_limit_bytes=GRANT)

    def f32(*shape):
        return jax.ShapeDtypeStruct(shape, jnp.float32)

    last = columns // LANES - 1
    first, second, scalars = pl.pallas_call(
        pack_columns_kernel,
        grid=(1,),
        out_shape=(f32(rows, LANES), f32(rows, LANES), f32(4 * poles, LANES)),
        in_specs=[
            pl.BlockSpec((3, rows, LANES), lambda i: (0, 0, 0)),
            pl.BlockSpec((3, rows, LANES), lambda i: (0, 0, last)),
            pl.BlockSpec((rows, LANES), lambda i: (0, 0)),
            pl.BlockSpec((rows, LANES), lambda i: (0, last)),
            smem,
            smem,
            smem,
        ],
        out_specs=(vmem, vmem, vmem),
        name="pack_columns",
    )(state, state, depth, depth, pole_real, pole_imag, pole_weight)
    first = swap(first, "pole", 0)
    second = swap(second, "pole", 1)
    halo = f32(5 * SUB, columns)
    far, near = pl.pallas_call(
        pack_rows_kernel,
        out_shape=(halo, halo),
        in_specs=[vmem] * 4,
        out_specs=(vmem, vmem),
        compiler_params=small,
        name="pack_rows",
    )(state, depth, first, second)
    far = swap(far, "tile", 1)
    near = swap(near, "tile", 0)
    count = lax.axis_size("pole")
    others = jnp.stack([shift(scalars, "pole", step) for step in range(2, count - 1)])
    sums = pl.pallas_call(
        pole_sums_kernel,
        out_shape=f32(9 * ITERS + 2, SUB, LANES),
        in_specs=[vmem] * 4,
        out_specs=vmem,
        compiler_params=small,
        name="pole_sums",
    )(scalars, first, second, others)
    height = rows + 2 * REACH
    return pl.pallas_call(
        step_kernel,
        out_shape=f32(*state.shape),
        in_specs=[vmem] * 7,
        out_specs=vmem,
        scratch_shapes=[
            pltpu.VMEM((height * 4 * SUB, LANES), jnp.float32),
            pltpu.VMEM((3, ITERS, height, SUB, LANES), jnp.float32),
            pltpu.VMEM((4, height, SUB, LANES), jnp.float32),
            pltpu.VMEM((3, rows * SUB, LANES), jnp.float32),
        ],
        compiler_params=small,
        name="step",
    )(state, depth, far, near, first, second, sums)


def solution(mesh):
    return jax.shard_map(
        shards,
        mesh=mesh,
        in_specs=(
            P(None, "tile", "pole"),
            P("tile", "pole"),
            P("pole"),
            P("pole"),
            P(None, "pole"),
        ),
        out_specs=P(None, "tile", "pole"),
        check_vma=False,
    )
```

time: 23.4 us -> 18.7 us (0.80)
  local copies, waits for them, and re-layouts: 2.4 us -> 0.01 us
  Pallas kernels: 6.39 us -> 4.79 us
  starting transfers between devices: 8.65 us -> 7.71 us
  waiting for transfers between devices: 5.65 us -> 6.04 us
    unnamed x14 -> x6, local copies, waits for them, and re-layouts: 2.4 us -> 0.01 us
    ppermute x4, starting transfers between devices: 8.15 us -> 6.19 us  [swap(): return lax.ppermute(block, axis, pairs(lax.axis_size(axis), phase))]
    pallas_call x3 -> x4, Pallas kernels: 6.39 us -> 4.79 us  [the longest x1 2.96 us: shards(): pl.pallas_call(step_kernel, out_shape=f32(*state.shape), in_specs=[vmem]...]
    ppermute x4, waiting for transfers between devices: 2.51 us -> 3.91 us  [swap(): return lax.ppermute(block, axis, pairs(lax.axis_size(axis), phase))]
    ppermute x1, starting transfers between devices: 0.51 us -> 1.52 us  [shift(): lax.ppermute(block, axis, [(i, (i + step) % count) for i in range(count)])]
    ppermute x1, waiting for transfers between devices: 3.14 us -> 2.13 us  [shift(): lax.ppermute(block, axis, [(i, (i + step) % count) for i in range(count)])]
  transfers between devices with their start and end apart: 5 -> 5, of which waited for: 2 -> 4; matrix products, arithmetic and copies ran while one was open for 0% -> 0% of each run, Pallas kernels for 0% -> 2%
where the time goes in v4:
time: 18.7 us; the launch traced here: 18.6 us
  starting transfers between devices  7.71 us (41%)
  waiting for transfers between devices  6.04 us (32%)
  Pallas kernels  4.79 us (26%)
    ppermute x4, starting transfers between devices, swap(): return lax.ppermute(block, axis, pairs(lax.axis_size(axis), phase))  6.19 us
    ppermute x4, waiting for transfers between devices, swap(): return lax.ppermute(block, axis, pairs(lax.axis_size(axis), phase))  3.91 us
    pallas_call x1, Pallas kernels, shards(): pl.pallas_call(step_kernel, out_shape=f32(*state.shape), in_specs=[vmem]...  2.96 us
    ppermute x1, waiting for transfers between devices, shift(): lax.ppermute(block, axis, [(i, (i + step) % count) for i in range(count)])  2.13 us
    pallas_call x1, Pallas kernels, shards(): pl.pallas_call(pack_columns_kernel, grid=(1,), out_shape=(f32(rows, LANES...  1.53 us
    ppermute x1, starting transfers between devices, shift(): lax.ppermute(block, axis, [(i, (i + step) % count) for i in range(count)])  1.52 us
  transfers between devices with their start and end apart: 5, of which 4 were waited for; matrix products, arithmetic and copies ran while one was open for 0% of the time, Pallas kernels for 2%

profile of v4, /device:TPU:0, one launch (start us, length us, event | category | flops | bytes accessed | tf_op | source)
XLA Modules:
  0.0 18.6 jit_solution(12348665281235389010)
XLA Ops:
  0.0 0.0 copy-start.1
  0.0 0.0 copy-start
  0.0 1.5 %pack_columns.1 = (f32[16,128]{1,0:T(8,128)}, f32[16,128]{1,0:T(8,128)}, f32[16,128]{1,0:T(8,128)}) custom-call(f32[3,16,512]{2,1,0:T(8,128)} %state.3, f32[3,16,512]{2,1,0:T(8,128)} %state.3, f32[16,512]{1,0:T(8,128)} %depth.3, f32[16,512]{1,0:T(8,128)} %depth.3, f32[4]{0:T(128)} %real.1, f32[4]{0:T(128)} %imag.1, f32[2,4]{1,0:T(2,128)} %weight.1), custom_call_target="tpu_custom_call" | custom-call | tf_op jit(solution)/shard_map/pack_columns/pallas_call | solution.py:356
  1.5 2.9 %collective-permute-start = (f32[16,128]{1,0:T(8,128)}, f32[16,128]{1,0:T(8,128)S(1)}, u32[]{:S(2)}, u32[]{:S(2)}) collective-permute-start(f32[16,128]{1,0:T(8,128)} %get-tuple-element.10), channel_id=1, source_target_pairs={{0,8},{8,0},{16,24},{24,16},{1,9},{9,1},{17,25},{25,17},{2,10},{10... | collective-permute-start | bytes 24584 | tf_op jit(solution)/shard_map/ppermute | solution.py:32
  4.5 0.0 copy-start.2
  4.5 1.5 %collective-permute-start.1 = (f32[16,128]{1,0:T(8,128)}, f32[16,128]{1,0:T(8,128)S(1)}, u32[]{:S(2)}, u32[]{:S(2)}) collective-permute-start(f32[16,128]{1,0:T(8,128)} %get-tuple-element.11), channel_id=1, source_target_pairs={{8,16},{16,8},{24,0},{0,24},{9,17},{17,9},{25,1},{1,25},{10,18},{1... | collective-permute-start | bytes 24584 | tf_op jit(solution)/shard_map/ppermute | solution.py:32
  6.0 0.3 %collective-permute-done.first = f32[16,128]{1,0:T(8,128)S(1)} collective-permute-done((f32[16,128]{1,0:T(8,128)}, f32[16,128]{1,0:T(8,128)S(1)}, u32[]{:S(2)}, u32[]{:S(2)}) %collective-permute-start) | collective-permute-done | bytes 8224 | tf_op jit(solution)/shard_map/ppermute | solution.py:32
  6.3 2.9 %collective-permute-done.1.second = f32[16,128]{1,0:T(8,128)S(1)} collective-permute-done((f32[16,128]{1,0:T(8,128)}, f32[16,128]{1,0:T(8,128)S(1)}, u32[]{:S(2)}, u32[]{:S(2)}) %collective-permute-start.1) | collective-permute-done | bytes 8224 | tf_op jit(solution)/shard_map/ppermute | solution.py:32
  9.2 0.0 copy-done.1
  9.2 0.0 copy-done
  9.3 1.7 %collective-permute-start.2 = (f32[40,512]{1,0:T(8,128)S(1)}, f32[40,512]{1,0:T(8,128)S(1)}, u32[]{:S(2)}, u32[]{:S(2)}) collective-permute-start(f32[40,512]{1,0:T(8,128)S(1)} %get-tuple-element.12), channel_id=1, source_target_pairs={{1,2},{2,1},{3,4},{4,3},{5,6},{6,5},{7,0},{0,7},{9,10},{10,9},{11,... | collective-permute-start | bytes 245768 | tf_op jit(solution)/shard_map/ppermute | solution.py:32
  11.0 0.0 collective-permute-start.3
  11.0 0.0 copy-done.2
  11.0 1.5 %collective-permute-start.4 = (f32[16,128]{1,0:T(8,128)S(1)}, f32[16,128]{1,0:T(8,128)S(1)}, u32[]{:S(2)}, u32[]{:S(2)}) collective-permute-start(f32[16,128]{1,0:T(8,128)S(1)} %copy-done.2), channel_id=1, source_target_pairs={{0,16},{8,24},{16,0},{24,8},{1,17},{9,25},{17,1},{25,9},{2,18},{10... | collective-permute-start | bytes 24584 | tf_op jit(solution)/shard_map/ppermute | solution.py:37
  12.5 2.1 %collective-permute-done.4 = f32[16,128]{1,0:T(8,128)S(1)} collective-permute-done((f32[16,128]{1,0:T(8,128)S(1)}, f32[16,128]{1,0:T(8,128)S(1)}, u32[]{:S(2)}, u32[]{:S(2)}) %collective-permute-start.4) | collective-permute-done | bytes 8224 | tf_op jit(solution)/shard_map/ppermute | solution.py:37
  14.7 0.3 %pole_sums.1.sums = f32[74,8,128]{2,1,0:T(8,128)S(1)} custom-call(f32[16,128]{1,0:T(8,128)S(1)} %copy-done.2, f32[16,128]{1,0:T(8,128)S(1)} %collective-permute-done.first, f32[16,128]{1,0:T(8,128)S(1)} %collective-permute-done.1.second, f32[1,16,128]{2,1,0:T(8,128)S(1)} %bitcast.1), custom_call_target="tpu_custom_call" | custom-call | tf_op jit(solution)/shard_map/pole_sums/pallas_call | solution.py:387
  15.0 0.6 %collective-permute-done.2.far = f32[40,512]{1,0:T(8,128)S(1)} collective-permute-done((f32[40,512]{1,0:T(8,128)S(1)}, f32[40,512]{1,0:T(8,128)S(1)}, u32[]{:S(2)}, u32[]{:S(2)}) %collective-permute-start.2) | collective-permute-done | bytes 81952 | tf_op jit(solution)/shard_map/ppermute | solution.py:32
  15.6 0.0 collective-permute-done.3.near
  15.6 3.0 %step.1 = f32[3,16,512]{2,1,0:T(8,128)} custom-call(f32[3,16,512]{2,1,0:T(8,128)S(1)} %copy-done, f32[16,512]{1,0:T(8,128)S(1)} %copy-done.1, f32[40,512]{1,0:T(8,128)S(1)} %collective-permute-done.2.far, f32[40,512]{1,0:T(8,128)S(1)} %collective-permute-done.3.near, f32[16,128]{1,0:T(8,128)S(1)} %collective-permute-done.first, ...), custom_call_target="tpu_custom_call" | custom-call | tf_op jit(solution)/shard_map/step/pallas_call | solution.py:396
  (1 shorter events, 0.0 us)
Async XLA Ops:
  0.0 9.2 %copy-start.1 = (f32[16,512]{1,0:T(8,128)S(1)}, f32[16,512]{1,0:T(8,128)}, u32[]{:S(2)}) copy-start(f32[16,512]{1,0:T(8,128)} %depth.3) | copy-start | bytes 98308
  0.0 9.2 %copy-start = (f32[3,16,512]{2,1,0:T(8,128)S(1)}, f32[3,16,512]{2,1,0:T(8,128)}, u32[]{:S(2)}) copy-start(f32[3,16,512]{2,1,0:T(8,128)} %state.3) | copy-start | bytes 294916
  1.5 4.8 %collective-permute-start = (f32[16,128]{1,0:T(8,128)}, f32[16,128]{1,0:T(8,128)S(1)}, u32[]{:S(2)}, u32[]{:S(2)}) collective-permute-start(f32[16,128]{1,0:T(8,128)} %get-tuple-element.10), channel_id=1, source_target_pairs={{0,8},{8,0},{16,24},{24,16},{1,9},{9,1},{17,25},{25,17},{2,10},{10... | collective-permute-start | bytes 24584 | tf_op jit(solution)/shard_map/ppermute | solution.py:32
  4.5 6.6 %copy-start.2 = (f32[16,128]{1,0:T(8,128)S(1)}, f32[16,128]{1,0:T(8,128)}, u32[]{:S(2)}) copy-start(f32[16,128]{1,0:T(8,128)} %get-tuple-element.14.scalars) | copy-start | bytes 24580
  4.5 4.8 %collective-permute-start.1 = (f32[16,128]{1,0:T(8,128)}, f32[16,128]{1,0:T(8,128)S(1)}, u32[]{:S(2)}, u32[]{:S(2)}) collective-permute-start(f32[16,128]{1,0:T(8,128)} %get-tuple-element.11), channel_id=1, source_target_pairs={{8,16},{16,8},{24,0},{0,24},{9,17},{17,9},{25,1},{1,25},{10,18},{1... | collective-permute-start | bytes 24584 | tf_op jit(solution)/shard_map/ppermute | solution.py:32
  9.3 6.3 %collective-permute-start.2 = (f32[40,512]{1,0:T(8,128)S(1)}, f32[40,512]{1,0:T(8,128)S(1)}, u32[]{:S(2)}, u32[]{:S(2)}) collective-permute-start(f32[40,512]{1,0:T(8,128)S(1)} %get-tuple-element.12), channel_id=1, source_target_pairs={{1,2},{2,1},{3,4},{4,3},{5,6},{6,5},{7,0},{0,7},{9,10},{10,9},{11,... | collective-permute-start | bytes 245768 | tf_op jit(solution)/shard_map/ppermute | solution.py:32
  11.0 4.6 %collective-permute-start.3 = (f32[40,512]{1,0:T(8,128)S(1)}, f32[40,512]{1,0:T(8,128)S(1)}, u32[]{:S(2)}, u32[]{:S(2)}) collective-permute-start(f32[40,512]{1,0:T(8,128)S(1)} %get-tuple-element.13), channel_id=1, source_target_pairs={{0,1},{1,0},{2,3},{3,2},{4,5},{5,4},{6,7},{7,6},{8,9},{9,8},{10,11... | collective-permute-start | bytes 245768 | tf_op jit(solution)/shard_map/ppermute | solution.py:32
  11.0 3.7 %collective-permute-start.4 = (f32[16,128]{1,0:T(8,128)S(1)}, f32[16,128]{1,0:T(8,128)S(1)}, u32[]{:S(2)}, u32[]{:S(2)}) collective-permute-start(f32[16,128]{1,0:T(8,128)S(1)} %copy-done.2), channel_id=1, source_target_pairs={{0,16},{8,24},{16,0},{24,8},{1,17},{9,25},{17,1},{25,9},{2,18},{10... | collective-permute-start | bytes 24584 | tf_op jit(solution)/shard_map/ppermute | solution.py:37

commit v5 on v4

--- a/solution.py
+++ b/solution.py
@@ -116,7 +116,7 @@
         pl.when(jnp.logical_not(low))(lambda: fill(rows - SUB, rows - SUB - 1))
 
 
-def pole_sums_kernel(scalars, first, second, others, sums):
+def pole_sums_kernel(scalars, first, second, others, poly, sums, sol):
     odd = lax.rem(lax.axis_index("pole"), 2) == 1
     count = scalars.shape[0]
     lane = lax.broadcasted_iota(jnp.int32, (SUB, LANES), 1)
@@ -198,6 +198,26 @@
     sums[9 * ITERS] = total(products["ba/s"][0])
     sums[9 * ITERS + 1] = coriolis * total(products["b/s"][0])
 
+    odd_tile = lax.rem(lax.axis_index("tile"), 2) == 1
+    rows = sol.shape[1] - 2
+    start = jnp.where(odd_tile, REACH - 1, 2 * REACH - 1)
+    weighted_sums(poly, sums, sol, start, rows + 2 - REACH)
+
+
+def weighted_sums(poly, sums, sol, start, count, block=6):
+    for r0 in range(0, count, block):
+        span = range(r0, min(r0 + block, count))
+        acc = {}
+        for f in range(3):
+            for m in range(ITERS):
+                value = [poly[f, m, start + r] for r in span]
+                for g in range(3):
+                    c = sums[(g * 3 + f) * ITERS + m]
+                    for r, v in zip(span, value):
+                        acc[g, r] = acc[g, r] + c * v if (g, r) in acc else c * v
+        for (g, r), v in acc.items():
+            sol[g, start + r - (REACH - 1)] = v
+
 
 def strips_of(tiles, side):
     lane = lax.broadcasted_iota(jnp.int32, (SUB, LANES), 1)
@@ -211,71 +231,59 @@
     return out
 
 
-def step_kernel(state, depth, far, near, first, second, sums, out, grid, poly, coef, result):
-    rows, columns = depth.shape
-    groups = rows // SUB
-    tiles = columns // LANES
-    odd_tile = lax.rem(lax.axis_index("tile"), 2) == 1
-    own = [state.at[0], state.at[1], state.at[2], depth]
-    lane = lax.broadcasted_iota(jnp.int32, (SUB, LANES), 1)
+def lay(grid, block, side, at, size, stride):
+    cut = [block[:, t * LANES : (t + 1) * LANES] for t in range(block.shape[1] // LANES)]
+    for s, strip in enumerate(strips_of(cut, side)):
+        grid[pl.Slice(at * SUB + s, size, stride * SUB), :] = strip[0:size]
+
+
+def place(side, f):
+    return turn(side, SIDE - EDGE - EDGE * f)
+
+
+def lay_halo(grid, halo, main, ext):
     sub = lax.broadcasted_iota(jnp.int32, (SUB, LANES), 0)
-
-    def lay(block, side, at, size, stride):
-        cut = [block[:, t * LANES : (t + 1) * LANES] for t in range(tiles)]
-        for s, strip in enumerate(strips_of(cut, side)):
-            grid[pl.Slice(at * SUB + s, size, stride * SUB), :] = strip[0:size]
-
-    def place(side, f):
-        return turn(side, SIDE - EDGE - EDGE * f)
-
-    for g in range(groups):
-        side = sides_of(first, second, pl.ds(g * SUB, SUB))
-        for f in range(4):
-            block = own[f][pl.ds(g * SUB, SUB), :]
-            lay(block, place(side, f), (REACH + g * SUB) * 4 + f, SUB, 4)
-    below = REACH + rows
-    near_main = jnp.where(odd_tile, 1, below)
-    far_main = jnp.where(odd_tile, below, 1)
-    near_ext = jnp.where(odd_tile, 0, below + SUB)
-    far_ext = jnp.where(odd_tile, below + SUB, 0)
     base = 4 * SUB + 4
-    for halo, main, ext in ((near, near_main, near_ext), (far, far_main, far_ext)):
-        side = jnp.concatenate(
-            [halo[base : base + 4, 0:LANES], halo[base : base + 4, LANES : 2 * LANES]], axis=0
-        )
-        for f in range(4):
-            lay(halo[pl.ds(f * SUB, SUB), :], place(side, f), main * 4 + f, SUB, 4)
-        line = halo[base : base + 1, 2 * LANES : 3 * LANES]
-        line = jnp.broadcast_to(line, (SUB, LANES))
-        side = place(line, 0)
-        for f in range(1, 4):
-            side = jnp.where(sub == f, place(line, f), side)
-        lay(halo[pl.ds(4 * SUB, SUB), :], side, ext * 4, 4, 1)
-
-    def cell(f, r):
-        return grid[pl.ds((r * 4 + f) * SUB, SUB), :]
-
-    def left(x):
-        return pltpu.roll(x, 1, 1)
-
-    def right(x):
-        return pltpu.roll(x, LANES - 1, 1)
-
-    height = rows + 2 * REACH
-
+    side = jnp.concatenate(
+        [halo[base : base + 4, 0:LANES], halo[base : base + 4, LANES : 2 * LANES]], axis=0
+    )
+    for f in range(4):
+        lay(grid, halo[pl.ds(f * SUB, SUB), :], place(side, f), main * 4 + f, SUB, 4)
+    line = halo[base : base + 1, 2 * LANES : 3 * LANES]
+    line = jnp.broadcast_to(line, (SUB, LANES))
+    side = place(line, 0)
+    for f in range(1, 4):
+        side = jnp.where(sub == f, place(line, f), side)
+    lay(grid, halo[pl.ds(4 * SUB, SUB), :], side, ext * 4, 4, 1)
+
+
+def cell(grid, f, r):
+    return grid[pl.ds(pl.multiple_of((r * 4 + f) * SUB, SUB), SUB), :]
+
+
+def left(x):
+    return pltpu.roll(x, 1, 1)
+
+
+def right(x):
+    return pltpu.roll(x, LANES - 1, 1)
+
+
+def prepare(grid, poly, coef, start, count):
     flux_east = [None] * 3
     flux_north = [None] * 3
     depths = [None] * 2
     across = None
-    for r in range(height):
-        h = cell(3, r)
-        flux_east = flux_east[1:] + [h * cell(1, r)]
-        flux_north = flux_north[1:] + [h * cell(2, r)]
+    for k in range(count + 2):
+        r = start + k
+        h = cell(grid, 3, r)
+        flux_east = flux_east[1:] + [h * cell(grid, 1, r)]
+        flux_north = flux_north[1:] + [h * cell(grid, 2, r)]
         depths = depths[1:] + [h]
-        if r >= 1:
+        if k >= 1:
             before, across = across, 0.125 * (depths[0] + depths[1])
             coef[0, r - 1] = across
-        if r >= 2:
+        if k >= 2:
             c = r - 1
             north = 0.125 * (depths[0] + right(depths[0]))
             south = left(north)
@@ -288,54 +296,74 @@
             east_slope = flux_north[2] - flux_north[0]
             north_slope = right(flux_east[1]) - left(flux_east[1])
             poly[2, 0, c] = 0.5 * (east_slope - north_slope)
-            poly[0, 0, c] = cell(0, c)
-
+            poly[0, 0, c] = cell(grid, 0, c)
+
+
+def sweep(poly, coef, m, start, count):
+    back = [poly[f, m, start - 1] for f in range(3)]
+    here = [poly[f, m, start] for f in range(3)]
+    below = coef[0, start - 1]
+    for k in range(count):
+        r = start + k
+        above, north, south, diag = coef[0, r], coef[1, r], coef[2, r], coef[3, r]
+        ahead = [poly[f, m, r + 1] for f in range(3)]
+        for f in range(3):
+            value = diag * here[f] + (above * ahead[f] + below * back[f])
+            value = value + (north * right(here[f]) + south * left(here[f]))
+            value = 0.5 * value if m == 0 else value - poly[f, m - 1, r]
+            poly[f, m + 1, r] = value
+        back, here, below = here, ahead, above
+
+
+def inner_kernel(state, depth, near, first, second, grid, poly, coef):
+    rows = depth.shape[0]
+    odd_tile = lax.rem(lax.axis_index("tile"), 2) == 1
+    own = [state.at[0], state.at[1], state.at[2], depth]
+    for g in range(rows // SUB):
+        side = sides_of(first, second, pl.ds(g * SUB, SUB))
+        for f in range(4):
+            block = own[f][pl.ds(g * SUB, SUB), :]
+            lay(grid, block, place(side, f), (REACH + g * SUB) * 4 + f, SUB, 4)
+    below = REACH + rows
+    main = jnp.where(odd_tile, 1, below)
+    ext = jnp.where(odd_tile, 0, below + SUB)
+    lay_halo(grid, near, main, ext)
+    start = jnp.where(odd_tile, 0, REACH)
+    prepare(grid, poly, coef, start, rows + REACH - 2)
     for m in range(ITERS - 1):
-        low, high = m + 2, height - m - 2
-        back = [poly[f, m, low - 1] for f in range(3)]
-        here = [poly[f, m, low] for f in range(3)]
-        below_ = coef[0, low - 1]
-        for r in range(low, high):
-            above, north, south, diag = coef[0, r], coef[1, r], coef[2, r], coef[3, r]
-            ahead = [poly[f, m, r + 1] for f in range(3)]
-            for f in range(3):
-                value = diag * here[f] + (above * ahead[f] + below_ * back[f])
-                value = value + (north * right(here[f]) + south * left(here[f]))
-                value = 0.5 * value if m == 0 else value - poly[f, m - 1, r]
-                poly[f, m + 1, r] = value
-            back, here, below_ = here, ahead, above
-
-    sol = {}
-    block = 6
-    for r0 in range(REACH - 1, REACH + rows + 1, block):
-        span = range(r0, min(r0 + block, REACH + rows + 1))
-        acc = {}
-        for f in range(3):
-            for m in range(ITERS):
-                value = [poly[f, m, r] for r in span]
-                for g in range(3):
-                    c = sums[(g * 3 + f) * ITERS + m]
-                    for r, v in zip(span, value):
-                        if g == 0 and not REACH <= r < REACH + rows:
-                            continue
-                        acc[g, r] = acc[g, r] + c * v if (g, r) in acc else c * v
-        sol.update(acc)
+        sweep(poly, coef, m, start + m + 2, rows + REACH - 4 - 2 * m)
+
+
+def outer_kernel(far, sums, grid_in, poly_in, coef_in, sol_in, out, grid, poly, coef, sol, result):
+    rows, columns = out.shape[1:]
+    odd_tile = lax.rem(lax.axis_index("tile"), 2) == 1
+    lane = lax.broadcasted_iota(jnp.int32, (SUB, LANES), 1)
+    below = REACH + rows
+    main = jnp.where(odd_tile, below, 1)
+    ext = jnp.where(odd_tile, below + SUB, 0)
+    lay_halo(grid, far, main, ext)
+    start = jnp.where(odd_tile, below - 2, 0)
+    prepare(grid, poly, coef, start, REACH)
+    step = jnp.where(odd_tile, -1, 1)
+    for m in range(ITERS - 1):
+        sweep(poly, coef, m, start + 1 + step * (m + 1), REACH)
+    first = jnp.where(odd_tile, rows + 1, REACH - 1)
+    weighted_sums(poly, sums, sol, first, REACH)
     push = sums[9 * ITERS]
     lift = sums[9 * ITERS + 1]
     for i in range(rows):
-        r = REACH + i
-        u, v = cell(1, r), cell(2, r)
-        result[0, pl.ds(i * SUB, SUB)] = sol[0, r]
-        east = 0.5 * (sol[1, r + 1] - sol[1, r - 1])
-        north = 0.5 * (right(sol[2, r]) - left(sol[2, r]))
+        u, v = cell(grid, 1, REACH + i), cell(grid, 2, REACH + i)
+        result[0, pl.ds(i * SUB, SUB)] = sol[0, i + 1]
+        east = 0.5 * (sol[1, i + 2] - sol[1, i])
+        north = 0.5 * (right(sol[2, i + 1]) - left(sol[2, i + 1]))
         result[1, pl.ds(i * SUB, SUB)] = (push * u + lift * v) - (east + coriolis * north)
-        east = 0.5 * (sol[2, r + 1] - sol[2, r - 1])
-        north = 0.5 * (right(sol[1, r]) - left(sol[1, r]))
+        east = 0.5 * (sol[2, i + 2] - sol[2, i])
+        north = 0.5 * (right(sol[1, i + 1]) - left(sol[1, i + 1]))
         result[2, pl.ds(i * SUB, SUB)] = (push * v - lift * u) + (coriolis * east - north)
 
     for k in range(3):
-        for g in range(groups):
-            for t in range(tiles):
+        for g in range(rows // SUB):
+            for t in range(columns // LANES):
                 one = result[k, pl.Slice(g * SUB * SUB + 2 * t, SUB, SUB), :]
                 two = result[k, pl.Slice(g * SUB * SUB + 2 * t + 1, SUB, SUB), :]
                 joined = jnp.where(lane < HALF, turn(one, -SIDE), turn(two, SIDE))
@@ -384,29 +412,41 @@
     near = swap(near, "tile", 0)
     count = lax.axis_size("pole")
     others = jnp.stack([shift(scalars, "pole", step) for step in range(2, count - 1)])
-    sums = pl.pallas_call(
+    height = rows + 2 * REACH
+    grid = f32(height * 4 * SUB, LANES)
+    poly = f32(3, ITERS, height, SUB, LANES)
+    coef = f32(4, height, SUB, LANES)
+    sol = f32(3, rows + 2, SUB, LANES)
+    held = 4 * SUB * LANES * height * (4 + 3 * ITERS + 4)
+    inner = pl.pallas_call(
+        inner_kernel,
+        out_shape=(grid, poly, coef),
+        in_specs=[vmem] * 5,
+        out_specs=(vmem, vmem, vmem),
+        compiler_params=small,
+        cost_estimate=pl.CostEstimate(
+            flops=40 * 3 * ITERS * height * SUB * LANES, bytes_accessed=held, transcendentals=0
+        ),
+        name="inner",
+    )(state, depth, near, first, second)
+    sums, part = pl.pallas_call(
         pole_sums_kernel,
-        out_shape=f32(9 * ITERS + 2, SUB, LANES),
-        in_specs=[vmem] * 4,
-        out_specs=vmem,
+        out_shape=(f32(9 * ITERS + 2, SUB, LANES), sol),
+        in_specs=[vmem] * 5,
+        out_specs=(vmem, vmem),
         compiler_params=small,
         name="pole_sums",
-    )(scalars, first, second, others)
-    height = rows + 2 * REACH
+    )(scalars, first, second, others, inner[1])
     return pl.pallas_call(
-        step_kernel,
-        out_shape=f32(*state.shape),
-        in_specs=[vmem] * 7,
-        out_specs=vmem,
-        scratch_shapes=[
-            pltpu.VMEM((height * 4 * SUB, LANES), jnp.float32),
-            pltpu.VMEM((3, ITERS, height, SUB, LANES), jnp.float32),
-            pltpu.VMEM((4, height, SUB, LANES), jnp.float32),
-            pltpu.VMEM((3, rows * SUB, LANES), jnp.float32),
-        ],
+        outer_kernel,
+        out_shape=(f32(*state.shape), grid, poly, coef, sol),
+        in_specs=[vmem] * 6,
+        out_specs=(vmem,) * 5,
+        input_output_aliases={2: 1, 3: 2, 4: 3, 5: 4},
+        scratch_shapes=[pltpu.VMEM((3, rows * SUB, LANES), jnp.float32)],
         compiler_params=small,
-        name="step",
-    )(state, depth, far, near, first, second, sums)
+        name="outer",
+    )(far, sums, *inner, part)[0]
 
 
 def solution(mesh):

time: 18.7 us -> 22.3 us (1.19)
  local copies, waits for them, and re-layouts: 0.01 us -> 2.35 us
  starting transfers between devices: 7.71 us -> 9.72 us
  waiting for transfers between devices: 6.04 us -> 4.12 us
  Pallas kernels: 4.79 us -> 5.72 us
    unnamed x6, local copies, waits for them, and re-layouts: 0.01 us -> 2.35 us
    ppermute x4, starting transfers between devices: 6.19 us -> 8.2 us  [swap(): return lax.ppermute(block, axis, pairs(lax.axis_size(axis), phase))]
    ppermute x1, waiting for transfers between devices: 2.13 us -> 0.85 us  [shift(): lax.ppermute(block, axis, [(i, (i + step) % count) for i in range(count)])]
    pallas_call x2 -> x3, Pallas kernels: 3.25 us -> 4.17 us  [the longest x1 2.23 us: shards(): pl.pallas_call(outer_kernel, out_shape=(f32(*state.shape), grid, poly, co...]
    ppermute x4, waiting for transfers between devices: 3.91 us -> 3.27 us  [swap(): return lax.ppermute(block, axis, pairs(lax.axis_size(axis), phase))]
  transfers between devices with their start and end apart: 5 -> 5, of which waited for: 4 -> 3; matrix products, arithmetic and copies ran while one was open for 0% -> 0% of each run, Pallas kernels for 2% -> 9%
where the time goes in v5:
time: 22.3 us; the launch traced here: 21.9 us
  starting transfers between devices  9.72 us (44%)
  Pallas kernels  5.72 us (26%)
  waiting for transfers between devices  4.12 us (18%)
  local copies, waits for them, and re-layouts  2.35 us (11%)
    ppermute x4, starting transfers between devices, swap(): return lax.ppermute(block, axis, pairs(lax.axis_size(axis), phase))  8.2 us
    ppermute x4, waiting for transfers between devices, swap(): return lax.ppermute(block, axis, pairs(lax.axis_size(axis), phase))  3.27 us
    unnamed x6, local copies, waits for them, and re-layouts  2.35 us
    pallas_call x1, Pallas kernels, shards(): pl.pallas_call(outer_kernel, out_shape=(f32(*state.shape), grid, poly, co...  2.23 us
    pallas_call x1, Pallas kernels, shards(): pl.pallas_call(pack_columns_kernel, grid=(1,), out_shape=(f32(rows, LANES...  1.53 us
    ppermute x1, starting transfers between devices, shift(): lax.ppermute(block, axis, [(i, (i + step) % count) for i in range(count)])  1.52 us
    pallas_call x1, Pallas kernels, shards(): pl.pallas_call(inner_kernel, out_shape=(grid, poly, coef), in_specs=[vmem...  1.49 us
    ppermute x1, waiting for transfers between devices, shift(): lax.ppermute(block, axis, [(i, (i + step) % count) for i in range(count)])  0.85 us
  transfers between devices with their start and end apart: 5, of which 3 were waited for; matrix products, arithmetic and copies ran while one was open for 0% of the time, Pallas kernels for 9%

profile of v5, /device:TPU:0, one launch (start us, length us, event | category | flops | bytes accessed | tf_op | source)
XLA Modules:
  0.0 21.9 jit_solution(17602982410201325058)
XLA Ops:
  0.0 1.5 %pack_columns.1 = (f32[16,128]{1,0:T(8,128)}, f32[16,128]{1,0:T(8,128)}, f32[16,128]{1,0:T(8,128)}) custom-call(f32[3,16,512]{2,1,0:T(8,128)} %state.3, f32[3,16,512]{2,1,0:T(8,128)} %state.3, f32[16,512]{1,0:T(8,128)} %depth.3, f32[16,512]{1,0:T(8,128)} %depth.3, f32[4]{0:T(128)} %real.1, f32[4]{0:T(128)} %imag.1, f32[2,4]{1,0:T(2,128)} %weight.1), custom_call_target="tpu_custom_call" | custom-call | tf_op jit(solution)/shard_map/pack_columns/pallas_call | solution.py:384
  1.5 2.9 %collective-permute-start = (f32[16,128]{1,0:T(8,128)}, f32[16,128]{1,0:T(8,128)S(1)}, u32[]{:S(2)}, u32[]{:S(2)}) collective-permute-start(f32[16,128]{1,0:T(8,128)} %get-tuple-element.16), channel_id=1, source_target_pairs={{0,8},{8,0},{16,24},{24,16},{1,9},{9,1},{17,25},{25,17},{2,10},{10... | collective-permute-start | bytes 24584 | tf_op jit(solution)/shard_map/ppermute | solution.py:32
  4.5 1.5 %collective-permute-start.1 = (f32[16,128]{1,0:T(8,128)}, f32[16,128]{1,0:T(8,128)S(1)}, u32[]{:S(2)}, u32[]{:S(2)}) collective-permute-start(f32[16,128]{1,0:T(8,128)} %get-tuple-element.17), channel_id=1, source_target_pairs={{8,16},{16,8},{24,0},{0,24},{9,17},{17,9},{25,1},{1,25},{10,18},{1... | collective-permute-start | bytes 24584 | tf_op jit(solution)/shard_map/ppermute | solution.py:32
  6.0 0.3 %collective-permute-done.first = f32[16,128]{1,0:T(8,128)S(1)} collective-permute-done((f32[16,128]{1,0:T(8,128)}, f32[16,128]{1,0:T(8,128)S(1)}, u32[]{:S(2)}, u32[]{:S(2)}) %collective-permute-start) | collective-permute-done | bytes 8224 | tf_op jit(solution)/shard_map/ppermute | solution.py:32
  6.3 2.9 %collective-permute-done.1.second = f32[16,128]{1,0:T(8,128)S(1)} collective-permute-done((f32[16,128]{1,0:T(8,128)}, f32[16,128]{1,0:T(8,128)S(1)}, u32[]{:S(2)}, u32[]{:S(2)}) %collective-permute-start.1) | collective-permute-done | bytes 8224 | tf_op jit(solution)/shard_map/ppermute | solution.py:32
  9.2 0.0 copy-start
  9.2 0.9 %copy-done = f32[3,16,512]{2,1,0:T(8,128)S(1)} copy-done((f32[3,16,512]{2,1,0:T(8,128)S(1)}, f32[3,16,512]{2,1,0:T(8,128)}, u32[]{:S(2)}) %copy-start) | copy-done | bytes 98328
  10.1 0.0 copy-start.1
  10.1 0.8 %copy-done.1 = f32[16,512]{1,0:T(8,128)S(1)} copy-done((f32[16,512]{1,0:T(8,128)S(1)}, f32[16,512]{1,0:T(8,128)}, u32[]{:S(2)}) %copy-start.1) | copy-done | bytes 32792
  10.9 0.1 collective-permute-start.4
  11.0 3.7 %collective-permute-start.2 = (f32[40,512]{1,0:T(8,128)S(1)}, f32[40,512]{1,0:T(8,128)S(1)}, u32[]{:S(2)}, u32[]{:S(2)}) collective-permute-start(f32[40,512]{1,0:T(8,128)S(1)} %get-tuple-element.18), channel_id=1, source_target_pairs={{1,2},{2,1},{3,4},{4,3},{5,6},{6,5},{7,0},{0,7},{9,10},{10,9},{11,... | collective-permute-start | bytes 245768 | tf_op jit(solution)/shard_map/ppermute | solution.py:32
  14.7 1.5 %collective-permute-start.3 = (f32[16,128]{1,0:T(8,128)}, f32[16,128]{1,0:T(8,128)S(1)}, u32[]{:S(2)}, u32[]{:S(2)}) collective-permute-start(f32[16,128]{1,0:T(8,128)} %get-tuple-element.19.scalars), channel_id=1, source_target_pairs={{0,16},{8,24},{16,0},{24,8},{1,17},{9,25},{17,1},{25,9},{2,18},{10... | collective-permute-start | bytes 24584 | tf_op jit(solution)/shard_map/ppermute | solution.py:37
  16.2 0.0 collective-permute-done.4.near
  16.2 1.5 %inner.1 = (f32[1088,128]{1,0:T(8,128)S(1)}, f32[3,8,34,8,128]{4,3,2,1,0:T(8,128)S(1)}, f32[4,34,8,128]{3,2,1,0:T(8,128)S(1)}) custom-call(f32[3,16,512]{2,1,0:T(8,128)S(1)} %copy-done, f32[16,512]{1,0:T(8,128)S(1)} %copy-done.1, f32[40,512]{1,0:T(8,128)S(1)} %collective-permute-done.4.near, f32[16,128]{1,0:T(8,128)S(1)} %collective-permute-done.first, ...), custom_call_target="tpu_custom_call" | custom-call | flops 33423360 | bytes 4456448 | tf_op jit(solution)/shard_map/inner/pallas_call | solution.py:421
  17.7 0.8 %collective-permute-done.3 = f32[16,128]{1,0:T(8,128)S(1)} collective-permute-done((f32[16,128]{1,0:T(8,128)}, f32[16,128]{1,0:T(8,128)S(1)}, u32[]{:S(2)}, u32[]{:S(2)}) %collective-permute-start.3) | collective-permute-done | bytes 8224 | tf_op jit(solution)/shard_map/ppermute | solution.py:37
  18.5 0.0 copy-start.2
  18.5 0.7 %copy-done.2 = f32[16,128]{1,0:T(8,128)S(1)} copy-done((f32[16,128]{1,0:T(8,128)S(1)}, f32[16,128]{1,0:T(8,128)}, u32[]{:S(2)}) %copy-start.2) | copy-done | bytes 8216
  19.2 0.5 %pole_sums.1 = (f32[74,8,128]{2,1,0:T(8,128)S(1)}, f32[3,18,8,128]{3,2,1,0:T(8,128)S(1)}) custom-call(f32[16,128]{1,0:T(8,128)S(1)} %copy-done.2, f32[16,128]{1,0:T(8,128)S(1)} %collective-permute-done.first, f32[16,128]{1,0:T(8,128)S(1)} %collective-permute-done.1.second, f32[1,16,128]{2,1,0:T(8,128)S(1)} %bitcast.1, ...), custom_call_target="tpu_custom_call" | custom-call | tf_op jit(solution)/shard_map/pole_sums/pallas_call | solution.py:432
  19.7 0.0 collective-permute-done.2.far
  19.7 2.2 %outer.1 = (f32[3,16,512]{2,1,0:T(8,128)}, f32[1088,128]{1,0:T(8,128)S(1)}, f32[3,8,34,8,128]{4,3,2,1,0:T(8,128)S(1)}, f32[4,34,8,128]{3,2,1,0:T(8,128)S(1)}, f32[3,18,8,128]{3,2,1,0:T(8,128)S(1)}) custom-call(f32[40,512]{1,0:T(8,128)S(1)} %collective-permute-done.2.far, ...), custom_call_target="tpu_custom_call", output_to_operand_aliasing={{1}: (2, {}), {2}: (3, {}), {3}: (4, {}), {4}: (5, {})} | custom-call | tf_op jit(solution)/shard_map/outer/pallas_call | solution.py:440
  (1 shorter events, 0.0 us)
Async XLA Ops:
  1.5 4.8 %collective-permute-start = (f32[16,128]{1,0:T(8,128)}, f32[16,128]{1,0:T(8,128)S(1)}, u32[]{:S(2)}, u32[]{:S(2)}) collective-permute-start(f32[16,128]{1,0:T(8,128)} %get-tuple-element.16), channel_id=1, source_target_pairs={{0,8},{8,0},{16,24},{24,16},{1,9},{9,1},{17,25},{25,17},{2,10},{10... | collective-permute-start | bytes 24584 | tf_op jit(solution)/shard_map/ppermute | solution.py:32
  4.5 4.8 %collective-permute-start.1 = (f32[16,128]{1,0:T(8,128)}, f32[16,128]{1,0:T(8,128)S(1)}, u32[]{:S(2)}, u32[]{:S(2)}) collective-permute-start(f32[16,128]{1,0:T(8,128)} %get-tuple-element.17), channel_id=1, source_target_pairs={{8,16},{16,8},{24,0},{0,24},{9,17},{17,9},{25,1},{1,25},{10,18},{1... | collective-permute-start | bytes 24584 | tf_op jit(solution)/shard_map/ppermute | solution.py:32
  9.2 0.9 %copy-start = (f32[3,16,512]{2,1,0:T(8,128)S(1)}, f32[3,16,512]{2,1,0:T(8,128)}, u32[]{:S(2)}) copy-start(f32[3,16,512]{2,1,0:T(8,128)} %state.3) | copy-start | bytes 294916
  10.1 0.8 %copy-start.1 = (f32[16,512]{1,0:T(8,128)S(1)}, f32[16,512]{1,0:T(8,128)}, u32[]{:S(2)}) copy-start(f32[16,512]{1,0:T(8,128)} %depth.3) | copy-start | bytes 98308
  10.9 5.3 %collective-permute-start.4 = (f32[40,512]{1,0:T(8,128)S(1)}, f32[40,512]{1,0:T(8,128)S(1)}, u32[]{:S(2)}, u32[]{:S(2)}) collective-permute-start(f32[40,512]{1,0:T(8,128)S(1)} %get-tuple-element.20), channel_id=1, source_target_pairs={{0,1},{1,0},{2,3},{3,2},{4,5},{5,4},{6,7},{7,6},{8,9},{9,8},{10,11... | collective-permute-start | bytes 245768 | tf_op jit(solution)/shard_map/ppermute | solution.py:32
  11.0 8.7 %collective-permute-start.2 = (f32[40,512]{1,0:T(8,128)S(1)}, f32[40,512]{1,0:T(8,128)S(1)}, u32[]{:S(2)}, u32[]{:S(2)}) collective-permute-start(f32[40,512]{1,0:T(8,128)S(1)} %get-tuple-element.18), channel_id=1, source_target_pairs={{1,2},{2,1},{3,4},{4,3},{5,6},{6,5},{7,0},{0,7},{9,10},{10,9},{11,... | collective-permute-start | bytes 245768 | tf_op jit(solution)/shard_map/ppermute | solution.py:32
  14.7 3.9 %collective-permute-start.3 = (f32[16,128]{1,0:T(8,128)}, f32[16,128]{1,0:T(8,128)S(1)}, u32[]{:S(2)}, u32[]{:S(2)}) collective-permute-start(f32[16,128]{1,0:T(8,128)} %get-tuple-element.19.scalars), channel_id=1, source_target_pairs={{0,16},{8,24},{16,0},{24,8},{1,17},{9,25},{17,1},{25,9},{2,18},{10... | collective-permute-start | bytes 24584 | tf_op jit(solution)/shard_map/ppermute | solution.py:37
  18.5 0.7 %copy-start.2 = (f32[16,128]{1,0:T(8,128)S(1)}, f32[16,128]{1,0:T(8,128)}, u32[]{:S(2)}) copy-start(f32[16,128]{1,0:T(8,128)} %get-tuple-element.19.scalars) | copy-start | bytes 24580

commit v6 on v5

--- a/solution.py
+++ b/solution.py
@@ -55,15 +55,26 @@
 
 
 def pack_columns_kernel(
-    state_west, state_east, depth_west, depth_east, real, imag, weight, first, second, scalars
+    state, depth, real, imag, weight, fields, first, second, scalars, real_in, imag_in, weight_in, done
 ):
+    moves = [
+        pltpu.make_async_copy(state, fields.at[pl.ds(0, 3)], done.at[0]),
+        pltpu.make_async_copy(depth, fields.at[3], done.at[1]),
+        pltpu.make_async_copy(real, real_in, done.at[2]),
+        pltpu.make_async_copy(imag, imag_in, done.at[3]),
+        pltpu.make_async_copy(weight, weight_in, done.at[4]),
+    ]
+    for move in moves:
+        move.start()
+    for move in moves:
+        move.wait()
     odd = lax.rem(lax.axis_index("pole"), 2) == 1
-    rows = depth_west.shape[0]
+    rows, columns = fields.shape[1:]
     lane = lax.broadcasted_iota(jnp.int32, (SUB, LANES), 1)
     sub = lax.broadcasted_iota(jnp.int32, (SUB, LANES), 0)
     poles = real.shape[0]
-    values = [real[i] for i in range(poles)] + [imag[i] for i in range(poles)]
-    values += [weight[0, i] for i in range(poles)] + [weight[1, i] for i in range(poles)]
+    values = [real_in[i] for i in range(poles)] + [imag_in[i] for i in range(poles)]
+    values += [weight_in[0, i] for i in range(poles)] + [weight_in[1, i] for i in range(poles)]
     spread = []
     for g in range(len(values) // SUB):
         block = jnp.full((SUB, LANES), values[g * SUB], jnp.float32)
@@ -77,8 +88,8 @@
         eastward = rest
         westward = rest
         for f in range(4):
-            west = depth_west[cut, :] if f == 3 else state_west[f, cut, :]
-            east = depth_east[cut, :] if f == 3 else state_east[f, cut, :]
+            west = fields[f, cut, 0:LANES]
+            east = fields[f, cut, columns - LANES : columns]
             low, high = EDGE * f, EDGE * (f + 1)
             take = jnp.logical_and(lane >= low, lane < high)
             eastward = jnp.where(take, turn(east, low + EDGE), eastward)
@@ -95,15 +106,14 @@
     return jnp.where(from_first, first[cut, :], second[cut, :])
 
 
-def pack_rows_kernel(state, depth, first, second, far, near):
+def pack_rows_kernel(fields, second, first, far, near):
     odd = lax.rem(lax.axis_index("tile"), 2) == 1
-    rows = depth.shape[0]
-    fields = [state.at[0], state.at[1], state.at[2], depth]
+    rows = fields.shape[1]
     for target, low in ((far, jnp.logical_not(odd)), (near, odd)):
         def fill(main, ext):
             for f in range(4):
-                target[f * SUB : (f + 1) * SUB] = fields[f][main : main + SUB]
-                target[4 * SUB + f : 4 * SUB + f + 1] = fields[f][ext : ext + 1]
+                target[f * SUB : (f + 1) * SUB] = fields[f, main : main + SUB]
+                target[4 * SUB + f : 4 * SUB + f + 1] = fields[f, ext : ext + 1]
             side = sides_of(first, second, pl.ds(main, SUB))
             base = 4 * SUB + 4
             target[base : base + 4, 0:LANES] = side[0:4]
@@ -198,25 +208,38 @@
     sums[9 * ITERS] = total(products["ba/s"][0])
     sums[9 * ITERS + 1] = coriolis * total(products["b/s"][0])
 
-    odd_tile = lax.rem(lax.axis_index("tile"), 2) == 1
     rows = sol.shape[1] - 2
-    start = jnp.where(odd_tile, REACH - 1, 2 * REACH - 1)
-    weighted_sums(poly, sums, sol, start, rows + 2 - REACH)
-
-
-def weighted_sums(poly, sums, sol, start, count, block=6):
-    for r0 in range(0, count, block):
-        span = range(r0, min(r0 + block, count))
+    span = range(REACH + 1, REACH + rows - 1)
+    weighted_sums(poly, sums, sol, {r: range(known(rows, r) + 1) for r in span}, False)
+
+
+def known(rows, r):
+    return min(ITERS - 2, r - (REACH + 1), REACH + rows - 2 - r)
+
+
+def weighted_sums(poly, sums, sol, terms, more, block=6):
+    low = REACH - 1
+    order = sorted(terms)
+    for i in range(0, len(order), block):
+        span = order[i : i + block]
         acc = {}
+        if more:
+            for r in span:
+                if len(terms[r]) < ITERS:
+                    for g in range(3):
+                        acc[g, r] = sol[g, r - low]
         for f in range(3):
             for m in range(ITERS):
-                value = [poly[f, m, start + r] for r in span]
+                part = [r for r in span if m in terms[r]]
+                if not part:
+                    continue
+                value = [poly[f, m, r] for r in part]
                 for g in range(3):
                     c = sums[(g * 3 + f) * ITERS + m]
-                    for r, v in zip(span, value):
+                    for r, v in zip(part, value):
                         acc[g, r] = acc[g, r] + c * v if (g, r) in acc else c * v
         for (g, r), v in acc.items():
-            sol[g, start + r - (REACH - 1)] = v
+            sol[g, r - low] = v
 
 
 def strips_of(tiles, side):
@@ -315,40 +338,36 @@
         back, here, below = here, ahead, above
 
 
-def inner_kernel(state, depth, near, first, second, grid, poly, coef):
-    rows = depth.shape[0]
-    odd_tile = lax.rem(lax.axis_index("tile"), 2) == 1
-    own = [state.at[0], state.at[1], state.at[2], depth]
+def inner_kernel(fields, first, second, grid, poly, coef):
+    rows = fields.shape[1]
     for g in range(rows // SUB):
         side = sides_of(first, second, pl.ds(g * SUB, SUB))
         for f in range(4):
-            block = own[f][pl.ds(g * SUB, SUB), :]
+            block = fields[f, pl.ds(g * SUB, SUB), :]
             lay(grid, block, place(side, f), (REACH + g * SUB) * 4 + f, SUB, 4)
-    below = REACH + rows
-    main = jnp.where(odd_tile, 1, below)
-    ext = jnp.where(odd_tile, 0, below + SUB)
-    lay_halo(grid, near, main, ext)
-    start = jnp.where(odd_tile, 0, REACH)
-    prepare(grid, poly, coef, start, rows + REACH - 2)
+    prepare(grid, poly, coef, REACH, rows - 2)
     for m in range(ITERS - 1):
-        sweep(poly, coef, m, start + m + 2, rows + REACH - 4 - 2 * m)
-
-
-def outer_kernel(far, sums, grid_in, poly_in, coef_in, sol_in, out, grid, poly, coef, sol, result):
+        if rows - 4 - 2 * m > 0:
+            sweep(poly, coef, m, REACH + 2 + m, rows - 4 - 2 * m)
+
+
+def outer_kernel(far, near, sums, grid_in, poly_in, coef_in, sol_in, out, grid, poly, coef, sol, result):
     rows, columns = out.shape[1:]
     odd_tile = lax.rem(lax.axis_index("tile"), 2) == 1
     lane = lax.broadcasted_iota(jnp.int32, (SUB, LANES), 1)
     below = REACH + rows
-    main = jnp.where(odd_tile, below, 1)
-    ext = jnp.where(odd_tile, below + SUB, 0)
-    lay_halo(grid, far, main, ext)
-    start = jnp.where(odd_tile, below - 2, 0)
-    prepare(grid, poly, coef, start, REACH)
-    step = jnp.where(odd_tile, -1, 1)
+    for halo, above in ((near, odd_tile), (far, jnp.logical_not(odd_tile))):
+        main = jnp.where(above, 1, below)
+        ext = jnp.where(above, 0, below + SUB)
+        lay_halo(grid, halo, main, ext)
+    prepare(grid, poly, coef, 0, REACH)
+    prepare(grid, poly, coef, below - 2, REACH)
     for m in range(ITERS - 1):
-        sweep(poly, coef, m, start + 1 + step * (m + 1), REACH)
-    first = jnp.where(odd_tile, rows + 1, REACH - 1)
-    weighted_sums(poly, sums, sol, first, REACH)
+        sweep(poly, coef, m, 2 + m, REACH)
+        sweep(poly, coef, m, below - 2 - m, REACH)
+    span = range(REACH - 1, REACH + rows + 1)
+    terms = {r: range(max(known(rows, r), -1) + 1, ITERS) for r in span}
+    weighted_sums(poly, sums, sol, terms, True)
     push = sums[9 * ITERS]
     lift = sums[9 * ITERS + 1]
     for i in range(rows):
@@ -374,40 +393,47 @@
     rows, columns = depth.shape
     poles = pole_real.shape[0]
     vmem = pl.BlockSpec(memory_space=pltpu.VMEM)
-    smem = pl.BlockSpec(memory_space=pltpu.SMEM)
     small = pltpu.CompilerParams(vmem_limit_bytes=GRANT)
 
     def f32(*shape):
         return jax.ShapeDtypeStruct(shape, jnp.float32)
 
-    last = columns // LANES - 1
-    first, second, scalars = pl.pallas_call(
+    given = [
+        pltpu.with_memory_space_constraint(x, pltpu.HBM)
+        for x in (state, depth, pole_real, pole_imag, pole_weight)
+    ]
+    hbm = pl.BlockSpec(memory_space=pltpu.HBM)
+    message = pltpu.VMEM((rows, LANES), jnp.float32)
+    fields, first, second, scalars = pl.pallas_call(
         pack_columns_kernel,
-        grid=(1,),
-        out_shape=(f32(rows, LANES), f32(rows, LANES), f32(4 * poles, LANES)),
-        in_specs=[
-            pl.BlockSpec((3, rows, LANES), lambda i: (0, 0, 0)),
-            pl.BlockSpec((3, rows, LANES), lambda i: (0, 0, last)),
-            pl.BlockSpec((rows, LANES), lambda i: (0, 0)),
-            pl.BlockSpec((rows, LANES), lambda i: (0, last)),
-            smem,
-            smem,
-            smem,
+        out_shape=(
+            pltpu.VMEM((4, rows, columns), jnp.float32),
+            message,
+            message,
+            pltpu.VMEM((4 * poles, LANES), jnp.float32),
+        ),
+        in_specs=[hbm] * 5,
+        out_specs=(vmem,) * 4,
+        scratch_shapes=[
+            pltpu.SMEM(pole_real.shape, jnp.float32),
+            pltpu.SMEM(pole_imag.shape, jnp.float32),
+            pltpu.SMEM(pole_weight.shape, jnp.float32),
+            pltpu.SemaphoreType.DMA((5,)),
         ],
-        out_specs=(vmem, vmem, vmem),
+        compiler_params=small,
         name="pack_columns",
-    )(state, state, depth, depth, pole_real, pole_imag, pole_weight)
+    )(*given)
+    second = swap(second, "pole", 1)
     first = swap(first, "pole", 0)
-    second = swap(second, "pole", 1)
     halo = f32(5 * SUB, columns)
     far, near = pl.pallas_call(
         pack_rows_kernel,
         out_shape=(halo, halo),
-        in_specs=[vmem] * 4,
+        in_specs=[vmem] * 3,
         out_specs=(vmem, vmem),
         compiler_params=small,
         name="pack_rows",
-    )(state, depth, first, second)
+    )(fields, second, first)
     far = swap(far, "tile", 1)
     near = swap(near, "tile", 0)
     count = lax.axis_size("pole")
@@ -421,14 +447,14 @@
     inner = pl.pallas_call(
         inner_kernel,
         out_shape=(grid, poly, coef),
-        in_specs=[vmem] * 5,
+        in_specs=[vmem] * 3,
         out_specs=(vmem, vmem, vmem),
         compiler_params=small,
         cost_estimate=pl.CostEstimate(
             flops=40 * 3 * ITERS * height * SUB * LANES, bytes_accessed=held, transcendentals=0
         ),
         name="inner",
-    )(state, depth, near, first, second)
+    )(fields, first, second)
     sums, part = pl.pallas_call(
         pole_sums_kernel,
         out_shape=(f32(9 * ITERS + 2, SUB, LANES), sol),
@@ -440,13 +466,13 @@
     return pl.pallas_call(
         outer_kernel,
         out_shape=(f32(*state.shape), grid, poly, coef, sol),
-        in_specs=[vmem] * 6,
+        in_specs=[vmem] * 7,
         out_specs=(vmem,) * 5,
-        input_output_aliases={2: 1, 3: 2, 4: 3, 5: 4},
+        input_output_aliases={3: 1, 4: 2, 5: 3, 6: 4},
         scratch_shapes=[pltpu.VMEM((3, rows * SUB, LANES), jnp.float32)],
         compiler_params=small,
         name="outer",
-    )(far, sums, *inner, part)[0]
+    )(far, near, sums, *inner, part)[0]
 
 
 def solution(mesh):

time: 22.3 us -> 17.4 us (0.78); the launches traced: 21.9 us -> 17.3 us
  starting transfers between devices: 9.72 us -> 6.76 us
  local copies, waits for them, and re-layouts: 2.35 us -> 0 us
  waiting for transfers between devices: 4.12 us -> 5.98 us
  Pallas kernels: 5.72 us -> 4.52 us
    unnamed x6 -> x0, local copies, waits for them, and re-layouts: 2.35 us -> none
    ppermute x4, starting transfers between devices: 8.2 us -> 6.34 us  [swap(): return lax.ppermute(block, axis, pairs(lax.axis_size(axis), phase))]
    ppermute x1, waiting for transfers between devices: 0.85 us -> 2.43 us  [shift(): lax.ppermute(block, axis, [(i, (i + step) % count) for i in range(count)])]
    ppermute x1, starting transfers between devices: 1.52 us -> 0.42 us  [shift(): lax.ppermute(block, axis, [(i, (i + step) % count) for i in range(count)])]
    pallas_call x1, Pallas kernels: 1.49 us -> 0.8 us  [shards(): pl.pallas_call(inner_kernel, out_shape=(grid, poly, coef), in_specs=[vmem...]
    pallas_call x1, Pallas kernels: 1.53 us -> 1.05 us  [shards(): pl.pallas_call(pack_columns_kernel, out_shape=(pltpu.VMEM((4, rows, colum...]
    ppermute x4, waiting for transfers between devices: 3.27 us -> 3.55 us  [swap(): return lax.ppermute(block, axis, pairs(lax.axis_size(axis), phase))]
  transfers between devices with their start and end apart: 5 -> 5, of which waited for: 3 -> 4; matrix products, arithmetic and copies ran while one was open for 0% -> 0% of each run, Pallas kernels for 9% -> 7%
where the time goes in v6:
time: 17.4 us; the launch traced here: 17.3 us
  starting transfers between devices  6.76 us (39%)
  waiting for transfers between devices  5.98 us (34%)
  Pallas kernels  4.52 us (26%)
    ppermute x4, starting transfers between devices, swap(): return lax.ppermute(block, axis, pairs(lax.axis_size(axis), phase))  6.34 us
    ppermute x4, waiting for transfers between devices, swap(): return lax.ppermute(block, axis, pairs(lax.axis_size(axis), phase))  3.55 us
    ppermute x1, waiting for transfers between devices, shift(): lax.ppermute(block, axis, [(i, (i + step) % count) for i in range(count)])  2.43 us
    pallas_call x1, Pallas kernels, shards(): pl.pallas_call(outer_kernel, out_shape=(f32(*state.shape), grid, poly, co...  2.24 us
    pallas_call x1, Pallas kernels, shards(): pl.pallas_call(pack_columns_kernel, out_shape=(pltpu.VMEM((4, rows, colum...  1.05 us
    pallas_call x1, Pallas kernels, shards(): pl.pallas_call(inner_kernel, out_shape=(grid, poly, coef), in_specs=[vmem...  0.8 us
    ppermute x1, starting transfers between devices, shift(): lax.ppermute(block, axis, [(i, (i + step) % count) for i in range(count)])  0.42 us
    pallas_call x1, Pallas kernels, shards(): pl.pallas_call(pole_sums_kernel, out_shape=(f32(9 * ITERS + 2, SUB, LANES...  0.41 us
  transfers between devices with their start and end apart: 5, of which 4 were waited for; matrix products, arithmetic and copies ran while one was open for 0% of the time, Pallas kernels for 7%

profile of v6, /device:TPU:0, one launch (start us, length us, event | category | flops | bytes accessed | tf_op | source)
XLA Modules:
  0.0 17.3 jit_solution(6011460795803372690)
XLA Ops:
  0.0 1.0 %pack_columns.1 = (f32[4,16,512]{2,1,0:T(8,128)S(1)}, f32[16,128]{1,0:T(8,128)S(1)}, f32[16,128]{1,0:T(8,128)S(1)}, f32[16,128]{1,0:T(8,128)S(1)}) custom-call(f32[3,16,512]{2,1,0:T(8,128)} %state.1, f32[16,512]{1,0:T(8,128)} %depth.1, f32[4]{0:T(128)} %real.1, f32[4]{0:T(128)} %imag.1, f32[2,4]{1,0:T(2,128)} %weight.1), custom_call_target="tpu_custom_call" | custom-call | tf_op jit(solution)/shard_map/pack_columns/pallas_call | solution.py:407
  1.1 4.0 %collective-permute-start = (f32[16,128]{1,0:T(8,128)S(1)}, f32[16,128]{1,0:T(8,128)S(1)}, u32[]{:S(2)}, u32[]{:S(2)}) collective-permute-start(f32[16,128]{1,0:T(8,128)S(1)} %get-tuple-element.18), channel_id=1, source_target_pairs={{8,16},{16,8},{24,0},{0,24},{9,17},{17,9},{25,1},{1,25},{10,18},{1... | collective-permute-start | bytes 24584 | tf_op jit(solution)/shard_map/ppermute | solution.py:32
  5.0 0.5 %collective-permute-start.1 = (f32[16,128]{1,0:T(8,128)S(1)}, f32[16,128]{1,0:T(8,128)S(1)}, u32[]{:S(2)}, u32[]{:S(2)}) collective-permute-start(f32[16,128]{1,0:T(8,128)S(1)} %get-tuple-element.19), channel_id=1, source_target_pairs={{0,8},{8,0},{16,24},{24,16},{1,9},{9,1},{17,25},{25,17},{2,10},{10... | collective-permute-start | bytes 24584 | tf_op jit(solution)/shard_map/ppermute | solution.py:32
  5.6 1.1 %collective-permute-done.second = f32[16,128]{1,0:T(8,128)S(1)} collective-permute-done((f32[16,128]{1,0:T(8,128)S(1)}, f32[16,128]{1,0:T(8,128)S(1)}, u32[]{:S(2)}, u32[]{:S(2)}) %collective-permute-start) | collective-permute-done | bytes 8224 | tf_op jit(solution)/shard_map/ppermute | solution.py:32
  6.6 2.0 %collective-permute-done.1.first = f32[16,128]{1,0:T(8,128)S(1)} collective-permute-done((f32[16,128]{1,0:T(8,128)S(1)}, f32[16,128]{1,0:T(8,128)S(1)}, u32[]{:S(2)}, u32[]{:S(2)}) %collective-permute-start.1) | collective-permute-done | bytes 8224 | tf_op jit(solution)/shard_map/ppermute | solution.py:32
  8.7 1.8 %collective-permute-start.2 = (f32[40,512]{1,0:T(8,128)S(1)}, f32[40,512]{1,0:T(8,128)S(1)}, u32[]{:S(2)}, u32[]{:S(2)}) collective-permute-start(f32[40,512]{1,0:T(8,128)S(1)} %get-tuple-element.20), channel_id=1, source_target_pairs={{1,2},{2,1},{3,4},{4,3},{5,6},{6,5},{7,0},{0,7},{9,10},{10,9},{11,... | collective-permute-start | bytes 245768 | tf_op jit(solution)/shard_map/ppermute | solution.py:32
  10.5 0.0 collective-permute-start.3
  10.5 0.4 %collective-permute-start.4 = (f32[16,128]{1,0:T(8,128)S(1)}, f32[16,128]{1,0:T(8,128)S(1)}, u32[]{:S(2)}, u32[]{:S(2)}) collective-permute-start(f32[16,128]{1,0:T(8,128)S(1)} %get-tuple-element.22.scalars), channel_id=1, source_target_pairs={{0,16},{8,24},{16,0},{24,8},{1,17},{9,25},{17,1},{25,9},{2,18},{10... | collective-permute-start | bytes 24584 | tf_op jit(solution)/shard_map/ppermute | solution.py:37
  11.0 0.8 %inner.1 = (f32[1088,128]{1,0:T(8,128)S(1)}, f32[3,8,34,8,128]{4,3,2,1,0:T(8,128)S(1)}, f32[4,34,8,128]{3,2,1,0:T(8,128)S(1)}) custom-call(f32[4,16,512]{2,1,0:T(8,128)S(1)} %get-tuple-element.17.fields, f32[16,128]{1,0:T(8,128)S(1)} %collective-permute-done.1.first, f32[16,128]{1,0:T(8,128)S(1)} %collective-permute-done.second), custom_call_target="tpu_custom_call" | custom-call | flops 33423360 | bytes 4456448 | tf_op jit(solution)/shard_map/inner/pallas_call | solution.py:447
  11.8 2.4 %collective-permute-done.4 = f32[16,128]{1,0:T(8,128)S(1)} collective-permute-done((f32[16,128]{1,0:T(8,128)S(1)}, f32[16,128]{1,0:T(8,128)S(1)}, u32[]{:S(2)}, u32[]{:S(2)}) %collective-permute-start.4) | collective-permute-done | bytes 8224 | tf_op jit(solution)/shard_map/ppermute | solution.py:37
  14.2 0.4 %pole_sums.1 = (f32[74,8,128]{2,1,0:T(8,128)S(1)}, f32[3,18,8,128]{3,2,1,0:T(8,128)S(1)}) custom-call(f32[16,128]{1,0:T(8,128)S(1)} %get-tuple-element.22.scalars, f32[16,128]{1,0:T(8,128)S(1)} %collective-permute-done.1.first, f32[16,128]{1,0:T(8,128)S(1)} %collective-permute-done.second, f32[1,16,128]{2,1,0:T(8,128)S(1)} %bitcast.1, ...), custom_call_target="tpu_custom_call" | custom-call | tf_op jit(solution)/shard_map/pole_sums/pallas_call | solution.py:458
  14.6 0.4 %collective-permute-done.2.far = f32[40,512]{1,0:T(8,128)S(1)} collective-permute-done((f32[40,512]{1,0:T(8,128)S(1)}, f32[40,512]{1,0:T(8,128)S(1)}, u32[]{:S(2)}, u32[]{:S(2)}) %collective-permute-start.2) | collective-permute-done | bytes 81952 | tf_op jit(solution)/shard_map/ppermute | solution.py:32
  15.0 0.0 collective-permute-done.3.near
  15.0 2.2 %outer.1 = (f32[3,16,512]{2,1,0:T(8,128)}, f32[1088,128]{1,0:T(8,128)S(1)}, f32[3,8,34,8,128]{4,3,2,1,0:T(8,128)S(1)}, f32[4,34,8,128]{3,2,1,0:T(8,128)S(1)}, f32[3,18,8,128]{3,2,1,0:T(8,128)S(1)}) custom-call(f32[40,512]{1,0:T(8,128)S(1)} %collective-permute-done.2.far, ...), custom_call_target="tpu_custom_call", output_to_operand_aliasing={{1}: (3, {}), {2}: (4, {}), {3}: (5, {}), {4}: (6, {})} | custom-call | tf_op jit(solution)/shard_map/outer/pallas_call | solution.py:466
  (1 shorter events, 0.0 us)
Async XLA Ops:
  1.1 5.6 %collective-permute-start = (f32[16,128]{1,0:T(8,128)S(1)}, f32[16,128]{1,0:T(8,128)S(1)}, u32[]{:S(2)}, u32[]{:S(2)}) collective-permute-start(f32[16,128]{1,0:T(8,128)S(1)} %get-tuple-element.18), channel_id=1, source_target_pairs={{8,16},{16,8},{24,0},{0,24},{9,17},{17,9},{25,1},{1,25},{10,18},{1... | collective-permute-start | bytes 24584 | tf_op jit(solution)/shard_map/ppermute | solution.py:32
  5.0 3.7 %collective-permute-start.1 = (f32[16,128]{1,0:T(8,128)S(1)}, f32[16,128]{1,0:T(8,128)S(1)}, u32[]{:S(2)}, u32[]{:S(2)}) collective-permute-start(f32[16,128]{1,0:T(8,128)S(1)} %get-tuple-element.19), channel_id=1, source_target_pairs={{0,8},{8,0},{16,24},{24,16},{1,9},{9,1},{17,25},{25,17},{2,10},{10... | collective-permute-start | bytes 24584 | tf_op jit(solution)/shard_map/ppermute | solution.py:32
  8.7 6.3 %collective-permute-start.2 = (f32[40,512]{1,0:T(8,128)S(1)}, f32[40,512]{1,0:T(8,128)S(1)}, u32[]{:S(2)}, u32[]{:S(2)}) collective-permute-start(f32[40,512]{1,0:T(8,128)S(1)} %get-tuple-element.20), channel_id=1, source_target_pairs={{1,2},{2,1},{3,4},{4,3},{5,6},{6,5},{7,0},{0,7},{9,10},{10,9},{11,... | collective-permute-start | bytes 245768 | tf_op jit(solution)/shard_map/ppermute | solution.py:32
  10.5 4.5 %collective-permute-start.3 = (f32[40,512]{1,0:T(8,128)S(1)}, f32[40,512]{1,0:T(8,128)S(1)}, u32[]{:S(2)}, u32[]{:S(2)}) collective-permute-start(f32[40,512]{1,0:T(8,128)S(1)} %get-tuple-element.21), channel_id=1, source_target_pairs={{0,1},{1,0},{2,3},{3,2},{4,5},{5,4},{6,7},{7,6},{8,9},{9,8},{10,11... | collective-permute-start | bytes 245768 | tf_op jit(solution)/shard_map/ppermute | solution.py:32
  10.5 3.7 %collective-permute-start.4 = (f32[16,128]{1,0:T(8,128)S(1)}, f32[16,128]{1,0:T(8,128)S(1)}, u32[]{:S(2)}, u32[]{:S(2)}) collective-permute-start(f32[16,128]{1,0:T(8,128)S(1)} %get-tuple-element.22.scalars), channel_id=1, source_target_pairs={{0,16},{8,24},{16,0},{24,8},{1,17},{9,25},{17,1},{25,9},{2,18},{10... | collective-permute-start | bytes 24584 | tf_op jit(solution)/shard_map/ppermute | solution.py:37

commit v7 on v6

--- a/solution.py
+++ b/solution.py
@@ -55,7 +55,21 @@
 
 
 def pack_columns_kernel(
-    state, depth, real, imag, weight, fields, first, second, scalars, real_in, imag_in, weight_in, done
+    state,
+    depth,
+    real,
+    imag,
+    weight,
+    fields,
+    first,
+    second,
+    scalars,
+    far,
+    near,
+    real_in,
+    imag_in,
+    weight_in,
+    done,
 ):
     moves = [
         pltpu.make_async_copy(state, fields.at[pl.ds(0, 3)], done.at[0]),
@@ -97,6 +111,25 @@
             westward = jnp.where(take, turn(west, EAST + low), westward)
         first[cut, :] = jnp.where(odd, westward, eastward)
         second[cut, :] = jnp.where(odd, eastward, westward)
+    odd = lax.rem(lax.axis_index("tile"), 2) == 1
+    for target, low in ((far, jnp.logical_not(odd)), (near, odd)):
+        pl.when(low)(lambda: pack_rows(target, fields, 0, SUB))
+        pl.when(jnp.logical_not(low))(
+            lambda: pack_rows(target, fields, rows - SUB, rows - SUB - 1)
+        )
+
+
+def pack_rows(target, fields, main, ext):
+    tiles = fields.shape[2] // LANES
+    for f in range(4):
+        for t in range(tiles):
+            block = fields[f, main : main + SUB, t * LANES : (t + 1) * LANES]
+            target[pl.ds((f * tiles + t) * SUB, SUB)] = block
+    for f in (1, 2):
+        flux = fields[3, ext : ext + 1, :] * fields[f, ext : ext + 1, :]
+        for t in range(tiles):
+            at = (4 * SUB + f - 1) * tiles + t
+            target[at : at + 1] = flux[:, t * LANES : (t + 1) * LANES]
 
 
 def sides_of(first, second, cut):
@@ -106,21 +139,17 @@
     return jnp.where(from_first, first[cut, :], second[cut, :])
 
 
-def pack_rows_kernel(fields, second, first, far, near):
+def pack_corners_kernel(second, first, far, near):
     odd = lax.rem(lax.axis_index("tile"), 2) == 1
-    rows = fields.shape[1]
+    rows = first.shape[0]
     for target, low in ((far, jnp.logical_not(odd)), (near, odd)):
+
         def fill(main, ext):
-            for f in range(4):
-                target[f * SUB : (f + 1) * SUB] = fields[f, main : main + SUB]
-                target[4 * SUB + f : 4 * SUB + f + 1] = fields[f, ext : ext + 1]
-            side = sides_of(first, second, pl.ds(main, SUB))
-            base = 4 * SUB + 4
-            target[base : base + 4, 0:LANES] = side[0:4]
-            target[base : base + 4, LANES : 2 * LANES] = side[4:8]
+            target[0:SUB] = sides_of(first, second, pl.ds(main, SUB))
             group = ext // SUB * SUB
             side = sides_of(first, second, pl.ds(group, SUB))
-            target[base : base + 1, 2 * LANES : 3 * LANES] = side[ext - group : ext - group + 1]
+            line = side[ext - group : ext - group + 1]
+            target[SUB : 2 * SUB] = jnp.broadcast_to(line, (SUB, LANES))
 
         pl.when(low)(lambda: fill(0, SUB))
         pl.when(jnp.logical_not(low))(lambda: fill(rows - SUB, rows - SUB - 1))
@@ -254,30 +283,38 @@
     return out
 
 
-def lay(grid, block, side, at, size, stride):
-    cut = [block[:, t * LANES : (t + 1) * LANES] for t in range(block.shape[1] // LANES)]
+def lay(grid, cut, side, at, stride):
     for s, strip in enumerate(strips_of(cut, side)):
-        grid[pl.Slice(at * SUB + s, size, stride * SUB), :] = strip[0:size]
+        grid[pl.Slice(at * SUB + s, SUB, stride * SUB), :] = strip
 
 
 def place(side, f):
     return turn(side, SIDE - EDGE - EDGE * f)
 
 
-def lay_halo(grid, halo, main, ext):
+def lay_halo(grid, halo, corner, main, ext):
+    lane = lax.broadcasted_iota(jnp.int32, (SUB, LANES), 1)
     sub = lax.broadcasted_iota(jnp.int32, (SUB, LANES), 0)
-    base = 4 * SUB + 4
-    side = jnp.concatenate(
-        [halo[base : base + 4, 0:LANES], halo[base : base + 4, LANES : 2 * LANES]], axis=0
-    )
+    tiles = SUB // 2
+    side = corner[0:SUB]
     for f in range(4):
-        lay(grid, halo[pl.ds(f * SUB, SUB), :], place(side, f), main * 4 + f, SUB, 4)
-    line = halo[base : base + 1, 2 * LANES : 3 * LANES]
-    line = jnp.broadcast_to(line, (SUB, LANES))
-    side = place(line, 0)
-    for f in range(1, 4):
-        side = jnp.where(sub == f, place(line, f), side)
-    lay(grid, halo[pl.ds(4 * SUB, SUB), :], side, ext * 4, 4, 1)
+        cut = [halo[pl.ds((f * tiles + t) * SUB, SUB)] for t in range(tiles)]
+        lay(grid, cut, place(side, f), main * 4 + f, 4)
+    line = corner[SUB : 2 * SUB]
+    east_flux = place(line * turn(line, -2 * EDGE), 1)
+    north_flux = place(line * turn(line, -EDGE), 2)
+    side = jnp.where(sub < tiles, east_flux, north_flux)
+    block = halo[pl.ds(4 * tiles * SUB, SUB)]
+    up, down = turn(block, SIDE), turn(block, -SIDE)
+    before = jnp.where(sub % tiles == 0, side, pltpu.roll(up, 1, 0))
+    after = jnp.where(sub % tiles == tiles - 1, side, pltpu.roll(down, SUB - 1, 0))
+    even = jnp.where(lane < SIDE, before, up)
+    odd = jnp.where(lane < LANES - SIDE, down, after)
+    for f in (1, 2):
+        at = (ext * 4 + f) * SUB
+        cut = slice((f - 1) * tiles, f * tiles)
+        grid[pl.Slice(at, tiles, 2), :] = even[cut]
+        grid[pl.Slice(at + 1, tiles, 2), :] = odd[cut]
 
 
 def cell(grid, f, r):
@@ -296,7 +333,6 @@
     flux_east = [None] * 3
     flux_north = [None] * 3
     depths = [None] * 2
-    across = None
     for k in range(count + 2):
         r = start + k
         h = cell(grid, 3, r)
@@ -304,15 +340,10 @@
         flux_north = flux_north[1:] + [h * cell(grid, 2, r)]
         depths = depths[1:] + [h]
         if k >= 1:
-            before, across = across, 0.125 * (depths[0] + depths[1])
-            coef[0, r - 1] = across
+            coef[0, r - 1] = 0.125 * (depths[0] + depths[1])
         if k >= 2:
             c = r - 1
-            north = 0.125 * (depths[0] + right(depths[0]))
-            south = left(north)
-            coef[1, c] = north
-            coef[2, c] = south
-            coef[3, c] = 2.0 - ((across + before) + (north + south))
+            coef[1, c] = 0.125 * (depths[0] + right(depths[0]))
             east_slope = flux_east[2] - flux_east[0]
             north_slope = right(flux_north[1]) - left(flux_north[1])
             poly[1, 0, c] = 0.5 * (east_slope + north_slope)
@@ -323,19 +354,24 @@
 
 
 def sweep(poly, coef, m, start, count):
-    back = [poly[f, m, start - 1] for f in range(3)]
     here = [poly[f, m, start] for f in range(3)]
-    below = coef[0, start - 1]
+    across = coef[0, start - 1]
+    back = [across * (here[f] - poly[f, m, start - 1]) for f in range(3)]
     for k in range(count):
         r = start + k
-        above, north, south, diag = coef[0, r], coef[1, r], coef[2, r], coef[3, r]
-        ahead = [poly[f, m, r + 1] for f in range(3)]
+        across, along = coef[0, r], coef[1, r]
         for f in range(3):
-            value = diag * here[f] + (above * ahead[f] + below * back[f])
-            value = value + (north * right(here[f]) + south * left(here[f]))
-            value = 0.5 * value if m == 0 else value - poly[f, m - 1, r]
+            w = here[f]
+            ahead = poly[f, m, r + 1]
+            east = across * (ahead - w)
+            north = along * (right(w) - w)
+            change = (east - back[f]) + (north - left(north))
+            if m == 0:
+                value = w + 0.5 * change
+            else:
+                value = (w - poly[f, m - 1, r]) + (w + change)
             poly[f, m + 1, r] = value
-        back, here, below = here, ahead, above
+            here[f], back[f] = ahead, east
 
 
 def inner_kernel(fields, first, second, grid, poly, coef):
@@ -343,23 +379,45 @@
     for g in range(rows // SUB):
         side = sides_of(first, second, pl.ds(g * SUB, SUB))
         for f in range(4):
-            block = fields[f, pl.ds(g * SUB, SUB), :]
-            lay(grid, block, place(side, f), (REACH + g * SUB) * 4 + f, SUB, 4)
+            cut = [
+                fields[f, pl.ds(g * SUB, SUB), pl.ds(t * LANES, LANES)]
+                for t in range(fields.shape[2] // LANES)
+            ]
+            lay(grid, cut, place(side, f), (REACH + g * SUB) * 4 + f, 4)
     prepare(grid, poly, coef, REACH, rows - 2)
     for m in range(ITERS - 1):
         if rows - 4 - 2 * m > 0:
             sweep(poly, coef, m, REACH + 2 + m, rows - 4 - 2 * m)
 
 
-def outer_kernel(far, near, sums, grid_in, poly_in, coef_in, sol_in, out, grid, poly, coef, sol, result):
+def outer_kernel(
+    far,
+    near,
+    far_corner,
+    near_corner,
+    sums,
+    grid_in,
+    poly_in,
+    coef_in,
+    sol_in,
+    out,
+    grid,
+    poly,
+    coef,
+    sol,
+    result,
+):
     rows, columns = out.shape[1:]
     odd_tile = lax.rem(lax.axis_index("tile"), 2) == 1
     lane = lax.broadcasted_iota(jnp.int32, (SUB, LANES), 1)
     below = REACH + rows
-    for halo, above in ((near, odd_tile), (far, jnp.logical_not(odd_tile))):
+    for r in (0, below + SUB):
+        grid[pl.ds((r * 4 + 3) * SUB, SUB), :] = jnp.ones((SUB, LANES), jnp.float32)
+    halos = ((near, near_corner, odd_tile), (far, far_corner, jnp.logical_not(odd_tile)))
+    for halo, corner, above in halos:
         main = jnp.where(above, 1, below)
         ext = jnp.where(above, 0, below + SUB)
-        lay_halo(grid, halo, main, ext)
+        lay_halo(grid, halo, corner, main, ext)
     prepare(grid, poly, coef, 0, REACH)
     prepare(grid, poly, coef, below - 2, REACH)
     for m in range(ITERS - 1):
@@ -404,16 +462,19 @@
     ]
     hbm = pl.BlockSpec(memory_space=pltpu.HBM)
     message = pltpu.VMEM((rows, LANES), jnp.float32)
-    fields, first, second, scalars = pl.pallas_call(
+    halo = pltpu.VMEM(((4 * SUB + 2) * columns // LANES, LANES), jnp.float32)
+    fields, first, second, scalars, far, near = pl.pallas_call(
         pack_columns_kernel,
         out_shape=(
             pltpu.VMEM((4, rows, columns), jnp.float32),
             message,
             message,
             pltpu.VMEM((4 * poles, LANES), jnp.float32),
+            halo,
+            halo,
         ),
         in_specs=[hbm] * 5,
-        out_specs=(vmem,) * 4,
+        out_specs=(vmem,) * 6,
         scratch_shapes=[
             pltpu.SMEM(pole_real.shape, jnp.float32),
             pltpu.SMEM(pole_imag.shape, jnp.float32),
@@ -425,25 +486,27 @@
     )(*given)
     second = swap(second, "pole", 1)
     first = swap(first, "pole", 0)
-    halo = f32(5 * SUB, columns)
-    far, near = pl.pallas_call(
-        pack_rows_kernel,
-        out_shape=(halo, halo),
-        in_specs=[vmem] * 3,
+    far = swap(far, "tile", 1)
+    near = swap(near, "tile", 0)
+    corner = f32(2 * SUB, LANES)
+    far_corner, near_corner = pl.pallas_call(
+        pack_corners_kernel,
+        out_shape=(corner, corner),
+        in_specs=[vmem] * 2,
         out_specs=(vmem, vmem),
         compiler_params=small,
-        name="pack_rows",
-    )(fields, second, first)
-    far = swap(far, "tile", 1)
-    near = swap(near, "tile", 0)
+        name="pack_corners",
+    )(second, first)
+    far_corner = swap(far_corner, "tile", 1)
+    near_corner = swap(near_corner, "tile", 0)
     count = lax.axis_size("pole")
     others = jnp.stack([shift(scalars, "pole", step) for step in range(2, count - 1)])
     height = rows + 2 * REACH
     grid = f32(height * 4 * SUB, LANES)
     poly = f32(3, ITERS, height, SUB, LANES)
-    coef = f32(4, height, SUB, LANES)
+    coef = f32(2, height, SUB, LANES)
     sol = f32(3, rows + 2, SUB, LANES)
-    held = 4 * SUB * LANES * height * (4 + 3 * ITERS + 4)
+    held = 4 * SUB * LANES * rows * (4 + 2 * ITERS + 2)
     inner = pl.pallas_call(
         inner_kernel,
         out_shape=(grid, poly, coef),
@@ -451,7 +514,7 @@
         out_specs=(vmem, vmem, vmem),
         compiler_params=small,
         cost_estimate=pl.CostEstimate(
-            flops=40 * 3 * ITERS * height * SUB * LANES, bytes_accessed=held, transcendentals=0
+            flops=10 * ITERS * rows * SUB * LANES, bytes_accessed=held, transcendentals=0
         ),
         name="inner",
     )(fields, first, second)
@@ -466,13 +529,13 @@
     return pl.pallas_call(
         outer_kernel,
         out_shape=(f32(*state.shape), grid, poly, coef, sol),
-        in_specs=[vmem] * 7,
+        in_specs=[vmem] * 9,
         out_specs=(vmem,) * 5,
-        input_output_aliases={3: 1, 4: 2, 5: 3, 6: 4},
+        input_output_aliases={5: 1, 6: 2, 7: 3, 8: 4},
         scratch_shapes=[pltpu.VMEM((3, rows * SUB, LANES), jnp.float32)],
         compiler_params=small,
         name="outer",
-    )(far, near, sums, *inner, part)[0]
+    )(far, near, far_corner, near_corner, sums, *inner, part)[0]
 
 
 def solution(mesh):

time: 17.4 us -> 19.8 us (1.14)
  starting transfers between devices: 6.76 us -> 8.44 us
  Pallas kernels: 4.52 us -> 5.6 us
  waiting for transfers between devices: 5.98 us -> 5.57 us
    ppermute x1, waiting for transfers between devices: 2.43 us -> 0.01 us  [shift(): lax.ppermute(block, axis, [(i, (i + step) % count) for i in range(count)])]
    ppermute x4 -> x6, waiting for transfers between devices: 3.55 us -> 5.56 us  [swap(): return lax.ppermute(block, axis, pairs(lax.axis_size(axis), phase))]
    ppermute x4 -> x6, starting transfers between devices: 6.34 us -> 7.94 us  [swap(): return lax.ppermute(block, axis, pairs(lax.axis_size(axis), phase))]
    pallas_call x1, Pallas kernels: 2.24 us -> 2.96 us  [shards(): pl.pallas_call(outer_kernel, out_shape=(f32(*state.shape), grid, poly, co...]
    pallas_call x1, Pallas kernels: 0.8 us -> 1.15 us  [shards(): pl.pallas_call(inner_kernel, out_shape=(grid, poly, coef), in_specs=[vmem...]
  transfers between devices with their start and end apart: 5 -> 7, of which waited for: 4 -> 3; matrix products, arithmetic and copies ran while one was open for 0% -> 0% of each run, Pallas kernels for 7% -> 8%
where the time goes in v7:
time: 19.8 us; the launch traced here: 19.7 us
  starting transfers between devices  8.44 us (43%)
  Pallas kernels  5.6 us (28%)
  waiting for transfers between devices  5.57 us (28%)
    ppermute x6, starting transfers between devices, swap(): return lax.ppermute(block, axis, pairs(lax.axis_size(axis), phase))  7.94 us
    ppermute x6, waiting for transfers between devices, swap(): return lax.ppermute(block, axis, pairs(lax.axis_size(axis), phase))  5.56 us
    pallas_call x1, Pallas kernels, shards(): pl.pallas_call(outer_kernel, out_shape=(f32(*state.shape), grid, poly, co...  2.96 us
    pallas_call x1, Pallas kernels, shards(): pl.pallas_call(inner_kernel, out_shape=(grid, poly, coef), in_specs=[vmem...  1.15 us
    pallas_call x1, Pallas kernels, shards(): pl.pallas_call(pack_columns_kernel, out_shape=(pltpu.VMEM((4, rows, colum...  1.06 us
    ppermute x1, starting transfers between devices, shift(): lax.ppermute(block, axis, [(i, (i + step) % count) for i in range(count)])  0.51 us
    pallas_call x1, Pallas kernels, shards(): pl.pallas_call(pole_sums_kernel, out_shape=(f32(9 * ITERS + 2, SUB, LANES...  0.42 us
  transfers between devices with their start and end apart: 7, of which 3 were waited for; matrix products, arithmetic and copies ran while one was open for 0% of the time, Pallas kernels for 8%

profile of v7, /device:TPU:0, one launch (start us, length us, event | category | flops | bytes accessed | tf_op | source)
XLA Modules:
  0.0 19.7 jit_solution(9019538099163166937)
XLA Ops:
  0.0 1.1 %pack_columns.1 = (f32[4,16,512]{2,1,0:T(8,128)S(1)}, f32[16,128]{1,0:T(8,128)S(1)}, f32[16,128]{1,0:T(8,128)S(1)}, f32[16,128]{1,0:T(8,128)S(1)}, f32[136,128]{1,0:T(8,128)S(1)}, /*index=5*/f32[136,128]{1,0:T(8,128)S(1)}) custom-call(f32[3,16,512]{2,1,0:T(8,128)} %state.1, f32[16,512]{1,0:T(8,128)} %depth.1, f32[4]{0:T(128)} %real.1, f32[4]{0:T(128)} %imag.1, ...), custom_call_target="tpu_custom_call" | custom-call | tf_op jit(solution)/shard_map/pack_columns/pallas_call | solution.py:466
  1.1 4.6 %collective-permute-start = (f32[136,128]{1,0:T(8,128)S(1)}, f32[136,128]{1,0:T(8,128)S(1)}, u32[]{:S(2)}, u32[]{:S(2)}) collective-permute-start(f32[136,128]{1,0:T(8,128)S(1)} %get-tuple-element.19), channel_id=1, source_target_pairs={{1,2},{2,1},{3,4},{4,3},{5,6},{6,5},{7,0},{0,7},{9,10},{10,9},{11,... | collective-permute-start | bytes 208904 | tf_op jit(solution)/shard_map/ppermute | solution.py:32
  5.6 0.0 collective-permute-start.1
  5.6 2.4 %collective-permute-start.2 = (f32[16,128]{1,0:T(8,128)S(1)}, f32[16,128]{1,0:T(8,128)S(1)}, u32[]{:S(2)}, u32[]{:S(2)}) collective-permute-start(f32[16,128]{1,0:T(8,128)S(1)} %get-tuple-element.21), channel_id=1, source_target_pairs={{8,16},{16,8},{24,0},{0,24},{9,17},{17,9},{25,1},{1,25},{10,18},{1... | collective-permute-start | bytes 24584 | tf_op jit(solution)/shard_map/ppermute | solution.py:32
  8.1 0.5 %collective-permute-start.3 = (f32[16,128]{1,0:T(8,128)S(1)}, f32[16,128]{1,0:T(8,128)S(1)}, u32[]{:S(2)}, u32[]{:S(2)}) collective-permute-start(f32[16,128]{1,0:T(8,128)S(1)} %get-tuple-element.22), channel_id=1, source_target_pairs={{0,8},{8,0},{16,24},{24,16},{1,9},{9,1},{17,25},{25,17},{2,10},{10... | collective-permute-start | bytes 24584 | tf_op jit(solution)/shard_map/ppermute | solution.py:32
  8.6 0.5 %collective-permute-start.6 = (f32[16,128]{1,0:T(8,128)S(1)}, f32[16,128]{1,0:T(8,128)S(1)}, u32[]{:S(2)}, u32[]{:S(2)}) collective-permute-start(f32[16,128]{1,0:T(8,128)S(1)} %get-tuple-element.25.scalars), channel_id=1, source_target_pairs={{0,16},{8,24},{16,0},{24,8},{1,17},{9,25},{17,1},{25,9},{2,18},{10... | collective-permute-start | bytes 24584 | tf_op jit(solution)/shard_map/ppermute | solution.py:37
  9.1 1.1 %collective-permute-done.2.second = f32[16,128]{1,0:T(8,128)S(1)} collective-permute-done((f32[16,128]{1,0:T(8,128)S(1)}, f32[16,128]{1,0:T(8,128)S(1)}, u32[]{:S(2)}, u32[]{:S(2)}) %collective-permute-start.2) | collective-permute-done | bytes 8224 | tf_op jit(solution)/shard_map/ppermute | solution.py:32
  10.2 1.5 %collective-permute-done.3.first = f32[16,128]{1,0:T(8,128)S(1)} collective-permute-done((f32[16,128]{1,0:T(8,128)S(1)}, f32[16,128]{1,0:T(8,128)S(1)}, u32[]{:S(2)}, u32[]{:S(2)}) %collective-permute-start.3) | collective-permute-done | bytes 8224 | tf_op jit(solution)/shard_map/ppermute | solution.py:32
  11.8 0.1 collective-permute-start.4
  11.8 0.3 %collective-permute-start.5 = (f32[16,128]{1,0:T(8,128)S(1)}, f32[16,128]{1,0:T(8,128)S(1)}, u32[]{:S(2)}, u32[]{:S(2)}) collective-permute-start(f32[16,128]{1,0:T(8,128)S(1)} %get-tuple-element.24), channel_id=1, source_target_pairs={{0,1},{1,0},{2,3},{3,2},{4,5},{5,4},{6,7},{7,6},{8,9},{9,8},{10,11... | collective-permute-start | bytes 24584 | tf_op jit(solution)/shard_map/ppermute | solution.py:32
  12.2 1.1 %inner.1 = (f32[1088,128]{1,0:T(8,128)S(1)}, f32[3,8,34,8,128]{4,3,2,1,0:T(8,128)S(1)}, f32[2,34,8,128]{3,2,1,0:T(8,128)S(1)}) custom-call(f32[4,16,512]{2,1,0:T(8,128)S(1)} %get-tuple-element.26.fields, f32[16,128]{1,0:T(8,128)S(1)} %collective-permute-done.3.first, f32[16,128]{1,0:T(8,128)S(1)} %collective-permute-done.2.second), custom_call_target="tpu_custom_call" | custom-call | flops 1310720 | bytes 1441792 | tf_op jit(solution)/shard_map/inner/pallas_call | solution.py:510
  13.3 0.0 collective-permute-done.6
  13.3 0.4 %pole_sums.1 = (f32[74,8,128]{2,1,0:T(8,128)S(1)}, f32[3,18,8,128]{3,2,1,0:T(8,128)S(1)}) custom-call(f32[16,128]{1,0:T(8,128)S(1)} %get-tuple-element.25.scalars, f32[16,128]{1,0:T(8,128)S(1)} %collective-permute-done.3.first, f32[16,128]{1,0:T(8,128)S(1)} %collective-permute-done.2.second, f32[1,16,128]{2,1,0:T(8,128)S(1)} %bitcast.1, ...), custom_call_target="tpu_custom_call" | custom-call | tf_op jit(solution)/shard_map/pole_sums/pallas_call | solution.py:521
  13.7 2.9 %collective-permute-done.4.far_corner = f32[16,128]{1,0:T(8,128)S(1)} collective-permute-done((f32[16,128]{1,0:T(8,128)S(1)}, f32[16,128]{1,0:T(8,128)S(1)}, u32[]{:S(2)}, u32[]{:S(2)}) %collective-permute-start.4) | collective-permute-done | bytes 8224 | tf_op jit(solution)/shard_map/ppermute | solution.py:32
  16.7 0.0 collective-permute-done.5.near_corner
  16.7 0.0 collective-permute-done.far
  16.7 0.0 collective-permute-done.1.near
  16.7 3.0 %outer.1 = (f32[3,16,512]{2,1,0:T(8,128)}, f32[1088,128]{1,0:T(8,128)S(1)}, f32[3,8,34,8,128]{4,3,2,1,0:T(8,128)S(1)}, f32[2,34,8,128]{3,2,1,0:T(8,128)S(1)}, f32[3,18,8,128]{3,2,1,0:T(8,128)S(1)}) custom-call(f32[136,128]{1,0:T(8,128)S(1)} %collective-permute-done.far, ...), custom_call_target="tpu_custom_call", output_to_operand_aliasing={{1}: (5, {}), {2}: (6, {}), {3}: (7, {}), {4}: (8, {})} | custom-call | tf_op jit(solution)/shard_map/outer/pallas_call | solution.py:529
  (1 shorter events, 0.0 us)
Async XLA Ops:
  1.1 15.6 %collective-permute-start = (f32[136,128]{1,0:T(8,128)S(1)}, f32[136,128]{1,0:T(8,128)S(1)}, u32[]{:S(2)}, u32[]{:S(2)}) collective-permute-start(f32[136,128]{1,0:T(8,128)S(1)} %get-tuple-element.19), channel_id=1, source_target_pairs={{1,2},{2,1},{3,4},{4,3},{5,6},{6,5},{7,0},{0,7},{9,10},{10,9},{11,... | collective-permute-start | bytes 208904 | tf_op jit(solution)/shard_map/ppermute | solution.py:32
  5.6 11.1 %collective-permute-start.1 = (f32[136,128]{1,0:T(8,128)S(1)}, f32[136,128]{1,0:T(8,128)S(1)}, u32[]{:S(2)}, u32[]{:S(2)}) collective-permute-start(f32[136,128]{1,0:T(8,128)S(1)} %get-tuple-element.20), channel_id=1, source_target_pairs={{0,1},{1,0},{2,3},{3,2},{4,5},{5,4},{6,7},{7,6},{8,9},{9,8},{10,11... | collective-permute-start | bytes 208904 | tf_op jit(solution)/shard_map/ppermute | solution.py:32
  5.6 4.5 %collective-permute-start.2 = (f32[16,128]{1,0:T(8,128)S(1)}, f32[16,128]{1,0:T(8,128)S(1)}, u32[]{:S(2)}, u32[]{:S(2)}) collective-permute-start(f32[16,128]{1,0:T(8,128)S(1)} %get-tuple-element.21), channel_id=1, source_target_pairs={{8,16},{16,8},{24,0},{0,24},{9,17},{17,9},{25,1},{1,25},{10,18},{1... | collective-permute-start | bytes 24584 | tf_op jit(solution)/shard_map/ppermute | solution.py:32
  8.1 3.7 %collective-permute-start.3 = (f32[16,128]{1,0:T(8,128)S(1)}, f32[16,128]{1,0:T(8,128)S(1)}, u32[]{:S(2)}, u32[]{:S(2)}) collective-permute-start(f32[16,128]{1,0:T(8,128)S(1)} %get-tuple-element.22), channel_id=1, source_target_pairs={{0,8},{8,0},{16,24},{24,16},{1,9},{9,1},{17,25},{25,17},{2,10},{10... | collective-permute-start | bytes 24584 | tf_op jit(solution)/shard_map/ppermute | solution.py:32
  8.6 4.7 %collective-permute-start.6 = (f32[16,128]{1,0:T(8,128)S(1)}, f32[16,128]{1,0:T(8,128)S(1)}, u32[]{:S(2)}, u32[]{:S(2)}) collective-permute-start(f32[16,128]{1,0:T(8,128)S(1)} %get-tuple-element.25.scalars), channel_id=1, source_target_pairs={{0,16},{8,24},{16,0},{24,8},{1,17},{9,25},{17,1},{25,9},{2,18},{10... | collective-permute-start | bytes 24584 | tf_op jit(solution)/shard_map/ppermute | solution.py:37
  11.8 4.9 %collective-permute-start.4 = (f32[16,128]{1,0:T(8,128)S(1)}, f32[16,128]{1,0:T(8,128)S(1)}, u32[]{:S(2)}, u32[]{:S(2)}) collective-permute-start(f32[16,128]{1,0:T(8,128)S(1)} %get-tuple-element.23), channel_id=1, source_target_pairs={{1,2},{2,1},{3,4},{4,3},{5,6},{6,5},{7,0},{0,7},{9,10},{10,9},{11,... | collective-permute-start | bytes 24584 | tf_op jit(solution)/shard_map/ppermute | solution.py:32
  11.8 4.9 %collective-permute-start.5 = (f32[16,128]{1,0:T(8,128)S(1)}, f32[16,128]{1,0:T(8,128)S(1)}, u32[]{:S(2)}, u32[]{:S(2)}) collective-permute-start(f32[16,128]{1,0:T(8,128)S(1)} %get-tuple-element.24), channel_id=1, source_target_pairs={{0,1},{1,0},{2,3},{3,2},{4,5},{5,4},{6,7},{7,6},{8,9},{9,8},{10,11... | collective-permute-start | bytes 24584 | tf_op jit(solution)/shard_map/ppermute | solution.py:32

commit v8 on v6

--- a/solution.py
+++ b/solution.py
@@ -55,7 +55,19 @@
 
 
 def pack_columns_kernel(
-    state, depth, real, imag, weight, fields, first, second, scalars, real_in, imag_in, weight_in, done
+    state,
+    depth,
+    real,
+    imag,
+    weight,
+    fields,
+    first,
+    second,
+    scalars,
+    real_in,
+    imag_in,
+    weight_in,
+    done,
 ):
     moves = [
         pltpu.make_async_copy(state, fields.at[pl.ds(0, 3)], done.at[0]),
@@ -110,20 +122,36 @@
     odd = lax.rem(lax.axis_index("tile"), 2) == 1
     rows = fields.shape[1]
     for target, low in ((far, jnp.logical_not(odd)), (near, odd)):
-        def fill(main, ext):
-            for f in range(4):
-                target[f * SUB : (f + 1) * SUB] = fields[f, main : main + SUB]
-                target[4 * SUB + f : 4 * SUB + f + 1] = fields[f, ext : ext + 1]
-            side = sides_of(first, second, pl.ds(main, SUB))
-            base = 4 * SUB + 4
-            target[base : base + 4, 0:LANES] = side[0:4]
-            target[base : base + 4, LANES : 2 * LANES] = side[4:8]
-            group = ext // SUB * SUB
-            side = sides_of(first, second, pl.ds(group, SUB))
-            target[base : base + 1, 2 * LANES : 3 * LANES] = side[ext - group : ext - group + 1]
-
+        fill = lambda main, ext: pack_rows(target, fields, second, first, main, ext)
         pl.when(low)(lambda: fill(0, SUB))
         pl.when(jnp.logical_not(low))(lambda: fill(rows - SUB, rows - SUB - 1))
+
+
+def pack_rows(target, fields, second, first, main, ext):
+    sub = lax.broadcasted_iota(jnp.int32, (SUB, LANES), 0)
+    lane = lax.broadcasted_iota(jnp.int32, (SUB, LANES), 1)
+    tiles = fields.shape[2] // LANES
+    for f in range(4):
+        for t in range(tiles):
+            block = fields[f, main : main + SUB, t * LANES : (t + 1) * LANES]
+            target[pl.ds((f * tiles + t) * SUB, SUB)] = block
+    for f in (1, 2):
+        flux = fields[3, ext : ext + 1, :] * fields[f, ext : ext + 1, :]
+        for t in range(tiles):
+            at = (4 * SUB + f - 1) * tiles + t
+            target[at : at + 1] = flux[:, t * LANES : (t + 1) * LANES]
+    side = sides_of(first, second, pl.ds(main, SUB))
+    group = ext // SUB * SUB
+    line = sides_of(first, second, pl.ds(group, SUB))[ext - group : ext - group + 1]
+    line = jnp.broadcast_to(line, (SUB, LANES))
+    for f in (1, 2):
+        flux = line * turn(line, -(3 - f) * EDGE)
+        west = turn(flux, (4 - f) * EDGE)
+        east = turn(flux, 5 * EDGE - (EAST + f * EDGE))
+        spare = jnp.where(lane < 5 * EDGE, west, east)
+        take = jnp.logical_and(lane >= 4 * EDGE, lane < 6 * EDGE)
+        side = jnp.where(jnp.logical_and(take, sub == f - 1), spare, side)
+    target[pl.ds((4 * SUB + 2) * tiles, SUB)] = side
 
 
 def pole_sums_kernel(scalars, first, second, others, poly, sums, sol):
@@ -254,10 +282,9 @@
     return out
 
 
-def lay(grid, block, side, at, size, stride):
-    cut = [block[:, t * LANES : (t + 1) * LANES] for t in range(block.shape[1] // LANES)]
+def lay(grid, cut, side, at, stride):
     for s, strip in enumerate(strips_of(cut, side)):
-        grid[pl.Slice(at * SUB + s, size, stride * SUB), :] = strip[0:size]
+        grid[pl.Slice(at * SUB + s, SUB, stride * SUB), :] = strip
 
 
 def place(side, f):
@@ -265,19 +292,27 @@
 
 
 def lay_halo(grid, halo, main, ext):
+    lane = lax.broadcasted_iota(jnp.int32, (SUB, LANES), 1)
     sub = lax.broadcasted_iota(jnp.int32, (SUB, LANES), 0)
-    base = 4 * SUB + 4
-    side = jnp.concatenate(
-        [halo[base : base + 4, 0:LANES], halo[base : base + 4, LANES : 2 * LANES]], axis=0
-    )
+    tiles = SUB // 2
+    side = halo[pl.ds((4 * SUB + 2) * tiles, SUB)]
     for f in range(4):
-        lay(grid, halo[pl.ds(f * SUB, SUB), :], place(side, f), main * 4 + f, SUB, 4)
-    line = halo[base : base + 1, 2 * LANES : 3 * LANES]
-    line = jnp.broadcast_to(line, (SUB, LANES))
-    side = place(line, 0)
-    for f in range(1, 4):
-        side = jnp.where(sub == f, place(line, f), side)
-    lay(grid, halo[pl.ds(4 * SUB, SUB), :], side, ext * 4, 4, 1)
+        cut = [halo[pl.ds((f * tiles + t) * SUB, SUB)] for t in range(tiles)]
+        lay(grid, cut, place(side, f), main * 4 + f, 4)
+    line = jnp.where(sub < tiles, side[0:1], side[1:2])
+    line = jnp.where(lane < HALF, turn(line, SIDE - 5 * EDGE), turn(line, -SIDE - 5 * EDGE))
+    side = line
+    block = halo[pl.ds(4 * tiles * SUB, SUB)]
+    up, down = turn(block, SIDE), turn(block, -SIDE)
+    before = jnp.where(sub % tiles == 0, side, pltpu.roll(up, 1, 0))
+    after = jnp.where(sub % tiles == tiles - 1, side, pltpu.roll(down, SUB - 1, 0))
+    even = jnp.where(lane < SIDE, before, up)
+    odd = jnp.where(lane < LANES - SIDE, down, after)
+    for f in (1, 2):
+        at = (ext * 4 + f) * SUB
+        cut = slice((f - 1) * tiles, f * tiles)
+        grid[pl.Slice(at, tiles, 2), :] = even[cut]
+        grid[pl.Slice(at + 1, tiles, 2), :] = odd[cut]
 
 
 def cell(grid, f, r):
@@ -309,7 +344,7 @@
         if k >= 2:
             c = r - 1
             north = 0.125 * (depths[0] + right(depths[0]))
-            south = left(north)
+            south = 0.125 * (depths[0] + left(depths[0]))
             coef[1, c] = north
             coef[2, c] = south
             coef[3, c] = 2.0 - ((across + before) + (north + south))
@@ -331,10 +366,14 @@
         above, north, south, diag = coef[0, r], coef[1, r], coef[2, r], coef[3, r]
         ahead = [poly[f, m, r + 1] for f in range(3)]
         for f in range(3):
-            value = diag * here[f] + (above * ahead[f] + below * back[f])
-            value = value + (north * right(here[f]) + south * left(here[f]))
-            value = 0.5 * value if m == 0 else value - poly[f, m - 1, r]
-            poly[f, m + 1, r] = value
+            value = diag * here[f]
+            if m > 0:
+                value = value - poly[f, m - 1, r]
+            value = value + above * ahead[f]
+            value = value + below * back[f]
+            value = value + north * right(here[f])
+            value = value + south * left(here[f])
+            poly[f, m + 1, r] = 0.5 * value if m == 0 else value
         back, here, below = here, ahead, above
 
 
@@ -343,19 +382,38 @@
     for g in range(rows // SUB):
         side = sides_of(first, second, pl.ds(g * SUB, SUB))
         for f in range(4):
-            block = fields[f, pl.ds(g * SUB, SUB), :]
-            lay(grid, block, place(side, f), (REACH + g * SUB) * 4 + f, SUB, 4)
+            cut = [
+                fields[f, pl.ds(g * SUB, SUB), pl.ds(t * LANES, LANES)]
+                for t in range(fields.shape[2] // LANES)
+            ]
+            lay(grid, cut, place(side, f), (REACH + g * SUB) * 4 + f, 4)
     prepare(grid, poly, coef, REACH, rows - 2)
     for m in range(ITERS - 1):
         if rows - 4 - 2 * m > 0:
             sweep(poly, coef, m, REACH + 2 + m, rows - 4 - 2 * m)
 
 
-def outer_kernel(far, near, sums, grid_in, poly_in, coef_in, sol_in, out, grid, poly, coef, sol, result):
+def outer_kernel(
+    far,
+    near,
+    sums,
+    grid_in,
+    poly_in,
+    coef_in,
+    sol_in,
+    out,
+    grid,
+    poly,
+    coef,
+    sol,
+    result,
+):
     rows, columns = out.shape[1:]
     odd_tile = lax.rem(lax.axis_index("tile"), 2) == 1
     lane = lax.broadcasted_iota(jnp.int32, (SUB, LANES), 1)
     below = REACH + rows
+    for r in (0, below + SUB):
+        grid[pl.ds((r * 4 + 3) * SUB, SUB), :] = jnp.ones((SUB, LANES), jnp.float32)
     for halo, above in ((near, odd_tile), (far, jnp.logical_not(odd_tile))):
         main = jnp.where(above, 1, below)
         ext = jnp.where(above, 0, below + SUB)
@@ -425,7 +483,7 @@
     )(*given)
     second = swap(second, "pole", 1)
     first = swap(first, "pole", 0)
-    halo = f32(5 * SUB, columns)
+    halo = f32((4 * SUB + 2) * columns // LANES + SUB, LANES)
     far, near = pl.pallas_call(
         pack_rows_kernel,
         out_shape=(halo, halo),
@@ -443,7 +501,7 @@
     poly = f32(3, ITERS, height, SUB, LANES)
     coef = f32(4, height, SUB, LANES)
     sol = f32(3, rows + 2, SUB, LANES)
-    held = 4 * SUB * LANES * height * (4 + 3 * ITERS + 4)
+    held = 4 * SUB * LANES * rows * (4 + 2 * ITERS + 2)
     inner = pl.pallas_call(
         inner_kernel,
         out_shape=(grid, poly, coef),
@@ -451,7 +509,7 @@
         out_specs=(vmem, vmem, vmem),
         compiler_params=small,
         cost_estimate=pl.CostEstimate(
-            flops=40 * 3 * ITERS * height * SUB * LANES, bytes_accessed=held, transcendentals=0
+            flops=10 * ITERS * rows * SUB * LANES, bytes_accessed=held, transcendentals=0
         ),
         name="inner",
     )(fields, first, second)

time: 17.4 us -> 17.4 us (level)
    pallas_call x1, Pallas kernels: 0.03 us -> 0.3 us  [shards(): pl.pallas_call(pack_rows_kernel, out_shape=(halo, halo), in_specs=[vmem]...]
where the time goes in v8:
time: 17.4 us; the launch traced here: 17.2 us
  starting transfers between devices  6.7 us (39%)
  waiting for transfers between devices  5.82 us (33%)
  Pallas kernels  4.69 us (27%)
    ppermute x4, starting transfers between devices, swap(): return lax.ppermute(block, axis, pairs(lax.axis_size(axis), phase))  6.19 us
    ppermute x4, waiting for transfers between devices, swap(): return lax.ppermute(block, axis, pairs(lax.axis_size(axis), phase))  3.46 us
    ppermute x1, waiting for transfers between devices, shift(): lax.ppermute(block, axis, [(i, (i + step) % count) for i in range(count)])  2.36 us
    pallas_call x1, Pallas kernels, shards(): pl.pallas_call(outer_kernel, out_shape=(f32(*state.shape), grid, poly, co...  2.15 us
    pallas_call x1, Pallas kernels, shards(): pl.pallas_call(pack_columns_kernel, out_shape=(pltpu.VMEM((4, rows, colum...  1.05 us
    pallas_call x1, Pallas kernels, shards(): pl.pallas_call(inner_kernel, out_shape=(grid, poly, coef), in_specs=[vmem...  0.78 us
    ppermute x1, starting transfers between devices, shift(): lax.ppermute(block, axis, [(i, (i + step) % count) for i in range(count)])  0.51 us
    pallas_call x1, Pallas kernels, shards(): pl.pallas_call(pole_sums_kernel, out_shape=(f32(9 * ITERS + 2, SUB, LANES...  0.41 us
  transfers between devices with their start and end apart: 5, of which 4 were waited for; matrix products, arithmetic and copies ran while one was open for 0% of the time, Pallas kernels for 7%

profile of v8, /device:TPU:0, one launch (start us, length us, event | category | flops | bytes accessed | tf_op | source)
XLA Modules:
  0.0 17.2 jit_solution(15996800334874472504)
XLA Ops:
  0.0 1.0 %pack_columns.1 = (f32[4,16,512]{2,1,0:T(8,128)S(1)}, f32[16,128]{1,0:T(8,128)S(1)}, f32[16,128]{1,0:T(8,128)S(1)}, f32[16,128]{1,0:T(8,128)S(1)}) custom-call(f32[3,16,512]{2,1,0:T(8,128)} %state.1, f32[16,512]{1,0:T(8,128)} %depth.1, f32[4]{0:T(128)} %real.1, f32[4]{0:T(128)} %imag.1, f32[2,4]{1,0:T(2,128)} %weight.1), custom_call_target="tpu_custom_call" | custom-call | tf_op jit(solution)/shard_map/pack_columns/pallas_call | solution.py:465
  1.1 4.0 %collective-permute-start = (f32[16,128]{1,0:T(8,128)S(1)}, f32[16,128]{1,0:T(8,128)S(1)}, u32[]{:S(2)}, u32[]{:S(2)}) collective-permute-start(f32[16,128]{1,0:T(8,128)S(1)} %get-tuple-element.18), channel_id=1, source_target_pairs={{8,16},{16,8},{24,0},{0,24},{9,17},{17,9},{25,1},{1,25},{10,18},{1... | collective-permute-start | bytes 24584 | tf_op jit(solution)/shard_map/ppermute | solution.py:32
  5.0 0.5 %collective-permute-start.1 = (f32[16,128]{1,0:T(8,128)S(1)}, f32[16,128]{1,0:T(8,128)S(1)}, u32[]{:S(2)}, u32[]{:S(2)}) collective-permute-start(f32[16,128]{1,0:T(8,128)S(1)} %get-tuple-element.19), channel_id=1, source_target_pairs={{0,8},{8,0},{16,24},{24,16},{1,9},{9,1},{17,25},{25,17},{2,10},{10... | collective-permute-start | bytes 24584 | tf_op jit(solution)/shard_map/ppermute | solution.py:32
  5.6 1.1 %collective-permute-done.second = f32[16,128]{1,0:T(8,128)S(1)} collective-permute-done((f32[16,128]{1,0:T(8,128)S(1)}, f32[16,128]{1,0:T(8,128)S(1)}, u32[]{:S(2)}, u32[]{:S(2)}) %collective-permute-start) | collective-permute-done | bytes 8224 | tf_op jit(solution)/shard_map/ppermute | solution.py:32
  6.6 2.0 %collective-permute-done.1.first = f32[16,128]{1,0:T(8,128)S(1)} collective-permute-done((f32[16,128]{1,0:T(8,128)S(1)}, f32[16,128]{1,0:T(8,128)S(1)}, u32[]{:S(2)}, u32[]{:S(2)}) %collective-permute-start.1) | collective-permute-done | bytes 8224 | tf_op jit(solution)/shard_map/ppermute | solution.py:32
  8.7 0.3 %pack_rows.1 = (f32[144,128]{1,0:T(8,128)S(1)}, f32[144,128]{1,0:T(8,128)S(1)}) custom-call(f32[4,16,512]{2,1,0:T(8,128)S(1)} %get-tuple-element.17.fields, f32[16,128]{1,0:T(8,128)S(1)} %collective-permute-done.second, f32[16,128]{1,0:T(8,128)S(1)} %collective-permute-done.1.first), custom_call_target="tpu_custom_call" | custom-call | tf_op jit(solution)/shard_map/pack_rows/pallas_call | solution.py:487
  9.0 1.7 %collective-permute-start.2 = (f32[144,128]{1,0:T(8,128)S(1)}, f32[144,128]{1,0:T(8,128)S(1)}, u32[]{:S(2)}, u32[]{:S(2)}) collective-permute-start(f32[144,128]{1,0:T(8,128)S(1)} %get-tuple-element.20), channel_id=1, source_target_pairs={{1,2},{2,1},{3,4},{4,3},{5,6},{6,5},{7,0},{0,7},{9,10},{10,9},{11,... | collective-permute-start | bytes 221192 | tf_op jit(solution)/shard_map/ppermute | solution.py:32
  10.6 0.0 collective-permute-start.3
  10.7 0.5 %collective-permute-start.4 = (f32[16,128]{1,0:T(8,128)S(1)}, f32[16,128]{1,0:T(8,128)S(1)}, u32[]{:S(2)}, u32[]{:S(2)}) collective-permute-start(f32[16,128]{1,0:T(8,128)S(1)} %get-tuple-element.22.scalars), channel_id=1, source_target_pairs={{0,16},{8,24},{16,0},{24,8},{1,17},{9,25},{17,1},{25,9},{2,18},{10... | collective-permute-start | bytes 24584 | tf_op jit(solution)/shard_map/ppermute | solution.py:37
  11.2 0.8 %inner.1 = (f32[1088,128]{1,0:T(8,128)S(1)}, f32[3,8,34,8,128]{4,3,2,1,0:T(8,128)S(1)}, f32[4,34,8,128]{3,2,1,0:T(8,128)S(1)}) custom-call(f32[4,16,512]{2,1,0:T(8,128)S(1)} %get-tuple-element.17.fields, f32[16,128]{1,0:T(8,128)S(1)} %collective-permute-done.1.first, f32[16,128]{1,0:T(8,128)S(1)} %collective-permute-done.second), custom_call_target="tpu_custom_call" | custom-call | flops 1310720 | bytes 1441792 | tf_op jit(solution)/shard_map/inner/pallas_call | solution.py:505
  12.0 2.4 %collective-permute-done.4 = f32[16,128]{1,0:T(8,128)S(1)} collective-permute-done((f32[16,128]{1,0:T(8,128)S(1)}, f32[16,128]{1,0:T(8,128)S(1)}, u32[]{:S(2)}, u32[]{:S(2)}) %collective-permute-start.4) | collective-permute-done | bytes 8224 | tf_op jit(solution)/shard_map/ppermute | solution.py:37
  14.3 0.4 %pole_sums.1 = (f32[74,8,128]{2,1,0:T(8,128)S(1)}, f32[3,18,8,128]{3,2,1,0:T(8,128)S(1)}) custom-call(f32[16,128]{1,0:T(8,128)S(1)} %get-tuple-element.22.scalars, f32[16,128]{1,0:T(8,128)S(1)} %collective-permute-done.1.first, f32[16,128]{1,0:T(8,128)S(1)} %collective-permute-done.second, f32[1,16,128]{2,1,0:T(8,128)S(1)} %bitcast.1, ...), custom_call_target="tpu_custom_call" | custom-call | tf_op jit(solution)/shard_map/pole_sums/pallas_call | solution.py:516
  14.7 0.3 %collective-permute-done.2.far = f32[144,128]{1,0:T(8,128)S(1)} collective-permute-done((f32[144,128]{1,0:T(8,128)S(1)}, f32[144,128]{1,0:T(8,128)S(1)}, u32[]{:S(2)}, u32[]{:S(2)}) %collective-permute-start.2) | collective-permute-done | bytes 73760 | tf_op jit(solution)/shard_map/ppermute | solution.py:32
  15.1 0.0 collective-permute-done.3.near
  15.1 2.2 %outer.1 = (f32[3,16,512]{2,1,0:T(8,128)}, f32[1088,128]{1,0:T(8,128)S(1)}, f32[3,8,34,8,128]{4,3,2,1,0:T(8,128)S(1)}, f32[4,34,8,128]{3,2,1,0:T(8,128)S(1)}, f32[3,18,8,128]{3,2,1,0:T(8,128)S(1)}) custom-call(f32[144,128]{1,0:T(8,128)S(1)} %collective-permute-done.2.far, ...), custom_call_target="tpu_custom_call", output_to_operand_aliasing={{1}: (3, {}), {2}: (4, {}), {3}: (5, {}), {4}: (6, {})} | custom-call | tf_op jit(solution)/shard_map/outer/pallas_call | solution.py:524
Async XLA Ops:
  1.1 5.6 %collective-permute-start = (f32[16,128]{1,0:T(8,128)S(1)}, f32[16,128]{1,0:T(8,128)S(1)}, u32[]{:S(2)}, u32[]{:S(2)}) collective-permute-start(f32[16,128]{1,0:T(8,128)S(1)} %get-tuple-element.18), channel_id=1, source_target_pairs={{8,16},{16,8},{24,0},{0,24},{9,17},{17,9},{25,1},{1,25},{10,18},{1... | collective-permute-start | bytes 24584 | tf_op jit(solution)/shard_map/ppermute | solution.py:32
  5.0 3.7 %collective-permute-start.1 = (f32[16,128]{1,0:T(8,128)S(1)}, f32[16,128]{1,0:T(8,128)S(1)}, u32[]{:S(2)}, u32[]{:S(2)}) collective-permute-start(f32[16,128]{1,0:T(8,128)S(1)} %get-tuple-element.19), channel_id=1, source_target_pairs={{0,8},{8,0},{16,24},{24,16},{1,9},{9,1},{17,25},{25,17},{2,10},{10... | collective-permute-start | bytes 24584 | tf_op jit(solution)/shard_map/ppermute | solution.py:32
  9.0 6.1 %collective-permute-start.2 = (f32[144,128]{1,0:T(8,128)S(1)}, f32[144,128]{1,0:T(8,128)S(1)}, u32[]{:S(2)}, u32[]{:S(2)}) collective-permute-start(f32[144,128]{1,0:T(8,128)S(1)} %get-tuple-element.20), channel_id=1, source_target_pairs={{1,2},{2,1},{3,4},{4,3},{5,6},{6,5},{7,0},{0,7},{9,10},{10,9},{11,... | collective-permute-start | bytes 221192 | tf_op jit(solution)/shard_map/ppermute | solution.py:32
  10.6 4.5 %collective-permute-start.3 = (f32[144,128]{1,0:T(8,128)S(1)}, f32[144,128]{1,0:T(8,128)S(1)}, u32[]{:S(2)}, u32[]{:S(2)}) collective-permute-start(f32[144,128]{1,0:T(8,128)S(1)} %get-tuple-element.21), channel_id=1, source_target_pairs={{0,1},{1,0},{2,3},{3,2},{4,5},{5,4},{6,7},{7,6},{8,9},{9,8},{10,11... | collective-permute-start | bytes 221192 | tf_op jit(solution)/shard_map/ppermute | solution.py:32
  10.7 3.7 %collective-permute-start.4 = (f32[16,128]{1,0:T(8,128)S(1)}, f32[16,128]{1,0:T(8,128)S(1)}, u32[]{:S(2)}, u32[]{:S(2)}) collective-permute-start(f32[16,128]{1,0:T(8,128)S(1)} %get-tuple-element.22.scalars), channel_id=1, source_target_pairs={{0,16},{8,24},{16,0},{24,8},{1,17},{9,25},{17,1},{25,9},{2,18},{10... | collective-permute-start | bytes 24584 | tf_op jit(solution)/shard_map/ppermute | solution.py:37

commit v9 on v8

--- a/solution.py
+++ b/solution.py
@@ -64,6 +64,8 @@
     first,
     second,
     scalars,
+    far,
+    near,
     real_in,
     imag_in,
     weight_in,
@@ -109,27 +111,19 @@
             westward = jnp.where(take, turn(west, EAST + low), westward)
         first[cut, :] = jnp.where(odd, westward, eastward)
         second[cut, :] = jnp.where(odd, eastward, westward)
-
-
-def sides_of(first, second, cut):
-    odd = lax.rem(lax.axis_index("pole"), 2) == 1
-    lane = lax.broadcasted_iota(jnp.int32, (SUB, LANES), 1)
-    from_first = jnp.logical_xor(lane >= HALF, odd)
-    return jnp.where(from_first, first[cut, :], second[cut, :])
-
-
-def pack_rows_kernel(fields, second, first, far, near):
+    for target, low in towards(far, near):
+        pl.when(low)(lambda: pack_rows(target, fields, 0, SUB))
+        pl.when(jnp.logical_not(low))(
+            lambda: pack_rows(target, fields, rows - SUB, rows - SUB - 1)
+        )
+
+
+def towards(far, near):
     odd = lax.rem(lax.axis_index("tile"), 2) == 1
-    rows = fields.shape[1]
-    for target, low in ((far, jnp.logical_not(odd)), (near, odd)):
-        fill = lambda main, ext: pack_rows(target, fields, second, first, main, ext)
-        pl.when(low)(lambda: fill(0, SUB))
-        pl.when(jnp.logical_not(low))(lambda: fill(rows - SUB, rows - SUB - 1))
-
-
-def pack_rows(target, fields, second, first, main, ext):
-    sub = lax.broadcasted_iota(jnp.int32, (SUB, LANES), 0)
-    lane = lax.broadcasted_iota(jnp.int32, (SUB, LANES), 1)
+    return ((far, jnp.logical_not(odd)), (near, odd))
+
+
+def pack_rows(target, fields, main, ext):
     tiles = fields.shape[2] // LANES
     for f in range(4):
         for t in range(tiles):
@@ -140,9 +134,35 @@
         for t in range(tiles):
             at = (4 * SUB + f - 1) * tiles + t
             target[at : at + 1] = flux[:, t * LANES : (t + 1) * LANES]
-    side = sides_of(first, second, pl.ds(main, SUB))
-    group = ext // SUB * SUB
-    line = sides_of(first, second, pl.ds(group, SUB))[ext - group : ext - group + 1]
+
+
+def sides_of(first, second, cut):
+    odd = lax.rem(lax.axis_index("pole"), 2) == 1
+    lane = lax.broadcasted_iota(jnp.int32, (SUB, LANES), 1)
+    from_first = jnp.logical_xor(lane >= HALF, odd)
+    return jnp.where(from_first, first[cut, :], second[cut, :])
+
+
+def pack_sides_kernel(second, first, far_in, far, near_side):
+    (_, far_low), (_, near_low) = towards(None, None)
+    far[pl.ds(far.shape[0] - SUB, SUB)] = pack_sides(second, first, far_low)
+    near_side[...] = pack_sides(second, first, near_low)
+
+
+def pack_sides(second, first, low):
+    rows = first.shape[0]
+    sub = lax.broadcasted_iota(jnp.int32, (SUB, LANES), 0)
+    lane = lax.broadcasted_iota(jnp.int32, (SUB, LANES), 1)
+    side = jnp.where(
+        low,
+        sides_of(first, second, pl.ds(0, SUB)),
+        sides_of(first, second, pl.ds(rows - SUB, SUB)),
+    )
+    line = jnp.where(
+        low,
+        sides_of(first, second, pl.ds(SUB, SUB))[0:1],
+        sides_of(first, second, pl.ds(rows - 2 * SUB, SUB))[SUB - 1 : SUB],
+    )
     line = jnp.broadcast_to(line, (SUB, LANES))
     for f in (1, 2):
         flux = line * turn(line, -(3 - f) * EDGE)
@@ -151,7 +171,7 @@
         spare = jnp.where(lane < 5 * EDGE, west, east)
         take = jnp.logical_and(lane >= 4 * EDGE, lane < 6 * EDGE)
         side = jnp.where(jnp.logical_and(take, sub == f - 1), spare, side)
-    target[pl.ds((4 * SUB + 2) * tiles, SUB)] = side
+    return side
 
 
 def pole_sums_kernel(scalars, first, second, others, poly, sums, sol):
@@ -291,11 +311,10 @@
     return turn(side, SIDE - EDGE - EDGE * f)
 
 
-def lay_halo(grid, halo, main, ext):
+def lay_halo(grid, halo, side, main, ext):
     lane = lax.broadcasted_iota(jnp.int32, (SUB, LANES), 1)
     sub = lax.broadcasted_iota(jnp.int32, (SUB, LANES), 0)
     tiles = SUB // 2
-    side = halo[pl.ds((4 * SUB + 2) * tiles, SUB)]
     for f in range(4):
         cut = [halo[pl.ds((f * tiles + t) * SUB, SUB)] for t in range(tiles)]
         lay(grid, cut, place(side, f), main * 4 + f, 4)
@@ -393,39 +412,38 @@
             sweep(poly, coef, m, REACH + 2 + m, rows - 4 - 2 * m)
 
 
+def one_side(halo, side, above, sums, grid, poly, coef, sol):
+    rows = sol.shape[1] - 2
+    below = REACH + rows
+    main, ext, start = (1, 0, 0) if above else (below, below + SUB, below - 2)
+    grid[pl.ds((ext * 4 + 3) * SUB, SUB), :] = jnp.ones((SUB, LANES), jnp.float32)
+    lay_halo(grid, halo, side, main, ext)
+    prepare(grid, poly, coef, start, REACH)
+    for m in range(ITERS - 1):
+        sweep(poly, coef, m, 2 + m if above else below - 2 - m, REACH)
+    low = REACH - 1 if above else below - ITERS
+    terms = {r: range(max(known(rows, r), -1) + 1, ITERS) for r in range(low, low + REACH)}
+    weighted_sums(poly, sums, sol, terms, True)
+
+
+def both_ways(above, *rest):
+    pl.when(above)(lambda: one_side(*rest[:2], True, *rest[2:]))
+    pl.when(jnp.logical_not(above))(lambda: one_side(*rest[:2], False, *rest[2:]))
+
+
+def mid_kernel(near, side, sums, grid_in, poly_in, coef_in, sol_in, grid, poly, coef, sol):
+    _, (_, above) = towards(None, None)
+    both_ways(above, near, side[...], sums, grid, poly, coef, sol)
+
+
 def outer_kernel(
-    far,
-    near,
-    sums,
-    grid_in,
-    poly_in,
-    coef_in,
-    sol_in,
-    out,
-    grid,
-    poly,
-    coef,
-    sol,
-    result,
+    far, sums, grid_in, poly_in, coef_in, sol_in, out, grid, poly, coef, sol, result
 ):
     rows, columns = out.shape[1:]
-    odd_tile = lax.rem(lax.axis_index("tile"), 2) == 1
-    lane = lax.broadcasted_iota(jnp.int32, (SUB, LANES), 1)
-    below = REACH + rows
-    for r in (0, below + SUB):
-        grid[pl.ds((r * 4 + 3) * SUB, SUB), :] = jnp.ones((SUB, LANES), jnp.float32)
-    for halo, above in ((near, odd_tile), (far, jnp.logical_not(odd_tile))):
-        main = jnp.where(above, 1, below)
-        ext = jnp.where(above, 0, below + SUB)
-        lay_halo(grid, halo, main, ext)
-    prepare(grid, poly, coef, 0, REACH)
-    prepare(grid, poly, coef, below - 2, REACH)
-    for m in range(ITERS - 1):
-        sweep(poly, coef, m, 2 + m, REACH)
-        sweep(poly, coef, m, below - 2 - m, REACH)
-    span = range(REACH - 1, REACH + rows + 1)
-    terms = {r: range(max(known(rows, r), -1) + 1, ITERS) for r in span}
-    weighted_sums(poly, sums, sol, terms, True)
+    lane = lax.broadcasted_iota(jnp.int32, (SUB, LANES), 1)
+    (_, above), _ = towards(None, None)
+    side = far[pl.ds(far.shape[0] - SUB, SUB)]
+    both_ways(above, far, side, sums, grid, poly, coef, sol)
     push = sums[9 * ITERS]
     lift = sums[9 * ITERS + 1]
     for i in range(rows):
@@ -462,16 +480,19 @@
     ]
     hbm = pl.BlockSpec(memory_space=pltpu.HBM)
     message = pltpu.VMEM((rows, LANES), jnp.float32)
-    fields, first, second, scalars = pl.pallas_call(
+    count = (4 * SUB + 2) * columns // LANES
+    fields, first, second, scalars, far, near = pl.pallas_call(
         pack_columns_kernel,
         out_shape=(
             pltpu.VMEM((4, rows, columns), jnp.float32),
             message,
             message,
             pltpu.VMEM((4 * poles, LANES), jnp.float32),
+            pltpu.VMEM((count + SUB, LANES), jnp.float32),
+            pltpu.VMEM((count, LANES), jnp.float32),
         ),
         in_specs=[hbm] * 5,
-        out_specs=(vmem,) * 4,
+        out_specs=(vmem,) * 6,
         scratch_shapes=[
             pltpu.SMEM(pole_real.shape, jnp.float32),
             pltpu.SMEM(pole_imag.shape, jnp.float32),
@@ -483,17 +504,18 @@
     )(*given)
     second = swap(second, "pole", 1)
     first = swap(first, "pole", 0)
-    halo = f32((4 * SUB + 2) * columns // LANES + SUB, LANES)
-    far, near = pl.pallas_call(
-        pack_rows_kernel,
-        out_shape=(halo, halo),
+    far, near_side = pl.pallas_call(
+        pack_sides_kernel,
+        out_shape=(f32(*far.shape), f32(SUB, LANES)),
         in_specs=[vmem] * 3,
         out_specs=(vmem, vmem),
+        input_output_aliases={2: 0},
         compiler_params=small,
-        name="pack_rows",
-    )(fields, second, first)
+        name="pack_sides",
+    )(second, first, far)
     far = swap(far, "tile", 1)
     near = swap(near, "tile", 0)
+    near_side = swap(near_side, "tile", 0)
     count = lax.axis_size("pole")
     others = jnp.stack([shift(scalars, "pole", step) for step in range(2, count - 1)])
     height = rows + 2 * REACH
@@ -501,16 +523,18 @@
     poly = f32(3, ITERS, height, SUB, LANES)
     coef = f32(4, height, SUB, LANES)
     sol = f32(3, rows + 2, SUB, LANES)
-    held = 4 * SUB * LANES * rows * (4 + 2 * ITERS + 2)
+    cost = pl.CostEstimate(
+        flops=10 * ITERS * rows * SUB * LANES,
+        bytes_accessed=4 * SUB * LANES * rows * (4 + 2 * ITERS + 2),
+        transcendentals=0,
+    )
     inner = pl.pallas_call(
         inner_kernel,
         out_shape=(grid, poly, coef),
         in_specs=[vmem] * 3,
         out_specs=(vmem, vmem, vmem),
         compiler_params=small,
-        cost_estimate=pl.CostEstimate(
-            flops=10 * ITERS * rows * SUB * LANES, bytes_accessed=held, transcendentals=0
-        ),
+        cost_estimate=cost,
         name="inner",
     )(fields, first, second)
     sums, part = pl.pallas_call(
@@ -521,16 +545,27 @@
         compiler_params=small,
         name="pole_sums",
     )(scalars, first, second, others, inner[1])
+    held = (*inner, part)
+    held = pl.pallas_call(
+        mid_kernel,
+        out_shape=(grid, poly, coef, sol),
+        in_specs=[vmem] * 7,
+        out_specs=(vmem,) * 4,
+        input_output_aliases={3: 0, 4: 1, 5: 2, 6: 3},
+        compiler_params=small,
+        cost_estimate=cost,
+        name="mid",
+    )(near, near_side, sums, *held)
     return pl.pallas_call(
         outer_kernel,
         out_shape=(f32(*state.shape), grid, poly, coef, sol),
-        in_specs=[vmem] * 7,
+        in_specs=[vmem] * 6,
         out_specs=(vmem,) * 5,
-        input_output_aliases={3: 1, 4: 2, 5: 3, 6: 4},
+        input_output_aliases={2: 1, 3: 2, 4: 3, 5: 4},
         scratch_shapes=[pltpu.VMEM((3, rows * SUB, LANES), jnp.float32)],
         compiler_params=small,
         name="outer",
-    )(far, near, sums, *inner, part)[0]
+    )(far, sums, *held)[0]
 
 
 def solution(mesh):

time: 17.4 us -> 17.8 us (1.023)
  Pallas kernels: 4.69 us -> 5.32 us
  waiting for transfers between devices: 5.82 us -> 5.41 us
    pallas_call x1 -> x2, Pallas kernels: 0.3 us -> 1.09 us  [the longest x1 0.94 us: shards(): pl.pallas_call(mid_kernel, out_shape=(grid, poly, coef, sol), in_specs=[v...]
    ppermute x4 -> x5, waiting for transfers between devices: 3.46 us -> 3.12 us  [swap(): return lax.ppermute(block, axis, pairs(lax.axis_size(axis), phase))]
    ppermute x4 -> x5, starting transfers between devices: 6.19 us -> 6.45 us  [swap(): return lax.ppermute(block, axis, pairs(lax.axis_size(axis), phase))]
    pallas_call x1, Pallas kernels: 2.15 us -> 1.98 us  [shards(): pl.pallas_call(outer_kernel, out_shape=(f32(*state.shape), grid, poly, co...]
  transfers between devices with their start and end apart: 5 -> 6, of which waited for: 4 -> 3; matrix products, arithmetic and copies ran while one was open for 0% -> 0% of each run, Pallas kernels for 7% -> 12%
where the time goes in v9:
time: 17.8 us; the launch traced here: 17.6 us
  starting transfers between devices  6.86 us (39%)
  waiting for transfers between devices  5.41 us (30%)
  Pallas kernels  5.32 us (30%)
    ppermute x5, starting transfers between devices, swap(): return lax.ppermute(block, axis, pairs(lax.axis_size(axis), phase))  6.45 us
    ppermute x5, waiting for transfers between devices, swap(): return lax.ppermute(block, axis, pairs(lax.axis_size(axis), phase))  3.12 us
    ppermute x1, waiting for transfers between devices, shift(): lax.ppermute(block, axis, [(i, (i + step) % count) for i in range(count)])  2.29 us
    pallas_call x1, Pallas kernels, shards(): pl.pallas_call(outer_kernel, out_shape=(f32(*state.shape), grid, poly, co...  1.98 us
    pallas_call x1, Pallas kernels, shards(): pl.pallas_call(pack_columns_kernel, out_shape=(pltpu.VMEM((4, rows, colum...  1.06 us
    pallas_call x1, Pallas kernels, shards(): pl.pallas_call(mid_kernel, out_shape=(grid, poly, coef, sol), in_specs=[v...  0.94 us
    pallas_call x1, Pallas kernels, shards(): pl.pallas_call(inner_kernel, out_shape=(grid, poly, coef), in_specs=[vmem...  0.78 us
    pallas_call x1, Pallas kernels, shards(): pl.pallas_call(pole_sums_kernel, out_shape=(f32(9 * ITERS + 2, SUB, LANES...  0.42 us
  transfers between devices with their start and end apart: 6, of which 3 were waited for; matrix products, arithmetic and copies ran while one was open for 0% of the time, Pallas kernels for 12%

profile of v9, /device:TPU:0, one launch (start us, length us, event | category | flops | bytes accessed | tf_op | source)
XLA Modules:
  0.0 17.6 jit_solution(11247709472758895815)
XLA Ops:
  0.0 1.1 %pack_columns.1 = (f32[4,16,512]{2,1,0:T(8,128)S(1)}, f32[16,128]{1,0:T(8,128)S(1)}, f32[16,128]{1,0:T(8,128)S(1)}, f32[16,128]{1,0:T(8,128)S(1)}, f32[144,128]{1,0:T(8,128)S(1)}, /*index=5*/f32[136,128]{1,0:T(8,128)S(1)}) custom-call(f32[3,16,512]{2,1,0:T(8,128)} %state.1, f32[16,512]{1,0:T(8,128)} %depth.1, f32[4]{0:T(128)} %real.1, f32[4]{0:T(128)} %imag.1, ...), custom_call_target="tpu_custom_call" | custom-call | tf_op jit(solution)/shard_map/pack_columns/pallas_call | solution.py:484
  1.1 4.0 %collective-permute-start = (f32[16,128]{1,0:T(8,128)S(1)}, f32[16,128]{1,0:T(8,128)S(1)}, u32[]{:S(2)}, u32[]{:S(2)}) collective-permute-start(f32[16,128]{1,0:T(8,128)S(1)} %get-tuple-element.23), channel_id=1, source_target_pairs={{8,16},{16,8},{24,0},{0,24},{9,17},{17,9},{25,1},{1,25},{10,18},{1... | collective-permute-start | bytes 24584 | tf_op jit(solution)/shard_map/ppermute | solution.py:32
  5.0 0.5 %collective-permute-start.1 = (f32[16,128]{1,0:T(8,128)S(1)}, f32[16,128]{1,0:T(8,128)S(1)}, u32[]{:S(2)}, u32[]{:S(2)}) collective-permute-start(f32[16,128]{1,0:T(8,128)S(1)} %get-tuple-element.24), channel_id=1, source_target_pairs={{0,8},{8,0},{16,24},{24,16},{1,9},{9,1},{17,25},{25,17},{2,10},{10... | collective-permute-start | bytes 24584 | tf_op jit(solution)/shard_map/ppermute | solution.py:32
  5.6 1.1 %collective-permute-done.second = f32[16,128]{1,0:T(8,128)S(1)} collective-permute-done((f32[16,128]{1,0:T(8,128)S(1)}, f32[16,128]{1,0:T(8,128)S(1)}, u32[]{:S(2)}, u32[]{:S(2)}) %collective-permute-start) | collective-permute-done | bytes 8224 | tf_op jit(solution)/shard_map/ppermute | solution.py:32
  6.7 2.0 %collective-permute-done.1.first = f32[16,128]{1,0:T(8,128)S(1)} collective-permute-done((f32[16,128]{1,0:T(8,128)S(1)}, f32[16,128]{1,0:T(8,128)S(1)}, u32[]{:S(2)}, u32[]{:S(2)}) %collective-permute-start.1) | collective-permute-done | bytes 8224 | tf_op jit(solution)/shard_map/ppermute | solution.py:32
  8.7 0.1 pack_sides.1
  8.8 1.8 %collective-permute-start.2 = (f32[144,128]{1,0:T(8,128)S(1)}, f32[144,128]{1,0:T(8,128)S(1)}, u32[]{:S(2)}, u32[]{:S(2)}) collective-permute-start(f32[144,128]{1,0:T(8,128)S(1)} %get-tuple-element.26), channel_id=1, source_target_pairs={{1,2},{2,1},{3,4},{4,3},{5,6},{6,5},{7,0},{0,7},{9,10},{10,9},{11,... | collective-permute-start | bytes 221192 | tf_op jit(solution)/shard_map/ppermute | solution.py:32
  10.6 0.0 collective-permute-start.4
  10.6 0.4 %collective-permute-start.3 = (f32[16,128]{1,0:T(8,128)S(1)}, f32[16,128]{1,0:T(8,128)S(1)}, u32[]{:S(2)}, u32[]{:S(2)}) collective-permute-start(f32[16,128]{1,0:T(8,128)S(1)} %get-tuple-element.27.scalars), channel_id=1, source_target_pairs={{0,16},{8,24},{16,0},{24,8},{1,17},{9,25},{17,1},{25,9},{2,18},{10... | collective-permute-start | bytes 24584 | tf_op jit(solution)/shard_map/ppermute | solution.py:37
  11.0 0.2 collective-permute-start.5
  11.2 0.8 %inner.1 = (f32[1088,128]{1,0:T(8,128)S(1)}, f32[3,8,34,8,128]{4,3,2,1,0:T(8,128)S(1)}, f32[4,34,8,128]{3,2,1,0:T(8,128)S(1)}) custom-call(f32[4,16,512]{2,1,0:T(8,128)S(1)} %get-tuple-element.28.fields, f32[16,128]{1,0:T(8,128)S(1)} %collective-permute-done.1.first, f32[16,128]{1,0:T(8,128)S(1)} %collective-permute-done.second), custom_call_target="tpu_custom_call" | custom-call | flops 1310720 | bytes 1441792 | tf_op jit(solution)/shard_map/inner/pallas_call | solution.py:531
  12.0 2.3 %collective-permute-done.3 = f32[16,128]{1,0:T(8,128)S(1)} collective-permute-done((f32[16,128]{1,0:T(8,128)S(1)}, f32[16,128]{1,0:T(8,128)S(1)}, u32[]{:S(2)}, u32[]{:S(2)}) %collective-permute-start.3) | collective-permute-done | bytes 8224 | tf_op jit(solution)/shard_map/ppermute | solution.py:37
  14.3 0.4 %pole_sums.1 = (f32[74,8,128]{2,1,0:T(8,128)S(1)}, f32[3,18,8,128]{3,2,1,0:T(8,128)S(1)}) custom-call(f32[16,128]{1,0:T(8,128)S(1)} %get-tuple-element.27.scalars, f32[16,128]{1,0:T(8,128)S(1)} %collective-permute-done.1.first, f32[16,128]{1,0:T(8,128)S(1)} %collective-permute-done.second, f32[1,16,128]{2,1,0:T(8,128)S(1)} %bitcast.1, ...), custom_call_target="tpu_custom_call" | custom-call | tf_op jit(solution)/shard_map/pole_sums/pallas_call | solution.py:540
  14.7 0.0 collective-permute-done.5.side
  14.7 0.0 collective-permute-done.4.near
  14.7 0.9 %mid.1 = (f32[1088,128]{1,0:T(8,128)S(1)}, f32[3,8,34,8,128]{4,3,2,1,0:T(8,128)S(1)}, f32[4,34,8,128]{3,2,1,0:T(8,128)S(1)}, f32[3,18,8,128]{3,2,1,0:T(8,128)S(1)}) custom-call(f32[136,128]{1,0:T(8,128)S(1)} %collective-permute-done.4.near, ...), custom_call_target="tpu_custom_call", output_to_operand_aliasing={{0}: (3, {}), {1}: (4, {}), {2}: (5, {}), {3}: (6, {})} | custom-call | flops 1310720 | bytes 1441792 | tf_op jit(solution)/shard_map/mid/pallas_call | solution.py:549
  15.7 0.0 collective-permute-done.2.far
  15.7 2.0 %outer.1 = (f32[3,16,512]{2,1,0:T(8,128)}, f32[1088,128]{1,0:T(8,128)S(1)}, f32[3,8,34,8,128]{4,3,2,1,0:T(8,128)S(1)}, f32[4,34,8,128]{3,2,1,0:T(8,128)S(1)}, f32[3,18,8,128]{3,2,1,0:T(8,128)S(1)}) custom-call(f32[144,128]{1,0:T(8,128)S(1)} %collective-permute-done.2.far, ...), custom_call_target="tpu_custom_call", output_to_operand_aliasing={{1}: (2, {}), {2}: (3, {}), {3}: (4, {}), {4}: (5, {})} | custom-call | tf_op jit(solution)/shard_map/outer/pallas_call | solution.py:559
Async XLA Ops:
  1.1 5.6 %collective-permute-start = (f32[16,128]{1,0:T(8,128)S(1)}, f32[16,128]{1,0:T(8,128)S(1)}, u32[]{:S(2)}, u32[]{:S(2)}) collective-permute-start(f32[16,128]{1,0:T(8,128)S(1)} %get-tuple-element.23), channel_id=1, source_target_pairs={{8,16},{16,8},{24,0},{0,24},{9,17},{17,9},{25,1},{1,25},{10,18},{1... | collective-permute-start | bytes 24584 | tf_op jit(solution)/shard_map/ppermute | solution.py:32
  5.0 3.7 %collective-permute-start.1 = (f32[16,128]{1,0:T(8,128)S(1)}, f32[16,128]{1,0:T(8,128)S(1)}, u32[]{:S(2)}, u32[]{:S(2)}) collective-permute-start(f32[16,128]{1,0:T(8,128)S(1)} %get-tuple-element.24), channel_id=1, source_target_pairs={{0,8},{8,0},{16,24},{24,16},{1,9},{9,1},{17,25},{25,17},{2,10},{10... | collective-permute-start | bytes 24584 | tf_op jit(solution)/shard_map/ppermute | solution.py:32
  8.8 6.8 %collective-permute-start.2 = (f32[144,128]{1,0:T(8,128)S(1)}, f32[144,128]{1,0:T(8,128)S(1)}, u32[]{:S(2)}, u32[]{:S(2)}) collective-permute-start(f32[144,128]{1,0:T(8,128)S(1)} %get-tuple-element.26), channel_id=1, source_target_pairs={{1,2},{2,1},{3,4},{4,3},{5,6},{6,5},{7,0},{0,7},{9,10},{10,9},{11,... | collective-permute-start | bytes 221192 | tf_op jit(solution)/shard_map/ppermute | solution.py:32
  10.6 4.1 %collective-permute-start.4 = (f32[136,128]{1,0:T(8,128)S(1)}, f32[136,128]{1,0:T(8,128)S(1)}, u32[]{:S(2)}, u32[]{:S(2)}) collective-permute-start(f32[136,128]{1,0:T(8,128)S(1)} %get-tuple-element.31), channel_id=1, source_target_pairs={{0,1},{1,0},{2,3},{3,2},{4,5},{5,4},{6,7},{7,6},{8,9},{9,8},{10,11... | collective-permute-start | bytes 208904 | tf_op jit(solution)/shard_map/ppermute | solution.py:32
  10.6 3.7 %collective-permute-start.3 = (f32[16,128]{1,0:T(8,128)S(1)}, f32[16,128]{1,0:T(8,128)S(1)}, u32[]{:S(2)}, u32[]{:S(2)}) collective-permute-start(f32[16,128]{1,0:T(8,128)S(1)} %get-tuple-element.27.scalars), channel_id=1, source_target_pairs={{0,16},{8,24},{16,0},{24,8},{1,17},{9,25},{17,1},{25,9},{2,18},{10... | collective-permute-start | bytes 24584 | tf_op jit(solution)/shard_map/ppermute | solution.py:37
  11.0 3.7 %collective-permute-start.5 = (f32[8,128]{1,0:T(8,128)S(1)}, f32[8,128]{1,0:T(8,128)S(1)}, u32[]{:S(2)}, u32[]{:S(2)}) collective-permute-start(f32[8,128]{1,0:T(8,128)S(1)} %get-tuple-element.32), channel_id=1, source_target_pairs={{0,1},{1,0},{2,3},{3,2},{4,5},{5,4},{6,7},{7,6},{8,9},{9,8},{10,11... | collective-permute-start | bytes 12296 | tf_op jit(solution)/shard_map/ppermute | solution.py:32

commit v10 on v9

--- a/solution.py
+++ b/solution.py
@@ -174,7 +174,7 @@
     return side
 
 
-def pole_sums_kernel(scalars, first, second, others, poly, sums, sol):
+def pole_sums_kernel(scalars, first, second, others, grid, poly, sums, sol, result):
     odd = lax.rem(lax.axis_index("pole"), 2) == 1
     count = scalars.shape[0]
     lane = lax.broadcasted_iota(jnp.int32, (SUB, LANES), 1)
@@ -256,9 +256,41 @@
     sums[9 * ITERS] = total(products["ba/s"][0])
     sums[9 * ITERS + 1] = coriolis * total(products["b/s"][0])
 
-    rows = sol.shape[1] - 2
-    span = range(REACH + 1, REACH + rows - 1)
-    weighted_sums(poly, sums, sol, {r: range(known(rows, r) + 1) for r in span}, False)
+    _, (_, above) = towards(None, None)
+
+    def near_rows(above):
+        rows = sol.shape[1] - 2
+        whole = side_rows(rows, above)
+        terms = {r: range(ITERS) for r in whole}
+        for r in side_rows(rows, not above):
+            if known(rows, r) >= 0:
+                terms[r] = range(known(rows, r) + 1)
+        weighted_sums(poly, sums, sol, terms, False)
+        inside = [r for r in whole if r - 1 in whole and r + 1 in whole]
+        finish(grid, sums, sol, result, [r for r in inside if REACH <= r < REACH + rows])
+
+    pl.when(above)(lambda: near_rows(True))
+    pl.when(jnp.logical_not(above))(lambda: near_rows(False))
+
+
+def side_rows(rows, above):
+    middle = REACH + rows // 2
+    return range(REACH - 1, middle) if above else range(middle, REACH + rows + 1)
+
+
+def finish(grid, sums, sol, result, span):
+    push = sums[9 * ITERS]
+    lift = sums[9 * ITERS + 1]
+    for r in span:
+        i = r - REACH
+        u, v = cell(grid, 1, r), cell(grid, 2, r)
+        result[0, pl.ds(i * SUB, SUB)] = sol[0, i + 1]
+        east = 0.5 * (sol[1, i + 2] - sol[1, i])
+        north = 0.5 * (right(sol[2, i + 1]) - left(sol[2, i + 1]))
+        result[1, pl.ds(i * SUB, SUB)] = (push * u + lift * v) - (east + coriolis * north)
+        east = 0.5 * (sol[2, i + 2] - sol[2, i])
+        north = 0.5 * (right(sol[1, i + 1]) - left(sol[1, i + 1]))
+        result[2, pl.ds(i * SUB, SUB)] = (push * v - lift * u) + (coriolis * east - north)
 
 
 def known(rows, r):
@@ -412,8 +444,8 @@
             sweep(poly, coef, m, REACH + 2 + m, rows - 4 - 2 * m)
 
 
-def one_side(halo, side, above, sums, grid, poly, coef, sol):
-    rows = sol.shape[1] - 2
+def one_side(halo, side, above, height, grid, poly, coef):
+    rows = height - 2 * REACH
     below = REACH + rows
     main, ext, start = (1, 0, 0) if above else (below, below + SUB, below - 2)
     grid[pl.ds((ext * 4 + 3) * SUB, SUB), :] = jnp.ones((SUB, LANES), jnp.float32)
@@ -421,40 +453,45 @@
     prepare(grid, poly, coef, start, REACH)
     for m in range(ITERS - 1):
         sweep(poly, coef, m, 2 + m if above else below - 2 - m, REACH)
-    low = REACH - 1 if above else below - ITERS
-    terms = {r: range(max(known(rows, r), -1) + 1, ITERS) for r in range(low, low + REACH)}
-    weighted_sums(poly, sums, sol, terms, True)
-
-
-def both_ways(above, *rest):
-    pl.when(above)(lambda: one_side(*rest[:2], True, *rest[2:]))
-    pl.when(jnp.logical_not(above))(lambda: one_side(*rest[:2], False, *rest[2:]))
-
-
-def mid_kernel(near, side, sums, grid_in, poly_in, coef_in, sol_in, grid, poly, coef, sol):
+
+
+def mid_kernel(near, side, grid_in, poly_in, coef_in, grid, poly, coef):
     _, (_, above) = towards(None, None)
-    both_ways(above, near, side[...], sums, grid, poly, coef, sol)
+    height = poly.shape[2]
+    for way, here in ((True, above), (False, jnp.logical_not(above))):
+        pl.when(here)(lambda: one_side(near, side[...], way, height, grid, poly, coef))
 
 
 def outer_kernel(
-    far, sums, grid_in, poly_in, coef_in, sol_in, out, grid, poly, coef, sol, result
+    far,
+    sums,
+    grid_in,
+    poly_in,
+    coef_in,
+    sol_in,
+    result_in,
+    out,
+    grid,
+    poly,
+    coef,
+    sol,
+    result,
 ):
     rows, columns = out.shape[1:]
     lane = lax.broadcasted_iota(jnp.int32, (SUB, LANES), 1)
     (_, above), _ = towards(None, None)
-    side = far[pl.ds(far.shape[0] - SUB, SUB)]
-    both_ways(above, far, side, sums, grid, poly, coef, sol)
-    push = sums[9 * ITERS]
-    lift = sums[9 * ITERS + 1]
-    for i in range(rows):
-        u, v = cell(grid, 1, REACH + i), cell(grid, 2, REACH + i)
-        result[0, pl.ds(i * SUB, SUB)] = sol[0, i + 1]
-        east = 0.5 * (sol[1, i + 2] - sol[1, i])
-        north = 0.5 * (right(sol[2, i + 1]) - left(sol[2, i + 1]))
-        result[1, pl.ds(i * SUB, SUB)] = (push * u + lift * v) - (east + coriolis * north)
-        east = 0.5 * (sol[2, i + 2] - sol[2, i])
-        north = 0.5 * (right(sol[1, i + 1]) - left(sol[1, i + 1]))
-        result[2, pl.ds(i * SUB, SUB)] = (push * v - lift * u) + (coriolis * east - north)
+
+    def far_rows(above):
+        side = far[pl.ds(far.shape[0] - SUB, SUB)]
+        one_side(far, side, above, poly.shape[2], grid, poly, coef)
+        whole = side_rows(rows, above)
+        terms = {r: range(max(known(rows, r), -1) + 1, ITERS) for r in whole}
+        weighted_sums(poly, sums, sol, terms, True)
+        edge = whole.stop if above else whole.start - 1
+        finish(grid, sums, sol, result, [r for r in (*whole, edge) if REACH <= r < REACH + rows])
+
+    pl.when(above)(lambda: far_rows(True))
+    pl.when(jnp.logical_not(above))(lambda: far_rows(False))
 
     for k in range(3):
         for g in range(rows // SUB):
@@ -523,6 +560,7 @@
     poly = f32(3, ITERS, height, SUB, LANES)
     coef = f32(4, height, SUB, LANES)
     sol = f32(3, rows + 2, SUB, LANES)
+    result = f32(3, rows * SUB, LANES)
     cost = pl.CostEstimate(
         flops=10 * ITERS * rows * SUB * LANES,
         bytes_accessed=4 * SUB * LANES * rows * (4 + 2 * ITERS + 2),
@@ -537,35 +575,33 @@
         cost_estimate=cost,
         name="inner",
     )(fields, first, second)
-    sums, part = pl.pallas_call(
-        pole_sums_kernel,
-        out_shape=(f32(9 * ITERS + 2, SUB, LANES), sol),
-        in_specs=[vmem] * 5,
-        out_specs=(vmem, vmem),
-        compiler_params=small,
-        name="pole_sums",
-    )(scalars, first, second, others, inner[1])
-    held = (*inner, part)
     held = pl.pallas_call(
         mid_kernel,
-        out_shape=(grid, poly, coef, sol),
-        in_specs=[vmem] * 7,
-        out_specs=(vmem,) * 4,
-        input_output_aliases={3: 0, 4: 1, 5: 2, 6: 3},
+        out_shape=(grid, poly, coef),
+        in_specs=[vmem] * 5,
+        out_specs=(vmem,) * 3,
+        input_output_aliases={2: 0, 3: 1, 4: 2},
         compiler_params=small,
         cost_estimate=cost,
         name="mid",
-    )(near, near_side, sums, *held)
+    )(near, near_side, *inner)
+    sums, *part = pl.pallas_call(
+        pole_sums_kernel,
+        out_shape=(f32(9 * ITERS + 2, SUB, LANES), sol, result),
+        in_specs=[vmem] * 6,
+        out_specs=(vmem,) * 3,
+        compiler_params=small,
+        name="pole_sums",
+    )(scalars, first, second, others, *held[:2])
     return pl.pallas_call(
         outer_kernel,
-        out_shape=(f32(*state.shape), grid, poly, coef, sol),
-        in_specs=[vmem] * 6,
-        out_specs=(vmem,) * 5,
-        input_output_aliases={2: 1, 3: 2, 4: 3, 5: 4},
-        scratch_shapes=[pltpu.VMEM((3, rows * SUB, LANES), jnp.float32)],
+        out_shape=(f32(*state.shape), grid, poly, coef, sol, result),
+        in_specs=[vmem] * 7,
+        out_specs=(vmem,) * 6,
+        input_output_aliases={i: i - 1 for i in range(2, 7)},
         compiler_params=small,
         name="outer",
-    )(far, sums, *held)[0]
+    )(far, sums, *held, *part)[0]
 
 
 def solution(mesh):

time: 17.8 us -> 17 us (0.955)
  waiting for transfers between devices: 5.41 us -> 4.57 us
    ppermute x1, waiting for transfers between devices: 2.29 us -> 1.2 us  [shift(): lax.ppermute(block, axis, [(i, (i + step) % count) for i in range(count)])]
    ppermute x5, waiting for transfers between devices: 3.12 us -> 3.36 us  [swap(): return lax.ppermute(block, axis, pairs(lax.axis_size(axis), phase))]
    pallas_call x1, Pallas kernels: 0.42 us -> 0.63 us  [shards(): pl.pallas_call(pole_sums_kernel, out_shape=(f32(9 * ITERS + 2, SUB, LANES...]
  transfers between devices with their start and end apart: 6 -> 6, of which waited for: 3 -> 4; matrix products, arithmetic and copies ran while one was open for 0% -> 0% of each run, Pallas kernels for 12% -> 14%
where the time goes in v10:
time: 17 us; the launch traced here: 16.8 us
  starting transfers between devices  6.86 us (40%)
  Pallas kernels  5.38 us (32%)
  waiting for transfers between devices  4.57 us (27%)
    ppermute x5, starting transfers between devices, swap(): return lax.ppermute(block, axis, pairs(lax.axis_size(axis), phase))  6.45 us
    ppermute x5, waiting for transfers between devices, swap(): return lax.ppermute(block, axis, pairs(lax.axis_size(axis), phase))  3.36 us
    pallas_call x1, Pallas kernels, shards(): pl.pallas_call(outer_kernel, out_shape=(f32(*state.shape), grid, poly, co...  1.9 us
    ppermute x1, waiting for transfers between devices, shift(): lax.ppermute(block, axis, [(i, (i + step) % count) for i in range(count)])  1.2 us
    pallas_call x1, Pallas kernels, shards(): pl.pallas_call(pack_columns_kernel, out_shape=(pltpu.VMEM((4, rows, colum...  1.06 us
    pallas_call x1, Pallas kernels, shards(): pl.pallas_call(mid_kernel, out_shape=(grid, poly, coef), in_specs=[vmem]...  0.86 us
    pallas_call x1, Pallas kernels, shards(): pl.pallas_call(inner_kernel, out_shape=(grid, poly, coef), in_specs=[vmem...  0.78 us
    pallas_call x1, Pallas kernels, shards(): pl.pallas_call(pole_sums_kernel, out_shape=(f32(9 * ITERS + 2, SUB, LANES...  0.63 us
  transfers between devices with their start and end apart: 6, of which 4 were waited for; matrix products, arithmetic and copies ran while one was open for 0% of the time, Pallas kernels for 14%

profile of v10, /device:TPU:0, one launch (start us, length us, event | category | flops | bytes accessed | tf_op | source)
XLA Modules:
  0.0 16.8 jit_solution(221632306680722261)
XLA Ops:
  0.0 1.1 %pack_columns.1 = (f32[4,16,512]{2,1,0:T(8,128)S(1)}, f32[16,128]{1,0:T(8,128)S(1)}, f32[16,128]{1,0:T(8,128)S(1)}, f32[16,128]{1,0:T(8,128)S(1)}, f32[144,128]{1,0:T(8,128)S(1)}, /*index=5*/f32[136,128]{1,0:T(8,128)S(1)}) custom-call(f32[3,16,512]{2,1,0:T(8,128)} %state.1, f32[16,512]{1,0:T(8,128)} %depth.1, f32[4]{0:T(128)} %real.1, f32[4]{0:T(128)} %imag.1, ...), custom_call_target="tpu_custom_call" | custom-call | tf_op jit(solution)/shard_map/pack_columns/pallas_call | solution.py:521
  1.1 4.0 %collective-permute-start = (f32[16,128]{1,0:T(8,128)S(1)}, f32[16,128]{1,0:T(8,128)S(1)}, u32[]{:S(2)}, u32[]{:S(2)}) collective-permute-start(f32[16,128]{1,0:T(8,128)S(1)} %get-tuple-element.23), channel_id=1, source_target_pairs={{8,16},{16,8},{24,0},{0,24},{9,17},{17,9},{25,1},{1,25},{10,18},{1... | collective-permute-start | bytes 24584 | tf_op jit(solution)/shard_map/ppermute | solution.py:32
  5.0 0.5 %collective-permute-start.1 = (f32[16,128]{1,0:T(8,128)S(1)}, f32[16,128]{1,0:T(8,128)S(1)}, u32[]{:S(2)}, u32[]{:S(2)}) collective-permute-start(f32[16,128]{1,0:T(8,128)S(1)} %get-tuple-element.24), channel_id=1, source_target_pairs={{0,8},{8,0},{16,24},{24,16},{1,9},{9,1},{17,25},{25,17},{2,10},{10... | collective-permute-start | bytes 24584 | tf_op jit(solution)/shard_map/ppermute | solution.py:32
  5.6 1.1 %collective-permute-done.second = f32[16,128]{1,0:T(8,128)S(1)} collective-permute-done((f32[16,128]{1,0:T(8,128)S(1)}, f32[16,128]{1,0:T(8,128)S(1)}, u32[]{:S(2)}, u32[]{:S(2)}) %collective-permute-start) | collective-permute-done | bytes 8224 | tf_op jit(solution)/shard_map/ppermute | solution.py:32
  6.7 2.0 %collective-permute-done.1.first = f32[16,128]{1,0:T(8,128)S(1)} collective-permute-done((f32[16,128]{1,0:T(8,128)S(1)}, f32[16,128]{1,0:T(8,128)S(1)}, u32[]{:S(2)}, u32[]{:S(2)}) %collective-permute-start.1) | collective-permute-done | bytes 8224 | tf_op jit(solution)/shard_map/ppermute | solution.py:32
  8.7 0.1 pack_sides.1
  8.8 1.8 %collective-permute-start.2 = (f32[144,128]{1,0:T(8,128)S(1)}, f32[144,128]{1,0:T(8,128)S(1)}, u32[]{:S(2)}, u32[]{:S(2)}) collective-permute-start(f32[144,128]{1,0:T(8,128)S(1)} %get-tuple-element.26), channel_id=1, source_target_pairs={{1,2},{2,1},{3,4},{4,3},{5,6},{6,5},{7,0},{0,7},{9,10},{10,9},{11,... | collective-permute-start | bytes 221192 | tf_op jit(solution)/shard_map/ppermute | solution.py:32
  10.6 0.0 collective-permute-start.4
  10.6 0.4 %collective-permute-start.3 = (f32[16,128]{1,0:T(8,128)S(1)}, f32[16,128]{1,0:T(8,128)S(1)}, u32[]{:S(2)}, u32[]{:S(2)}) collective-permute-start(f32[16,128]{1,0:T(8,128)S(1)} %get-tuple-element.27.scalars), channel_id=1, source_target_pairs={{0,16},{8,24},{16,0},{24,8},{1,17},{9,25},{17,1},{25,9},{2,18},{10... | collective-permute-start | bytes 24584 | tf_op jit(solution)/shard_map/ppermute | solution.py:37
  11.0 0.2 collective-permute-start.5
  11.2 0.8 %inner.1 = (f32[1088,128]{1,0:T(8,128)S(1)}, f32[3,8,34,8,128]{4,3,2,1,0:T(8,128)S(1)}, f32[4,34,8,128]{3,2,1,0:T(8,128)S(1)}) custom-call(f32[4,16,512]{2,1,0:T(8,128)S(1)} %get-tuple-element.30.fields, f32[16,128]{1,0:T(8,128)S(1)} %collective-permute-done.1.first, f32[16,128]{1,0:T(8,128)S(1)} %collective-permute-done.second), custom_call_target="tpu_custom_call" | custom-call | flops 1310720 | bytes 1441792 | tf_op jit(solution)/shard_map/inner/pallas_call | solution.py:569
  12.0 0.2 %collective-permute-done.5.side = f32[8,128]{1,0:T(8,128)S(1)} collective-permute-done((f32[8,128]{1,0:T(8,128)S(1)}, f32[8,128]{1,0:T(8,128)S(1)}, u32[]{:S(2)}, u32[]{:S(2)}) %collective-permute-start.5) | collective-permute-done | bytes 4128 | tf_op jit(solution)/shard_map/ppermute | solution.py:32
  12.2 0.0 collective-permute-done.4.near
  12.2 0.9 %mid.1 = (f32[1088,128]{1,0:T(8,128)S(1)}, f32[3,8,34,8,128]{4,3,2,1,0:T(8,128)S(1)}, f32[4,34,8,128]{3,2,1,0:T(8,128)S(1)}) custom-call(f32[136,128]{1,0:T(8,128)S(1)} %collective-permute-done.4.near, f32[8,128]{1,0:T(8,128)S(1)} %collective-permute-done.5.side, ...), custom_call_target="tpu_custom_call", output_to_operand_aliasing={{0}: (2, {}), {1}: (3, {}), {2}: (4, {})} | custom-call | flops 1310720 | bytes 1441792 | tf_op jit(solution)/shard_map/mid/pallas_call | solution.py:578
  13.1 1.2 %collective-permute-done.3 = f32[16,128]{1,0:T(8,128)S(1)} collective-permute-done((f32[16,128]{1,0:T(8,128)S(1)}, f32[16,128]{1,0:T(8,128)S(1)}, u32[]{:S(2)}, u32[]{:S(2)}) %collective-permute-start.3) | collective-permute-done | bytes 8224 | tf_op jit(solution)/shard_map/ppermute | solution.py:37
  14.3 0.6 %pole_sums.1 = (f32[74,8,128]{2,1,0:T(8,128)S(1)}, f32[3,18,8,128]{3,2,1,0:T(8,128)S(1)}, f32[3,128,128]{2,1,0:T(8,128)S(1)}) custom-call(f32[16,128]{1,0:T(8,128)S(1)} %get-tuple-element.27.scalars, f32[16,128]{1,0:T(8,128)S(1)} %collective-permute-done.1.first, f32[16,128]{1,0:T(8,128)S(1)} %collective-permute-done.second, f32[1,16,128]{2,1,0:T(8,128)S(1)} %bitcast.1, ...), custom_call_target="tpu_custom_call" | custom-call | tf_op jit(solution)/shard_map/pole_sums/pallas_call | solution.py:588
  14.9 0.0 collective-permute-done.2.far
  14.9 1.9 %outer.1 = (f32[3,16,512]{2,1,0:T(8,128)}, f32[1088,128]{1,0:T(8,128)S(1)}, f32[3,8,34,8,128]{4,3,2,1,0:T(8,128)S(1)}, f32[4,34,8,128]{3,2,1,0:T(8,128)S(1)}, f3...) custom-call(f32[144,128]{1,0:T(8,128)S(1)} %collective-permute-done., ...), custom_call_target="tpu_custom_call", output_to_operand_aliasing={{1}: (2, {}), {2}: (3, {}), {3}: (4, {}), {4}: (5, {}), {5}... | custom-call | tf_op jit(solution)/shard_map/outer/pallas_call | solution.py:596
Async XLA Ops:
  1.1 5.6 %collective-permute-start = (f32[16,128]{1,0:T(8,128)S(1)}, f32[16,128]{1,0:T(8,128)S(1)}, u32[]{:S(2)}, u32[]{:S(2)}) collective-permute-start(f32[16,128]{1,0:T(8,128)S(1)} %get-tuple-element.23), channel_id=1, source_target_pairs={{8,16},{16,8},{24,0},{0,24},{9,17},{17,9},{25,1},{1,25},{10,18},{1... | collective-permute-start | bytes 24584 | tf_op jit(solution)/shard_map/ppermute | solution.py:32
  5.0 3.7 %collective-permute-start.1 = (f32[16,128]{1,0:T(8,128)S(1)}, f32[16,128]{1,0:T(8,128)S(1)}, u32[]{:S(2)}, u32[]{:S(2)}) collective-permute-start(f32[16,128]{1,0:T(8,128)S(1)} %get-tuple-element.24), channel_id=1, source_target_pairs={{0,8},{8,0},{16,24},{24,16},{1,9},{9,1},{17,25},{25,17},{2,10},{10... | collective-permute-start | bytes 24584 | tf_op jit(solution)/shard_map/ppermute | solution.py:32
  8.8 6.1 %collective-permute-start.2 = (f32[144,128]{1,0:T(8,128)S(1)}, f32[144,128]{1,0:T(8,128)S(1)}, u32[]{:S(2)}, u32[]{:S(2)}) collective-permute-start(f32[144,128]{1,0:T(8,128)S(1)} %get-tuple-element.26), channel_id=1, source_target_pairs={{1,2},{2,1},{3,4},{4,3},{5,6},{6,5},{7,0},{0,7},{9,10},{10,9},{11,... | collective-permute-start | bytes 221192 | tf_op jit(solution)/shard_map/ppermute | solution.py:32
  10.6 1.6 %collective-permute-start.4 = (f32[136,128]{1,0:T(8,128)S(1)}, f32[136,128]{1,0:T(8,128)S(1)}, u32[]{:S(2)}, u32[]{:S(2)}) collective-permute-start(f32[136,128]{1,0:T(8,128)S(1)} %get-tuple-element.28), channel_id=1, source_target_pairs={{0,1},{1,0},{2,3},{3,2},{4,5},{5,4},{6,7},{7,6},{8,9},{9,8},{10,11... | collective-permute-start | bytes 208904 | tf_op jit(solution)/shard_map/ppermute | solution.py:32
  10.6 3.7 %collective-permute-start.3 = (f32[16,128]{1,0:T(8,128)S(1)}, f32[16,128]{1,0:T(8,128)S(1)}, u32[]{:S(2)}, u32[]{:S(2)}) collective-permute-start(f32[16,128]{1,0:T(8,128)S(1)} %get-tuple-element.27.scalars), channel_id=1, source_target_pairs={{0,16},{8,24},{16,0},{24,8},{1,17},{9,25},{17,1},{25,9},{2,18},{10... | collective-permute-start | bytes 24584 | tf_op jit(solution)/shard_map/ppermute | solution.py:37
  11.0 1.2 %collective-permute-start.5 = (f32[8,128]{1,0:T(8,128)S(1)}, f32[8,128]{1,0:T(8,128)S(1)}, u32[]{:S(2)}, u32[]{:S(2)}) collective-permute-start(f32[8,128]{1,0:T(8,128)S(1)} %get-tuple-element.29), channel_id=1, source_target_pairs={{0,1},{1,0},{2,3},{3,2},{4,5},{5,4},{6,7},{7,6},{8,9},{9,8},{10,11... | collective-permute-start | bytes 12296 | tf_op jit(solution)/shard_map/ppermute | solution.py:32

commit v11 on v9

--- a/solution.py
+++ b/solution.py
@@ -11,7 +11,7 @@
 LANES = 128
 HALF = LANES // 2
 SIDE = 32
-EDGE = 12
+EDGE = REACH
 EAST = HALF + EDGE
 GRANT = 16 * 1024 * 1024
 
@@ -101,14 +101,16 @@
         rest = spread[g] if g < len(spread) else jnp.zeros((SUB, LANES), jnp.float32)
         eastward = rest
         westward = rest
-        for f in range(4):
-            west = fields[f, cut, 0:LANES]
-            east = fields[f, cut, columns - LANES : columns]
+        west = [fields[f, cut, 0:LANES] for f in range(4)]
+        east = [fields[f, cut, columns - LANES : columns] for f in range(4)]
+        west += [west[3] * west[1], west[3] * west[2]]
+        east += [east[3] * east[1], east[3] * east[2]]
+        for f in range(6):
             low, high = EDGE * f, EDGE * (f + 1)
             take = jnp.logical_and(lane >= low, lane < high)
-            eastward = jnp.where(take, turn(east, low + EDGE), eastward)
+            eastward = jnp.where(take, turn(east[f], low + EDGE), eastward)
             take = jnp.logical_and(lane >= EAST + low, lane < EAST + high)
-            westward = jnp.where(take, turn(west, EAST + low), westward)
+            westward = jnp.where(take, turn(west[f], EAST + low), westward)
         first[cut, :] = jnp.where(odd, westward, eastward)
         second[cut, :] = jnp.where(odd, eastward, westward)
     for target, low in towards(far, near):
@@ -164,17 +166,17 @@
         sides_of(first, second, pl.ds(rows - 2 * SUB, SUB))[SUB - 1 : SUB],
     )
     line = jnp.broadcast_to(line, (SUB, LANES))
-    for f in (1, 2):
-        flux = line * turn(line, -(3 - f) * EDGE)
-        west = turn(flux, (4 - f) * EDGE)
-        east = turn(flux, 5 * EDGE - (EAST + f * EDGE))
-        spare = jnp.where(lane < 5 * EDGE, west, east)
-        take = jnp.logical_and(lane >= 4 * EDGE, lane < 6 * EDGE)
-        side = jnp.where(jnp.logical_and(take, sub == f - 1), spare, side)
+    low, high = 4 * EDGE, 6 * EDGE
+    take = jnp.logical_or(
+        jnp.logical_and(lane >= low, lane < high),
+        jnp.logical_and(lane >= EAST + low, lane < EAST + high),
+    )
+    side = jnp.where(jnp.logical_and(take, sub == 0), line, side)
     return side
 
 
-def pole_sums_kernel(scalars, first, second, others, poly, sums, sol):
+def pole_sums_kernel(scalars, first, second, others, grid, *rest):
+    poly, (sums, sol, result) = rest[:ITERS], rest[ITERS:]
     odd = lax.rem(lax.axis_index("pole"), 2) == 1
     count = scalars.shape[0]
     lane = lax.broadcasted_iota(jnp.int32, (SUB, LANES), 1)
@@ -256,38 +258,65 @@
     sums[9 * ITERS] = total(products["ba/s"][0])
     sums[9 * ITERS + 1] = coriolis * total(products["b/s"][0])
 
+    _, (_, above) = towards(None, None)
     rows = sol.shape[1] - 2
-    span = range(REACH + 1, REACH + rows - 1)
-    weighted_sums(poly, sums, sol, {r: range(known(rows, r) + 1) for r in span}, False)
-
-
-def known(rows, r):
-    return min(ITERS - 2, r - (REACH + 1), REACH + rows - 2 - r)
-
-
-def weighted_sums(poly, sums, sol, terms, more, block=6):
+    near = side_rows(rows, above)
+    weighted_sums(poly, sums, sol, near, {k: range(ITERS) for k in range(len(near))}, False)
+    far = side_rows(rows, jnp.logical_not(above))
+    some = {k: range(known(k) + 1) for k in range(len(far)) if known(k) >= 0}
+    weighted_sums(poly, sums, sol, far, some, False)
+    low = REACH + jnp.where(above, 0, rows // 2 + 1)
+    finish(grid, sums, sol, result, low, rows // 2 - 1)
+
+
+def side_rows(rows, above):
+    low, high = REACH - 1, REACH + rows
+    return [jnp.where(above, low + k, high - k) for k in range(rows // 2 + 1)]
+
+
+def known(k):
+    return max(min(ITERS - 2, k - 2), -1)
+
+
+def weighted_sums(poly, sums, sol, rows, terms, more, block=6):
     low = REACH - 1
     order = sorted(terms)
     for i in range(0, len(order), block):
         span = order[i : i + block]
         acc = {}
         if more:
-            for r in span:
-                if len(terms[r]) < ITERS:
+            for k in span:
+                if len(terms[k]) < ITERS:
                     for g in range(3):
-                        acc[g, r] = sol[g, r - low]
+                        acc[g, k] = sol[g, rows[k] - low]
         for f in range(3):
             for m in range(ITERS):
-                part = [r for r in span if m in terms[r]]
+                part = [k for k in span if m in terms[k]]
                 if not part:
                     continue
-                value = [poly[f, m, r] for r in part]
+                value = [poly[m][f, rows[k]] for k in part]
                 for g in range(3):
                     c = sums[(g * 3 + f) * ITERS + m]
-                    for r, v in zip(part, value):
-                        acc[g, r] = acc[g, r] + c * v if (g, r) in acc else c * v
-        for (g, r), v in acc.items():
-            sol[g, r - low] = v
+                    for k, v in zip(part, value):
+                        acc[g, k] = acc[g, k] + c * v if (g, k) in acc else c * v
+        for (g, k), v in acc.items():
+            sol[g, rows[k] - low] = v
+
+
+def finish(grid, sums, sol, result, low, count):
+    push = sums[9 * ITERS]
+    lift = sums[9 * ITERS + 1]
+    for k in range(count):
+        i = low - REACH + k
+        u, v = cell(grid, 1, low + k), cell(grid, 2, low + k)
+        at = pl.ds(pl.multiple_of(i * SUB, SUB), SUB)
+        result[0, at] = sol[0, i + 1]
+        east = 0.5 * (sol[1, i + 2] - sol[1, i])
+        north = 0.5 * (right(sol[2, i + 1]) - left(sol[2, i + 1]))
+        result[1, at] = (push * u + lift * v) - (east + coriolis * north)
+        east = 0.5 * (sol[2, i + 2] - sol[2, i])
+        north = 0.5 * (right(sol[1, i + 1]) - left(sol[1, i + 1]))
+        result[2, at] = (push * v - lift * u) + (coriolis * east - north)
 
 
 def strips_of(tiles, side):
@@ -318,9 +347,8 @@
     for f in range(4):
         cut = [halo[pl.ds((f * tiles + t) * SUB, SUB)] for t in range(tiles)]
         lay(grid, cut, place(side, f), main * 4 + f, 4)
-    line = jnp.where(sub < tiles, side[0:1], side[1:2])
-    line = jnp.where(lane < HALF, turn(line, SIDE - 5 * EDGE), turn(line, -SIDE - 5 * EDGE))
-    side = line
+    line = jnp.broadcast_to(side[0:1], (SUB, LANES))
+    side = jnp.where(sub < tiles, place(line, 4), place(line, 5))
     block = halo[pl.ds(4 * tiles * SUB, SUB)]
     up, down = turn(block, SIDE), turn(block, -SIDE)
     before = jnp.where(sub % tiles == 0, side, pltpu.roll(up, 1, 0))
@@ -369,34 +397,34 @@
             coef[3, c] = 2.0 - ((across + before) + (north + south))
             east_slope = flux_east[2] - flux_east[0]
             north_slope = right(flux_north[1]) - left(flux_north[1])
-            poly[1, 0, c] = 0.5 * (east_slope + north_slope)
+            poly[0][1, c] = 0.5 * (east_slope + north_slope)
             east_slope = flux_north[2] - flux_north[0]
             north_slope = right(flux_east[1]) - left(flux_east[1])
-            poly[2, 0, c] = 0.5 * (east_slope - north_slope)
-            poly[0, 0, c] = cell(grid, 0, c)
+            poly[0][2, c] = 0.5 * (east_slope - north_slope)
+            poly[0][0, c] = cell(grid, 0, c)
 
 
 def sweep(poly, coef, m, start, count):
-    back = [poly[f, m, start - 1] for f in range(3)]
-    here = [poly[f, m, start] for f in range(3)]
+    back = [poly[m][f, start - 1] for f in range(3)]
+    here = [poly[m][f, start] for f in range(3)]
     below = coef[0, start - 1]
     for k in range(count):
         r = start + k
         above, north, south, diag = coef[0, r], coef[1, r], coef[2, r], coef[3, r]
-        ahead = [poly[f, m, r + 1] for f in range(3)]
+        ahead = [poly[m][f, r + 1] for f in range(3)]
         for f in range(3):
             value = diag * here[f]
             if m > 0:
-                value = value - poly[f, m - 1, r]
+                value = value - poly[m - 1][f, r]
             value = value + above * ahead[f]
             value = value + below * back[f]
             value = value + north * right(here[f])
             value = value + south * left(here[f])
-            poly[f, m + 1, r] = 0.5 * value if m == 0 else value
+            poly[m + 1][f, r] = 0.5 * value if m == 0 else value
         back, here, below = here, ahead, above
 
 
-def inner_kernel(fields, first, second, grid, poly, coef):
+def inner_kernel(fields, first, second, grid, coef, *poly):
     rows = fields.shape[1]
     for g in range(rows // SUB):
         side = sides_of(first, second, pl.ds(g * SUB, SUB))
@@ -412,49 +440,38 @@
             sweep(poly, coef, m, REACH + 2 + m, rows - 4 - 2 * m)
 
 
-def one_side(halo, side, above, sums, grid, poly, coef, sol):
-    rows = sol.shape[1] - 2
-    below = REACH + rows
-    main, ext, start = (1, 0, 0) if above else (below, below + SUB, below - 2)
-    grid[pl.ds((ext * 4 + 3) * SUB, SUB), :] = jnp.ones((SUB, LANES), jnp.float32)
+def one_side(halo, side, above, grid, coef, poly):
+    height = coef.shape[1]
+    below = height - REACH
+    main = jnp.where(above, 1, below)
+    ext = jnp.where(above, 0, below + SUB)
+    start = jnp.where(above, 0, below - 2)
+    at = pl.multiple_of((ext * 4 + 3) * SUB, SUB)
+    grid[pl.ds(at, SUB), :] = jnp.ones((SUB, LANES), jnp.float32)
     lay_halo(grid, halo, side, main, ext)
     prepare(grid, poly, coef, start, REACH)
     for m in range(ITERS - 1):
-        sweep(poly, coef, m, 2 + m if above else below - 2 - m, REACH)
-    low = REACH - 1 if above else below - ITERS
-    terms = {r: range(max(known(rows, r), -1) + 1, ITERS) for r in range(low, low + REACH)}
-    weighted_sums(poly, sums, sol, terms, True)
-
-
-def both_ways(above, *rest):
-    pl.when(above)(lambda: one_side(*rest[:2], True, *rest[2:]))
-    pl.when(jnp.logical_not(above))(lambda: one_side(*rest[:2], False, *rest[2:]))
-
-
-def mid_kernel(near, side, sums, grid_in, poly_in, coef_in, sol_in, grid, poly, coef, sol):
+        sweep(poly, coef, m, jnp.where(above, 2 + m, below - 2 - m), REACH)
+
+
+def mid_kernel(near, side, *rest):
+    grid, coef, *poly = rest[len(rest) // 2 :]
     _, (_, above) = towards(None, None)
-    both_ways(above, near, side[...], sums, grid, poly, coef, sol)
-
-
-def outer_kernel(
-    far, sums, grid_in, poly_in, coef_in, sol_in, out, grid, poly, coef, sol, result
-):
+    one_side(near, side[...], above, grid, coef, poly)
+
+
+def outer_kernel(far, sums, *rest):
+    out, grid, coef, sol, result, *poly = rest[len(rest) // 2 :]
     rows, columns = out.shape[1:]
     lane = lax.broadcasted_iota(jnp.int32, (SUB, LANES), 1)
     (_, above), _ = towards(None, None)
     side = far[pl.ds(far.shape[0] - SUB, SUB)]
-    both_ways(above, far, side, sums, grid, poly, coef, sol)
-    push = sums[9 * ITERS]
-    lift = sums[9 * ITERS + 1]
-    for i in range(rows):
-        u, v = cell(grid, 1, REACH + i), cell(grid, 2, REACH + i)
-        result[0, pl.ds(i * SUB, SUB)] = sol[0, i + 1]
-        east = 0.5 * (sol[1, i + 2] - sol[1, i])
-        north = 0.5 * (right(sol[2, i + 1]) - left(sol[2, i + 1]))
-        result[1, pl.ds(i * SUB, SUB)] = (push * u + lift * v) - (east + coriolis * north)
-        east = 0.5 * (sol[2, i + 2] - sol[2, i])
-        north = 0.5 * (right(sol[1, i + 1]) - left(sol[1, i + 1]))
-        result[2, pl.ds(i * SUB, SUB)] = (push * v - lift * u) + (coriolis * east - north)
+    one_side(far, side, above, grid, coef, poly)
+    whole = side_rows(rows, above)
+    terms = {k: range(known(k) + 1, ITERS) for k in range(len(whole))}
+    weighted_sums(poly, sums, sol, whole, terms, True)
+    low = REACH + jnp.where(above, 0, rows // 2 - 1)
+    finish(grid, sums, sol, result, low, rows // 2 + 1)
 
     for k in range(3):
         for g in range(rows // SUB):
@@ -520,52 +537,54 @@
     others = jnp.stack([shift(scalars, "pole", step) for step in range(2, count - 1)])
     height = rows + 2 * REACH
     grid = f32(height * 4 * SUB, LANES)
-    poly = f32(3, ITERS, height, SUB, LANES)
+    poly = [f32(3, height, SUB, LANES)] * ITERS
     coef = f32(4, height, SUB, LANES)
     sol = f32(3, rows + 2, SUB, LANES)
+    result = f32(3, rows * SUB, LANES)
+    state_of = (grid, coef, *poly)
     cost = pl.CostEstimate(
         flops=10 * ITERS * rows * SUB * LANES,
         bytes_accessed=4 * SUB * LANES * rows * (4 + 2 * ITERS + 2),
         transcendentals=0,
     )
-    inner = pl.pallas_call(
+    held = pl.pallas_call(
         inner_kernel,
-        out_shape=(grid, poly, coef),
+        out_shape=state_of,
         in_specs=[vmem] * 3,
-        out_specs=(vmem, vmem, vmem),
+        out_specs=(vmem,) * len(state_of),
         compiler_params=small,
         cost_estimate=cost,
         name="inner",
     )(fields, first, second)
-    sums, part = pl.pallas_call(
-        pole_sums_kernel,
-        out_shape=(f32(9 * ITERS + 2, SUB, LANES), sol),
-        in_specs=[vmem] * 5,
-        out_specs=(vmem, vmem),
-        compiler_params=small,
-        name="pole_sums",
-    )(scalars, first, second, others, inner[1])
-    held = (*inner, part)
     held = pl.pallas_call(
         mid_kernel,
-        out_shape=(grid, poly, coef, sol),
-        in_specs=[vmem] * 7,
-        out_specs=(vmem,) * 4,
-        input_output_aliases={3: 0, 4: 1, 5: 2, 6: 3},
+        out_shape=state_of,
+        in_specs=[vmem] * (2 + len(state_of)),
+        out_specs=(vmem,) * len(state_of),
+        input_output_aliases={2 + i: i for i in range(len(state_of))},
         compiler_params=small,
         cost_estimate=cost,
         name="mid",
-    )(near, near_side, sums, *held)
+    )(near, near_side, *held)
+    grid_held, coef_held, *poly_held = held
+    sums, *part = pl.pallas_call(
+        pole_sums_kernel,
+        out_shape=(f32(9 * ITERS + 2, SUB, LANES), sol, result),
+        in_specs=[vmem] * (5 + ITERS),
+        out_specs=(vmem,) * 3,
+        compiler_params=small,
+        name="pole_sums",
+    )(scalars, first, second, others, grid_held, *poly_held)
+    kept = (grid, coef, sol, result, *poly)
     return pl.pallas_call(
         outer_kernel,
-        out_shape=(f32(*state.shape), grid, poly, coef, sol),
-        in_specs=[vmem] * 6,
-        out_specs=(vmem,) * 5,
-        input_output_aliases={2: 1, 3: 2, 4: 3, 5: 4},
-        scratch_shapes=[pltpu.VMEM((3, rows * SUB, LANES), jnp.float32)],
+        out_shape=(f32(*state.shape), *kept),
+        in_specs=[vmem] * (2 + len(kept)),
+        out_specs=(vmem,) * (1 + len(kept)),
+        input_output_aliases={2 + i: 1 + i for i in range(len(kept))},
         compiler_params=small,
         name="outer",
-    )(far, sums, *held)[0]
+    )(far, sums, grid_held, coef_held, *part, *poly_held)[0]
 
 
 def solution(mesh):

time: 17.8 us -> 17 us (0.955)
  waiting for transfers between devices: 5.41 us -> 4.36 us
  Pallas kernels: 5.32 us -> 5.57 us
    ppermute x1, waiting for transfers between devices: 2.29 us -> 1.02 us  [shift(): lax.ppermute(block, axis, [(i, (i + step) % count) for i in range(count)])]
    pallas_call x1, Pallas kernels: 0.42 us -> 0.69 us  [shards(): pl.pallas_call(pole_sums_kernel, out_shape=(f32(9 * ITERS + 2, SUB, LANES...]
    ppermute x5, waiting for transfers between devices: 3.12 us -> 3.34 us  [swap(): return lax.ppermute(block, axis, pairs(lax.axis_size(axis), phase))]
  transfers between devices with their start and end apart: 6 -> 6, of which waited for: 3 -> 4; matrix products, arithmetic and copies ran while one was open for 0% -> 0% of each run, Pallas kernels for 12% -> 15%
where the time goes in v11:
time: 17 us; the launch traced here: 16.9 us
  starting transfers between devices  6.92 us (41%)
  Pallas kernels  5.57 us (33%)
  waiting for transfers between devices  4.36 us (26%)
    ppermute x5, starting transfers between devices, swap(): return lax.ppermute(block, axis, pairs(lax.axis_size(axis), phase))  6.5 us
    ppermute x5, waiting for transfers between devices, swap(): return lax.ppermute(block, axis, pairs(lax.axis_size(axis), phase))  3.34 us
    pallas_call x1, Pallas kernels, shards(): pl.pallas_call(outer_kernel, out_shape=(f32(*state.shape), *kept), in_spe...  1.98 us
    pallas_call x1, Pallas kernels, shards(): pl.pallas_call(pack_columns_kernel, out_shape=(pltpu.VMEM((4, rows, colum...  1.07 us
    pallas_call x1, Pallas kernels, shards(): pl.pallas_call(mid_kernel, out_shape=state_of, in_specs=[vmem] * (2 + len...  1.04 us
    ppermute x1, waiting for transfers between devices, shift(): lax.ppermute(block, axis, [(i, (i + step) % count) for i in range(count)])  1.02 us
    pallas_call x1, Pallas kernels, shards(): pl.pallas_call(inner_kernel, out_shape=state_of, in_specs=[vmem] * 3, out...  0.78 us
    pallas_call x1, Pallas kernels, shards(): pl.pallas_call(pole_sums_kernel, out_shape=(f32(9 * ITERS + 2, SUB, LANES...  0.69 us
  transfers between devices with their start and end apart: 6, of which 4 were waited for; matrix products, arithmetic and copies ran while one was open for 0% of the time, Pallas kernels for 15%

profile of v11, /device:TPU:0, one launch (start us, length us, event | category | flops | bytes accessed | tf_op | source)
XLA Modules:
  0.0 16.9 jit_solution(12676596280117528743)
XLA Ops:
  0.0 1.1 %pack_columns.1 = (f32[4,16,512]{2,1,0:T(8,128)S(1)}, f32[16,128]{1,0:T(8,128)S(1)}, f32[16,128]{1,0:T(8,128)S(1)}, f32[16,128]{1,0:T(8,128)S(1)}, f32[144,128]{1,0:T(8,128)S(1)}, /*index=5*/f32[136,128]{1,0:T(8,128)S(1)}) custom-call(f32[3,16,512]{2,1,0:T(8,128)} %state.1, f32[16,512]{1,0:T(8,128)} %depth.1, f32[4]{0:T(128)} %real.1, f32[4]{0:T(128)} %imag.1, ...), custom_call_target="tpu_custom_call" | custom-call | tf_op jit(solution)/shard_map/pack_columns/pallas_call | solution.py:501
  1.1 4.0 %collective-permute-start = (f32[16,128]{1,0:T(8,128)S(1)}, f32[16,128]{1,0:T(8,128)S(1)}, u32[]{:S(2)}, u32[]{:S(2)}) collective-permute-start(f32[16,128]{1,0:T(8,128)S(1)} %get-tuple-element.37), channel_id=1, source_target_pairs={{8,16},{16,8},{24,0},{0,24},{9,17},{17,9},{25,1},{1,25},{10,18},{1... | collective-permute-start | bytes 24584 | tf_op jit(solution)/shard_map/ppermute | solution.py:32
  5.0 0.5 %collective-permute-start.1 = (f32[16,128]{1,0:T(8,128)S(1)}, f32[16,128]{1,0:T(8,128)S(1)}, u32[]{:S(2)}, u32[]{:S(2)}) collective-permute-start(f32[16,128]{1,0:T(8,128)S(1)} %get-tuple-element.38), channel_id=1, source_target_pairs={{0,8},{8,0},{16,24},{24,16},{1,9},{9,1},{17,25},{25,17},{2,10},{10... | collective-permute-start | bytes 24584 | tf_op jit(solution)/shard_map/ppermute | solution.py:32
  5.6 1.1 %collective-permute-done.second = f32[16,128]{1,0:T(8,128)S(1)} collective-permute-done((f32[16,128]{1,0:T(8,128)S(1)}, f32[16,128]{1,0:T(8,128)S(1)}, u32[]{:S(2)}, u32[]{:S(2)}) %collective-permute-start) | collective-permute-done | bytes 8224 | tf_op jit(solution)/shard_map/ppermute | solution.py:32
  6.7 2.0 %collective-permute-done.1.first = f32[16,128]{1,0:T(8,128)S(1)} collective-permute-done((f32[16,128]{1,0:T(8,128)S(1)}, f32[16,128]{1,0:T(8,128)S(1)}, u32[]{:S(2)}, u32[]{:S(2)}) %collective-permute-start.1) | collective-permute-done | bytes 8224 | tf_op jit(solution)/shard_map/ppermute | solution.py:32
  8.7 1.8 %collective-permute-start.2 = (f32[144,128]{1,0:T(8,128)S(1)}, f32[144,128]{1,0:T(8,128)S(1)}, u32[]{:S(2)}, u32[]{:S(2)}) collective-permute-start(f32[144,128]{1,0:T(8,128)S(1)} %get-tuple-element.40), channel_id=1, source_target_pairs={{1,2},{2,1},{3,4},{4,3},{5,6},{6,5},{7,0},{0,7},{9,10},{10,9},{11,... | collective-permute-start | bytes 221192 | tf_op jit(solution)/shard_map/ppermute | solution.py:32
  10.5 0.0 collective-permute-start.4
  10.5 0.4 %collective-permute-start.3 = (f32[16,128]{1,0:T(8,128)S(1)}, f32[16,128]{1,0:T(8,128)S(1)}, u32[]{:S(2)}, u32[]{:S(2)}) collective-permute-start(f32[16,128]{1,0:T(8,128)S(1)} %get-tuple-element.41.scalars), channel_id=1, source_target_pairs={{0,16},{8,24},{16,0},{24,8},{1,17},{9,25},{17,1},{25,9},{2,18},{10... | collective-permute-start | bytes 24584 | tf_op jit(solution)/shard_map/ppermute | solution.py:37
  11.0 0.2 collective-permute-start.5
  11.1 0.8 %inner.1 = (f32[1088,128]{1,0:T(8,128)S(1)}, f32[4,34,8,128]{3,2,1,0:T(8,128)S(1)}, f32[3,34,8,128]{3,2,1,0:T(8,128)S(1)}, f32[3,34,8,128]{3,2,1,0:T(8,128)S(1)}...) custom-call(f32[4,16,512]{2,1,0:T(8,128)S(1)} %get-tuple-element.44., ...), custom_call_target="tpu_custom_call" | custom-call | flops 1310720 | bytes 1441792 | tf_op jit(solution)/shard_map/inner/pallas_call | solution.py:550
  11.9 0.2 %collective-permute-done.5.side = f32[8,128]{1,0:T(8,128)S(1)} collective-permute-done((f32[8,128]{1,0:T(8,128)S(1)}, f32[8,128]{1,0:T(8,128)S(1)}, u32[]{:S(2)}, u32[]{:S(2)}) %collective-permute-start.5) | collective-permute-done | bytes 4128 | tf_op jit(solution)/shard_map/ppermute | solution.py:32
  12.1 0.0 collective-permute-done.4.near
  12.1 1.0 %mid.1 = (f32[1088,128]{1,0:T(8,128)S(1)}, f32[4,34,8,128]{3,2,1,0:T(8,128)S(1)}, f32[3,34,8,128]{3,2,1,0:T(8,128)S(1)}, f32[3,34,8,128]{3,2,1,0:T(8,128)S(1)}, ...) custom-call(f32[136,128]{1,0:T(8,128)S(1)} %collective-permute-done., ...), custom_call_target="tpu_custom_call", output_to_operand_aliasing={{0}: (2, {}), {1}: (3, {}), {2}: (4, {}), {3}: (5, {}), {4}... | custom-call | flops 1310720 | bytes 1441792 | tf_op jit(solution)/shard_map/mid/pallas_call | solution.py:559
  13.2 1.0 %collective-permute-done.3 = f32[16,128]{1,0:T(8,128)S(1)} collective-permute-done((f32[16,128]{1,0:T(8,128)S(1)}, f32[16,128]{1,0:T(8,128)S(1)}, u32[]{:S(2)}, u32[]{:S(2)}) %collective-permute-start.3) | collective-permute-done | bytes 8224 | tf_op jit(solution)/shard_map/ppermute | solution.py:37
  14.2 0.7 %pole_sums.1 = (f32[74,8,128]{2,1,0:T(8,128)S(1)}, f32[3,18,8,128]{3,2,1,0:T(8,128)S(1)}, f32[3,128,128]{2,1,0:T(8,128)S(1)}) custom-call(f32[16,128]{1,0:T(8,128)S(1)} %get-tuple-element.41.scalars, f32[16,128]{1,0:T(8,128)S(1)} %collective-permute-done.1.first, f32[16,128]{1,0:T(8,128)S(1)} %collective-permute-done.second, f32[1,16,128]{2,1,0:T(8,128)S(1)} %bitcast.1, ...), custom_call_target="tpu_custom_call" | custom-call | tf_op jit(solution)/shard_map/pole_sums/pallas_call | solution.py:570
  14.9 0.0 collective-permute-done.2.far
  14.9 2.0 %outer.1 = (f32[3,16,512]{2,1,0:T(8,128)}, f32[1088,128]{1,0:T(8,128)S(1)}, f32[4,34,8,128]{3,2,1,0:T(8,128)S(1)}, f32[3,18,8,128]{3,2,1,0:T(8,128)S(1)}, f32[3,...) custom-call(f32[144,128]{1,0:T(8,128)S(1)} %collective-permute-done., ...), custom_call_target="tpu_custom_call", output_to_operand_aliasing={{1}: (2, {}), {2}: (3, {}), {3}: (4, {}), {4}: (5, {}), {5}... | custom-call | tf_op jit(solution)/shard_map/outer/pallas_call | solution.py:579
  (1 shorter events, 0.0 us)
Async XLA Ops:
  1.1 5.6 %collective-permute-start = (f32[16,128]{1,0:T(8,128)S(1)}, f32[16,128]{1,0:T(8,128)S(1)}, u32[]{:S(2)}, u32[]{:S(2)}) collective-permute-start(f32[16,128]{1,0:T(8,128)S(1)} %get-tuple-element.37), channel_id=1, source_target_pairs={{8,16},{16,8},{24,0},{0,24},{9,17},{17,9},{25,1},{1,25},{10,18},{1... | collective-permute-start | bytes 24584 | tf_op jit(solution)/shard_map/ppermute | solution.py:32
  5.0 3.7 %collective-permute-start.1 = (f32[16,128]{1,0:T(8,128)S(1)}, f32[16,128]{1,0:T(8,128)S(1)}, u32[]{:S(2)}, u32[]{:S(2)}) collective-permute-start(f32[16,128]{1,0:T(8,128)S(1)} %get-tuple-element.38), channel_id=1, source_target_pairs={{0,8},{8,0},{16,24},{24,16},{1,9},{9,1},{17,25},{25,17},{2,10},{10... | collective-permute-start | bytes 24584 | tf_op jit(solution)/shard_map/ppermute | solution.py:32
  8.7 6.2 %collective-permute-start.2 = (f32[144,128]{1,0:T(8,128)S(1)}, f32[144,128]{1,0:T(8,128)S(1)}, u32[]{:S(2)}, u32[]{:S(2)}) collective-permute-start(f32[144,128]{1,0:T(8,128)S(1)} %get-tuple-element.40), channel_id=1, source_target_pairs={{1,2},{2,1},{3,4},{4,3},{5,6},{6,5},{7,0},{0,7},{9,10},{10,9},{11,... | collective-permute-start | bytes 221192 | tf_op jit(solution)/shard_map/ppermute | solution.py:32
  10.5 1.6 %collective-permute-start.4 = (f32[136,128]{1,0:T(8,128)S(1)}, f32[136,128]{1,0:T(8,128)S(1)}, u32[]{:S(2)}, u32[]{:S(2)}) collective-permute-start(f32[136,128]{1,0:T(8,128)S(1)} %get-tuple-element.42), channel_id=1, source_target_pairs={{0,1},{1,0},{2,3},{3,2},{4,5},{5,4},{6,7},{7,6},{8,9},{9,8},{10,11... | collective-permute-start | bytes 208904 | tf_op jit(solution)/shard_map/ppermute | solution.py:32
  10.5 3.7 %collective-permute-start.3 = (f32[16,128]{1,0:T(8,128)S(1)}, f32[16,128]{1,0:T(8,128)S(1)}, u32[]{:S(2)}, u32[]{:S(2)}) collective-permute-start(f32[16,128]{1,0:T(8,128)S(1)} %get-tuple-element.41.scalars), channel_id=1, source_target_pairs={{0,16},{8,24},{16,0},{24,8},{1,17},{9,25},{17,1},{25,9},{2,18},{10... | collective-permute-start | bytes 24584 | tf_op jit(solution)/shard_map/ppermute | solution.py:37
  11.0 1.2 %collective-permute-start.5 = (f32[8,128]{1,0:T(8,128)S(1)}, f32[8,128]{1,0:T(8,128)S(1)}, u32[]{:S(2)}, u32[]{:S(2)}) collective-permute-start(f32[8,128]{1,0:T(8,128)S(1)} %get-tuple-element.43), channel_id=1, source_target_pairs={{0,1},{1,0},{2,3},{3,2},{4,5},{5,4},{6,7},{7,6},{8,9},{9,8},{10,11... | collective-permute-start | bytes 12296 | tf_op jit(solution)/shard_map/ppermute | solution.py:32

commit v12 on v11

--- a/solution.py
+++ b/solution.py
@@ -54,36 +54,41 @@
     return (a[0] * factor, a[1] * factor)
 
 
+def all_at_once(*pairs_of):
+    moves = [pltpu.make_async_copy(*pair) for pair in pairs_of]
+    for move in moves:
+        move.start()
+    for move in moves:
+        move.wait()
+
+
 def pack_columns_kernel(
     state,
     depth,
     real,
     imag,
     weight,
-    fields,
     first,
     second,
     scalars,
-    far,
-    near,
+    edges,
     real_in,
     imag_in,
     weight_in,
     done,
 ):
-    moves = [
-        pltpu.make_async_copy(state, fields.at[pl.ds(0, 3)], done.at[0]),
-        pltpu.make_async_copy(depth, fields.at[3], done.at[1]),
-        pltpu.make_async_copy(real, real_in, done.at[2]),
-        pltpu.make_async_copy(imag, imag_in, done.at[3]),
-        pltpu.make_async_copy(weight, weight_in, done.at[4]),
-    ]
-    for move in moves:
-        move.start()
-    for move in moves:
-        move.wait()
+    rows, columns = depth.shape
+    west_tile, east_tile = pl.ds(0, LANES), pl.ds(columns - LANES, LANES)
+    all_at_once(
+        (state.at[:, :, west_tile], edges.at[0, pl.ds(0, 3)], done.at[0]),
+        (depth.at[:, west_tile], edges.at[0, 3], done.at[1]),
+        (state.at[:, :, east_tile], edges.at[1, pl.ds(0, 3)], done.at[2]),
+        (depth.at[:, east_tile], edges.at[1, 3], done.at[3]),
+        (real, real_in, done.at[4]),
+        (imag, imag_in, done.at[5]),
+        (weight, weight_in, done.at[6]),
+    )
     odd = lax.rem(lax.axis_index("pole"), 2) == 1
-    rows, columns = fields.shape[1:]
     lane = lax.broadcasted_iota(jnp.int32, (SUB, LANES), 1)
     sub = lax.broadcasted_iota(jnp.int32, (SUB, LANES), 0)
     poles = real.shape[0]
@@ -101,8 +106,8 @@
         rest = spread[g] if g < len(spread) else jnp.zeros((SUB, LANES), jnp.float32)
         eastward = rest
         westward = rest
-        west = [fields[f, cut, 0:LANES] for f in range(4)]
-        east = [fields[f, cut, columns - LANES : columns] for f in range(4)]
+        west = [edges[0, f, cut] for f in range(4)]
+        east = [edges[1, f, cut] for f in range(4)]
         west += [west[3] * west[1], west[3] * west[2]]
         east += [east[3] * east[1], east[3] * east[2]]
         for f in range(6):
@@ -113,6 +118,14 @@
             westward = jnp.where(take, turn(west[f], EAST + low), westward)
         first[cut, :] = jnp.where(odd, westward, eastward)
         second[cut, :] = jnp.where(odd, eastward, westward)
+
+
+def load_fields_kernel(state, depth, fields, far, near, done):
+    rows = depth.shape[0]
+    all_at_once(
+        (state, fields.at[pl.ds(0, 3)], done.at[0]),
+        (depth, fields.at[3], done.at[1]),
+    )
     for target, low in towards(far, near):
         pl.when(low)(lambda: pack_rows(target, fields, 0, SUB))
         pl.when(jnp.logical_not(low))(
@@ -260,62 +273,55 @@
 
     _, (_, above) = towards(None, None)
     rows = sol.shape[1] - 2
-    near = side_rows(rows, above)
-    weighted_sums(poly, sums, sol, near, {k: range(ITERS) for k in range(len(near))}, False)
-    far = side_rows(rows, jnp.logical_not(above))
-    some = {k: range(known(k) + 1) for k in range(len(far)) if known(k) >= 0}
-    weighted_sums(poly, sums, sol, far, some, False)
-    low = REACH + jnp.where(above, 0, rows // 2 + 1)
-    finish(grid, sums, sol, result, low, rows // 2 - 1)
+
+    def near_rows(above):
+        near, far = side_rows(rows, above), side_rows(rows, not above)
+        acc = {}
+        for m in range(ITERS):
+            add(acc, sums, poly, m, near)
+        for m in range(ITERS - 1):
+            add(acc, sums, poly, m, [r for k, r in enumerate(far) if known(k) >= m])
+        for (g, r), v in acc.items():
+            sol[g, r - (REACH - 1)] = v
+        inside = sorted(near)[1:-1]
+        finish(grid, sums, result, acc, [r for r in inside if REACH <= r < REACH + rows])
+
+    pl.when(above)(lambda: near_rows(True))
+    pl.when(jnp.logical_not(above))(lambda: near_rows(False))
 
 
 def side_rows(rows, above):
     low, high = REACH - 1, REACH + rows
-    return [jnp.where(above, low + k, high - k) for k in range(rows // 2 + 1)]
+    return [low + k if above else high - k for k in range(rows // 2 + 1)]
 
 
 def known(k):
     return max(min(ITERS - 2, k - 2), -1)
 
 
-def weighted_sums(poly, sums, sol, rows, terms, more, block=6):
-    low = REACH - 1
-    order = sorted(terms)
-    for i in range(0, len(order), block):
-        span = order[i : i + block]
-        acc = {}
-        if more:
-            for k in span:
-                if len(terms[k]) < ITERS:
-                    for g in range(3):
-                        acc[g, k] = sol[g, rows[k] - low]
-        for f in range(3):
-            for m in range(ITERS):
-                part = [k for k in span if m in terms[k]]
-                if not part:
-                    continue
-                value = [poly[m][f, rows[k]] for k in part]
-                for g in range(3):
-                    c = sums[(g * 3 + f) * ITERS + m]
-                    for k, v in zip(part, value):
-                        acc[g, k] = acc[g, k] + c * v if (g, k) in acc else c * v
-        for (g, k), v in acc.items():
-            sol[g, rows[k] - low] = v
-
-
-def finish(grid, sums, sol, result, low, count):
+def add(acc, sums, poly, m, rows, values=None):
+    for f in range(3):
+        if not rows:
+            return
+        value = {r: poly[m][f, r] if values is None else values[f, r] for r in rows}
+        for g in range(3):
+            c = sums[(g * 3 + f) * ITERS + m]
+            for r in rows:
+                acc[g, r] = acc[g, r] + c * value[r] if (g, r) in acc else c * value[r]
+
+
+def finish(grid, sums, result, acc, span):
     push = sums[9 * ITERS]
     lift = sums[9 * ITERS + 1]
-    for k in range(count):
-        i = low - REACH + k
-        u, v = cell(grid, 1, low + k), cell(grid, 2, low + k)
-        at = pl.ds(pl.multiple_of(i * SUB, SUB), SUB)
-        result[0, at] = sol[0, i + 1]
-        east = 0.5 * (sol[1, i + 2] - sol[1, i])
-        north = 0.5 * (right(sol[2, i + 1]) - left(sol[2, i + 1]))
+    for r in span:
+        u, v = cell(grid, 1, r), cell(grid, 2, r)
+        at = pl.ds((r - REACH) * SUB, SUB)
+        result[0, at] = acc[0, r]
+        east = 0.5 * (acc[1, r + 1] - acc[1, r - 1])
+        north = 0.5 * (right(acc[2, r]) - left(acc[2, r]))
         result[1, at] = (push * u + lift * v) - (east + coriolis * north)
-        east = 0.5 * (sol[2, i + 2] - sol[2, i])
-        north = 0.5 * (right(sol[1, i + 1]) - left(sol[1, i + 1]))
+        east = 0.5 * (acc[2, r + 1] - acc[2, r - 1])
+        north = 0.5 * (right(acc[1, r]) - left(acc[1, r]))
         result[2, at] = (push * v - lift * u) + (coriolis * east - north)
 
 
@@ -404,24 +410,30 @@
             poly[0][0, c] = cell(grid, 0, c)
 
 
-def sweep(poly, coef, m, start, count):
-    back = [poly[m][f, start - 1] for f in range(3)]
-    here = [poly[m][f, start] for f in range(3)]
-    below = coef[0, start - 1]
-    for k in range(count):
-        r = start + k
-        above, north, south, diag = coef[0, r], coef[1, r], coef[2, r], coef[3, r]
-        ahead = [poly[m][f, r + 1] for f in range(3)]
+def sweep(poly, coef, m, start, count, upwards=False):
+    step = -1 if upwards else 1
+    order = range(start, start + count)[::step]
+    back = [poly[m][f, order[0] - step] for f in range(3)]
+    here = [poly[m][f, order[0]] for f in range(3)]
+    found = {}
+    for r in order:
+        north, south, diag = coef[1, r], coef[2, r], coef[3, r]
+        above, below = coef[0, r], coef[0, r - 1]
+        ahead = [poly[m][f, r + step] for f in range(3)]
         for f in range(3):
+            up, down = (back, ahead) if upwards else (ahead, back)
             value = diag * here[f]
             if m > 0:
                 value = value - poly[m - 1][f, r]
-            value = value + above * ahead[f]
-            value = value + below * back[f]
+            value = value + above * up[f]
+            value = value + below * down[f]
             value = value + north * right(here[f])
             value = value + south * left(here[f])
-            poly[m + 1][f, r] = 0.5 * value if m == 0 else value
-        back, here, below = here, ahead, above
+            value = 0.5 * value if m == 0 else value
+            poly[m + 1][f, r] = value
+            found[f, r] = value
+        back, here = here, ahead
+    return found
 
 
 def inner_kernel(fields, first, second, grid, coef, *poly):
@@ -440,24 +452,25 @@
             sweep(poly, coef, m, REACH + 2 + m, rows - 4 - 2 * m)
 
 
-def one_side(halo, side, above, grid, coef, poly):
-    height = coef.shape[1]
-    below = height - REACH
-    main = jnp.where(above, 1, below)
-    ext = jnp.where(above, 0, below + SUB)
-    start = jnp.where(above, 0, below - 2)
-    at = pl.multiple_of((ext * 4 + 3) * SUB, SUB)
-    grid[pl.ds(at, SUB), :] = jnp.ones((SUB, LANES), jnp.float32)
+def one_side(halo, side, above, grid, coef, poly, each):
+    below = coef.shape[1] - REACH
+    main, ext, start = (1, 0, 0) if above else (below, below + SUB, below - 2)
+    grid[pl.ds((ext * 4 + 3) * SUB, SUB), :] = jnp.ones((SUB, LANES), jnp.float32)
     lay_halo(grid, halo, side, main, ext)
     prepare(grid, poly, coef, start, REACH)
+    each(0, None)
     for m in range(ITERS - 1):
-        sweep(poly, coef, m, jnp.where(above, 2 + m, below - 2 - m), REACH)
+        found = sweep(poly, coef, m, 2 + m if above else below - 2 - m, REACH, above)
+        each(m + 1, found)
 
 
 def mid_kernel(near, side, *rest):
     grid, coef, *poly = rest[len(rest) // 2 :]
     _, (_, above) = towards(None, None)
-    one_side(near, side[...], above, grid, coef, poly)
+    for way, here in ((True, above), (False, jnp.logical_not(above))):
+        pl.when(here)(
+            lambda: one_side(near, side[...], way, grid, coef, poly, lambda m, found: None)
+        )
 
 
 def outer_kernel(far, sums, *rest):
@@ -465,13 +478,31 @@
     rows, columns = out.shape[1:]
     lane = lax.broadcasted_iota(jnp.int32, (SUB, LANES), 1)
     (_, above), _ = towards(None, None)
-    side = far[pl.ds(far.shape[0] - SUB, SUB)]
-    one_side(far, side, above, grid, coef, poly)
-    whole = side_rows(rows, above)
-    terms = {k: range(known(k) + 1, ITERS) for k in range(len(whole))}
-    weighted_sums(poly, sums, sol, whole, terms, True)
-    low = REACH + jnp.where(above, 0, rows // 2 - 1)
-    finish(grid, sums, sol, result, low, rows // 2 + 1)
+
+    def far_rows(above):
+        side = far[pl.ds(far.shape[0] - SUB, SUB)]
+        whole = side_rows(rows, above)
+        inside = 1 if above else -1
+        edges = [whole[-1] + inside, whole[-1] + 2 * inside]
+        acc = {}
+        for r in edges + [r for k, r in enumerate(whole) if known(k) >= 0]:
+            for g in range(3):
+                acc[g, r] = sol[g, r - (REACH - 1)]
+
+        def each(m, found):
+            part = [r for k, r in enumerate(whole) if known(k) < m]
+            if found is not None:
+                held = [r for r in part if (0, r) in found]
+                add(acc, sums, poly, m, held, found)
+                part = [r for r in part if r not in held]
+            add(acc, sums, poly, m, part)
+
+        one_side(far, side, above, grid, coef, poly, each)
+        span = [r for r in whole + edges[:1] if REACH <= r < REACH + rows]
+        finish(grid, sums, result, acc, span)
+
+    pl.when(above)(lambda: far_rows(True))
+    pl.when(jnp.logical_not(above))(lambda: far_rows(False))
 
     for k in range(3):
         for g in range(rows // SUB):
@@ -497,28 +528,35 @@
     ]
     hbm = pl.BlockSpec(memory_space=pltpu.HBM)
     message = pltpu.VMEM((rows, LANES), jnp.float32)
-    count = (4 * SUB + 2) * columns // LANES
-    fields, first, second, scalars, far, near = pl.pallas_call(
+    first, second, scalars = pl.pallas_call(
         pack_columns_kernel,
-        out_shape=(
-            pltpu.VMEM((4, rows, columns), jnp.float32),
-            message,
-            message,
-            pltpu.VMEM((4 * poles, LANES), jnp.float32),
-            pltpu.VMEM((count + SUB, LANES), jnp.float32),
-            pltpu.VMEM((count, LANES), jnp.float32),
-        ),
+        out_shape=(message, message, pltpu.VMEM((4 * poles, LANES), jnp.float32)),
         in_specs=[hbm] * 5,
-        out_specs=(vmem,) * 6,
+        out_specs=(vmem,) * 3,
         scratch_shapes=[
+            pltpu.VMEM((2, 4, rows, LANES), jnp.float32),
             pltpu.SMEM(pole_real.shape, jnp.float32),
             pltpu.SMEM(pole_imag.shape, jnp.float32),
             pltpu.SMEM(pole_weight.shape, jnp.float32),
-            pltpu.SemaphoreType.DMA((5,)),
+            pltpu.SemaphoreType.DMA((7,)),
         ],
         compiler_params=small,
         name="pack_columns",
     )(*given)
+    count = (4 * SUB + 2) * columns // LANES
+    fields, far, near = pl.pallas_call(
+        load_fields_kernel,
+        out_shape=(
+            pltpu.VMEM((4, rows, columns), jnp.float32),
+            pltpu.VMEM((count + SUB, LANES), jnp.float32),
+            pltpu.VMEM((count, LANES), jnp.float32),
+        ),
+        in_specs=[hbm] * 2,
+        out_specs=(vmem,) * 3,
+        scratch_shapes=[pltpu.SemaphoreType.DMA((2,))],
+        compiler_params=small,
+        name="load_fields",
+    )(*given[:2])
     second = swap(second, "pole", 1)
     first = swap(first, "pole", 0)
     far, near_side = pl.pallas_call(

time: 17 us -> 16.8 us (0.988)
  waiting for transfers between devices: 4.36 us -> 3.62 us
  Pallas kernels: 5.57 us -> 6.03 us
    ppermute x5, waiting for transfers between devices: 3.34 us -> 2.42 us  [swap(): return lax.ppermute(block, axis, pairs(lax.axis_size(axis), phase))]
    pallas_call x1 -> x2, Pallas kernels: 1.07 us -> 1.92 us  [the longest x1 0.99 us: shards(): pl.pallas_call(pack_columns_kernel, out_shape=(message, message, pltpu.VM...]
    ppermute x1, waiting for transfers between devices: 1.02 us -> 1.2 us  [shift(): lax.ppermute(block, axis, [(i, (i + step) % count) for i in range(count)])]
  transfers between devices with their start and end apart: 6 -> 6, of which waited for: 4 -> 4; matrix products, arithmetic and copies ran while one was open for 0% -> 0% of each run, Pallas kernels for 15% -> 19%
where the time goes in v12:
time: 16.8 us; the launch traced here: 16.6 us
  starting transfers between devices  6.92 us (41%)
  Pallas kernels  6.03 us (36%)
  waiting for transfers between devices  3.62 us (22%)
    ppermute x5, starting transfers between devices, swap(): return lax.ppermute(block, axis, pairs(lax.axis_size(axis), phase))  6.51 us
    ppermute x5, waiting for transfers between devices, swap(): return lax.ppermute(block, axis, pairs(lax.axis_size(axis), phase))  2.42 us
    pallas_call x1, Pallas kernels, shards(): pl.pallas_call(outer_kernel, out_shape=(f32(*state.shape), *kept), in_spe...  1.82 us
    ppermute x1, waiting for transfers between devices, shift(): lax.ppermute(block, axis, [(i, (i + step) % count) for i in range(count)])  1.2 us
    pallas_call x1, Pallas kernels, shards(): pl.pallas_call(pack_columns_kernel, out_shape=(message, message, pltpu.VM...  0.99 us
    pallas_call x1, Pallas kernels, shards(): pl.pallas_call(load_fields_kernel, out_shape=(pltpu.VMEM((4, rows, column...  0.93 us
    pallas_call x1, Pallas kernels, shards(): pl.pallas_call(mid_kernel, out_shape=state_of, in_specs=[vmem] * (2 + len...  0.87 us
    pallas_call x1, Pallas kernels, shards(): pl.pallas_call(inner_kernel, out_shape=state_of, in_specs=[vmem] * 3, out...  0.78 us
  transfers between devices with their start and end apart: 6, of which 4 were waited for; matrix products, arithmetic and copies ran while one was open for 0% of the time, Pallas kernels for 19%

profile of v12, /device:TPU:0, one launch (start us, length us, event | category | flops | bytes accessed | tf_op | source)
XLA Modules:
  0.0 16.6 jit_solution(14800042284703245728)
XLA Ops:
  0.0 1.0 %pack_columns.1 = (f32[16,128]{1,0:T(8,128)S(1)}, f32[16,128]{1,0:T(8,128)S(1)}, f32[16,128]{1,0:T(8,128)S(1)}) custom-call(f32[3,16,512]{2,1,0:T(8,128)} %state.3, f32[16,512]{1,0:T(8,128)} %depth.3, f32[4]{0:T(128)} %real.1, f32[4]{0:T(128)} %imag.1, f32[2,4]{1,0:T(2,128)} %weight.1), custom_call_target="tpu_custom_call" | custom-call | tf_op jit(solution)/shard_map/pack_columns/pallas_call | solution.py:531
  1.0 4.0 %collective-permute-start = (f32[16,128]{1,0:T(8,128)S(1)}, f32[16,128]{1,0:T(8,128)S(1)}, u32[]{:S(2)}, u32[]{:S(2)}) collective-permute-start(f32[16,128]{1,0:T(8,128)S(1)} %get-tuple-element.37), channel_id=1, source_target_pairs={{8,16},{16,8},{24,0},{0,24},{9,17},{17,9},{25,1},{1,25},{10,18},{1... | collective-permute-start | bytes 24584 | tf_op jit(solution)/shard_map/ppermute | solution.py:32
  5.0 0.5 %collective-permute-start.1 = (f32[16,128]{1,0:T(8,128)S(1)}, f32[16,128]{1,0:T(8,128)S(1)}, u32[]{:S(2)}, u32[]{:S(2)}) collective-permute-start(f32[16,128]{1,0:T(8,128)S(1)} %get-tuple-element.38), channel_id=1, source_target_pairs={{0,8},{8,0},{16,24},{24,16},{1,9},{9,1},{17,25},{25,17},{2,10},{10... | collective-permute-start | bytes 24584 | tf_op jit(solution)/shard_map/ppermute | solution.py:32
  5.5 0.9 %load_fields.1 = (f32[4,16,512]{2,1,0:T(8,128)S(1)}, f32[144,128]{1,0:T(8,128)S(1)}, f32[136,128]{1,0:T(8,128)S(1)}) custom-call(f32[3,16,512]{2,1,0:T(8,128)} %state.3, f32[16,512]{1,0:T(8,128)} %depth.3), custom_call_target="tpu_custom_call" | custom-call | tf_op jit(solution)/shard_map/load_fields/pallas_call | solution.py:547
  6.4 0.2 collective-permute-done.second
  6.6 2.0 %collective-permute-done.1.first = f32[16,128]{1,0:T(8,128)S(1)} collective-permute-done((f32[16,128]{1,0:T(8,128)S(1)}, f32[16,128]{1,0:T(8,128)S(1)}, u32[]{:S(2)}, u32[]{:S(2)}) %collective-permute-start.1) | collective-permute-done | bytes 8224 | tf_op jit(solution)/shard_map/ppermute | solution.py:32
  8.6 1.8 %collective-permute-start.2 = (f32[144,128]{1,0:T(8,128)S(1)}, f32[144,128]{1,0:T(8,128)S(1)}, u32[]{:S(2)}, u32[]{:S(2)}) collective-permute-start(f32[144,128]{1,0:T(8,128)S(1)} %get-tuple-element.40), channel_id=1, source_target_pairs={{1,2},{2,1},{3,4},{4,3},{5,6},{6,5},{7,0},{0,7},{9,10},{10,9},{11,... | collective-permute-start | bytes 221192 | tf_op jit(solution)/shard_map/ppermute | solution.py:32
  10.5 0.0 collective-permute-start.4
  10.5 0.4 %collective-permute-start.3 = (f32[16,128]{1,0:T(8,128)S(1)}, f32[16,128]{1,0:T(8,128)S(1)}, u32[]{:S(2)}, u32[]{:S(2)}) collective-permute-start(f32[16,128]{1,0:T(8,128)S(1)} %get-tuple-element.41.scalars), channel_id=1, source_target_pairs={{0,16},{8,24},{16,0},{24,8},{1,17},{9,25},{17,1},{25,9},{2,18},{10... | collective-permute-start | bytes 24584 | tf_op jit(solution)/shard_map/ppermute | solution.py:37
  10.9 0.2 collective-permute-start.5
  11.1 0.8 %inner.1 = (f32[1088,128]{1,0:T(8,128)S(1)}, f32[4,34,8,128]{3,2,1,0:T(8,128)S(1)}, f32[3,34,8,128]{3,2,1,0:T(8,128)S(1)}, f32[3,34,8,128]{3,2,1,0:T(8,128)S(1)}...) custom-call(f32[4,16,512]{2,1,0:T(8,128)S(1)} %get-tuple-element.44., ...), custom_call_target="tpu_custom_call" | custom-call | flops 1310720 | bytes 1441792 | tf_op jit(solution)/shard_map/inner/pallas_call | solution.py:588
  11.8 0.2 %collective-permute-done.5.side = f32[8,128]{1,0:T(8,128)S(1)} collective-permute-done((f32[8,128]{1,0:T(8,128)S(1)}, f32[8,128]{1,0:T(8,128)S(1)}, u32[]{:S(2)}, u32[]{:S(2)}) %collective-permute-start.5) | collective-permute-done | bytes 4128 | tf_op jit(solution)/shard_map/ppermute | solution.py:32
  12.1 0.0 collective-permute-done.4.near
  12.1 0.9 %mid.1 = (f32[1088,128]{1,0:T(8,128)S(1)}, f32[4,34,8,128]{3,2,1,0:T(8,128)S(1)}, f32[3,34,8,128]{3,2,1,0:T(8,128)S(1)}, f32[3,34,8,128]{3,2,1,0:T(8,128)S(1)}, ...) custom-call(f32[136,128]{1,0:T(8,128)S(1)} %collective-permute-done., ...), custom_call_target="tpu_custom_call", output_to_operand_aliasing={{0}: (2, {}), {1}: (3, {}), {2}: (4, {}), {3}: (5, {}), {4}... | custom-call | flops 1310720 | bytes 1441792 | tf_op jit(solution)/shard_map/mid/pallas_call | solution.py:597
  12.9 1.2 %collective-permute-done.3 = f32[16,128]{1,0:T(8,128)S(1)} collective-permute-done((f32[16,128]{1,0:T(8,128)S(1)}, f32[16,128]{1,0:T(8,128)S(1)}, u32[]{:S(2)}, u32[]{:S(2)}) %collective-permute-start.3) | collective-permute-done | bytes 8224 | tf_op jit(solution)/shard_map/ppermute | solution.py:37
  14.1 0.6 %pole_sums.1 = (f32[74,8,128]{2,1,0:T(8,128)S(1)}, f32[3,18,8,128]{3,2,1,0:T(8,128)S(1)}, f32[3,128,128]{2,1,0:T(8,128)S(1)}) custom-call(f32[16,128]{1,0:T(8,128)S(1)} %get-tuple-element.41.scalars, f32[16,128]{1,0:T(8,128)S(1)} %collective-permute-done.1.first, f32[16,128]{1,0:T(8,128)S(1)} %collective-permute-done.second, f32[1,16,128]{2,1,0:T(8,128)S(1)} %bitcast.1, ...), custom_call_target="tpu_custom_call" | custom-call | tf_op jit(solution)/shard_map/pole_sums/pallas_call | solution.py:608
  14.8 0.0 collective-permute-done.2.far
  14.8 1.8 %outer.1 = (f32[3,16,512]{2,1,0:T(8,128)}, f32[1088,128]{1,0:T(8,128)S(1)}, f32[4,34,8,128]{3,2,1,0:T(8,128)S(1)}, f32[3,18,8,128]{3,2,1,0:T(8,128)S(1)}, f32[3,...) custom-call(f32[144,128]{1,0:T(8,128)S(1)} %collective-permute-done., ...), custom_call_target="tpu_custom_call", output_to_operand_aliasing={{1}: (2, {}), {2}: (3, {}), {3}: (4, {}), {4}: (5, {}), {5}... | custom-call | tf_op jit(solution)/shard_map/outer/pallas_call | solution.py:617
  (1 shorter events, 0.0 us)
Async XLA Ops:
  1.0 5.6 %collective-permute-start = (f32[16,128]{1,0:T(8,128)S(1)}, f32[16,128]{1,0:T(8,128)S(1)}, u32[]{:S(2)}, u32[]{:S(2)}) collective-permute-start(f32[16,128]{1,0:T(8,128)S(1)} %get-tuple-element.37), channel_id=1, source_target_pairs={{8,16},{16,8},{24,0},{0,24},{9,17},{17,9},{25,1},{1,25},{10,18},{1... | collective-permute-start | bytes 24584 | tf_op jit(solution)/shard_map/ppermute | solution.py:32
  5.0 3.7 %collective-permute-start.1 = (f32[16,128]{1,0:T(8,128)S(1)}, f32[16,128]{1,0:T(8,128)S(1)}, u32[]{:S(2)}, u32[]{:S(2)}) collective-permute-start(f32[16,128]{1,0:T(8,128)S(1)} %get-tuple-element.38), channel_id=1, source_target_pairs={{0,8},{8,0},{16,24},{24,16},{1,9},{9,1},{17,25},{25,17},{2,10},{10... | collective-permute-start | bytes 24584 | tf_op jit(solution)/shard_map/ppermute | solution.py:32
  8.6 6.2 %collective-permute-start.2 = (f32[144,128]{1,0:T(8,128)S(1)}, f32[144,128]{1,0:T(8,128)S(1)}, u32[]{:S(2)}, u32[]{:S(2)}) collective-permute-start(f32[144,128]{1,0:T(8,128)S(1)} %get-tuple-element.40), channel_id=1, source_target_pairs={{1,2},{2,1},{3,4},{4,3},{5,6},{6,5},{7,0},{0,7},{9,10},{10,9},{11,... | collective-permute-start | bytes 221192 | tf_op jit(solution)/shard_map/ppermute | solution.py:32
  10.5 1.6 %collective-permute-start.4 = (f32[136,128]{1,0:T(8,128)S(1)}, f32[136,128]{1,0:T(8,128)S(1)}, u32[]{:S(2)}, u32[]{:S(2)}) collective-permute-start(f32[136,128]{1,0:T(8,128)S(1)} %get-tuple-element.42), channel_id=1, source_target_pairs={{0,1},{1,0},{2,3},{3,2},{4,5},{5,4},{6,7},{7,6},{8,9},{9,8},{10,11... | collective-permute-start | bytes 208904 | tf_op jit(solution)/shard_map/ppermute | solution.py:32
  10.5 3.7 %collective-permute-start.3 = (f32[16,128]{1,0:T(8,128)S(1)}, f32[16,128]{1,0:T(8,128)S(1)}, u32[]{:S(2)}, u32[]{:S(2)}) collective-permute-start(f32[16,128]{1,0:T(8,128)S(1)} %get-tuple-element.41.scalars), channel_id=1, source_target_pairs={{0,16},{8,24},{16,0},{24,8},{1,17},{9,25},{17,1},{25,9},{2,18},{10... | collective-permute-start | bytes 24584 | tf_op jit(solution)/shard_map/ppermute | solution.py:37
  10.9 1.2 %collective-permute-start.5 = (f32[8,128]{1,0:T(8,128)S(1)}, f32[8,128]{1,0:T(8,128)S(1)}, u32[]{:S(2)}, u32[]{:S(2)}) collective-permute-start(f32[8,128]{1,0:T(8,128)S(1)} %get-tuple-element.43), channel_id=1, source_target_pairs={{0,1},{1,0},{2,3},{3,2},{4,5},{5,4},{6,7},{7,6},{8,9},{9,8},{10,11... | collective-permute-start | bytes 12296 | tf_op jit(solution)/shard_map/ppermute | solution.py:32

commit v13 on v12

--- a/solution.py
+++ b/solution.py
@@ -68,27 +68,28 @@
     real,
     imag,
     weight,
+    fields,
     first,
     second,
     scalars,
-    edges,
+    far_early,
+    far,
+    near_early,
+    near,
     real_in,
     imag_in,
     weight_in,
     done,
 ):
-    rows, columns = depth.shape
-    west_tile, east_tile = pl.ds(0, LANES), pl.ds(columns - LANES, LANES)
     all_at_once(
-        (state.at[:, :, west_tile], edges.at[0, pl.ds(0, 3)], done.at[0]),
-        (depth.at[:, west_tile], edges.at[0, 3], done.at[1]),
-        (state.at[:, :, east_tile], edges.at[1, pl.ds(0, 3)], done.at[2]),
-        (depth.at[:, east_tile], edges.at[1, 3], done.at[3]),
-        (real, real_in, done.at[4]),
-        (imag, imag_in, done.at[5]),
-        (weight, weight_in, done.at[6]),
+        (state, fields.at[pl.ds(0, 3)], done.at[0]),
+        (depth, fields.at[3], done.at[1]),
+        (real, real_in, done.at[2]),
+        (imag, imag_in, done.at[3]),
+        (weight, weight_in, done.at[4]),
     )
     odd = lax.rem(lax.axis_index("pole"), 2) == 1
+    rows, columns = fields.shape[1:]
     lane = lax.broadcasted_iota(jnp.int32, (SUB, LANES), 1)
     sub = lax.broadcasted_iota(jnp.int32, (SUB, LANES), 0)
     poles = real.shape[0]
@@ -106,8 +107,8 @@
         rest = spread[g] if g < len(spread) else jnp.zeros((SUB, LANES), jnp.float32)
         eastward = rest
         westward = rest
-        west = [edges[0, f, cut] for f in range(4)]
-        east = [edges[1, f, cut] for f in range(4)]
+        west = [fields[f, cut, 0:LANES] for f in range(4)]
+        east = [fields[f, cut, columns - LANES : columns] for f in range(4)]
         west += [west[3] * west[1], west[3] * west[2]]
         east += [east[3] * east[1], east[3] * east[2]]
         for f in range(6):
@@ -118,19 +119,14 @@
             westward = jnp.where(take, turn(west[f], EAST + low), westward)
         first[cut, :] = jnp.where(odd, westward, eastward)
         second[cut, :] = jnp.where(odd, eastward, westward)
-
-
-def load_fields_kernel(state, depth, fields, far, near, done):
-    rows = depth.shape[0]
-    all_at_once(
-        (state, fields.at[pl.ds(0, 3)], done.at[0]),
-        (depth, fields.at[3], done.at[1]),
-    )
-    for target, low in towards(far, near):
-        pl.when(low)(lambda: pack_rows(target, fields, 0, SUB))
-        pl.when(jnp.logical_not(low))(
-            lambda: pack_rows(target, fields, rows - SUB, rows - SUB - 1)
-        )
+    for (parts, low) in towards((far_early, far), (near_early, near)):
+        at = 0
+        for part in parts:
+            pl.when(low)(lambda: pack_rows(part, at, fields, 0, SUB))
+            pl.when(jnp.logical_not(low))(
+                lambda: pack_rows(part, at, fields, rows - SUB, rows - SUB - 1)
+            )
+            at += part.shape[0] // SUB
 
 
 def towards(far, near):
@@ -138,17 +134,27 @@
     return ((far, jnp.logical_not(odd)), (near, odd))
 
 
-def pack_rows(target, fields, main, ext):
+def pack_rows(target, at, fields, main, ext):
     tiles = fields.shape[2] // LANES
-    for f in range(4):
-        for t in range(tiles):
+    for i in range(target.shape[0] // SUB):
+        f, t = divmod(at + i, tiles)
+        if f < 4:
             block = fields[f, main : main + SUB, t * LANES : (t + 1) * LANES]
-            target[pl.ds((f * tiles + t) * SUB, SUB)] = block
-    for f in (1, 2):
-        flux = fields[3, ext : ext + 1, :] * fields[f, ext : ext + 1, :]
-        for t in range(tiles):
-            at = (4 * SUB + f - 1) * tiles + t
-            target[at : at + 1] = flux[:, t * LANES : (t + 1) * LANES]
+            target[pl.ds(i * SUB, SUB)] = block
+        elif t == 0:
+            for f in (1, 2):
+                flux = fields[3, ext : ext + 1, :] * fields[f, ext : ext + 1, :]
+                for t in range(tiles):
+                    row = i * SUB + (f - 1) * tiles + t
+                    target[row : row + 1] = flux[:, t * LANES : (t + 1) * LANES]
+
+
+def block_of(parts, at):
+    early, late = parts
+    count = early.shape[0] // SUB
+    if at < count:
+        return early[pl.ds(at * SUB, SUB)]
+    return late[pl.ds((at - count) * SUB, SUB)]
 
 
 def sides_of(first, second, cut):
@@ -158,10 +164,9 @@
     return jnp.where(from_first, first[cut, :], second[cut, :])
 
 
-def pack_sides_kernel(second, first, far_in, far, near_side):
-    (_, far_low), (_, near_low) = towards(None, None)
-    far[pl.ds(far.shape[0] - SUB, SUB)] = pack_sides(second, first, far_low)
-    near_side[...] = pack_sides(second, first, near_low)
+def pack_sides_kernel(second, first, far_in, near_in, far, near):
+    for target, low in towards(far, near):
+        target[pl.ds(target.shape[0] - SUB, SUB)] = pack_sides(second, first, low)
 
 
 def pack_sides(second, first, low):
@@ -351,11 +356,11 @@
     sub = lax.broadcasted_iota(jnp.int32, (SUB, LANES), 0)
     tiles = SUB // 2
     for f in range(4):
-        cut = [halo[pl.ds((f * tiles + t) * SUB, SUB)] for t in range(tiles)]
+        cut = [block_of(halo, f * tiles + t) for t in range(tiles)]
         lay(grid, cut, place(side, f), main * 4 + f, 4)
     line = jnp.broadcast_to(side[0:1], (SUB, LANES))
     side = jnp.where(sub < tiles, place(line, 4), place(line, 5))
-    block = halo[pl.ds(4 * tiles * SUB, SUB)]
+    block = block_of(halo, 4 * tiles)
     up, down = turn(block, SIDE), turn(block, -SIDE)
     before = jnp.where(sub % tiles == 0, side, pltpu.roll(up, 1, 0))
     after = jnp.where(sub % tiles == tiles - 1, side, pltpu.roll(down, SUB - 1, 0))
@@ -464,16 +469,17 @@
         each(m + 1, found)
 
 
-def mid_kernel(near, side, *rest):
+def mid_kernel(near_early, near, *rest):
     grid, coef, *poly = rest[len(rest) // 2 :]
     _, (_, above) = towards(None, None)
+    side = near[pl.ds(near.shape[0] - SUB, SUB)]
     for way, here in ((True, above), (False, jnp.logical_not(above))):
         pl.when(here)(
-            lambda: one_side(near, side[...], way, grid, coef, poly, lambda m, found: None)
+            lambda: one_side((near_early, near), side, way, grid, coef, poly, lambda m, found: None)
         )
 
 
-def outer_kernel(far, sums, *rest):
+def outer_kernel(far_early, far, sums, *rest):
     out, grid, coef, sol, result, *poly = rest[len(rest) // 2 :]
     rows, columns = out.shape[1:]
     lane = lax.broadcasted_iota(jnp.int32, (SUB, LANES), 1)
@@ -497,7 +503,7 @@
                 part = [r for r in part if r not in held]
             add(acc, sums, poly, m, part)
 
-        one_side(far, side, above, grid, coef, poly, each)
+        one_side((far_early, far), side, above, grid, coef, poly, each)
         span = [r for r in whole + edges[:1] if REACH <= r < REACH + rows]
         finish(grid, sums, result, acc, span)
 
@@ -528,49 +534,43 @@
     ]
     hbm = pl.BlockSpec(memory_space=pltpu.HBM)
     message = pltpu.VMEM((rows, LANES), jnp.float32)
-    first, second, scalars = pl.pallas_call(
+    blocks = 4 * columns // LANES + 2
+    parts = (blocks // 2, blocks - blocks // 2, blocks // 2 + 1, blocks - blocks // 2 - 1)
+    fields, first, second, scalars, far_early, far, near_early, near = pl.pallas_call(
         pack_columns_kernel,
-        out_shape=(message, message, pltpu.VMEM((4 * poles, LANES), jnp.float32)),
+        out_shape=(
+            pltpu.VMEM((4, rows, columns), jnp.float32),
+            message,
+            message,
+            pltpu.VMEM((4 * poles, LANES), jnp.float32),
+            *(pltpu.VMEM((part * SUB, LANES), jnp.float32) for part in parts),
+        ),
         in_specs=[hbm] * 5,
-        out_specs=(vmem,) * 3,
+        out_specs=(vmem,) * 8,
         scratch_shapes=[
-            pltpu.VMEM((2, 4, rows, LANES), jnp.float32),
             pltpu.SMEM(pole_real.shape, jnp.float32),
             pltpu.SMEM(pole_imag.shape, jnp.float32),
             pltpu.SMEM(pole_weight.shape, jnp.float32),
-            pltpu.SemaphoreType.DMA((7,)),
+            pltpu.SemaphoreType.DMA((5,)),
         ],
         compiler_params=small,
         name="pack_columns",
     )(*given)
-    count = (4 * SUB + 2) * columns // LANES
-    fields, far, near = pl.pallas_call(
-        load_fields_kernel,
-        out_shape=(
-            pltpu.VMEM((4, rows, columns), jnp.float32),
-            pltpu.VMEM((count + SUB, LANES), jnp.float32),
-            pltpu.VMEM((count, LANES), jnp.float32),
-        ),
-        in_specs=[hbm] * 2,
-        out_specs=(vmem,) * 3,
-        scratch_shapes=[pltpu.SemaphoreType.DMA((2,))],
-        compiler_params=small,
-        name="load_fields",
-    )(*given[:2])
     second = swap(second, "pole", 1)
     first = swap(first, "pole", 0)
-    far, near_side = pl.pallas_call(
+    far, near = pl.pallas_call(
         pack_sides_kernel,
-        out_shape=(f32(*far.shape), f32(SUB, LANES)),
-        in_specs=[vmem] * 3,
+        out_shape=(f32(*far.shape), f32(*near.shape)),
+        in_specs=[vmem] * 4,
         out_specs=(vmem, vmem),
-        input_output_aliases={2: 0},
+        input_output_aliases={2: 0, 3: 1},
         compiler_params=small,
         name="pack_sides",
-    )(second, first, far)
+    )(second, first, far, near)
+    far_early = swap(far_early, "tile", 1)
     far = swap(far, "tile", 1)
+    near_early = swap(near_early, "tile", 0)
     near = swap(near, "tile", 0)
-    near_side = swap(near_side, "tile", 0)
     count = lax.axis_size("pole")
     others = jnp.stack([shift(scalars, "pole", step) for step in range(2, count - 1)])
     height = rows + 2 * REACH
@@ -603,7 +603,7 @@
         compiler_params=small,
         cost_estimate=cost,
         name="mid",
-    )(near, near_side, *held)
+    )(near_early, near, *held)
     grid_held, coef_held, *poly_held = held
     sums, *part = pl.pallas_call(
         pole_sums_kernel,
@@ -617,12 +617,12 @@
     return pl.pallas_call(
         outer_kernel,
         out_shape=(f32(*state.shape), *kept),
-        in_specs=[vmem] * (2 + len(kept)),
+        in_specs=[vmem] * (3 + len(kept)),
         out_specs=(vmem,) * (1 + len(kept)),
-        input_output_aliases={2 + i: 1 + i for i in range(len(kept))},
+        input_output_aliases={3 + i: 1 + i for i in range(len(kept))},
         compiler_params=small,
         name="outer",
-    )(far, sums, grid_held, coef_held, *part, *poly_held)[0]
+    )(far_early, far, sums, grid_held, coef_held, *part, *poly_held)[0]
 
 
 def solution(mesh):

time: 16.8 us -> 16.8 us (level)
  starting transfers between devices: 6.92 us -> 9.86 us
  waiting for transfers between devices: 3.62 us -> 1.56 us
  Pallas kernels: 6.03 us -> 5.24 us
    ppermute x5 -> x6, starting transfers between devices: 6.51 us -> 9.44 us  [swap(): return lax.ppermute(block, axis, pairs(lax.axis_size(axis), phase))]
    ppermute x5 -> x6, waiting for transfers between devices: 2.42 us -> 0.02 us  [swap(): return lax.ppermute(block, axis, pairs(lax.axis_size(axis), phase))]
    pallas_call x3 -> x2, Pallas kernels: 1.93 us -> 1.1 us  [the longest x1 1.08 us: shards(): pl.pallas_call(pack_columns_kernel, out_shape=(pltpu.VMEM((4, rows, colum...]
    ppermute x1, waiting for transfers between devices: 1.2 us -> 1.54 us  [shift(): lax.ppermute(block, axis, [(i, (i + step) % count) for i in range(count)])]
  transfers between devices with their start and end apart: 6 -> 7, of which waited for: 4 -> 1; matrix products, arithmetic and copies ran while one was open for 0% -> 0% of each run, Pallas kernels for 19% -> 14%
where the time goes in v13:
time: 16.8 us; the launch traced here: 16.7 us
  starting transfers between devices  9.86 us (59%)
  Pallas kernels  5.24 us (31%)
  waiting for transfers between devices  1.56 us (9%)
    ppermute x6, starting transfers between devices, swap(): return lax.ppermute(block, axis, pairs(lax.axis_size(axis), phase))  9.44 us
    pallas_call x1, Pallas kernels, shards(): pl.pallas_call(outer_kernel, out_shape=(f32(*state.shape), *kept), in_spe...  1.84 us
    ppermute x1, waiting for transfers between devices, shift(): lax.ppermute(block, axis, [(i, (i + step) % count) for i in range(count)])  1.54 us
    pallas_call x1, Pallas kernels, shards(): pl.pallas_call(pack_columns_kernel, out_shape=(pltpu.VMEM((4, rows, colum...  1.08 us
    pallas_call x1, Pallas kernels, shards(): pl.pallas_call(mid_kernel, out_shape=state_of, in_specs=[vmem] * (2 + len...  0.89 us
    pallas_call x1, Pallas kernels, shards(): pl.pallas_call(inner_kernel, out_shape=state_of, in_specs=[vmem] * 3, out...  0.78 us
    pallas_call x1, Pallas kernels, shards(): pl.pallas_call(pole_sums_kernel, out_shape=(f32(9 * ITERS + 2, SUB, LANES...  0.64 us
    ppermute x1, starting transfers between devices, shift(): lax.ppermute(block, axis, [(i, (i + step) % count) for i in range(count)])  0.42 us
  transfers between devices with their start and end apart: 7, of which 1 were waited for; matrix products, arithmetic and copies ran while one was open for 0% of the time, Pallas kernels for 14%

profile of v13, /device:TPU:0, one launch (start us, length us, event | category | flops | bytes accessed | tf_op | source)
XLA Modules:
  0.0 16.7 jit_solution(7809488246112926710)
XLA Ops:
  0.0 1.1 %pack_columns.1 = (f32[4,16,512]{2,1,0:T(8,128)S(1)}, f32[16,128]{1,0:T(8,128)S(1)}, f32[16,128]{1,0:T(8,128)S(1)}, f32[16,128]{1,0:T(8,128)S(1)}, f32[72,128]{1...) custom-call(f32[3,16,512]{2,1,0:T(8,128)} %state.1, f32[16,512]{1,0:T(8,128)} %depth.1, ...), custom_call_target="tpu_custom_call" | custom-call | tf_op jit(solution)/shard_map/pack_columns/pallas_call | solution.py:539
  1.1 4.0 %collective-permute-start.1 = (f32[16,128]{1,0:T(8,128)S(1)}, f32[16,128]{1,0:T(8,128)S(1)}, u32[]{:S(2)}, u32[]{:S(2)}) collective-permute-start(f32[16,128]{1,0:T(8,128)S(1)} %get-tuple-element.40), channel_id=1, source_target_pairs={{8,16},{16,8},{24,0},{0,24},{9,17},{17,9},{25,1},{1,25},{10,18},{1... | collective-permute-start | bytes 24584 | tf_op jit(solution)/shard_map/ppermute | solution.py:32
  5.0 0.5 %collective-permute-start.2 = (f32[16,128]{1,0:T(8,128)S(1)}, f32[16,128]{1,0:T(8,128)S(1)}, u32[]{:S(2)}, u32[]{:S(2)}) collective-permute-start(f32[16,128]{1,0:T(8,128)S(1)} %get-tuple-element.41), channel_id=1, source_target_pairs={{0,8},{8,0},{16,24},{24,16},{1,9},{9,1},{17,25},{25,17},{2,10},{10... | collective-permute-start | bytes 24584 | tf_op jit(solution)/shard_map/ppermute | solution.py:32
  5.6 0.0 collective-permute-start.5
  5.6 3.7 %collective-permute-start = (f32[72,128]{1,0:T(8,128)S(1)}, f32[72,128]{1,0:T(8,128)S(1)}, u32[]{:S(2)}, u32[]{:S(2)}) collective-permute-start(f32[72,128]{1,0:T(8,128)S(1)} %get-tuple-element.39), channel_id=1, source_target_pairs={{1,2},{2,1},{3,4},{4,3},{5,6},{6,5},{7,0},{0,7},{9,10},{10,9},{11,... | collective-permute-start | bytes 110600 | tf_op jit(solution)/shard_map/ppermute | solution.py:32
  9.3 0.0 collective-permute-done.1.second
  9.3 0.0 collective-permute-done.2.first
  9.3 1.2 %collective-permute-start.3 = (f32[72,128]{1,0:T(8,128)S(1)}, f32[72,128]{1,0:T(8,128)S(1)}, u32[]{:S(2)}, u32[]{:S(2)}) collective-permute-start(f32[72,128]{1,0:T(8,128)S(1)} %get-tuple-element.44), channel_id=1, source_target_pairs={{1,2},{2,1},{3,4},{4,3},{5,6},{6,5},{7,0},{0,7},{9,10},{10,9},{11,... | collective-permute-start | bytes 110600 | tf_op jit(solution)/shard_map/ppermute | solution.py:32
  10.6 0.0 collective-permute-start.6
  10.6 0.4 %collective-permute-start.4 = (f32[16,128]{1,0:T(8,128)S(1)}, f32[16,128]{1,0:T(8,128)S(1)}, u32[]{:S(2)}, u32[]{:S(2)}) collective-permute-start(f32[16,128]{1,0:T(8,128)S(1)} %get-tuple-element.45.scalars), channel_id=1, source_target_pairs={{0,16},{8,24},{16,0},{24,8},{1,17},{9,25},{17,1},{25,9},{2,18},{10... | collective-permute-start | bytes 24584 | tf_op jit(solution)/shard_map/ppermute | solution.py:37
  11.0 0.8 %inner.1 = (f32[1088,128]{1,0:T(8,128)S(1)}, f32[4,34,8,128]{3,2,1,0:T(8,128)S(1)}, f32[3,34,8,128]{3,2,1,0:T(8,128)S(1)}, f32[3,34,8,128]{3,2,1,0:T(8,128)S(1)}...) custom-call(f32[4,16,512]{2,1,0:T(8,128)S(1)} %get-tuple-element.48., ...), custom_call_target="tpu_custom_call" | custom-call | flops 1310720 | bytes 1441792 | tf_op jit(solution)/shard_map/inner/pallas_call | solution.py:588
  11.8 0.0 collective-permute-done.6.near
  11.8 0.0 collective-permute-done.5.near_early
  11.8 0.9 %mid.1 = (f32[1088,128]{1,0:T(8,128)S(1)}, f32[4,34,8,128]{3,2,1,0:T(8,128)S(1)}, f32[3,34,8,128]{3,2,1,0:T(8,128)S(1)}, f32[3,34,8,128]{3,2,1,0:T(8,128)S(1)}, ...) custom-call(f32[80,128]{1,0:T(8,128)S(1)} %collective-permute-done.5, ...), custom_call_target="tpu_custom_call", output_to_operand_aliasing={{0}: (2, {}), {1}: (3, {}), {2}: (4, {}), {3}: (5, {}), {4}... | custom-call | flops 1310720 | bytes 1441792 | tf_op jit(solution)/shard_map/mid/pallas_call | solution.py:597
  12.7 1.5 %collective-permute-done.4 = f32[16,128]{1,0:T(8,128)S(1)} collective-permute-done((f32[16,128]{1,0:T(8,128)S(1)}, f32[16,128]{1,0:T(8,128)S(1)}, u32[]{:S(2)}, u32[]{:S(2)}) %collective-permute-start.4) | collective-permute-done | bytes 8224 | tf_op jit(solution)/shard_map/ppermute | solution.py:37
  14.2 0.6 %pole_sums.1 = (f32[74,8,128]{2,1,0:T(8,128)S(1)}, f32[3,18,8,128]{3,2,1,0:T(8,128)S(1)}, f32[3,128,128]{2,1,0:T(8,128)S(1)}) custom-call(f32[16,128]{1,0:T(8,128)S(1)} %get-tuple-element.45.scalars, f32[16,128]{1,0:T(8,128)S(1)} %collective-permute-done.2.first, f32[16,128]{1,0:T(8,128)S(1)} %collective-permute-done.1.second, f32[1,16,128]{2,1,0:T(8,128)S(1)} %bitcast.1, ...), custom_call_target="tpu_custom_call" | custom-call | tf_op jit(solution)/shard_map/pole_sums/pallas_call | solution.py:608
  14.9 0.0 collective-permute-done.far_early
  14.9 0.0 collective-permute-done.3.far
  14.9 1.8 %outer.1 = (f32[3,16,512]{2,1,0:T(8,128)}, f32[1088,128]{1,0:T(8,128)S(1)}, f32[4,34,8,128]{3,2,1,0:T(8,128)S(1)}, f32[3,18,8,128]{3,2,1,0:T(8,128)S(1)}, f32[3,...) custom-call(f32[72,128]{1,0:T(8,128)S(1)} %collective-permute-done.f, ...), custom_call_target="tpu_custom_call", output_to_operand_aliasing={{1}: (3, {}), {2}: (4, {}), {3}: (5, {}), {4}: (6, {}), {5}... | custom-call | tf_op jit(solution)/shard_map/outer/pallas_call | solution.py:617
  (1 shorter events, 0.0 us)
Async XLA Ops:
  1.1 8.2 %collective-permute-start.1 = (f32[16,128]{1,0:T(8,128)S(1)}, f32[16,128]{1,0:T(8,128)S(1)}, u32[]{:S(2)}, u32[]{:S(2)}) collective-permute-start(f32[16,128]{1,0:T(8,128)S(1)} %get-tuple-element.40), channel_id=1, source_target_pairs={{8,16},{16,8},{24,0},{0,24},{9,17},{17,9},{25,1},{1,25},{10,18},{1... | collective-permute-start | bytes 24584 | tf_op jit(solution)/shard_map/ppermute | solution.py:32
  5.0 4.3 %collective-permute-start.2 = (f32[16,128]{1,0:T(8,128)S(1)}, f32[16,128]{1,0:T(8,128)S(1)}, u32[]{:S(2)}, u32[]{:S(2)}) collective-permute-start(f32[16,128]{1,0:T(8,128)S(1)} %get-tuple-element.41), channel_id=1, source_target_pairs={{0,8},{8,0},{16,24},{24,16},{1,9},{9,1},{17,25},{25,17},{2,10},{10... | collective-permute-start | bytes 24584 | tf_op jit(solution)/shard_map/ppermute | solution.py:32
  5.6 6.2 %collective-permute-start.5 = (f32[80,128]{1,0:T(8,128)S(1)}, f32[80,128]{1,0:T(8,128)S(1)}, u32[]{:S(2)}, u32[]{:S(2)}) collective-permute-start(f32[80,128]{1,0:T(8,128)S(1)} %get-tuple-element.46), channel_id=1, source_target_pairs={{0,1},{1,0},{2,3},{3,2},{4,5},{5,4},{6,7},{7,6},{8,9},{9,8},{10,11... | collective-permute-start | bytes 122888 | tf_op jit(solution)/shard_map/ppermute | solution.py:32
  5.6 9.3 %collective-permute-start = (f32[72,128]{1,0:T(8,128)S(1)}, f32[72,128]{1,0:T(8,128)S(1)}, u32[]{:S(2)}, u32[]{:S(2)}) collective-permute-start(f32[72,128]{1,0:T(8,128)S(1)} %get-tuple-element.39), channel_id=1, source_target_pairs={{1,2},{2,1},{3,4},{4,3},{5,6},{6,5},{7,0},{0,7},{9,10},{10,9},{11,... | collective-permute-start | bytes 110600 | tf_op jit(solution)/shard_map/ppermute | solution.py:32
  9.3 5.5 %collective-permute-start.3 = (f32[72,128]{1,0:T(8,128)S(1)}, f32[72,128]{1,0:T(8,128)S(1)}, u32[]{:S(2)}, u32[]{:S(2)}) collective-permute-start(f32[72,128]{1,0:T(8,128)S(1)} %get-tuple-element.44), channel_id=1, source_target_pairs={{1,2},{2,1},{3,4},{4,3},{5,6},{6,5},{7,0},{0,7},{9,10},{10,9},{11,... | collective-permute-start | bytes 110600 | tf_op jit(solution)/shard_map/ppermute | solution.py:32
  10.6 1.2 %collective-permute-start.6 = (f32[64,128]{1,0:T(8,128)S(1)}, f32[64,128]{1,0:T(8,128)S(1)}, u32[]{:S(2)}, u32[]{:S(2)}) collective-permute-start(f32[64,128]{1,0:T(8,128)S(1)} %get-tuple-element.47), channel_id=1, source_target_pairs={{0,1},{1,0},{2,3},{3,2},{4,5},{5,4},{6,7},{7,6},{8,9},{9,8},{10,11... | collective-permute-start | bytes 98312 | tf_op jit(solution)/shard_map/ppermute | solution.py:32
  10.6 3.7 %collective-permute-start.4 = (f32[16,128]{1,0:T(8,128)S(1)}, f32[16,128]{1,0:T(8,128)S(1)}, u32[]{:S(2)}, u32[]{:S(2)}) collective-permute-start(f32[16,128]{1,0:T(8,128)S(1)} %get-tuple-element.45.scalars), channel_id=1, source_target_pairs={{0,16},{8,24},{16,0},{24,8},{1,17},{9,25},{17,1},{25,9},{2,18},{10... | collective-permute-start | bytes 24584 | tf_op jit(solution)/shard_map/ppermute | solution.py:37

commit v14 on v13

--- a/solution.py
+++ b/solution.py
@@ -1,3 +1,5 @@
+import functools
+
 import jax
 import jax.numpy as jnp
 from jax import lax
@@ -102,6 +104,8 @@
             block = jnp.where(sub == i, values[g * SUB + i], block)
         scalars[pl.ds(g * SUB, SUB)] = block
         spread.append(block)
+    for g in range(len(spread), scalars.shape[0] // SUB):
+        scalars[pl.ds(g * SUB, SUB)] = jnp.zeros((SUB, LANES), jnp.float32)
     for g in range(rows // SUB):
         cut = pl.ds(g * SUB, SUB)
         rest = spread[g] if g < len(spread) else jnp.zeros((SUB, LANES), jnp.float32)
@@ -193,10 +197,9 @@
     return side
 
 
-def pole_sums_kernel(scalars, first, second, others, grid, *rest):
+def pole_sums_kernel(count, scalars, first, second, others, grid, *rest):
     poly, (sums, sol, result) = rest[:ITERS], rest[ITERS:]
     odd = lax.rem(lax.axis_index("pole"), 2) == 1
-    count = scalars.shape[0]
     lane = lax.broadcasted_iota(jnp.int32, (SUB, LANES), 1)
     blocks = [[scalars[pl.ds(g, SUB)] for g in range(0, count, SUB)]]
     for i, message in enumerate((first, second)):
@@ -536,13 +539,14 @@
     message = pltpu.VMEM((rows, LANES), jnp.float32)
     blocks = 4 * columns // LANES + 2
     parts = (blocks // 2, blocks - blocks // 2, blocks // 2 + 1, blocks - blocks // 2 - 1)
+    wide = max(4 * poles, (blocks // 2 + 0) * SUB)
     fields, first, second, scalars, far_early, far, near_early, near = pl.pallas_call(
         pack_columns_kernel,
         out_shape=(
             pltpu.VMEM((4, rows, columns), jnp.float32),
             message,
             message,
-            pltpu.VMEM((4 * poles, LANES), jnp.float32),
+            pltpu.VMEM((wide, LANES), jnp.float32),
             *(pltpu.VMEM((part * SUB, LANES), jnp.float32) for part in parts),
         ),
         in_specs=[hbm] * 5,
@@ -606,7 +610,7 @@
     )(near_early, near, *held)
     grid_held, coef_held, *poly_held = held
     sums, *part = pl.pallas_call(
-        pole_sums_kernel,
+        functools.partial(pole_sums_kernel, 4 * poles),
         out_shape=(f32(9 * ITERS + 2, SUB, LANES), sol, result),
         in_specs=[vmem] * (5 + ITERS),
         out_specs=(vmem,) * 3,

time: 16.8 us -> 16.8 us (level)
  starting transfers between devices: 9.86 us -> 9.44 us
  waiting for transfers between devices: 1.56 us -> 1.94 us
    ppermute x6, waiting for transfers between devices: 0.02 us -> 1.93 us  [swap(): return lax.ppermute(block, axis, pairs(lax.axis_size(axis), phase))]
    ppermute x1, waiting for transfers between devices: 1.54 us -> 0.01 us  [shift(): lax.ppermute(block, axis, [(i, (i + step) % count) for i in range(count)])]
    ppermute x1, starting transfers between devices: 0.42 us -> 0.11 us  [shift(): lax.ppermute(block, axis, [(i, (i + step) % count) for i in range(count)])]
  transfers between devices with their start and end apart: 7 -> 7, of which waited for: 1 -> 2; matrix products, arithmetic and copies ran while one was open for 0% -> 0% of each run, Pallas kernels for 14% -> 14%
where the time goes in v14:
time: 16.8 us; the launch traced here: 16.6 us
  starting transfers between devices  9.44 us (56%)
  Pallas kernels  5.21 us (31%)
  waiting for transfers between devices  1.94 us (12%)
    ppermute x6, starting transfers between devices, swap(): return lax.ppermute(block, axis, pairs(lax.axis_size(axis), phase))  9.33 us
    ppermute x6, waiting for transfers between devices, swap(): return lax.ppermute(block, axis, pairs(lax.axis_size(axis), phase))  1.93 us
    pallas_call x1, Pallas kernels, shards(): pl.pallas_call(outer_kernel, out_shape=(f32(*state.shape), *kept), in_spe...  1.82 us
    pallas_call x1, Pallas kernels, shards(): pl.pallas_call(pack_columns_kernel, out_shape=(pltpu.VMEM((4, rows, colum...  1.08 us
    pallas_call x1, Pallas kernels, shards(): pl.pallas_call(mid_kernel, out_shape=state_of, in_specs=[vmem] * (2 + len...  0.87 us
    pallas_call x1, Pallas kernels, shards(): pl.pallas_call(inner_kernel, out_shape=state_of, in_specs=[vmem] * 3, out...  0.78 us
    pallas_call x1, Pallas kernels, shards(): pl.pallas_call(functools.partial(pole_sums_kernel, 4 * poles), out_shape=...  0.65 us
  transfers between devices with their start and end apart: 7, of which 2 were waited for; matrix products, arithmetic and copies ran while one was open for 0% of the time, Pallas kernels for 14%

profile of v14, /device:TPU:0, one launch (start us, length us, event | category | flops | bytes accessed | tf_op | source)
XLA Modules:
  0.0 16.6 jit_solution(3970429248620038521)
XLA Ops:
  0.0 1.1 %pack_columns.1 = (f32[4,16,512]{2,1,0:T(8,128)S(1)}, f32[16,128]{1,0:T(8,128)S(1)}, f32[16,128]{1,0:T(8,128)S(1)}, f32[72,128]{1,0:T(8,128)S(1)}, f32[72,128]{1...) custom-call(f32[3,16,512]{2,1,0:T(8,128)} %state.1, f32[16,512]{1,0:T(8,128)} %depth.1, ...), custom_call_target="tpu_custom_call" | custom-call | tf_op jit(solution)/shard_map/pack_columns/pallas_call | solution.py:543
  1.1 4.0 %collective-permute-start.1 = (f32[16,128]{1,0:T(8,128)S(1)}, f32[16,128]{1,0:T(8,128)S(1)}, u32[]{:S(2)}, u32[]{:S(2)}) collective-permute-start(f32[16,128]{1,0:T(8,128)S(1)} %get-tuple-element.40), channel_id=1, source_target_pairs={{8,16},{16,8},{24,0},{0,24},{9,17},{17,9},{25,1},{1,25},{10,18},{1... | collective-permute-start | bytes 24584 | tf_op jit(solution)/shard_map/ppermute | solution.py:34
  5.0 0.5 %collective-permute-start.2 = (f32[16,128]{1,0:T(8,128)S(1)}, f32[16,128]{1,0:T(8,128)S(1)}, u32[]{:S(2)}, u32[]{:S(2)}) collective-permute-start(f32[16,128]{1,0:T(8,128)S(1)} %get-tuple-element.41), channel_id=1, source_target_pairs={{0,8},{8,0},{16,24},{24,16},{1,9},{9,1},{17,25},{25,17},{2,10},{10... | collective-permute-start | bytes 24584 | tf_op jit(solution)/shard_map/ppermute | solution.py:34
  5.6 0.0 collective-permute-start.5
  5.6 0.1 collective-permute-start.4
  5.7 3.8 %collective-permute-start = (f32[72,128]{1,0:T(8,128)S(1)}, f32[72,128]{1,0:T(8,128)S(1)}, u32[]{:S(2)}, u32[]{:S(2)}) collective-permute-start(f32[72,128]{1,0:T(8,128)S(1)} %get-tuple-element.39), channel_id=1, source_target_pairs={{1,2},{2,1},{3,4},{4,3},{5,6},{6,5},{7,0},{0,7},{9,10},{10,9},{11,... | collective-permute-start | bytes 110600 | tf_op jit(solution)/shard_map/ppermute | solution.py:34
  9.5 0.0 collective-permute-done.1.second
  9.5 0.0 collective-permute-done.2.first
  9.6 1.0 %collective-permute-start.3 = (f32[72,128]{1,0:T(8,128)S(1)}, f32[72,128]{1,0:T(8,128)S(1)}, u32[]{:S(2)}, u32[]{:S(2)}) collective-permute-start(f32[72,128]{1,0:T(8,128)S(1)} %get-tuple-element.44), channel_id=1, source_target_pairs={{1,2},{2,1},{3,4},{4,3},{5,6},{6,5},{7,0},{0,7},{9,10},{10,9},{11,... | collective-permute-start | bytes 110600 | tf_op jit(solution)/shard_map/ppermute | solution.py:34
  10.6 0.0 collective-permute-start.6
  10.6 0.8 %inner.1 = (f32[1088,128]{1,0:T(8,128)S(1)}, f32[4,34,8,128]{3,2,1,0:T(8,128)S(1)}, f32[3,34,8,128]{3,2,1,0:T(8,128)S(1)}, f32[3,34,8,128]{3,2,1,0:T(8,128)S(1)}...) custom-call(f32[4,16,512]{2,1,0:T(8,128)S(1)} %get-tuple-element.48., ...), custom_call_target="tpu_custom_call" | custom-call | flops 1310720 | bytes 1441792 | tf_op jit(solution)/shard_map/inner/pallas_call | solution.py:592
  11.3 0.4 %collective-permute-done.6.near = f32[64,128]{1,0:T(8,128)S(1)} collective-permute-done((f32[64,128]{1,0:T(8,128)S(1)}, f32[64,128]{1,0:T(8,128)S(1)}, u32[]{:S(2)}, u32[]{:S(2)}) %collective-permute-start.6) | collective-permute-done | bytes 32800 | tf_op jit(solution)/shard_map/ppermute | solution.py:34
  11.8 0.0 collective-permute-done.5.near_early
  11.8 0.9 %mid.1 = (f32[1088,128]{1,0:T(8,128)S(1)}, f32[4,34,8,128]{3,2,1,0:T(8,128)S(1)}, f32[3,34,8,128]{3,2,1,0:T(8,128)S(1)}, f32[3,34,8,128]{3,2,1,0:T(8,128)S(1)}, ...) custom-call(f32[80,128]{1,0:T(8,128)S(1)} %collective-permute-done.5, ...), custom_call_target="tpu_custom_call", output_to_operand_aliasing={{0}: (2, {}), {1}: (3, {}), {2}: (4, {}), {3}: (5, {}), {4}... | custom-call | flops 1310720 | bytes 1441792 | tf_op jit(solution)/shard_map/mid/pallas_call | solution.py:601
  12.6 0.0 collective-permute-done.4
  12.6 0.6 %pole_sums.1 = (f32[74,8,128]{2,1,0:T(8,128)S(1)}, f32[3,18,8,128]{3,2,1,0:T(8,128)S(1)}, f32[3,128,128]{2,1,0:T(8,128)S(1)}) custom-call(f32[72,128]{1,0:T(8,128)S(1)} %get-tuple-element.45.scalars, f32[16,128]{1,0:T(8,128)S(1)} %collective-permute-done.2.first, f32[16,128]{1,0:T(8,128)S(1)} %collective-permute-done.1.second, f32[1,72,128]{2,1,0:T(8,128)S(1)} %bitcast.1, ...), custom_call_target="tpu_custom_call" | custom-call | tf_op jit(solution)/shard_map/pole_sums/pallas_call | solution.py:612
  13.3 0.0 collective-permute-done.far_early
  13.3 1.5 %collective-permute-done.3.far = f32[72,128]{1,0:T(8,128)S(1)} collective-permute-done((f32[72,128]{1,0:T(8,128)S(1)}, f32[72,128]{1,0:T(8,128)S(1)}, u32[]{:S(2)}, u32[]{:S(2)}) %collective-permute-start.3) | collective-permute-done | bytes 36896 | tf_op jit(solution)/shard_map/ppermute | solution.py:34
  14.8 1.8 %outer.1 = (f32[3,16,512]{2,1,0:T(8,128)}, f32[1088,128]{1,0:T(8,128)S(1)}, f32[4,34,8,128]{3,2,1,0:T(8,128)S(1)}, f32[3,18,8,128]{3,2,1,0:T(8,128)S(1)}, f32[3,...) custom-call(f32[72,128]{1,0:T(8,128)S(1)} %collective-permute-done.f, ...), custom_call_target="tpu_custom_call", output_to_operand_aliasing={{1}: (3, {}), {2}: (4, {}), {3}: (5, {}), {4}: (6, {}), {5}... | custom-call | tf_op jit(solution)/shard_map/outer/pallas_call | solution.py:621
  (1 shorter events, 0.0 us)
Async XLA Ops:
  1.1 8.4 %collective-permute-start.1 = (f32[16,128]{1,0:T(8,128)S(1)}, f32[16,128]{1,0:T(8,128)S(1)}, u32[]{:S(2)}, u32[]{:S(2)}) collective-permute-start(f32[16,128]{1,0:T(8,128)S(1)} %get-tuple-element.40), channel_id=1, source_target_pairs={{8,16},{16,8},{24,0},{0,24},{9,17},{17,9},{25,1},{1,25},{10,18},{1... | collective-permute-start | bytes 24584 | tf_op jit(solution)/shard_map/ppermute | solution.py:34
  5.0 4.5 %collective-permute-start.2 = (f32[16,128]{1,0:T(8,128)S(1)}, f32[16,128]{1,0:T(8,128)S(1)}, u32[]{:S(2)}, u32[]{:S(2)}) collective-permute-start(f32[16,128]{1,0:T(8,128)S(1)} %get-tuple-element.41), channel_id=1, source_target_pairs={{0,8},{8,0},{16,24},{24,16},{1,9},{9,1},{17,25},{25,17},{2,10},{10... | collective-permute-start | bytes 24584 | tf_op jit(solution)/shard_map/ppermute | solution.py:34
  5.6 6.2 %collective-permute-start.5 = (f32[80,128]{1,0:T(8,128)S(1)}, f32[80,128]{1,0:T(8,128)S(1)}, u32[]{:S(2)}, u32[]{:S(2)}) collective-permute-start(f32[80,128]{1,0:T(8,128)S(1)} %get-tuple-element.46), channel_id=1, source_target_pairs={{0,1},{1,0},{2,3},{3,2},{4,5},{5,4},{6,7},{7,6},{8,9},{9,8},{10,11... | collective-permute-start | bytes 122888 | tf_op jit(solution)/shard_map/ppermute | solution.py:34
  5.6 7.1 %collective-permute-start.4 = (f32[72,128]{1,0:T(8,128)S(1)}, f32[72,128]{1,0:T(8,128)S(1)}, u32[]{:S(2)}, u32[]{:S(2)}) collective-permute-start(f32[72,128]{1,0:T(8,128)S(1)} %get-tuple-element.45.scalars), channel_id=1, source_target_pairs={{0,16},{8,24},{16,0},{24,8},{1,17},{9,25},{17,1},{25,9},{2,18},{10... | collective-permute-start | bytes 110600 | tf_op jit(solution)/shard_map/ppermute | solution.py:39
  5.7 7.6 %collective-permute-start = (f32[72,128]{1,0:T(8,128)S(1)}, f32[72,128]{1,0:T(8,128)S(1)}, u32[]{:S(2)}, u32[]{:S(2)}) collective-permute-start(f32[72,128]{1,0:T(8,128)S(1)} %get-tuple-element.39), channel_id=1, source_target_pairs={{1,2},{2,1},{3,4},{4,3},{5,6},{6,5},{7,0},{0,7},{9,10},{10,9},{11,... | collective-permute-start | bytes 110600 | tf_op jit(solution)/shard_map/ppermute | solution.py:34
  9.6 5.2 %collective-permute-start.3 = (f32[72,128]{1,0:T(8,128)S(1)}, f32[72,128]{1,0:T(8,128)S(1)}, u32[]{:S(2)}, u32[]{:S(2)}) collective-permute-start(f32[72,128]{1,0:T(8,128)S(1)} %get-tuple-element.44), channel_id=1, source_target_pairs={{1,2},{2,1},{3,4},{4,3},{5,6},{6,5},{7,0},{0,7},{9,10},{10,9},{11,... | collective-permute-start | bytes 110600 | tf_op jit(solution)/shard_map/ppermute | solution.py:34
  10.6 1.2 %collective-permute-start.6 = (f32[64,128]{1,0:T(8,128)S(1)}, f32[64,128]{1,0:T(8,128)S(1)}, u32[]{:S(2)}, u32[]{:S(2)}) collective-permute-start(f32[64,128]{1,0:T(8,128)S(1)} %get-tuple-element.47), channel_id=1, source_target_pairs={{0,1},{1,0},{2,3},{3,2},{4,5},{5,4},{6,7},{7,6},{8,9},{9,8},{10,11... | collective-permute-start | bytes 98312 | tf_op jit(solution)/shard_map/ppermute | solution.py:34

commit v15 on v14

--- a/solution.py
+++ b/solution.py
@@ -538,8 +538,9 @@
     hbm = pl.BlockSpec(memory_space=pltpu.HBM)
     message = pltpu.VMEM((rows, LANES), jnp.float32)
     blocks = 4 * columns // LANES + 2
-    parts = (blocks // 2, blocks - blocks // 2, blocks // 2 + 1, blocks - blocks // 2 - 1)
-    wide = max(4 * poles, (blocks // 2 + 0) * SUB)
+    half = blocks // 2 * SUB
+    parts = (half + SUB + 4, half, half + SUB, half - SUB)
+    wide = max(4 * poles, half)
     fields, first, second, scalars, far_early, far, near_early, near = pl.pallas_call(
         pack_columns_kernel,
         out_shape=(
@@ -547,7 +548,7 @@
             message,
             message,
             pltpu.VMEM((wide, LANES), jnp.float32),
-            *(pltpu.VMEM((part * SUB, LANES), jnp.float32) for part in parts),
+            *(pltpu.VMEM((part, LANES), jnp.float32) for part in parts),
         ),
         in_specs=[hbm] * 5,
         out_specs=(vmem,) * 8,

time: 16.8 us -> 16 us (0.952)
  waiting for transfers between devices: 1.94 us -> 1.33 us
    ppermute x6, waiting for transfers between devices: 1.93 us -> 1.33 us  [swap(): return lax.ppermute(block, axis, pairs(lax.axis_size(axis), phase))]
    ppermute x6, starting transfers between devices: 9.33 us -> 8.83 us  [swap(): return lax.ppermute(block, axis, pairs(lax.axis_size(axis), phase))]
    ppermute x1, starting transfers between devices: 0.11 us -> 0.51 us  [shift(): lax.ppermute(block, axis, [(i, (i + step) % count) for i in range(count)])]
  transfers between devices with their start and end apart: 7 -> 7, of which waited for: 2 -> 3; matrix products, arithmetic and copies ran while one was open for 0% -> 0% of each run, Pallas kernels for 14% -> 15%
where the time goes in v15:
time: 16 us; the launch traced here: 15.9 us
  starting transfers between devices  9.33 us (58%)
  Pallas kernels  5.22 us (33%)
  waiting for transfers between devices  1.33 us (8%)
    ppermute x6, starting transfers between devices, swap(): return lax.ppermute(block, axis, pairs(lax.axis_size(axis), phase))  8.83 us
    pallas_call x1, Pallas kernels, shards(): pl.pallas_call(outer_kernel, out_shape=(f32(*state.shape), *kept), in_spe...  1.82 us
    ppermute x6, waiting for transfers between devices, swap(): return lax.ppermute(block, axis, pairs(lax.axis_size(axis), phase))  1.33 us
    pallas_call x1, Pallas kernels, shards(): pl.pallas_call(pack_columns_kernel, out_shape=(pltpu.VMEM((4, rows, colum...  1.08 us
    pallas_call x1, Pallas kernels, shards(): pl.pallas_call(mid_kernel, out_shape=state_of, in_specs=[vmem] * (2 + len...  0.87 us
    pallas_call x1, Pallas kernels, shards(): pl.pallas_call(inner_kernel, out_shape=state_of, in_specs=[vmem] * 3, out...  0.78 us
    pallas_call x1, Pallas kernels, shards(): pl.pallas_call(functools.partial(pole_sums_kernel, 4 * poles), out_shape=...  0.65 us
    ppermute x1, starting transfers between devices, shift(): lax.ppermute(block, axis, [(i, (i + step) % count) for i in range(count)])  0.51 us
  transfers between devices with their start and end apart: 7, of which 3 were waited for; matrix products, arithmetic and copies ran while one was open for 0% of the time, Pallas kernels for 15%

profile of v15, /device:TPU:0, one launch (start us, length us, event | category | flops | bytes accessed | tf_op | source)
XLA Modules:
  0.0 15.9 jit_solution(14346558436250854379)
XLA Ops:
  0.0 1.1 %pack_columns.1 = (f32[4,16,512]{2,1,0:T(8,128)S(1)}, f32[16,128]{1,0:T(8,128)S(1)}, f32[16,128]{1,0:T(8,128)S(1)}, f32[72,128]{1,0:T(8,128)S(1)}, f32[84,128]{1...) custom-call(f32[3,16,512]{2,1,0:T(8,128)} %state.1, f32[16,512]{1,0:T(8,128)} %depth.1, ...), custom_call_target="tpu_custom_call" | custom-call | tf_op jit(solution)/shard_map/pack_columns/pallas_call | solution.py:544
  1.1 4.0 %collective-permute-start.1 = (f32[16,128]{1,0:T(8,128)S(1)}, f32[16,128]{1,0:T(8,128)S(1)}, u32[]{:S(2)}, u32[]{:S(2)}) collective-permute-start(f32[16,128]{1,0:T(8,128)S(1)} %get-tuple-element.40), channel_id=1, source_target_pairs={{8,16},{16,8},{24,0},{0,24},{9,17},{17,9},{25,1},{1,25},{10,18},{1... | collective-permute-start | bytes 24584 | tf_op jit(solution)/shard_map/ppermute | solution.py:34
  5.0 0.5 %collective-permute-start.2 = (f32[16,128]{1,0:T(8,128)S(1)}, f32[16,128]{1,0:T(8,128)S(1)}, u32[]{:S(2)}, u32[]{:S(2)}) collective-permute-start(f32[16,128]{1,0:T(8,128)S(1)} %get-tuple-element.41), channel_id=1, source_target_pairs={{0,8},{8,0},{16,24},{24,16},{1,9},{9,1},{17,25},{25,17},{2,10},{10... | collective-permute-start | bytes 24584 | tf_op jit(solution)/shard_map/ppermute | solution.py:34
  5.6 2.5 %collective-permute-start = (f32[84,128]{1,0:T(8,128)S(1)}, f32[84,128]{1,0:T(8,128)S(1)}, u32[]{:S(2)}, u32[]{:S(2)}) collective-permute-start(f32[84,128]{1,0:T(8,128)S(1)} %get-tuple-element.39), channel_id=1, source_target_pairs={{1,2},{2,1},{3,4},{4,3},{5,6},{6,5},{7,0},{0,7},{9,10},{10,9},{11,... | collective-permute-start | bytes 129032 | tf_op jit(solution)/shard_map/ppermute | solution.py:34
  8.1 0.0 collective-permute-start.5
  8.1 0.5 %collective-permute-start.4 = (f32[72,128]{1,0:T(8,128)S(1)}, f32[72,128]{1,0:T(8,128)S(1)}, u32[]{:S(2)}, u32[]{:S(2)}) collective-permute-start(f32[72,128]{1,0:T(8,128)S(1)} %get-tuple-element.45.scalars), channel_id=1, source_target_pairs={{0,16},{8,24},{16,0},{24,8},{1,17},{9,25},{17,1},{25,9},{2,18},{10... | collective-permute-start | bytes 110600 | tf_op jit(solution)/shard_map/ppermute | solution.py:39
  8.6 0.0 collective-permute-done.1.second
  8.6 0.1 collective-permute-done.2.first
  8.7 1.8 %collective-permute-start.3 = (f32[72,128]{1,0:T(8,128)S(1)}, f32[72,128]{1,0:T(8,128)S(1)}, u32[]{:S(2)}, u32[]{:S(2)}) collective-permute-start(f32[72,128]{1,0:T(8,128)S(1)} %get-tuple-element.44), channel_id=1, source_target_pairs={{1,2},{2,1},{3,4},{4,3},{5,6},{6,5},{7,0},{0,7},{9,10},{10,9},{11,... | collective-permute-start | bytes 110600 | tf_op jit(solution)/shard_map/ppermute | solution.py:34
  10.6 0.0 collective-permute-start.6
  10.6 0.8 %inner.1 = (f32[1088,128]{1,0:T(8,128)S(1)}, f32[4,34,8,128]{3,2,1,0:T(8,128)S(1)}, f32[3,34,8,128]{3,2,1,0:T(8,128)S(1)}, f32[3,34,8,128]{3,2,1,0:T(8,128)S(1)}...) custom-call(f32[4,16,512]{2,1,0:T(8,128)S(1)} %get-tuple-element.48., ...), custom_call_target="tpu_custom_call" | custom-call | flops 1310720 | bytes 1441792 | tf_op jit(solution)/shard_map/inner/pallas_call | solution.py:593
  11.3 0.4 %collective-permute-done.6.near = f32[64,128]{1,0:T(8,128)S(1)} collective-permute-done((f32[64,128]{1,0:T(8,128)S(1)}, f32[64,128]{1,0:T(8,128)S(1)}, u32[]{:S(2)}, u32[]{:S(2)}) %collective-permute-start.6) | collective-permute-done | bytes 32800 | tf_op jit(solution)/shard_map/ppermute | solution.py:34
  11.8 0.0 collective-permute-done.5.near_early
  11.8 0.9 %mid.1 = (f32[1088,128]{1,0:T(8,128)S(1)}, f32[4,34,8,128]{3,2,1,0:T(8,128)S(1)}, f32[3,34,8,128]{3,2,1,0:T(8,128)S(1)}, f32[3,34,8,128]{3,2,1,0:T(8,128)S(1)}, ...) custom-call(f32[80,128]{1,0:T(8,128)S(1)} %collective-permute-done.5, ...), custom_call_target="tpu_custom_call", output_to_operand_aliasing={{0}: (2, {}), {1}: (3, {}), {2}: (4, {}), {3}: (5, {}), {4}... | custom-call | flops 1310720 | bytes 1441792 | tf_op jit(solution)/shard_map/mid/pallas_call | solution.py:602
  12.6 0.0 collective-permute-done.4
  12.6 0.7 %pole_sums.1 = (f32[74,8,128]{2,1,0:T(8,128)S(1)}, f32[3,18,8,128]{3,2,1,0:T(8,128)S(1)}, f32[3,128,128]{2,1,0:T(8,128)S(1)}) custom-call(f32[72,128]{1,0:T(8,128)S(1)} %get-tuple-element.45.scalars, f32[16,128]{1,0:T(8,128)S(1)} %collective-permute-done.2.first, f32[16,128]{1,0:T(8,128)S(1)} %collective-permute-done.1.second, f32[1,72,128]{2,1,0:T(8,128)S(1)} %bitcast.1, ...), custom_call_target="tpu_custom_call" | custom-call | tf_op jit(solution)/shard_map/pole_sums/pallas_call | solution.py:613
  13.3 0.0 collective-permute-done.far_early
  13.3 0.8 %collective-permute-done.3.far = f32[72,128]{1,0:T(8,128)S(1)} collective-permute-done((f32[72,128]{1,0:T(8,128)S(1)}, f32[72,128]{1,0:T(8,128)S(1)}, u32[]{:S(2)}, u32[]{:S(2)}) %collective-permute-start.3) | collective-permute-done | bytes 36896 | tf_op jit(solution)/shard_map/ppermute | solution.py:34
  14.1 1.8 %outer.1 = (f32[3,16,512]{2,1,0:T(8,128)}, f32[1088,128]{1,0:T(8,128)S(1)}, f32[4,34,8,128]{3,2,1,0:T(8,128)S(1)}, f32[3,18,8,128]{3,2,1,0:T(8,128)S(1)}, f32[3,...) custom-call(f32[84,128]{1,0:T(8,128)S(1)} %collective-permute-done.f, ...), custom_call_target="tpu_custom_call", output_to_operand_aliasing={{1}: (3, {}), {2}: (4, {}), {3}: (5, {}), {4}: (6, {}), {5}... | custom-call | tf_op jit(solution)/shard_map/outer/pallas_call | solution.py:622
  (1 shorter events, 0.0 us)
Async XLA Ops:
  1.1 7.5 %collective-permute-start.1 = (f32[16,128]{1,0:T(8,128)S(1)}, f32[16,128]{1,0:T(8,128)S(1)}, u32[]{:S(2)}, u32[]{:S(2)}) collective-permute-start(f32[16,128]{1,0:T(8,128)S(1)} %get-tuple-element.40), channel_id=1, source_target_pairs={{8,16},{16,8},{24,0},{0,24},{9,17},{17,9},{25,1},{1,25},{10,18},{1... | collective-permute-start | bytes 24584 | tf_op jit(solution)/shard_map/ppermute | solution.py:34
  5.0 3.7 %collective-permute-start.2 = (f32[16,128]{1,0:T(8,128)S(1)}, f32[16,128]{1,0:T(8,128)S(1)}, u32[]{:S(2)}, u32[]{:S(2)}) collective-permute-start(f32[16,128]{1,0:T(8,128)S(1)} %get-tuple-element.41), channel_id=1, source_target_pairs={{0,8},{8,0},{16,24},{24,16},{1,9},{9,1},{17,25},{25,17},{2,10},{10... | collective-permute-start | bytes 24584 | tf_op jit(solution)/shard_map/ppermute | solution.py:34
  5.6 7.7 %collective-permute-start = (f32[84,128]{1,0:T(8,128)S(1)}, f32[84,128]{1,0:T(8,128)S(1)}, u32[]{:S(2)}, u32[]{:S(2)}) collective-permute-start(f32[84,128]{1,0:T(8,128)S(1)} %get-tuple-element.39), channel_id=1, source_target_pairs={{1,2},{2,1},{3,4},{4,3},{5,6},{6,5},{7,0},{0,7},{9,10},{10,9},{11,... | collective-permute-start | bytes 129032 | tf_op jit(solution)/shard_map/ppermute | solution.py:34
  8.1 3.7 %collective-permute-start.5 = (f32[80,128]{1,0:T(8,128)S(1)}, f32[80,128]{1,0:T(8,128)S(1)}, u32[]{:S(2)}, u32[]{:S(2)}) collective-permute-start(f32[80,128]{1,0:T(8,128)S(1)} %get-tuple-element.46), channel_id=1, source_target_pairs={{0,1},{1,0},{2,3},{3,2},{4,5},{5,4},{6,7},{7,6},{8,9},{9,8},{10,11... | collective-permute-start | bytes 122888 | tf_op jit(solution)/shard_map/ppermute | solution.py:34
  8.1 4.6 %collective-permute-start.4 = (f32[72,128]{1,0:T(8,128)S(1)}, f32[72,128]{1,0:T(8,128)S(1)}, u32[]{:S(2)}, u32[]{:S(2)}) collective-permute-start(f32[72,128]{1,0:T(8,128)S(1)} %get-tuple-element.45.scalars), channel_id=1, source_target_pairs={{0,16},{8,24},{16,0},{24,8},{1,17},{9,25},{17,1},{25,9},{2,18},{10... | collective-permute-start | bytes 110600 | tf_op jit(solution)/shard_map/ppermute | solution.py:39
  8.7 5.4 %collective-permute-start.3 = (f32[72,128]{1,0:T(8,128)S(1)}, f32[72,128]{1,0:T(8,128)S(1)}, u32[]{:S(2)}, u32[]{:S(2)}) collective-permute-start(f32[72,128]{1,0:T(8,128)S(1)} %get-tuple-element.44), channel_id=1, source_target_pairs={{1,2},{2,1},{3,4},{4,3},{5,6},{6,5},{7,0},{0,7},{9,10},{10,9},{11,... | collective-permute-start | bytes 110600 | tf_op jit(solution)/shard_map/ppermute | solution.py:34
  10.6 1.2 %collective-permute-start.6 = (f32[64,128]{1,0:T(8,128)S(1)}, f32[64,128]{1,0:T(8,128)S(1)}, u32[]{:S(2)}, u32[]{:S(2)}) collective-permute-start(f32[64,128]{1,0:T(8,128)S(1)} %get-tuple-element.47), channel_id=1, source_target_pairs={{0,1},{1,0},{2,3},{3,2},{4,5},{5,4},{6,7},{7,6},{8,9},{9,8},{10,11... | collective-permute-start | bytes 98312 | tf_op jit(solution)/shard_map/ppermute | solution.py:34

commit v16 on v15

--- a/solution.py
+++ b/solution.py
@@ -483,6 +483,7 @@
 
 
 def outer_kernel(far_early, far, sums, *rest):
+    *rest, lines, done = rest
     out, grid, coef, sol, result, *poly = rest[len(rest) // 2 :]
     rows, columns = out.shape[1:]
     lane = lax.broadcasted_iota(jnp.int32, (SUB, LANES), 1)
@@ -513,13 +514,20 @@
     pl.when(above)(lambda: far_rows(True))
     pl.when(jnp.logical_not(above))(lambda: far_rows(False))
 
+    moves = []
     for k in range(3):
         for g in range(rows // SUB):
+            cut = pl.ds(g * SUB, SUB)
             for t in range(columns // LANES):
                 one = result[k, pl.Slice(g * SUB * SUB + 2 * t, SUB, SUB), :]
                 two = result[k, pl.Slice(g * SUB * SUB + 2 * t + 1, SUB, SUB), :]
                 joined = jnp.where(lane < HALF, turn(one, -SIDE), turn(two, SIDE))
-                out[k, pl.ds(g * SUB, SUB), pl.ds(t * LANES, LANES)] = joined
+                lines[k, cut, pl.ds(t * LANES, LANES)] = joined
+            move = pltpu.make_async_copy(lines.at[k, cut], out.at[k, cut], done.at[k, g])
+            move.start()
+            moves.append(move)
+    for move in moves:
+        move.wait()
 
 
 def shards(state, depth, pole_real, pole_imag, pole_weight):
@@ -623,7 +631,11 @@
         outer_kernel,
         out_shape=(f32(*state.shape), *kept),
         in_specs=[vmem] * (3 + len(kept)),
-        out_specs=(vmem,) * (1 + len(kept)),
+        out_specs=(hbm, *(vmem,) * len(kept)),
+        scratch_shapes=[
+            pltpu.VMEM(state.shape, jnp.float32),
+            pltpu.SemaphoreType.DMA((3, rows // SUB)),
+        ],
         input_output_aliases={3 + i: 1 + i for i in range(len(kept))},
         compiler_params=small,
         name="outer",

time: 16 us -> 16.1 us (level)
  no operation moved by 1% of the time
where the time goes in v16:
time: 16.1 us; the launch traced here: 15.9 us
  starting transfers between devices  9.33 us (58%)
  Pallas kernels  5.23 us (32%)
  waiting for transfers between devices  1.33 us (8%)
    ppermute x6, starting transfers between devices, swap(): return lax.ppermute(block, axis, pairs(lax.axis_size(axis), phase))  8.83 us
    pallas_call x1, Pallas kernels, shards(): pl.pallas_call(outer_kernel, out_shape=(f32(*state.shape), *kept), in_spe...  1.83 us
    ppermute x6, waiting for transfers between devices, swap(): return lax.ppermute(block, axis, pairs(lax.axis_size(axis), phase))  1.33 us
    pallas_call x1, Pallas kernels, shards(): pl.pallas_call(pack_columns_kernel, out_shape=(pltpu.VMEM((4, rows, colum...  1.08 us
    pallas_call x1, Pallas kernels, shards(): pl.pallas_call(mid_kernel, out_shape=state_of, in_specs=[vmem] * (2 + len...  0.87 us
    pallas_call x1, Pallas kernels, shards(): pl.pallas_call(inner_kernel, out_shape=state_of, in_specs=[vmem] * 3, out...  0.78 us
    pallas_call x1, Pallas kernels, shards(): pl.pallas_call(functools.partial(pole_sums_kernel, 4 * poles), out_shape=...  0.65 us
    ppermute x1, starting transfers between devices, shift(): lax.ppermute(block, axis, [(i, (i + step) % count) for i in range(count)])  0.51 us
  transfers between devices with their start and end apart: 7, of which 3 were waited for; matrix products, arithmetic and copies ran while one was open for 0% of the time, Pallas kernels for 15%

profile of v16, /device:TPU:0, one launch (start us, length us, event | category | flops | bytes accessed | tf_op | source)
XLA Modules:
  0.0 15.9 jit_solution(11506049872401923390)
XLA Ops:
  0.0 1.1 %pack_columns.1 = (f32[4,16,512]{2,1,0:T(8,128)S(1)}, f32[16,128]{1,0:T(8,128)S(1)}, f32[16,128]{1,0:T(8,128)S(1)}, f32[72,128]{1,0:T(8,128)S(1)}, f32[84,128]{1...) custom-call(f32[3,16,512]{2,1,0:T(8,128)} %state.1, f32[16,512]{1,0:T(8,128)} %depth.1, ...), custom_call_target="tpu_custom_call" | custom-call | tf_op jit(solution)/shard_map/pack_columns/pallas_call | solution.py:552
  1.1 4.0 %collective-permute-start.1 = (f32[16,128]{1,0:T(8,128)S(1)}, f32[16,128]{1,0:T(8,128)S(1)}, u32[]{:S(2)}, u32[]{:S(2)}) collective-permute-start(f32[16,128]{1,0:T(8,128)S(1)} %get-tuple-element.40), channel_id=1, source_target_pairs={{8,16},{16,8},{24,0},{0,24},{9,17},{17,9},{25,1},{1,25},{10,18},{1... | collective-permute-start | bytes 24584 | tf_op jit(solution)/shard_map/ppermute | solution.py:34
  5.0 0.5 %collective-permute-start.2 = (f32[16,128]{1,0:T(8,128)S(1)}, f32[16,128]{1,0:T(8,128)S(1)}, u32[]{:S(2)}, u32[]{:S(2)}) collective-permute-start(f32[16,128]{1,0:T(8,128)S(1)} %get-tuple-element.41), channel_id=1, source_target_pairs={{0,8},{8,0},{16,24},{24,16},{1,9},{9,1},{17,25},{25,17},{2,10},{10... | collective-permute-start | bytes 24584 | tf_op jit(solution)/shard_map/ppermute | solution.py:34
  5.6 2.5 %collective-permute-start = (f32[84,128]{1,0:T(8,128)S(1)}, f32[84,128]{1,0:T(8,128)S(1)}, u32[]{:S(2)}, u32[]{:S(2)}) collective-permute-start(f32[84,128]{1,0:T(8,128)S(1)} %get-tuple-element.39), channel_id=1, source_target_pairs={{1,2},{2,1},{3,4},{4,3},{5,6},{6,5},{7,0},{0,7},{9,10},{10,9},{11,... | collective-permute-start | bytes 129032 | tf_op jit(solution)/shard_map/ppermute | solution.py:34
  8.1 0.0 collective-permute-start.5
  8.1 0.5 %collective-permute-start.4 = (f32[72,128]{1,0:T(8,128)S(1)}, f32[72,128]{1,0:T(8,128)S(1)}, u32[]{:S(2)}, u32[]{:S(2)}) collective-permute-start(f32[72,128]{1,0:T(8,128)S(1)} %get-tuple-element.45.scalars), channel_id=1, source_target_pairs={{0,16},{8,24},{16,0},{24,8},{1,17},{9,25},{17,1},{25,9},{2,18},{10... | collective-permute-start | bytes 110600 | tf_op jit(solution)/shard_map/ppermute | solution.py:39
  8.6 0.0 collective-permute-done.1.second
  8.6 0.1 collective-permute-done.2.first
  8.7 1.8 %collective-permute-start.3 = (f32[72,128]{1,0:T(8,128)S(1)}, f32[72,128]{1,0:T(8,128)S(1)}, u32[]{:S(2)}, u32[]{:S(2)}) collective-permute-start(f32[72,128]{1,0:T(8,128)S(1)} %get-tuple-element.44), channel_id=1, source_target_pairs={{1,2},{2,1},{3,4},{4,3},{5,6},{6,5},{7,0},{0,7},{9,10},{10,9},{11,... | collective-permute-start | bytes 110600 | tf_op jit(solution)/shard_map/ppermute | solution.py:34
  10.6 0.0 collective-permute-start.6
  10.6 0.8 %inner.1 = (f32[1088,128]{1,0:T(8,128)S(1)}, f32[4,34,8,128]{3,2,1,0:T(8,128)S(1)}, f32[3,34,8,128]{3,2,1,0:T(8,128)S(1)}, f32[3,34,8,128]{3,2,1,0:T(8,128)S(1)}...) custom-call(f32[4,16,512]{2,1,0:T(8,128)S(1)} %get-tuple-element.48., ...), custom_call_target="tpu_custom_call" | custom-call | flops 1310720 | bytes 1441792 | tf_op jit(solution)/shard_map/inner/pallas_call | solution.py:601
  11.3 0.4 %collective-permute-done.6.near = f32[64,128]{1,0:T(8,128)S(1)} collective-permute-done((f32[64,128]{1,0:T(8,128)S(1)}, f32[64,128]{1,0:T(8,128)S(1)}, u32[]{:S(2)}, u32[]{:S(2)}) %collective-permute-start.6) | collective-permute-done | bytes 32800 | tf_op jit(solution)/shard_map/ppermute | solution.py:34
  11.8 0.0 collective-permute-done.5.near_early
  11.8 0.9 %mid.1 = (f32[1088,128]{1,0:T(8,128)S(1)}, f32[4,34,8,128]{3,2,1,0:T(8,128)S(1)}, f32[3,34,8,128]{3,2,1,0:T(8,128)S(1)}, f32[3,34,8,128]{3,2,1,0:T(8,128)S(1)}, ...) custom-call(f32[80,128]{1,0:T(8,128)S(1)} %collective-permute-done.5, ...), custom_call_target="tpu_custom_call", output_to_operand_aliasing={{0}: (2, {}), {1}: (3, {}), {2}: (4, {}), {3}: (5, {}), {4}... | custom-call | flops 1310720 | bytes 1441792 | tf_op jit(solution)/shard_map/mid/pallas_call | solution.py:610
  12.6 0.0 collective-permute-done.4
  12.6 0.7 %pole_sums.1 = (f32[74,8,128]{2,1,0:T(8,128)S(1)}, f32[3,18,8,128]{3,2,1,0:T(8,128)S(1)}, f32[3,128,128]{2,1,0:T(8,128)S(1)}) custom-call(f32[72,128]{1,0:T(8,128)S(1)} %get-tuple-element.45.scalars, f32[16,128]{1,0:T(8,128)S(1)} %collective-permute-done.2.first, f32[16,128]{1,0:T(8,128)S(1)} %collective-permute-done.1.second, f32[1,72,128]{2,1,0:T(8,128)S(1)} %bitcast.1, ...), custom_call_target="tpu_custom_call" | custom-call | tf_op jit(solution)/shard_map/pole_sums/pallas_call | solution.py:621
  13.3 0.0 collective-permute-done.far_early
  13.3 0.8 %collective-permute-done.3.far = f32[72,128]{1,0:T(8,128)S(1)} collective-permute-done((f32[72,128]{1,0:T(8,128)S(1)}, f32[72,128]{1,0:T(8,128)S(1)}, u32[]{:S(2)}, u32[]{:S(2)}) %collective-permute-start.3) | collective-permute-done | bytes 36896 | tf_op jit(solution)/shard_map/ppermute | solution.py:34
  14.1 1.8 %outer.1 = (f32[3,16,512]{2,1,0:T(8,128)}, f32[1088,128]{1,0:T(8,128)S(1)}, f32[4,34,8,128]{3,2,1,0:T(8,128)S(1)}, f32[3,18,8,128]{3,2,1,0:T(8,128)S(1)}, f32[3,...) custom-call(f32[84,128]{1,0:T(8,128)S(1)} %collective-permute-done.f, ...), custom_call_target="tpu_custom_call", output_to_operand_aliasing={{1}: (3, {}), {2}: (4, {}), {3}: (5, {}), {4}: (6, {}), {5}... | custom-call | tf_op jit(solution)/shard_map/outer/pallas_call | solution.py:630
  (1 shorter events, 0.0 us)
Async XLA Ops:
  1.1 7.5 %collective-permute-start.1 = (f32[16,128]{1,0:T(8,128)S(1)}, f32[16,128]{1,0:T(8,128)S(1)}, u32[]{:S(2)}, u32[]{:S(2)}) collective-permute-start(f32[16,128]{1,0:T(8,128)S(1)} %get-tuple-element.40), channel_id=1, source_target_pairs={{8,16},{16,8},{24,0},{0,24},{9,17},{17,9},{25,1},{1,25},{10,18},{1... | collective-permute-start | bytes 24584 | tf_op jit(solution)/shard_map/ppermute | solution.py:34
  5.0 3.7 %collective-permute-start.2 = (f32[16,128]{1,0:T(8,128)S(1)}, f32[16,128]{1,0:T(8,128)S(1)}, u32[]{:S(2)}, u32[]{:S(2)}) collective-permute-start(f32[16,128]{1,0:T(8,128)S(1)} %get-tuple-element.41), channel_id=1, source_target_pairs={{0,8},{8,0},{16,24},{24,16},{1,9},{9,1},{17,25},{25,17},{2,10},{10... | collective-permute-start | bytes 24584 | tf_op jit(solution)/shard_map/ppermute | solution.py:34
  5.6 7.7 %collective-permute-start = (f32[84,128]{1,0:T(8,128)S(1)}, f32[84,128]{1,0:T(8,128)S(1)}, u32[]{:S(2)}, u32[]{:S(2)}) collective-permute-start(f32[84,128]{1,0:T(8,128)S(1)} %get-tuple-element.39), channel_id=1, source_target_pairs={{1,2},{2,1},{3,4},{4,3},{5,6},{6,5},{7,0},{0,7},{9,10},{10,9},{11,... | collective-permute-start | bytes 129032 | tf_op jit(solution)/shard_map/ppermute | solution.py:34
  8.1 3.7 %collective-permute-start.5 = (f32[80,128]{1,0:T(8,128)S(1)}, f32[80,128]{1,0:T(8,128)S(1)}, u32[]{:S(2)}, u32[]{:S(2)}) collective-permute-start(f32[80,128]{1,0:T(8,128)S(1)} %get-tuple-element.46), channel_id=1, source_target_pairs={{0,1},{1,0},{2,3},{3,2},{4,5},{5,4},{6,7},{7,6},{8,9},{9,8},{10,11... | collective-permute-start | bytes 122888 | tf_op jit(solution)/shard_map/ppermute | solution.py:34
  8.1 4.6 %collective-permute-start.4 = (f32[72,128]{1,0:T(8,128)S(1)}, f32[72,128]{1,0:T(8,128)S(1)}, u32[]{:S(2)}, u32[]{:S(2)}) collective-permute-start(f32[72,128]{1,0:T(8,128)S(1)} %get-tuple-element.45.scalars), channel_id=1, source_target_pairs={{0,16},{8,24},{16,0},{24,8},{1,17},{9,25},{17,1},{25,9},{2,18},{10... | collective-permute-start | bytes 110600 | tf_op jit(solution)/shard_map/ppermute | solution.py:39
  8.7 5.4 %collective-permute-start.3 = (f32[72,128]{1,0:T(8,128)S(1)}, f32[72,128]{1,0:T(8,128)S(1)}, u32[]{:S(2)}, u32[]{:S(2)}) collective-permute-start(f32[72,128]{1,0:T(8,128)S(1)} %get-tuple-element.44), channel_id=1, source_target_pairs={{1,2},{2,1},{3,4},{4,3},{5,6},{6,5},{7,0},{0,7},{9,10},{10,9},{11,... | collective-permute-start | bytes 110600 | tf_op jit(solution)/shard_map/ppermute | solution.py:34
  10.6 1.2 %collective-permute-start.6 = (f32[64,128]{1,0:T(8,128)S(1)}, f32[64,128]{1,0:T(8,128)S(1)}, u32[]{:S(2)}, u32[]{:S(2)}) collective-permute-start(f32[64,128]{1,0:T(8,128)S(1)} %get-tuple-element.47), channel_id=1, source_target_pairs={{0,1},{1,0},{2,3},{3,2},{4,5},{5,4},{6,7},{7,6},{8,9},{9,8},{10,11... | collective-permute-start | bytes 98312 | tf_op jit(solution)/shard_map/ppermute | solution.py:34

commit v17 on v16

--- a/solution.py
+++ b/solution.py
@@ -56,40 +56,20 @@
     return (a[0] * factor, a[1] * factor)
 
 
-def all_at_once(*pairs_of):
-    moves = [pltpu.make_async_copy(*pair) for pair in pairs_of]
+def pack_columns_kernel(
+    state, depth, real, imag, weight, fields, first, second, real_in, imag_in, weight_in, done
+):
+    moves = [
+        pltpu.make_async_copy(depth, fields.at[3], done.at[0]),
+        pltpu.make_async_copy(state, fields.at[pl.ds(0, 3)], done.at[1]),
+        pltpu.make_async_copy(real, real_in, done.at[2]),
+        pltpu.make_async_copy(imag, imag_in, done.at[3]),
+        pltpu.make_async_copy(weight, weight_in, done.at[4]),
+    ]
     for move in moves:
         move.start()
     for move in moves:
         move.wait()
-
-
-def pack_columns_kernel(
-    state,
-    depth,
-    real,
-    imag,
-    weight,
-    fields,
-    first,
-    second,
-    scalars,
-    far_early,
-    far,
-    near_early,
-    near,
-    real_in,
-    imag_in,
-    weight_in,
-    done,
-):
-    all_at_once(
-        (state, fields.at[pl.ds(0, 3)], done.at[0]),
-        (depth, fields.at[3], done.at[1]),
-        (real, real_in, done.at[2]),
-        (imag, imag_in, done.at[3]),
-        (weight, weight_in, done.at[4]),
-    )
     odd = lax.rem(lax.axis_index("pole"), 2) == 1
     rows, columns = fields.shape[1:]
     lane = lax.broadcasted_iota(jnp.int32, (SUB, LANES), 1)
@@ -97,24 +77,17 @@
     poles = real.shape[0]
     values = [real_in[i] for i in range(poles)] + [imag_in[i] for i in range(poles)]
     values += [weight_in[0, i] for i in range(poles)] + [weight_in[1, i] for i in range(poles)]
-    spread = []
-    for g in range(len(values) // SUB):
-        block = jnp.full((SUB, LANES), values[g * SUB], jnp.float32)
-        for i in range(1, SUB):
-            block = jnp.where(sub == i, values[g * SUB + i], block)
-        scalars[pl.ds(g * SUB, SUB)] = block
-        spread.append(block)
-    for g in range(len(spread), scalars.shape[0] // SUB):
-        scalars[pl.ds(g * SUB, SUB)] = jnp.zeros((SUB, LANES), jnp.float32)
     for g in range(rows // SUB):
         cut = pl.ds(g * SUB, SUB)
-        rest = spread[g] if g < len(spread) else jnp.zeros((SUB, LANES), jnp.float32)
-        eastward = rest
-        westward = rest
         west = [fields[f, cut, 0:LANES] for f in range(4)]
         east = [fields[f, cut, columns - LANES : columns] for f in range(4)]
         west += [west[3] * west[1], west[3] * west[2]]
         east += [east[3] * east[1], east[3] * east[2]]
+        rest = jnp.zeros((SUB, LANES), jnp.float32)
+        for i, value in enumerate(values[g * SUB : (g + 1) * SUB]):
+            rest = jnp.where(sub == i, value, rest)
+        eastward = rest
+        westward = rest
         for f in range(6):
             low, high = EDGE * f, EDGE * (f + 1)
             take = jnp.logical_and(lane >= low, lane < high)
@@ -123,7 +96,11 @@
             westward = jnp.where(take, turn(west[f], EAST + low), westward)
         first[cut, :] = jnp.where(odd, westward, eastward)
         second[cut, :] = jnp.where(odd, eastward, westward)
-    for (parts, low) in towards((far_early, far), (near_early, near)):
+
+
+def pack_rows_kernel(count, fields, second, first, far_early, far, near_early, near, scalars):
+    rows = fields.shape[1]
+    for parts, low in towards((far_early, far), (near_early, near)):
         at = 0
         for part in parts:
             pl.when(low)(lambda: pack_rows(part, at, fields, 0, SUB))
@@ -131,6 +108,15 @@
                 lambda: pack_rows(part, at, fields, rows - SUB, rows - SUB - 1)
             )
             at += part.shape[0] // SUB
+    odd = lax.rem(lax.axis_index("pole"), 2) == 1
+    lane = lax.broadcasted_iota(jnp.int32, (SUB, LANES), 1)
+    from_first = jnp.logical_xor(lane >= HALF, odd)
+    for g in range(0, scalars.shape[0], SUB):
+        if g < count:
+            block = jnp.where(from_first, first[pl.ds(g, SUB)], second[pl.ds(g, SUB)])
+        else:
+            block = jnp.zeros((SUB, LANES), jnp.float32)
+        scalars[pl.ds(g, SUB)] = block
 
 
 def towards(far, near):
@@ -545,21 +531,11 @@
     ]
     hbm = pl.BlockSpec(memory_space=pltpu.HBM)
     message = pltpu.VMEM((rows, LANES), jnp.float32)
-    blocks = 4 * columns // LANES + 2
-    half = blocks // 2 * SUB
-    parts = (half + SUB + 4, half, half + SUB, half - SUB)
-    wide = max(4 * poles, half)
-    fields, first, second, scalars, far_early, far, near_early, near = pl.pallas_call(
+    fields, first, second = pl.pallas_call(
         pack_columns_kernel,
-        out_shape=(
-            pltpu.VMEM((4, rows, columns), jnp.float32),
-            message,
-            message,
-            pltpu.VMEM((wide, LANES), jnp.float32),
-            *(pltpu.VMEM((part, LANES), jnp.float32) for part in parts),
-        ),
+        out_shape=(pltpu.VMEM((4, rows, columns), jnp.float32), message, message),
         in_specs=[hbm] * 5,
-        out_specs=(vmem,) * 8,
+        out_specs=(vmem,) * 3,
         scratch_shapes=[
             pltpu.SMEM(pole_real.shape, jnp.float32),
             pltpu.SMEM(pole_imag.shape, jnp.float32),
@@ -569,6 +545,17 @@
         compiler_params=small,
         name="pack_columns",
     )(*given)
+    blocks = 4 * columns // LANES + 2
+    half = blocks // 2 * SUB
+    parts = (half + SUB + 4, half, half + SUB, half - SUB, max(4 * poles, half))
+    far_early, far, near_early, near, scalars = pl.pallas_call(
+        functools.partial(pack_rows_kernel, 4 * poles),
+        out_shape=tuple(f32(part, LANES) for part in parts),
+        in_specs=[vmem] * 3,
+        out_specs=(vmem,) * 5,
+        compiler_params=small,
+        name="pack_rows",
+    )(fields, second, first)
     second = swap(second, "pole", 1)
     first = swap(first, "pole", 0)
     far, near = pl.pallas_call(

time: 16.1 us -> 16.1 us (level)
  transfers between devices with their start and end apart: 7 -> 7, of which waited for: 3 -> 2; matrix products, arithmetic and copies ran while one was open for 0% -> 0% of each run, Pallas kernels for 15% -> 15%
where the time goes in v17:
time: 16.1 us; the launch traced here: 15.9 us
  starting transfers between devices  9.4 us (58%)
  Pallas kernels  5.26 us (33%)
  waiting for transfers between devices  1.21 us (8%)
    ppermute x6, starting transfers between devices, swap(): return lax.ppermute(block, axis, pairs(lax.axis_size(axis), phase))  8.89 us
    pallas_call x1, Pallas kernels, shards(): pl.pallas_call(outer_kernel, out_shape=(f32(*state.shape), *kept), in_spe...  1.83 us
    ppermute x6, waiting for transfers between devices, swap(): return lax.ppermute(block, axis, pairs(lax.axis_size(axis), phase))  1.21 us
    pallas_call x1, Pallas kernels, shards(): pl.pallas_call(pack_columns_kernel, out_shape=(pltpu.VMEM((4, rows, colum...  1.07 us
    pallas_call x1, Pallas kernels, shards(): pl.pallas_call(mid_kernel, out_shape=state_of, in_specs=[vmem] * (2 + len...  0.87 us
    pallas_call x1, Pallas kernels, shards(): pl.pallas_call(inner_kernel, out_shape=state_of, in_specs=[vmem] * 3, out...  0.78 us
    pallas_call x1, Pallas kernels, shards(): pl.pallas_call(functools.partial(pole_sums_kernel, 4 * poles), out_shape=...  0.65 us
    ppermute x1, starting transfers between devices, shift(): lax.ppermute(block, axis, [(i, (i + step) % count) for i in range(count)])  0.51 us
  transfers between devices with their start and end apart: 7, of which 2 were waited for; matrix products, arithmetic and copies ran while one was open for 0% of the time, Pallas kernels for 15%

profile of v17, /device:TPU:0, one launch (start us, length us, event | category | flops | bytes accessed | tf_op | source)
XLA Modules:
  0.0 15.9 jit_solution(12196568909524153323)
XLA Ops:
  0.0 1.1 %pack_columns.1 = (f32[4,16,512]{2,1,0:T(8,128)S(1)}, f32[16,128]{1,0:T(8,128)S(1)}, f32[16,128]{1,0:T(8,128)S(1)}) custom-call(f32[3,16,512]{2,1,0:T(8,128)} %state.1, f32[16,512]{1,0:T(8,128)} %depth.1, f32[4]{0:T(128)} %real.1, f32[4]{0:T(128)} %imag.1, f32[2,4]{1,0:T(2,128)} %weight.1), custom_call_target="tpu_custom_call" | custom-call | tf_op jit(solution)/shard_map/pack_columns/pallas_call | solution.py:534
  1.1 4.0 %collective-permute-start.1 = (f32[16,128]{1,0:T(8,128)S(1)}, f32[16,128]{1,0:T(8,128)S(1)}, u32[]{:S(2)}, u32[]{:S(2)}) collective-permute-start(f32[16,128]{1,0:T(8,128)S(1)} %get-tuple-element.40.second), channel_id=1, source_target_pairs={{8,16},{16,8},{24,0},{0,24},{9,17},{17,9},{25,1},{1,25},{10,18},{1... | collective-permute-start | bytes 24584 | tf_op jit(solution)/shard_map/ppermute | solution.py:34
  5.0 0.5 %collective-permute-start.2 = (f32[16,128]{1,0:T(8,128)S(1)}, f32[16,128]{1,0:T(8,128)S(1)}, u32[]{:S(2)}, u32[]{:S(2)}) collective-permute-start(f32[16,128]{1,0:T(8,128)S(1)} %get-tuple-element.41.first), channel_id=1, source_target_pairs={{0,8},{8,0},{16,24},{24,16},{1,9},{9,1},{17,25},{25,17},{2,10},{10... | collective-permute-start | bytes 24584 | tf_op jit(solution)/shard_map/ppermute | solution.py:34
  5.6 2.5 %collective-permute-start = (f32[84,128]{1,0:T(8,128)S(1)}, f32[84,128]{1,0:T(8,128)S(1)}, u32[]{:S(2)}, u32[]{:S(2)}) collective-permute-start(f32[84,128]{1,0:T(8,128)S(1)} %get-tuple-element.42), channel_id=1, source_target_pairs={{1,2},{2,1},{3,4},{4,3},{5,6},{6,5},{7,0},{0,7},{9,10},{10,9},{11,... | collective-permute-start | bytes 129032 | tf_op jit(solution)/shard_map/ppermute | solution.py:34
  8.2 0.0 collective-permute-start.5
  8.2 0.5 %collective-permute-start.4 = (f32[72,128]{1,0:T(8,128)S(1)}, f32[72,128]{1,0:T(8,128)S(1)}, u32[]{:S(2)}, u32[]{:S(2)}) collective-permute-start(f32[72,128]{1,0:T(8,128)S(1)} %get-tuple-element.46.scalars), channel_id=1, source_target_pairs={{0,16},{8,24},{16,0},{24,8},{1,17},{9,25},{17,1},{25,9},{2,18},{10... | collective-permute-start | bytes 110600 | tf_op jit(solution)/shard_map/ppermute | solution.py:39
  8.7 0.0 collective-permute-done.1.second
  8.7 0.0 collective-permute-done.2.first
  8.7 1.8 %collective-permute-start.3 = (f32[72,128]{1,0:T(8,128)S(1)}, f32[72,128]{1,0:T(8,128)S(1)}, u32[]{:S(2)}, u32[]{:S(2)}) collective-permute-start(f32[72,128]{1,0:T(8,128)S(1)} %get-tuple-element.45), channel_id=1, source_target_pairs={{1,2},{2,1},{3,4},{4,3},{5,6},{6,5},{7,0},{0,7},{9,10},{10,9},{11,... | collective-permute-start | bytes 110600 | tf_op jit(solution)/shard_map/ppermute | solution.py:34
  10.6 0.0 collective-permute-start.6
  10.6 0.8 %inner.1 = (f32[1088,128]{1,0:T(8,128)S(1)}, f32[4,34,8,128]{3,2,1,0:T(8,128)S(1)}, f32[3,34,8,128]{3,2,1,0:T(8,128)S(1)}, f32[3,34,8,128]{3,2,1,0:T(8,128)S(1)}...) custom-call(f32[4,16,512]{2,1,0:T(8,128)S(1)} %get-tuple-element.39., ...), custom_call_target="tpu_custom_call" | custom-call | flops 1310720 | bytes 1441792 | tf_op jit(solution)/shard_map/inner/pallas_call | solution.py:588
  11.3 0.0 collective-permute-done.5.near_early
  11.4 0.4 %collective-permute-done.6.near = f32[64,128]{1,0:T(8,128)S(1)} collective-permute-done((f32[64,128]{1,0:T(8,128)S(1)}, f32[64,128]{1,0:T(8,128)S(1)}, u32[]{:S(2)}, u32[]{:S(2)}) %collective-permute-start.6) | collective-permute-done | bytes 32800 | tf_op jit(solution)/shard_map/ppermute | solution.py:34
  11.8 0.9 %mid.1 = (f32[1088,128]{1,0:T(8,128)S(1)}, f32[4,34,8,128]{3,2,1,0:T(8,128)S(1)}, f32[3,34,8,128]{3,2,1,0:T(8,128)S(1)}, f32[3,34,8,128]{3,2,1,0:T(8,128)S(1)}, ...) custom-call(f32[80,128]{1,0:T(8,128)S(1)} %collective-permute-done.5, ...), custom_call_target="tpu_custom_call", output_to_operand_aliasing={{0}: (2, {}), {1}: (3, {}), {2}: (4, {}), {3}: (5, {}), {4}... | custom-call | flops 1310720 | bytes 1441792 | tf_op jit(solution)/shard_map/mid/pallas_call | solution.py:597
  12.6 0.0 collective-permute-done.4
  12.6 0.7 %pole_sums.1 = (f32[74,8,128]{2,1,0:T(8,128)S(1)}, f32[3,18,8,128]{3,2,1,0:T(8,128)S(1)}, f32[3,128,128]{2,1,0:T(8,128)S(1)}) custom-call(f32[72,128]{1,0:T(8,128)S(1)} %get-tuple-element.46.scalars, f32[16,128]{1,0:T(8,128)S(1)} %collective-permute-done.2.first, f32[16,128]{1,0:T(8,128)S(1)} %collective-permute-done.1.second, f32[1,72,128]{2,1,0:T(8,128)S(1)} %bitcast.1, ...), custom_call_target="tpu_custom_call" | custom-call | tf_op jit(solution)/shard_map/pole_sums/pallas_call | solution.py:608
  13.3 0.0 collective-permute-done.far_early
  13.3 0.8 %collective-permute-done.3.far = f32[72,128]{1,0:T(8,128)S(1)} collective-permute-done((f32[72,128]{1,0:T(8,128)S(1)}, f32[72,128]{1,0:T(8,128)S(1)}, u32[]{:S(2)}, u32[]{:S(2)}) %collective-permute-start.3) | collective-permute-done | bytes 36896 | tf_op jit(solution)/shard_map/ppermute | solution.py:34
  14.1 1.8 %outer.1 = (f32[3,16,512]{2,1,0:T(8,128)}, f32[1088,128]{1,0:T(8,128)S(1)}, f32[4,34,8,128]{3,2,1,0:T(8,128)S(1)}, f32[3,18,8,128]{3,2,1,0:T(8,128)S(1)}, f32[3,...) custom-call(f32[84,128]{1,0:T(8,128)S(1)} %collective-permute-done.f, ...), custom_call_target="tpu_custom_call", output_to_operand_aliasing={{1}: (3, {}), {2}: (4, {}), {3}: (5, {}), {4}: (6, {}), {5}... | custom-call | tf_op jit(solution)/shard_map/outer/pallas_call | solution.py:617
  (2 shorter events, 0.0 us)
Async XLA Ops:
  1.1 7.6 %collective-permute-start.1 = (f32[16,128]{1,0:T(8,128)S(1)}, f32[16,128]{1,0:T(8,128)S(1)}, u32[]{:S(2)}, u32[]{:S(2)}) collective-permute-start(f32[16,128]{1,0:T(8,128)S(1)} %get-tuple-element.40.second), channel_id=1, source_target_pairs={{8,16},{16,8},{24,0},{0,24},{9,17},{17,9},{25,1},{1,25},{10,18},{1... | collective-permute-start | bytes 24584 | tf_op jit(solution)/shard_map/ppermute | solution.py:34
  5.0 3.7 %collective-permute-start.2 = (f32[16,128]{1,0:T(8,128)S(1)}, f32[16,128]{1,0:T(8,128)S(1)}, u32[]{:S(2)}, u32[]{:S(2)}) collective-permute-start(f32[16,128]{1,0:T(8,128)S(1)} %get-tuple-element.41.first), channel_id=1, source_target_pairs={{0,8},{8,0},{16,24},{24,16},{1,9},{9,1},{17,25},{25,17},{2,10},{10... | collective-permute-start | bytes 24584 | tf_op jit(solution)/shard_map/ppermute | solution.py:34
  5.6 7.7 %collective-permute-start = (f32[84,128]{1,0:T(8,128)S(1)}, f32[84,128]{1,0:T(8,128)S(1)}, u32[]{:S(2)}, u32[]{:S(2)}) collective-permute-start(f32[84,128]{1,0:T(8,128)S(1)} %get-tuple-element.42), channel_id=1, source_target_pairs={{1,2},{2,1},{3,4},{4,3},{5,6},{6,5},{7,0},{0,7},{9,10},{10,9},{11,... | collective-permute-start | bytes 129032 | tf_op jit(solution)/shard_map/ppermute | solution.py:34
  8.2 3.2 %collective-permute-start.5 = (f32[80,128]{1,0:T(8,128)S(1)}, f32[80,128]{1,0:T(8,128)S(1)}, u32[]{:S(2)}, u32[]{:S(2)}) collective-permute-start(f32[80,128]{1,0:T(8,128)S(1)} %get-tuple-element.47), channel_id=1, source_target_pairs={{0,1},{1,0},{2,3},{3,2},{4,5},{5,4},{6,7},{7,6},{8,9},{9,8},{10,11... | collective-permute-start | bytes 122888 | tf_op jit(solution)/shard_map/ppermute | solution.py:34
  8.2 4.5 %collective-permute-start.4 = (f32[72,128]{1,0:T(8,128)S(1)}, f32[72,128]{1,0:T(8,128)S(1)}, u32[]{:S(2)}, u32[]{:S(2)}) collective-permute-start(f32[72,128]{1,0:T(8,128)S(1)} %get-tuple-element.46.scalars), channel_id=1, source_target_pairs={{0,16},{8,24},{16,0},{24,8},{1,17},{9,25},{17,1},{25,9},{2,18},{10... | collective-permute-start | bytes 110600 | tf_op jit(solution)/shard_map/ppermute | solution.py:39
  8.7 5.4 %collective-permute-start.3 = (f32[72,128]{1,0:T(8,128)S(1)}, f32[72,128]{1,0:T(8,128)S(1)}, u32[]{:S(2)}, u32[]{:S(2)}) collective-permute-start(f32[72,128]{1,0:T(8,128)S(1)} %get-tuple-element.45), channel_id=1, source_target_pairs={{1,2},{2,1},{3,4},{4,3},{5,6},{6,5},{7,0},{0,7},{9,10},{10,9},{11,... | collective-permute-start | bytes 110600 | tf_op jit(solution)/shard_map/ppermute | solution.py:34
  10.6 1.2 %collective-permute-start.6 = (f32[64,128]{1,0:T(8,128)S(1)}, f32[64,128]{1,0:T(8,128)S(1)}, u32[]{:S(2)}, u32[]{:S(2)}) collective-permute-start(f32[64,128]{1,0:T(8,128)S(1)} %get-tuple-element.48), channel_id=1, source_target_pairs={{0,1},{1,0},{2,3},{3,2},{4,5},{5,4},{6,7},{7,6},{8,9},{9,8},{10,11... | collective-permute-start | bytes 98312 | tf_op jit(solution)/shard_map/ppermute | solution.py:34

commit v18 on v17

--- a/solution.py
+++ b/solution.py
@@ -379,6 +379,7 @@
     flux_north = [None] * 3
     depths = [None] * 2
     across = None
+    found = {}
     for k in range(count + 2):
         r = start + k
         h = cell(grid, 3, r)
@@ -397,23 +398,27 @@
             coef[3, c] = 2.0 - ((across + before) + (north + south))
             east_slope = flux_east[2] - flux_east[0]
             north_slope = right(flux_north[1]) - left(flux_north[1])
-            poly[0][1, c] = 0.5 * (east_slope + north_slope)
+            poly[0][1, c] = found[1, c] = 0.5 * (east_slope + north_slope)
             east_slope = flux_north[2] - flux_north[0]
             north_slope = right(flux_east[1]) - left(flux_east[1])
-            poly[0][2, c] = 0.5 * (east_slope - north_slope)
-            poly[0][0, c] = cell(grid, 0, c)
-
-
-def sweep(poly, coef, m, start, count, upwards=False):
+            poly[0][2, c] = found[2, c] = 0.5 * (east_slope - north_slope)
+            poly[0][0, c] = found[0, c] = cell(grid, 0, c)
+    return found
+
+
+def sweep(poly, coef, m, start, count, last, upwards=False):
+    def take(f, r):
+        return last[f, r] if (f, r) in last else poly[m][f, r]
+
     step = -1 if upwards else 1
     order = range(start, start + count)[::step]
-    back = [poly[m][f, order[0] - step] for f in range(3)]
-    here = [poly[m][f, order[0]] for f in range(3)]
+    back = [take(f, order[0] - step) for f in range(3)]
+    here = [take(f, order[0]) for f in range(3)]
     found = {}
     for r in order:
         north, south, diag = coef[1, r], coef[2, r], coef[3, r]
         above, below = coef[0, r], coef[0, r - 1]
-        ahead = [poly[m][f, r + step] for f in range(3)]
+        ahead = [take(f, r + step) for f in range(3)]
         for f in range(3):
             up, down = (back, ahead) if upwards else (ahead, back)
             value = diag * here[f]
@@ -440,10 +445,10 @@
                 for t in range(fields.shape[2] // LANES)
             ]
             lay(grid, cut, place(side, f), (REACH + g * SUB) * 4 + f, 4)
-    prepare(grid, poly, coef, REACH, rows - 2)
+    found = prepare(grid, poly, coef, REACH, rows - 2)
     for m in range(ITERS - 1):
         if rows - 4 - 2 * m > 0:
-            sweep(poly, coef, m, REACH + 2 + m, rows - 4 - 2 * m)
+            found = sweep(poly, coef, m, REACH + 2 + m, rows - 4 - 2 * m, found)
 
 
 def one_side(halo, side, above, grid, coef, poly, each):
@@ -451,10 +456,11 @@
     main, ext, start = (1, 0, 0) if above else (below, below + SUB, below - 2)
     grid[pl.ds((ext * 4 + 3) * SUB, SUB), :] = jnp.ones((SUB, LANES), jnp.float32)
     lay_halo(grid, halo, side, main, ext)
-    prepare(grid, poly, coef, start, REACH)
-    each(0, None)
+    found = prepare(grid, poly, coef, start, REACH)
+    each(0, found)
     for m in range(ITERS - 1):
-        found = sweep(poly, coef, m, 2 + m if above else below - 2 - m, REACH, above)
+        low = 2 + m if above else below - 2 - m
+        found = sweep(poly, coef, m, low, REACH, found, above)
         each(m + 1, found)
 
 
@@ -487,11 +493,9 @@
 
         def each(m, found):
             part = [r for k, r in enumerate(whole) if known(k) < m]
-            if found is not None:
-                held = [r for r in part if (0, r) in found]
-                add(acc, sums, poly, m, held, found)
-                part = [r for r in part if r not in held]
-            add(acc, sums, poly, m, part)
+            held = [r for r in part if (0, r) in found]
+            add(acc, sums, poly, m, held, found)
+            add(acc, sums, poly, m, [r for r in part if r not in held])
 
         one_side((far_early, far), side, above, grid, coef, poly, each)
         span = [r for r in whole + edges[:1] if REACH <= r < REACH + rows]

time: 16.1 us -> 16 us (level)
  no operation moved by 1% of the time
where the time goes in v18:
time: 16 us; the launch traced here: 15.9 us
  starting transfers between devices  9.4 us (59%)
  Pallas kernels  5.21 us (33%)
  waiting for transfers between devices  1.24 us (8%)
    ppermute x6, starting transfers between devices, swap(): return lax.ppermute(block, axis, pairs(lax.axis_size(axis), phase))  8.89 us
    pallas_call x1, Pallas kernels, shards(): pl.pallas_call(outer_kernel, out_shape=(f32(*state.shape), *kept), in_spe...  1.81 us
    ppermute x6, waiting for transfers between devices, swap(): return lax.ppermute(block, axis, pairs(lax.axis_size(axis), phase))  1.24 us
    pallas_call x1, Pallas kernels, shards(): pl.pallas_call(pack_columns_kernel, out_shape=(pltpu.VMEM((4, rows, colum...  1.07 us
    pallas_call x1, Pallas kernels, shards(): pl.pallas_call(mid_kernel, out_shape=state_of, in_specs=[vmem] * (2 + len...  0.84 us
    pallas_call x1, Pallas kernels, shards(): pl.pallas_call(inner_kernel, out_shape=state_of, in_specs=[vmem] * 3, out...  0.79 us
    pallas_call x1, Pallas kernels, shards(): pl.pallas_call(functools.partial(pole_sums_kernel, 4 * poles), out_shape=...  0.65 us
    ppermute x1, starting transfers between devices, shift(): lax.ppermute(block, axis, [(i, (i + step) % count) for i in range(count)])  0.51 us
  transfers between devices with their start and end apart: 7, of which 2 were waited for; matrix products, arithmetic and copies ran while one was open for 0% of the time, Pallas kernels for 15%

profile of v18, /device:TPU:0, one launch (start us, length us, event | category | flops | bytes accessed | tf_op | source)
XLA Modules:
  0.0 15.9 jit_solution(7583938450813459150)
XLA Ops:
  0.0 1.1 %pack_columns.1 = (f32[4,16,512]{2,1,0:T(8,128)S(1)}, f32[16,128]{1,0:T(8,128)S(1)}, f32[16,128]{1,0:T(8,128)S(1)}) custom-call(f32[3,16,512]{2,1,0:T(8,128)} %state.1, f32[16,512]{1,0:T(8,128)} %depth.1, f32[4]{0:T(128)} %real.1, f32[4]{0:T(128)} %imag.1, f32[2,4]{1,0:T(2,128)} %weight.1), custom_call_target="tpu_custom_call" | custom-call | tf_op jit(solution)/shard_map/pack_columns/pallas_call | solution.py:538
  1.1 4.0 %collective-permute-start.1 = (f32[16,128]{1,0:T(8,128)S(1)}, f32[16,128]{1,0:T(8,128)S(1)}, u32[]{:S(2)}, u32[]{:S(2)}) collective-permute-start(f32[16,128]{1,0:T(8,128)S(1)} %get-tuple-element.40.second), channel_id=1, source_target_pairs={{8,16},{16,8},{24,0},{0,24},{9,17},{17,9},{25,1},{1,25},{10,18},{1... | collective-permute-start | bytes 24584 | tf_op jit(solution)/shard_map/ppermute | solution.py:34
  5.0 0.5 %collective-permute-start.2 = (f32[16,128]{1,0:T(8,128)S(1)}, f32[16,128]{1,0:T(8,128)S(1)}, u32[]{:S(2)}, u32[]{:S(2)}) collective-permute-start(f32[16,128]{1,0:T(8,128)S(1)} %get-tuple-element.41.first), channel_id=1, source_target_pairs={{0,8},{8,0},{16,24},{24,16},{1,9},{9,1},{17,25},{25,17},{2,10},{10... | collective-permute-start | bytes 24584 | tf_op jit(solution)/shard_map/ppermute | solution.py:34
  5.6 2.5 %collective-permute-start = (f32[84,128]{1,0:T(8,128)S(1)}, f32[84,128]{1,0:T(8,128)S(1)}, u32[]{:S(2)}, u32[]{:S(2)}) collective-permute-start(f32[84,128]{1,0:T(8,128)S(1)} %get-tuple-element.42), channel_id=1, source_target_pairs={{1,2},{2,1},{3,4},{4,3},{5,6},{6,5},{7,0},{0,7},{9,10},{10,9},{11,... | collective-permute-start | bytes 129032 | tf_op jit(solution)/shard_map/ppermute | solution.py:34
  8.2 0.0 collective-permute-start.5
  8.2 0.5 %collective-permute-start.4 = (f32[72,128]{1,0:T(8,128)S(1)}, f32[72,128]{1,0:T(8,128)S(1)}, u32[]{:S(2)}, u32[]{:S(2)}) collective-permute-start(f32[72,128]{1,0:T(8,128)S(1)} %get-tuple-element.46.scalars), channel_id=1, source_target_pairs={{0,16},{8,24},{16,0},{24,8},{1,17},{9,25},{17,1},{25,9},{2,18},{10... | collective-permute-start | bytes 110600 | tf_op jit(solution)/shard_map/ppermute | solution.py:39
  8.7 0.0 collective-permute-done.1.second
  8.7 0.0 collective-permute-done.2.first
  8.7 1.8 %collective-permute-start.3 = (f32[72,128]{1,0:T(8,128)S(1)}, f32[72,128]{1,0:T(8,128)S(1)}, u32[]{:S(2)}, u32[]{:S(2)}) collective-permute-start(f32[72,128]{1,0:T(8,128)S(1)} %get-tuple-element.45), channel_id=1, source_target_pairs={{1,2},{2,1},{3,4},{4,3},{5,6},{6,5},{7,0},{0,7},{9,10},{10,9},{11,... | collective-permute-start | bytes 110600 | tf_op jit(solution)/shard_map/ppermute | solution.py:34
  10.6 0.0 collective-permute-start.6
  10.6 0.8 %inner.1 = (f32[1088,128]{1,0:T(8,128)S(1)}, f32[4,34,8,128]{3,2,1,0:T(8,128)S(1)}, f32[3,34,8,128]{3,2,1,0:T(8,128)S(1)}, f32[3,34,8,128]{3,2,1,0:T(8,128)S(1)}...) custom-call(f32[4,16,512]{2,1,0:T(8,128)S(1)} %get-tuple-element.39., ...), custom_call_target="tpu_custom_call" | custom-call | flops 1310720 | bytes 1441792 | tf_op jit(solution)/shard_map/inner/pallas_call | solution.py:592
  11.4 0.0 collective-permute-done.5.near_early
  11.4 0.4 %collective-permute-done.6.near = f32[64,128]{1,0:T(8,128)S(1)} collective-permute-done((f32[64,128]{1,0:T(8,128)S(1)}, f32[64,128]{1,0:T(8,128)S(1)}, u32[]{:S(2)}, u32[]{:S(2)}) %collective-permute-start.6) | collective-permute-done | bytes 32800 | tf_op jit(solution)/shard_map/ppermute | solution.py:34
  11.8 0.8 %mid.1 = (f32[1088,128]{1,0:T(8,128)S(1)}, f32[4,34,8,128]{3,2,1,0:T(8,128)S(1)}, f32[3,34,8,128]{3,2,1,0:T(8,128)S(1)}, f32[3,34,8,128]{3,2,1,0:T(8,128)S(1)}, ...) custom-call(f32[80,128]{1,0:T(8,128)S(1)} %collective-permute-done.5, ...), custom_call_target="tpu_custom_call", output_to_operand_aliasing={{0}: (2, {}), {1}: (3, {}), {2}: (4, {}), {3}: (5, {}), {4}... | custom-call | flops 1310720 | bytes 1441792 | tf_op jit(solution)/shard_map/mid/pallas_call | solution.py:601
  12.6 0.0 collective-permute-done.4
  12.6 0.7 %pole_sums.1 = (f32[74,8,128]{2,1,0:T(8,128)S(1)}, f32[3,18,8,128]{3,2,1,0:T(8,128)S(1)}, f32[3,128,128]{2,1,0:T(8,128)S(1)}) custom-call(f32[72,128]{1,0:T(8,128)S(1)} %get-tuple-element.46.scalars, f32[16,128]{1,0:T(8,128)S(1)} %collective-permute-done.2.first, f32[16,128]{1,0:T(8,128)S(1)} %collective-permute-done.1.second, f32[1,72,128]{2,1,0:T(8,128)S(1)} %bitcast.1, ...), custom_call_target="tpu_custom_call" | custom-call | tf_op jit(solution)/shard_map/pole_sums/pallas_call | solution.py:612
  13.3 0.0 collective-permute-done.far_early
  13.3 0.8 %collective-permute-done.3.far = f32[72,128]{1,0:T(8,128)S(1)} collective-permute-done((f32[72,128]{1,0:T(8,128)S(1)}, f32[72,128]{1,0:T(8,128)S(1)}, u32[]{:S(2)}, u32[]{:S(2)}) %collective-permute-start.3) | collective-permute-done | bytes 36896 | tf_op jit(solution)/shard_map/ppermute | solution.py:34
  14.1 1.8 %outer.1 = (f32[3,16,512]{2,1,0:T(8,128)}, f32[1088,128]{1,0:T(8,128)S(1)}, f32[4,34,8,128]{3,2,1,0:T(8,128)S(1)}, f32[3,18,8,128]{3,2,1,0:T(8,128)S(1)}, f32[3,...) custom-call(f32[84,128]{1,0:T(8,128)S(1)} %collective-permute-done.f, ...), custom_call_target="tpu_custom_call", output_to_operand_aliasing={{1}: (3, {}), {2}: (4, {}), {3}: (5, {}), {4}: (6, {}), {5}... | custom-call | tf_op jit(solution)/shard_map/outer/pallas_call | solution.py:621
  (2 shorter events, 0.0 us)
Async XLA Ops:
  1.1 7.6 %collective-permute-start.1 = (f32[16,128]{1,0:T(8,128)S(1)}, f32[16,128]{1,0:T(8,128)S(1)}, u32[]{:S(2)}, u32[]{:S(2)}) collective-permute-start(f32[16,128]{1,0:T(8,128)S(1)} %get-tuple-element.40.second), channel_id=1, source_target_pairs={{8,16},{16,8},{24,0},{0,24},{9,17},{17,9},{25,1},{1,25},{10,18},{1... | collective-permute-start | bytes 24584 | tf_op jit(solution)/shard_map/ppermute | solution.py:34
  5.0 3.7 %collective-permute-start.2 = (f32[16,128]{1,0:T(8,128)S(1)}, f32[16,128]{1,0:T(8,128)S(1)}, u32[]{:S(2)}, u32[]{:S(2)}) collective-permute-start(f32[16,128]{1,0:T(8,128)S(1)} %get-tuple-element.41.first), channel_id=1, source_target_pairs={{0,8},{8,0},{16,24},{24,16},{1,9},{9,1},{17,25},{25,17},{2,10},{10... | collective-permute-start | bytes 24584 | tf_op jit(solution)/shard_map/ppermute | solution.py:34
  5.6 7.6 %collective-permute-start = (f32[84,128]{1,0:T(8,128)S(1)}, f32[84,128]{1,0:T(8,128)S(1)}, u32[]{:S(2)}, u32[]{:S(2)}) collective-permute-start(f32[84,128]{1,0:T(8,128)S(1)} %get-tuple-element.42), channel_id=1, source_target_pairs={{1,2},{2,1},{3,4},{4,3},{5,6},{6,5},{7,0},{0,7},{9,10},{10,9},{11,... | collective-permute-start | bytes 129032 | tf_op jit(solution)/shard_map/ppermute | solution.py:34
  8.2 3.2 %collective-permute-start.5 = (f32[80,128]{1,0:T(8,128)S(1)}, f32[80,128]{1,0:T(8,128)S(1)}, u32[]{:S(2)}, u32[]{:S(2)}) collective-permute-start(f32[80,128]{1,0:T(8,128)S(1)} %get-tuple-element.47), channel_id=1, source_target_pairs={{0,1},{1,0},{2,3},{3,2},{4,5},{5,4},{6,7},{7,6},{8,9},{9,8},{10,11... | collective-permute-start | bytes 122888 | tf_op jit(solution)/shard_map/ppermute | solution.py:34
  8.2 4.4 %collective-permute-start.4 = (f32[72,128]{1,0:T(8,128)S(1)}, f32[72,128]{1,0:T(8,128)S(1)}, u32[]{:S(2)}, u32[]{:S(2)}) collective-permute-start(f32[72,128]{1,0:T(8,128)S(1)} %get-tuple-element.46.scalars), channel_id=1, source_target_pairs={{0,16},{8,24},{16,0},{24,8},{1,17},{9,25},{17,1},{25,9},{2,18},{10... | collective-permute-start | bytes 110600 | tf_op jit(solution)/shard_map/ppermute | solution.py:39
  8.7 5.4 %collective-permute-start.3 = (f32[72,128]{1,0:T(8,128)S(1)}, f32[72,128]{1,0:T(8,128)S(1)}, u32[]{:S(2)}, u32[]{:S(2)}) collective-permute-start(f32[72,128]{1,0:T(8,128)S(1)} %get-tuple-element.45), channel_id=1, source_target_pairs={{1,2},{2,1},{3,4},{4,3},{5,6},{6,5},{7,0},{0,7},{9,10},{10,9},{11,... | collective-permute-start | bytes 110600 | tf_op jit(solution)/shard_map/ppermute | solution.py:34
  10.6 1.2 %collective-permute-start.6 = (f32[64,128]{1,0:T(8,128)S(1)}, f32[64,128]{1,0:T(8,128)S(1)}, u32[]{:S(2)}, u32[]{:S(2)}) collective-permute-start(f32[64,128]{1,0:T(8,128)S(1)} %get-tuple-element.48), channel_id=1, source_target_pairs={{0,1},{1,0},{2,3},{3,2},{4,5},{5,4},{6,7},{7,6},{8,9},{9,8},{10,11... | collective-permute-start | bytes 98312 | tf_op jit(solution)/shard_map/ppermute | solution.py:34

commit v19 on v18

--- a/solution.py
+++ b/solution.py
@@ -73,19 +73,24 @@
     odd = lax.rem(lax.axis_index("pole"), 2) == 1
     rows, columns = fields.shape[1:]
     lane = lax.broadcasted_iota(jnp.int32, (SUB, LANES), 1)
-    sub = lax.broadcasted_iota(jnp.int32, (SUB, LANES), 0)
-    poles = real.shape[0]
-    values = [real_in[i] for i in range(poles)] + [imag_in[i] for i in range(poles)]
-    values += [weight_in[0, i] for i in range(poles)] + [weight_in[1, i] for i in range(poles)]
+    poles = real.shape[1]
+    quantity = jnp.concatenate([real_in[...], imag_in[...], weight_in[...]], axis=0)
+    diagonal = lax.broadcasted_iota(jnp.int32, (poles, poles), 0)
+    diagonal = diagonal == lax.broadcasted_iota(jnp.int32, (poles, poles), 1)
+    spread = []
+    for q in range(4):
+        line = jnp.where(diagonal, quantity[q : q + 1], 0.0)
+        spread.append(jnp.broadcast_to(jnp.sum(line, 1, keepdims=True), (poles, LANES)))
+    spread = jnp.concatenate(spread, axis=0)
     for g in range(rows // SUB):
         cut = pl.ds(g * SUB, SUB)
         west = [fields[f, cut, 0:LANES] for f in range(4)]
         east = [fields[f, cut, columns - LANES : columns] for f in range(4)]
         west += [west[3] * west[1], west[3] * west[2]]
         east += [east[3] * east[1], east[3] * east[2]]
-        rest = jnp.zeros((SUB, LANES), jnp.float32)
-        for i, value in enumerate(values[g * SUB : (g + 1) * SUB]):
-            rest = jnp.where(sub == i, value, rest)
+        rest = spread[g * SUB : (g + 1) * SUB]
+        if rest.shape[0] < SUB:
+            rest = jnp.zeros((SUB, LANES), jnp.float32)
         eastward = rest
         westward = rest
         for f in range(6):
@@ -531,7 +536,7 @@
 
     given = [
         pltpu.with_memory_space_constraint(x, pltpu.HBM)
-        for x in (state, depth, pole_real, pole_imag, pole_weight)
+        for x in (state, depth, pole_real[None], pole_imag[None], pole_weight)
     ]
     hbm = pl.BlockSpec(memory_space=pltpu.HBM)
     message = pltpu.VMEM((rows, LANES), jnp.float32)
@@ -541,9 +546,9 @@
         in_specs=[hbm] * 5,
         out_specs=(vmem,) * 3,
         scratch_shapes=[
-            pltpu.SMEM(pole_real.shape, jnp.float32),
-            pltpu.SMEM(pole_imag.shape, jnp.float32),
-            pltpu.SMEM(pole_weight.shape, jnp.float32),
+            pltpu.VMEM((1, poles), jnp.float32),
+            pltpu.VMEM((1, poles), jnp.float32),
+            pltpu.VMEM((2, poles), jnp.float32),
             pltpu.SemaphoreType.DMA((5,)),
         ],
         compiler_params=small,

time: 16 us -> 16 us (level)
  no operation moved by 1% of the time
where the time goes in v19:
time: 16 us; the launch traced here: 15.9 us
  starting transfers between devices  9.4 us (59%)
  Pallas kernels  5.21 us (33%)
  waiting for transfers between devices  1.24 us (8%)
    ppermute x6, starting transfers between devices, swap(): return lax.ppermute(block, axis, pairs(lax.axis_size(axis), phase))  8.89 us
    pallas_call x1, Pallas kernels, shards(): pl.pallas_call(outer_kernel, out_shape=(f32(*state.shape), *kept), in_spe...  1.81 us
    ppermute x6, waiting for transfers between devices, swap(): return lax.ppermute(block, axis, pairs(lax.axis_size(axis), phase))  1.24 us
    pallas_call x1, Pallas kernels, shards(): pl.pallas_call(pack_columns_kernel, out_shape=(pltpu.VMEM((4, rows, colum...  1.07 us
    pallas_call x1, Pallas kernels, shards(): pl.pallas_call(mid_kernel, out_shape=state_of, in_specs=[vmem] * (2 + len...  0.84 us
    pallas_call x1, Pallas kernels, shards(): pl.pallas_call(inner_kernel, out_shape=state_of, in_specs=[vmem] * 3, out...  0.79 us
    pallas_call x1, Pallas kernels, shards(): pl.pallas_call(functools.partial(pole_sums_kernel, 4 * poles), out_shape=...  0.65 us
    ppermute x1, starting transfers between devices, shift(): lax.ppermute(block, axis, [(i, (i + step) % count) for i in range(count)])  0.51 us
  transfers between devices with their start and end apart: 7, of which 2 were waited for; matrix products, arithmetic and copies ran while one was open for 0% of the time, Pallas kernels for 15%

profile of v19, /device:TPU:0, one launch (start us, length us, event | category | flops | bytes accessed | tf_op | source)
XLA Modules:
  0.0 15.9 jit_solution(6475702841339001220)
XLA Ops:
  0.0 1.1 %pack_columns.1 = (f32[4,16,512]{2,1,0:T(8,128)S(1)}, f32[16,128]{1,0:T(8,128)S(1)}, f32[16,128]{1,0:T(8,128)S(1)}) custom-call(f32[3,16,512]{2,1,0:T(8,128)} %state.1, f32[16,512]{1,0:T(8,128)} %depth.1, f32[1,4]{1,0:T(1,128)} %bitcast.4, f32[1,4]{1,0:T(1,128)} %bitcast.5, f32[2,4]{1,0:T(2,128)} %weight.1), custom_call_target="tpu_custom_call" | custom-call | tf_op jit(solution)/shard_map/pack_columns/pallas_call | solution.py:543
  1.1 4.0 %collective-permute-start.1 = (f32[16,128]{1,0:T(8,128)S(1)}, f32[16,128]{1,0:T(8,128)S(1)}, u32[]{:S(2)}, u32[]{:S(2)}) collective-permute-start(f32[16,128]{1,0:T(8,128)S(1)} %get-tuple-element.40.second), channel_id=1, source_target_pairs={{8,16},{16,8},{24,0},{0,24},{9,17},{17,9},{25,1},{1,25},{10,18},{1... | collective-permute-start | bytes 24584 | tf_op jit(solution)/shard_map/ppermute | solution.py:34
  5.0 0.5 %collective-permute-start.2 = (f32[16,128]{1,0:T(8,128)S(1)}, f32[16,128]{1,0:T(8,128)S(1)}, u32[]{:S(2)}, u32[]{:S(2)}) collective-permute-start(f32[16,128]{1,0:T(8,128)S(1)} %get-tuple-element.41.first), channel_id=1, source_target_pairs={{0,8},{8,0},{16,24},{24,16},{1,9},{9,1},{17,25},{25,17},{2,10},{10... | collective-permute-start | bytes 24584 | tf_op jit(solution)/shard_map/ppermute | solution.py:34
  5.6 2.5 %collective-permute-start = (f32[84,128]{1,0:T(8,128)S(1)}, f32[84,128]{1,0:T(8,128)S(1)}, u32[]{:S(2)}, u32[]{:S(2)}) collective-permute-start(f32[84,128]{1,0:T(8,128)S(1)} %get-tuple-element.42), channel_id=1, source_target_pairs={{1,2},{2,1},{3,4},{4,3},{5,6},{6,5},{7,0},{0,7},{9,10},{10,9},{11,... | collective-permute-start | bytes 129032 | tf_op jit(solution)/shard_map/ppermute | solution.py:34
  8.2 0.0 collective-permute-start.5
  8.2 0.5 %collective-permute-start.4 = (f32[72,128]{1,0:T(8,128)S(1)}, f32[72,128]{1,0:T(8,128)S(1)}, u32[]{:S(2)}, u32[]{:S(2)}) collective-permute-start(f32[72,128]{1,0:T(8,128)S(1)} %get-tuple-element.46.scalars), channel_id=1, source_target_pairs={{0,16},{8,24},{16,0},{24,8},{1,17},{9,25},{17,1},{25,9},{2,18},{10... | collective-permute-start | bytes 110600 | tf_op jit(solution)/shard_map/ppermute | solution.py:39
  8.7 0.0 collective-permute-done.1.second
  8.7 0.0 collective-permute-done.2.first
  8.7 1.8 %collective-permute-start.3 = (f32[72,128]{1,0:T(8,128)S(1)}, f32[72,128]{1,0:T(8,128)S(1)}, u32[]{:S(2)}, u32[]{:S(2)}) collective-permute-start(f32[72,128]{1,0:T(8,128)S(1)} %get-tuple-element.45), channel_id=1, source_target_pairs={{1,2},{2,1},{3,4},{4,3},{5,6},{6,5},{7,0},{0,7},{9,10},{10,9},{11,... | collective-permute-start | bytes 110600 | tf_op jit(solution)/shard_map/ppermute | solution.py:34
  10.6 0.0 collective-permute-start.6
  10.6 0.8 %inner.1 = (f32[1088,128]{1,0:T(8,128)S(1)}, f32[4,34,8,128]{3,2,1,0:T(8,128)S(1)}, f32[3,34,8,128]{3,2,1,0:T(8,128)S(1)}, f32[3,34,8,128]{3,2,1,0:T(8,128)S(1)}...) custom-call(f32[4,16,512]{2,1,0:T(8,128)S(1)} %get-tuple-element.39., ...), custom_call_target="tpu_custom_call" | custom-call | flops 1310720 | bytes 1441792 | tf_op jit(solution)/shard_map/inner/pallas_call | solution.py:597
  11.3 0.0 collective-permute-done.5.near_early
  11.4 0.4 %collective-permute-done.6.near = f32[64,128]{1,0:T(8,128)S(1)} collective-permute-done((f32[64,128]{1,0:T(8,128)S(1)}, f32[64,128]{1,0:T(8,128)S(1)}, u32[]{:S(2)}, u32[]{:S(2)}) %collective-permute-start.6) | collective-permute-done | bytes 32800 | tf_op jit(solution)/shard_map/ppermute | solution.py:34
  11.8 0.8 %mid.1 = (f32[1088,128]{1,0:T(8,128)S(1)}, f32[4,34,8,128]{3,2,1,0:T(8,128)S(1)}, f32[3,34,8,128]{3,2,1,0:T(8,128)S(1)}, f32[3,34,8,128]{3,2,1,0:T(8,128)S(1)}, ...) custom-call(f32[80,128]{1,0:T(8,128)S(1)} %collective-permute-done.5, ...), custom_call_target="tpu_custom_call", output_to_operand_aliasing={{0}: (2, {}), {1}: (3, {}), {2}: (4, {}), {3}: (5, {}), {4}... | custom-call | flops 1310720 | bytes 1441792 | tf_op jit(solution)/shard_map/mid/pallas_call | solution.py:606
  12.6 0.0 collective-permute-done.4
  12.6 0.7 %pole_sums.1 = (f32[74,8,128]{2,1,0:T(8,128)S(1)}, f32[3,18,8,128]{3,2,1,0:T(8,128)S(1)}, f32[3,128,128]{2,1,0:T(8,128)S(1)}) custom-call(f32[72,128]{1,0:T(8,128)S(1)} %get-tuple-element.46.scalars, f32[16,128]{1,0:T(8,128)S(1)} %collective-permute-done.2.first, f32[16,128]{1,0:T(8,128)S(1)} %collective-permute-done.1.second, f32[1,72,128]{2,1,0:T(8,128)S(1)} %bitcast.3, ...), custom_call_target="tpu_custom_call" | custom-call | tf_op jit(solution)/shard_map/pole_sums/pallas_call | solution.py:617
  13.3 0.0 collective-permute-done.far_early
  13.3 0.8 %collective-permute-done.3.far = f32[72,128]{1,0:T(8,128)S(1)} collective-permute-done((f32[72,128]{1,0:T(8,128)S(1)}, f32[72,128]{1,0:T(8,128)S(1)}, u32[]{:S(2)}, u32[]{:S(2)}) %collective-permute-start.3) | collective-permute-done | bytes 36896 | tf_op jit(solution)/shard_map/ppermute | solution.py:34
  14.1 1.8 %outer.1 = (f32[3,16,512]{2,1,0:T(8,128)}, f32[1088,128]{1,0:T(8,128)S(1)}, f32[4,34,8,128]{3,2,1,0:T(8,128)S(1)}, f32[3,18,8,128]{3,2,1,0:T(8,128)S(1)}, f32[3,...) custom-call(f32[84,128]{1,0:T(8,128)S(1)} %collective-permute-done.f, ...), custom_call_target="tpu_custom_call", output_to_operand_aliasing={{1}: (3, {}), {2}: (4, {}), {3}: (5, {}), {4}: (6, {}), {5}... | custom-call | tf_op jit(solution)/shard_map/outer/pallas_call | solution.py:626
  (2 shorter events, 0.0 us)
Async XLA Ops:
  1.1 7.6 %collective-permute-start.1 = (f32[16,128]{1,0:T(8,128)S(1)}, f32[16,128]{1,0:T(8,128)S(1)}, u32[]{:S(2)}, u32[]{:S(2)}) collective-permute-start(f32[16,128]{1,0:T(8,128)S(1)} %get-tuple-element.40.second), channel_id=1, source_target_pairs={{8,16},{16,8},{24,0},{0,24},{9,17},{17,9},{25,1},{1,25},{10,18},{1... | collective-permute-start | bytes 24584 | tf_op jit(solution)/shard_map/ppermute | solution.py:34
  5.0 3.7 %collective-permute-start.2 = (f32[16,128]{1,0:T(8,128)S(1)}, f32[16,128]{1,0:T(8,128)S(1)}, u32[]{:S(2)}, u32[]{:S(2)}) collective-permute-start(f32[16,128]{1,0:T(8,128)S(1)} %get-tuple-element.41.first), channel_id=1, source_target_pairs={{0,8},{8,0},{16,24},{24,16},{1,9},{9,1},{17,25},{25,17},{2,10},{10... | collective-permute-start | bytes 24584 | tf_op jit(solution)/shard_map/ppermute | solution.py:34
  5.6 7.6 %collective-permute-start = (f32[84,128]{1,0:T(8,128)S(1)}, f32[84,128]{1,0:T(8,128)S(1)}, u32[]{:S(2)}, u32[]{:S(2)}) collective-permute-start(f32[84,128]{1,0:T(8,128)S(1)} %get-tuple-element.42), channel_id=1, source_target_pairs={{1,2},{2,1},{3,4},{4,3},{5,6},{6,5},{7,0},{0,7},{9,10},{10,9},{11,... | collective-permute-start | bytes 129032 | tf_op jit(solution)/shard_map/ppermute | solution.py:34
  8.2 3.2 %collective-permute-start.5 = (f32[80,128]{1,0:T(8,128)S(1)}, f32[80,128]{1,0:T(8,128)S(1)}, u32[]{:S(2)}, u32[]{:S(2)}) collective-permute-start(f32[80,128]{1,0:T(8,128)S(1)} %get-tuple-element.47), channel_id=1, source_target_pairs={{0,1},{1,0},{2,3},{3,2},{4,5},{5,4},{6,7},{7,6},{8,9},{9,8},{10,11... | collective-permute-start | bytes 122888 | tf_op jit(solution)/shard_map/ppermute | solution.py:34
  8.2 4.4 %collective-permute-start.4 = (f32[72,128]{1,0:T(8,128)S(1)}, f32[72,128]{1,0:T(8,128)S(1)}, u32[]{:S(2)}, u32[]{:S(2)}) collective-permute-start(f32[72,128]{1,0:T(8,128)S(1)} %get-tuple-element.46.scalars), channel_id=1, source_target_pairs={{0,16},{8,24},{16,0},{24,8},{1,17},{9,25},{17,1},{25,9},{2,18},{10... | collective-permute-start | bytes 110600 | tf_op jit(solution)/shard_map/ppermute | solution.py:39
  8.7 5.4 %collective-permute-start.3 = (f32[72,128]{1,0:T(8,128)S(1)}, f32[72,128]{1,0:T(8,128)S(1)}, u32[]{:S(2)}, u32[]{:S(2)}) collective-permute-start(f32[72,128]{1,0:T(8,128)S(1)} %get-tuple-element.45), channel_id=1, source_target_pairs={{1,2},{2,1},{3,4},{4,3},{5,6},{6,5},{7,0},{0,7},{9,10},{10,9},{11,... | collective-permute-start | bytes 110600 | tf_op jit(solution)/shard_map/ppermute | solution.py:34
  10.6 1.2 %collective-permute-start.6 = (f32[64,128]{1,0:T(8,128)S(1)}, f32[64,128]{1,0:T(8,128)S(1)}, u32[]{:S(2)}, u32[]{:S(2)}) collective-permute-start(f32[64,128]{1,0:T(8,128)S(1)} %get-tuple-element.48), channel_id=1, source_target_pairs={{0,1},{1,0},{2,3},{3,2},{4,5},{5,4},{6,7},{7,6},{8,9},{9,8},{10,11... | collective-permute-start | bytes 98312 | tf_op jit(solution)/shard_map/ppermute | solution.py:34

commit v20 on v18

--- a/solution.py
+++ b/solution.py
@@ -59,19 +59,21 @@
 def pack_columns_kernel(
     state, depth, real, imag, weight, fields, first, second, real_in, imag_in, weight_in, done
 ):
-    moves = [
-        pltpu.make_async_copy(depth, fields.at[3], done.at[0]),
-        pltpu.make_async_copy(state, fields.at[pl.ds(0, 3)], done.at[1]),
-        pltpu.make_async_copy(real, real_in, done.at[2]),
-        pltpu.make_async_copy(imag, imag_in, done.at[3]),
-        pltpu.make_async_copy(weight, weight_in, done.at[4]),
-    ]
+    rows, columns = depth.shape
+    halves = [pl.ds(0, rows // 2), pl.ds(rows // 2, rows // 2)]
+    moves = []
+    for f in range(4):
+        source = depth if f == 3 else state.at[f]
+        for cut in halves:
+            move = (source.at[cut], fields.at[f, cut])
+            moves.append(pltpu.make_async_copy(*move, done.at[len(moves)]))
+    for move in ((real, real_in), (imag, imag_in), (weight, weight_in)):
+        moves.append(pltpu.make_async_copy(*move, done.at[len(moves)]))
     for move in moves:
         move.start()
     for move in moves:
         move.wait()
     odd = lax.rem(lax.axis_index("pole"), 2) == 1
-    rows, columns = fields.shape[1:]
     lane = lax.broadcasted_iota(jnp.int32, (SUB, LANES), 1)
     sub = lax.broadcasted_iota(jnp.int32, (SUB, LANES), 0)
     poles = real.shape[0]
@@ -544,7 +546,7 @@
             pltpu.SMEM(pole_real.shape, jnp.float32),
             pltpu.SMEM(pole_imag.shape, jnp.float32),
             pltpu.SMEM(pole_weight.shape, jnp.float32),
-            pltpu.SemaphoreType.DMA((5,)),
+            pltpu.SemaphoreType.DMA((11,)),
         ],
         compiler_params=small,
         name="pack_columns",
@@ -582,7 +584,7 @@
     poly = [f32(3, height, SUB, LANES)] * ITERS
     coef = f32(4, height, SUB, LANES)
     sol = f32(3, rows + 2, SUB, LANES)
-    result = f32(3, rows * SUB, LANES)
+    result = f32(3, (rows + 1) * SUB, LANES)
     state_of = (grid, coef, *poly)
     cost = pl.CostEstimate(
         flops=10 * ITERS * rows * SUB * LANES,

time: 16 us -> 16.1 us (level)
  no operation moved by 1% of the time
where the time goes in v20:
time: 16.1 us; the launch traced here: 15.9 us
  starting transfers between devices  9.4 us (58%)
  Pallas kernels  5.21 us (32%)
  waiting for transfers between devices  1.22 us (8%)
    ppermute x6, starting transfers between devices, swap(): return lax.ppermute(block, axis, pairs(lax.axis_size(axis), phase))  8.89 us
    pallas_call x1, Pallas kernels, shards(): pl.pallas_call(outer_kernel, out_shape=(f32(*state.shape), *kept), in_spe...  1.81 us
    ppermute x6, waiting for transfers between devices, swap(): return lax.ppermute(block, axis, pairs(lax.axis_size(axis), phase))  1.22 us
    pallas_call x1, Pallas kernels, shards(): pl.pallas_call(pack_columns_kernel, out_shape=(pltpu.VMEM((4, rows, colum...  1.05 us
    pallas_call x1, Pallas kernels, shards(): pl.pallas_call(mid_kernel, out_shape=state_of, in_specs=[vmem] * (2 + len...  0.85 us
    pallas_call x1, Pallas kernels, shards(): pl.pallas_call(inner_kernel, out_shape=state_of, in_specs=[vmem] * 3, out...  0.79 us
    pallas_call x1, Pallas kernels, shards(): pl.pallas_call(functools.partial(pole_sums_kernel, 4 * poles), out_shape=...  0.67 us
    ppermute x1, starting transfers between devices, shift(): lax.ppermute(block, axis, [(i, (i + step) % count) for i in range(count)])  0.51 us
  transfers between devices with their start and end apart: 7, of which 2 were waited for; matrix products, arithmetic and copies ran while one was open for 0% of the time, Pallas kernels for 15%

profile of v20, /device:TPU:0, one launch (start us, length us, event | category | flops | bytes accessed | tf_op | source)
XLA Modules:
  0.0 15.9 jit_solution(9046809489626812689)
XLA Ops:
  0.0 1.1 %pack_columns.1 = (f32[4,16,512]{2,1,0:T(8,128)S(1)}, f32[16,128]{1,0:T(8,128)S(1)}, f32[16,128]{1,0:T(8,128)S(1)}) custom-call(f32[3,16,512]{2,1,0:T(8,128)} %state.1, f32[16,512]{1,0:T(8,128)} %depth.1, f32[4]{0:T(128)} %real.1, f32[4]{0:T(128)} %imag.1, f32[2,4]{1,0:T(2,128)} %weight.1), custom_call_target="tpu_custom_call" | custom-call | tf_op jit(solution)/shard_map/pack_columns/pallas_call | solution.py:540
  1.1 4.0 %collective-permute-start.1 = (f32[16,128]{1,0:T(8,128)S(1)}, f32[16,128]{1,0:T(8,128)S(1)}, u32[]{:S(2)}, u32[]{:S(2)}) collective-permute-start(f32[16,128]{1,0:T(8,128)S(1)} %get-tuple-element.40.second), channel_id=1, source_target_pairs={{8,16},{16,8},{24,0},{0,24},{9,17},{17,9},{25,1},{1,25},{10,18},{1... | collective-permute-start | bytes 24584 | tf_op jit(solution)/shard_map/ppermute | solution.py:34
  5.0 0.5 %collective-permute-start.2 = (f32[16,128]{1,0:T(8,128)S(1)}, f32[16,128]{1,0:T(8,128)S(1)}, u32[]{:S(2)}, u32[]{:S(2)}) collective-permute-start(f32[16,128]{1,0:T(8,128)S(1)} %get-tuple-element.41.first), channel_id=1, source_target_pairs={{0,8},{8,0},{16,24},{24,16},{1,9},{9,1},{17,25},{25,17},{2,10},{10... | collective-permute-start | bytes 24584 | tf_op jit(solution)/shard_map/ppermute | solution.py:34
  5.6 2.5 %collective-permute-start = (f32[84,128]{1,0:T(8,128)S(1)}, f32[84,128]{1,0:T(8,128)S(1)}, u32[]{:S(2)}, u32[]{:S(2)}) collective-permute-start(f32[84,128]{1,0:T(8,128)S(1)} %get-tuple-element.42), channel_id=1, source_target_pairs={{1,2},{2,1},{3,4},{4,3},{5,6},{6,5},{7,0},{0,7},{9,10},{10,9},{11,... | collective-permute-start | bytes 129032 | tf_op jit(solution)/shard_map/ppermute | solution.py:34
  8.1 0.0 collective-permute-start.5
  8.1 0.5 %collective-permute-start.4 = (f32[72,128]{1,0:T(8,128)S(1)}, f32[72,128]{1,0:T(8,128)S(1)}, u32[]{:S(2)}, u32[]{:S(2)}) collective-permute-start(f32[72,128]{1,0:T(8,128)S(1)} %get-tuple-element.46.scalars), channel_id=1, source_target_pairs={{0,16},{8,24},{16,0},{24,8},{1,17},{9,25},{17,1},{25,9},{2,18},{10... | collective-permute-start | bytes 110600 | tf_op jit(solution)/shard_map/ppermute | solution.py:39
  8.7 0.0 collective-permute-done.1.second
  8.7 0.0 collective-permute-done.2.first
  8.7 1.8 %collective-permute-start.3 = (f32[72,128]{1,0:T(8,128)S(1)}, f32[72,128]{1,0:T(8,128)S(1)}, u32[]{:S(2)}, u32[]{:S(2)}) collective-permute-start(f32[72,128]{1,0:T(8,128)S(1)} %get-tuple-element.45), channel_id=1, source_target_pairs={{1,2},{2,1},{3,4},{4,3},{5,6},{6,5},{7,0},{0,7},{9,10},{10,9},{11,... | collective-permute-start | bytes 110600 | tf_op jit(solution)/shard_map/ppermute | solution.py:34
  10.5 0.0 collective-permute-start.6
  10.5 0.8 %inner.1 = (f32[1088,128]{1,0:T(8,128)S(1)}, f32[4,34,8,128]{3,2,1,0:T(8,128)S(1)}, f32[3,34,8,128]{3,2,1,0:T(8,128)S(1)}, f32[3,34,8,128]{3,2,1,0:T(8,128)S(1)}...) custom-call(f32[4,16,512]{2,1,0:T(8,128)S(1)} %get-tuple-element.39., ...), custom_call_target="tpu_custom_call" | custom-call | flops 1310720 | bytes 1441792 | tf_op jit(solution)/shard_map/inner/pallas_call | solution.py:594
  11.3 0.0 collective-permute-done.5.near_early
  11.3 0.4 %collective-permute-done.6.near = f32[64,128]{1,0:T(8,128)S(1)} collective-permute-done((f32[64,128]{1,0:T(8,128)S(1)}, f32[64,128]{1,0:T(8,128)S(1)}, u32[]{:S(2)}, u32[]{:S(2)}) %collective-permute-start.6) | collective-permute-done | bytes 32800 | tf_op jit(solution)/shard_map/ppermute | solution.py:34
  11.7 0.8 %mid.1 = (f32[1088,128]{1,0:T(8,128)S(1)}, f32[4,34,8,128]{3,2,1,0:T(8,128)S(1)}, f32[3,34,8,128]{3,2,1,0:T(8,128)S(1)}, f32[3,34,8,128]{3,2,1,0:T(8,128)S(1)}, ...) custom-call(f32[80,128]{1,0:T(8,128)S(1)} %collective-permute-done.5, ...), custom_call_target="tpu_custom_call", output_to_operand_aliasing={{0}: (2, {}), {1}: (3, {}), {2}: (4, {}), {3}: (5, {}), {4}... | custom-call | flops 1310720 | bytes 1441792 | tf_op jit(solution)/shard_map/mid/pallas_call | solution.py:603
  12.6 0.0 collective-permute-done.4
  12.6 0.7 %pole_sums.1 = (f32[74,8,128]{2,1,0:T(8,128)S(1)}, f32[3,18,8,128]{3,2,1,0:T(8,128)S(1)}, f32[3,136,128]{2,1,0:T(8,128)S(1)}) custom-call(f32[72,128]{1,0:T(8,128)S(1)} %get-tuple-element.46.scalars, f32[16,128]{1,0:T(8,128)S(1)} %collective-permute-done.2.first, f32[16,128]{1,0:T(8,128)S(1)} %collective-permute-done.1.second, f32[1,72,128]{2,1,0:T(8,128)S(1)} %bitcast.1, ...), custom_call_target="tpu_custom_call" | custom-call | tf_op jit(solution)/shard_map/pole_sums/pallas_call | solution.py:614
  13.3 0.0 collective-permute-done.far_early
  13.3 0.8 %collective-permute-done.3.far = f32[72,128]{1,0:T(8,128)S(1)} collective-permute-done((f32[72,128]{1,0:T(8,128)S(1)}, f32[72,128]{1,0:T(8,128)S(1)}, u32[]{:S(2)}, u32[]{:S(2)}) %collective-permute-start.3) | collective-permute-done | bytes 36896 | tf_op jit(solution)/shard_map/ppermute | solution.py:34
  14.1 1.8 %outer.1 = (f32[3,16,512]{2,1,0:T(8,128)}, f32[1088,128]{1,0:T(8,128)S(1)}, f32[4,34,8,128]{3,2,1,0:T(8,128)S(1)}, f32[3,18,8,128]{3,2,1,0:T(8,128)S(1)}, f32[3,...) custom-call(f32[84,128]{1,0:T(8,128)S(1)} %collective-permute-done.f, ...), custom_call_target="tpu_custom_call", output_to_operand_aliasing={{1}: (3, {}), {2}: (4, {}), {3}: (5, {}), {4}: (6, {}), {5}... | custom-call | tf_op jit(solution)/shard_map/outer/pallas_call | solution.py:623
  (2 shorter events, 0.0 us)
Async XLA Ops:
  1.1 7.6 %collective-permute-start.1 = (f32[16,128]{1,0:T(8,128)S(1)}, f32[16,128]{1,0:T(8,128)S(1)}, u32[]{:S(2)}, u32[]{:S(2)}) collective-permute-start(f32[16,128]{1,0:T(8,128)S(1)} %get-tuple-element.40.second), channel_id=1, source_target_pairs={{8,16},{16,8},{24,0},{0,24},{9,17},{17,9},{25,1},{1,25},{10,18},{1... | collective-permute-start | bytes 24584 | tf_op jit(solution)/shard_map/ppermute | solution.py:34
  5.0 3.7 %collective-permute-start.2 = (f32[16,128]{1,0:T(8,128)S(1)}, f32[16,128]{1,0:T(8,128)S(1)}, u32[]{:S(2)}, u32[]{:S(2)}) collective-permute-start(f32[16,128]{1,0:T(8,128)S(1)} %get-tuple-element.41.first), channel_id=1, source_target_pairs={{0,8},{8,0},{16,24},{24,16},{1,9},{9,1},{17,25},{25,17},{2,10},{10... | collective-permute-start | bytes 24584 | tf_op jit(solution)/shard_map/ppermute | solution.py:34
  5.6 7.7 %collective-permute-start = (f32[84,128]{1,0:T(8,128)S(1)}, f32[84,128]{1,0:T(8,128)S(1)}, u32[]{:S(2)}, u32[]{:S(2)}) collective-permute-start(f32[84,128]{1,0:T(8,128)S(1)} %get-tuple-element.42), channel_id=1, source_target_pairs={{1,2},{2,1},{3,4},{4,3},{5,6},{6,5},{7,0},{0,7},{9,10},{10,9},{11,... | collective-permute-start | bytes 129032 | tf_op jit(solution)/shard_map/ppermute | solution.py:34
  8.1 3.2 %collective-permute-start.5 = (f32[80,128]{1,0:T(8,128)S(1)}, f32[80,128]{1,0:T(8,128)S(1)}, u32[]{:S(2)}, u32[]{:S(2)}) collective-permute-start(f32[80,128]{1,0:T(8,128)S(1)} %get-tuple-element.47), channel_id=1, source_target_pairs={{0,1},{1,0},{2,3},{3,2},{4,5},{5,4},{6,7},{7,6},{8,9},{9,8},{10,11... | collective-permute-start | bytes 122888 | tf_op jit(solution)/shard_map/ppermute | solution.py:34
  8.1 4.4 %collective-permute-start.4 = (f32[72,128]{1,0:T(8,128)S(1)}, f32[72,128]{1,0:T(8,128)S(1)}, u32[]{:S(2)}, u32[]{:S(2)}) collective-permute-start(f32[72,128]{1,0:T(8,128)S(1)} %get-tuple-element.46.scalars), channel_id=1, source_target_pairs={{0,16},{8,24},{16,0},{24,8},{1,17},{9,25},{17,1},{25,9},{2,18},{10... | collective-permute-start | bytes 110600 | tf_op jit(solution)/shard_map/ppermute | solution.py:39
  8.7 5.4 %collective-permute-start.3 = (f32[72,128]{1,0:T(8,128)S(1)}, f32[72,128]{1,0:T(8,128)S(1)}, u32[]{:S(2)}, u32[]{:S(2)}) collective-permute-start(f32[72,128]{1,0:T(8,128)S(1)} %get-tuple-element.45), channel_id=1, source_target_pairs={{1,2},{2,1},{3,4},{4,3},{5,6},{6,5},{7,0},{0,7},{9,10},{10,9},{11,... | collective-permute-start | bytes 110600 | tf_op jit(solution)/shard_map/ppermute | solution.py:34
  10.5 1.2 %collective-permute-start.6 = (f32[64,128]{1,0:T(8,128)S(1)}, f32[64,128]{1,0:T(8,128)S(1)}, u32[]{:S(2)}, u32[]{:S(2)}) collective-permute-start(f32[64,128]{1,0:T(8,128)S(1)} %get-tuple-element.48), channel_id=1, source_target_pairs={{0,1},{1,0},{2,3},{3,2},{4,5},{5,4},{6,7},{7,6},{8,9},{9,8},{10,11... | collective-permute-start | bytes 98312 | tf_op jit(solution)/shard_map/ppermute | solution.py:34

commit v21 on v18

--- a/solution.py
+++ b/solution.py
@@ -406,7 +406,7 @@
     return found
 
 
-def sweep(poly, coef, m, start, count, last, upwards=False):
+def sweep(poly, coef, m, start, count, last, upwards=False, earlier=None):
     def take(f, r):
         return last[f, r] if (f, r) in last else poly[m][f, r]
 
@@ -423,13 +423,15 @@
             up, down = (back, ahead) if upwards else (ahead, back)
             value = diag * here[f]
             if m > 0:
-                value = value - poly[m - 1][f, r]
+                held = earlier is not None and (f, r) in earlier
+                value = value - (earlier[f, r] if held else poly[m - 1][f, r])
             value = value + above * up[f]
             value = value + below * down[f]
             value = value + north * right(here[f])
             value = value + south * left(here[f])
             value = 0.5 * value if m == 0 else value
-            poly[m + 1][f, r] = value
+            if earlier is None:
+                poly[m + 1][f, r] = value
             found[f, r] = value
         back, here = here, ahead
     return found
@@ -451,17 +453,21 @@
             found = sweep(poly, coef, m, REACH + 2 + m, rows - 4 - 2 * m, found)
 
 
-def one_side(halo, side, above, grid, coef, poly, each):
+def one_side(halo, side, above, grid, coef, poly, each=None):
     below = coef.shape[1] - REACH
     main, ext, start = (1, 0, 0) if above else (below, below + SUB, below - 2)
     grid[pl.ds((ext * 4 + 3) * SUB, SUB), :] = jnp.ones((SUB, LANES), jnp.float32)
     lay_halo(grid, halo, side, main, ext)
     found = prepare(grid, poly, coef, start, REACH)
-    each(0, found)
+    earlier = None if each is None else {}
     for m in range(ITERS - 1):
+        if each is not None:
+            each(m, found)
         low = 2 + m if above else below - 2 - m
-        found = sweep(poly, coef, m, low, REACH, found, above)
-        each(m + 1, found)
+        following = sweep(poly, coef, m, low, REACH, found, above, earlier)
+        earlier, found = (None if each is None else found), following
+    if each is not None:
+        each(ITERS - 1, found)
 
 
 def mid_kernel(near_early, near, *rest):
@@ -470,7 +476,7 @@
     side = near[pl.ds(near.shape[0] - SUB, SUB)]
     for way, here in ((True, above), (False, jnp.logical_not(above))):
         pl.when(here)(
-            lambda: one_side((near_early, near), side, way, grid, coef, poly, lambda m, found: None)
+            lambda: one_side((near_early, near), side, way, grid, coef, poly)
         )
 
 
@@ -582,7 +588,7 @@
     poly = [f32(3, height, SUB, LANES)] * ITERS
     coef = f32(4, height, SUB, LANES)
     sol = f32(3, rows + 2, SUB, LANES)
-    result = f32(3, rows * SUB, LANES)
+    result = f32(3, (rows + 1) * SUB, LANES)
     state_of = (grid, coef, *poly)
     cost = pl.CostEstimate(
         flops=10 * ITERS * rows * SUB * LANES,

time: 16 us -> 16 us (level)
  no operation moved by 1% of the time
where the time goes in v21:
time: 16 us; the launch traced here: 15.9 us
  starting transfers between devices  9.4 us (59%)
  Pallas kernels  5.23 us (33%)
  waiting for transfers between devices  1.22 us (8%)
    ppermute x6, starting transfers between devices, swap(): return lax.ppermute(block, axis, pairs(lax.axis_size(axis), phase))  8.89 us
    pallas_call x1, Pallas kernels, shards(): pl.pallas_call(outer_kernel, out_shape=(f32(*state.shape), *kept), in_spe...  1.81 us
    ppermute x6, waiting for transfers between devices, swap(): return lax.ppermute(block, axis, pairs(lax.axis_size(axis), phase))  1.22 us
    pallas_call x1, Pallas kernels, shards(): pl.pallas_call(pack_columns_kernel, out_shape=(pltpu.VMEM((4, rows, colum...  1.07 us
    pallas_call x1, Pallas kernels, shards(): pl.pallas_call(mid_kernel, out_shape=state_of, in_specs=[vmem] * (2 + len...  0.85 us
    pallas_call x1, Pallas kernels, shards(): pl.pallas_call(inner_kernel, out_shape=state_of, in_specs=[vmem] * 3, out...  0.79 us
    pallas_call x1, Pallas kernels, shards(): pl.pallas_call(functools.partial(pole_sums_kernel, 4 * poles), out_shape=...  0.67 us
    ppermute x1, starting transfers between devices, shift(): lax.ppermute(block, axis, [(i, (i + step) % count) for i in range(count)])  0.51 us
  transfers between devices with their start and end apart: 7, of which 2 were waited for; matrix products, arithmetic and copies ran while one was open for 0% of the time, Pallas kernels for 15%

profile of v21, /device:TPU:0, one launch (start us, length us, event | category | flops | bytes accessed | tf_op | source)
XLA Modules:
  0.0 15.9 jit_solution(7331446108341485475)
XLA Ops:
  0.0 1.1 %pack_columns.1 = (f32[4,16,512]{2,1,0:T(8,128)S(1)}, f32[16,128]{1,0:T(8,128)S(1)}, f32[16,128]{1,0:T(8,128)S(1)}) custom-call(f32[3,16,512]{2,1,0:T(8,128)} %state.1, f32[16,512]{1,0:T(8,128)} %depth.1, f32[4]{0:T(128)} %real.1, f32[4]{0:T(128)} %imag.1, f32[2,4]{1,0:T(2,128)} %weight.1), custom_call_target="tpu_custom_call" | custom-call | tf_op jit(solution)/shard_map/pack_columns/pallas_call | solution.py:544
  1.1 4.0 %collective-permute-start.1 = (f32[16,128]{1,0:T(8,128)S(1)}, f32[16,128]{1,0:T(8,128)S(1)}, u32[]{:S(2)}, u32[]{:S(2)}) collective-permute-start(f32[16,128]{1,0:T(8,128)S(1)} %get-tuple-element.40.second), channel_id=1, source_target_pairs={{8,16},{16,8},{24,0},{0,24},{9,17},{17,9},{25,1},{1,25},{10,18},{1... | collective-permute-start | bytes 24584 | tf_op jit(solution)/shard_map/ppermute | solution.py:34
  5.0 0.5 %collective-permute-start.2 = (f32[16,128]{1,0:T(8,128)S(1)}, f32[16,128]{1,0:T(8,128)S(1)}, u32[]{:S(2)}, u32[]{:S(2)}) collective-permute-start(f32[16,128]{1,0:T(8,128)S(1)} %get-tuple-element.41.first), channel_id=1, source_target_pairs={{0,8},{8,0},{16,24},{24,16},{1,9},{9,1},{17,25},{25,17},{2,10},{10... | collective-permute-start | bytes 24584 | tf_op jit(solution)/shard_map/ppermute | solution.py:34
  5.6 2.5 %collective-permute-start = (f32[84,128]{1,0:T(8,128)S(1)}, f32[84,128]{1,0:T(8,128)S(1)}, u32[]{:S(2)}, u32[]{:S(2)}) collective-permute-start(f32[84,128]{1,0:T(8,128)S(1)} %get-tuple-element.42), channel_id=1, source_target_pairs={{1,2},{2,1},{3,4},{4,3},{5,6},{6,5},{7,0},{0,7},{9,10},{10,9},{11,... | collective-permute-start | bytes 129032 | tf_op jit(solution)/shard_map/ppermute | solution.py:34
  8.2 0.0 collective-permute-start.5
  8.2 0.5 %collective-permute-start.4 = (f32[72,128]{1,0:T(8,128)S(1)}, f32[72,128]{1,0:T(8,128)S(1)}, u32[]{:S(2)}, u32[]{:S(2)}) collective-permute-start(f32[72,128]{1,0:T(8,128)S(1)} %get-tuple-element.46.scalars), channel_id=1, source_target_pairs={{0,16},{8,24},{16,0},{24,8},{1,17},{9,25},{17,1},{25,9},{2,18},{10... | collective-permute-start | bytes 110600 | tf_op jit(solution)/shard_map/ppermute | solution.py:39
  8.7 0.0 collective-permute-done.1.second
  8.7 0.0 collective-permute-done.2.first
  8.7 1.8 %collective-permute-start.3 = (f32[72,128]{1,0:T(8,128)S(1)}, f32[72,128]{1,0:T(8,128)S(1)}, u32[]{:S(2)}, u32[]{:S(2)}) collective-permute-start(f32[72,128]{1,0:T(8,128)S(1)} %get-tuple-element.45), channel_id=1, source_target_pairs={{1,2},{2,1},{3,4},{4,3},{5,6},{6,5},{7,0},{0,7},{9,10},{10,9},{11,... | collective-permute-start | bytes 110600 | tf_op jit(solution)/shard_map/ppermute | solution.py:34
  10.6 0.0 collective-permute-start.6
  10.6 0.8 %inner.1 = (f32[1088,128]{1,0:T(8,128)S(1)}, f32[4,34,8,128]{3,2,1,0:T(8,128)S(1)}, f32[3,34,8,128]{3,2,1,0:T(8,128)S(1)}, f32[3,34,8,128]{3,2,1,0:T(8,128)S(1)}...) custom-call(f32[4,16,512]{2,1,0:T(8,128)S(1)} %get-tuple-element.39., ...), custom_call_target="tpu_custom_call" | custom-call | flops 1310720 | bytes 1441792 | tf_op jit(solution)/shard_map/inner/pallas_call | solution.py:598
  11.3 0.0 collective-permute-done.5.near_early
  11.4 0.4 %collective-permute-done.6.near = f32[64,128]{1,0:T(8,128)S(1)} collective-permute-done((f32[64,128]{1,0:T(8,128)S(1)}, f32[64,128]{1,0:T(8,128)S(1)}, u32[]{:S(2)}, u32[]{:S(2)}) %collective-permute-start.6) | collective-permute-done | bytes 32800 | tf_op jit(solution)/shard_map/ppermute | solution.py:34
  11.8 0.8 %mid.1 = (f32[1088,128]{1,0:T(8,128)S(1)}, f32[4,34,8,128]{3,2,1,0:T(8,128)S(1)}, f32[3,34,8,128]{3,2,1,0:T(8,128)S(1)}, f32[3,34,8,128]{3,2,1,0:T(8,128)S(1)}, ...) custom-call(f32[80,128]{1,0:T(8,128)S(1)} %collective-permute-done.5, ...), custom_call_target="tpu_custom_call", output_to_operand_aliasing={{0}: (2, {}), {1}: (3, {}), {2}: (4, {}), {3}: (5, {}), {4}... | custom-call | flops 1310720 | bytes 1441792 | tf_op jit(solution)/shard_map/mid/pallas_call | solution.py:607
  12.6 0.0 collective-permute-done.4
  12.6 0.7 %pole_sums.1 = (f32[74,8,128]{2,1,0:T(8,128)S(1)}, f32[3,18,8,128]{3,2,1,0:T(8,128)S(1)}, f32[3,136,128]{2,1,0:T(8,128)S(1)}) custom-call(f32[72,128]{1,0:T(8,128)S(1)} %get-tuple-element.46.scalars, f32[16,128]{1,0:T(8,128)S(1)} %collective-permute-done.2.first, f32[16,128]{1,0:T(8,128)S(1)} %collective-permute-done.1.second, f32[1,72,128]{2,1,0:T(8,128)S(1)} %bitcast.1, ...), custom_call_target="tpu_custom_call" | custom-call | tf_op jit(solution)/shard_map/pole_sums/pallas_call | solution.py:618
  13.3 0.0 collective-permute-done.far_early
  13.3 0.8 %collective-permute-done.3.far = f32[72,128]{1,0:T(8,128)S(1)} collective-permute-done((f32[72,128]{1,0:T(8,128)S(1)}, f32[72,128]{1,0:T(8,128)S(1)}, u32[]{:S(2)}, u32[]{:S(2)}) %collective-permute-start.3) | collective-permute-done | bytes 36896 | tf_op jit(solution)/shard_map/ppermute | solution.py:34
  14.1 1.8 %outer.1 = (f32[3,16,512]{2,1,0:T(8,128)}, f32[1088,128]{1,0:T(8,128)S(1)}, f32[4,34,8,128]{3,2,1,0:T(8,128)S(1)}, f32[3,18,8,128]{3,2,1,0:T(8,128)S(1)}, f32[3,...) custom-call(f32[84,128]{1,0:T(8,128)S(1)} %collective-permute-done.f, ...), custom_call_target="tpu_custom_call", output_to_operand_aliasing={{1}: (3, {}), {2}: (4, {}), {3}: (5, {}), {4}: (6, {}), {5}... | custom-call | tf_op jit(solution)/shard_map/outer/pallas_call | solution.py:627
  (2 shorter events, 0.0 us)
Async XLA Ops:
  1.1 7.6 %collective-permute-start.1 = (f32[16,128]{1,0:T(8,128)S(1)}, f32[16,128]{1,0:T(8,128)S(1)}, u32[]{:S(2)}, u32[]{:S(2)}) collective-permute-start(f32[16,128]{1,0:T(8,128)S(1)} %get-tuple-element.40.second), channel_id=1, source_target_pairs={{8,16},{16,8},{24,0},{0,24},{9,17},{17,9},{25,1},{1,25},{10,18},{1... | collective-permute-start | bytes 24584 | tf_op jit(solution)/shard_map/ppermute | solution.py:34
  5.0 3.7 %collective-permute-start.2 = (f32[16,128]{1,0:T(8,128)S(1)}, f32[16,128]{1,0:T(8,128)S(1)}, u32[]{:S(2)}, u32[]{:S(2)}) collective-permute-start(f32[16,128]{1,0:T(8,128)S(1)} %get-tuple-element.41.first), channel_id=1, source_target_pairs={{0,8},{8,0},{16,24},{24,16},{1,9},{9,1},{17,25},{25,17},{2,10},{10... | collective-permute-start | bytes 24584 | tf_op jit(solution)/shard_map/ppermute | solution.py:34
  5.6 7.7 %collective-permute-start = (f32[84,128]{1,0:T(8,128)S(1)}, f32[84,128]{1,0:T(8,128)S(1)}, u32[]{:S(2)}, u32[]{:S(2)}) collective-permute-start(f32[84,128]{1,0:T(8,128)S(1)} %get-tuple-element.42), channel_id=1, source_target_pairs={{1,2},{2,1},{3,4},{4,3},{5,6},{6,5},{7,0},{0,7},{9,10},{10,9},{11,... | collective-permute-start | bytes 129032 | tf_op jit(solution)/shard_map/ppermute | solution.py:34
  8.2 3.2 %collective-permute-start.5 = (f32[80,128]{1,0:T(8,128)S(1)}, f32[80,128]{1,0:T(8,128)S(1)}, u32[]{:S(2)}, u32[]{:S(2)}) collective-permute-start(f32[80,128]{1,0:T(8,128)S(1)} %get-tuple-element.47), channel_id=1, source_target_pairs={{0,1},{1,0},{2,3},{3,2},{4,5},{5,4},{6,7},{7,6},{8,9},{9,8},{10,11... | collective-permute-start | bytes 122888 | tf_op jit(solution)/shard_map/ppermute | solution.py:34
  8.2 4.4 %collective-permute-start.4 = (f32[72,128]{1,0:T(8,128)S(1)}, f32[72,128]{1,0:T(8,128)S(1)}, u32[]{:S(2)}, u32[]{:S(2)}) collective-permute-start(f32[72,128]{1,0:T(8,128)S(1)} %get-tuple-element.46.scalars), channel_id=1, source_target_pairs={{0,16},{8,24},{16,0},{24,8},{1,17},{9,25},{17,1},{25,9},{2,18},{10... | collective-permute-start | bytes 110600 | tf_op jit(solution)/shard_map/ppermute | solution.py:39
  8.7 5.4 %collective-permute-start.3 = (f32[72,128]{1,0:T(8,128)S(1)}, f32[72,128]{1,0:T(8,128)S(1)}, u32[]{:S(2)}, u32[]{:S(2)}) collective-permute-start(f32[72,128]{1,0:T(8,128)S(1)} %get-tuple-element.45), channel_id=1, source_target_pairs={{1,2},{2,1},{3,4},{4,3},{5,6},{6,5},{7,0},{0,7},{9,10},{10,9},{11,... | collective-permute-start | bytes 110600 | tf_op jit(solution)/shard_map/ppermute | solution.py:34
  10.6 1.2 %collective-permute-start.6 = (f32[64,128]{1,0:T(8,128)S(1)}, f32[64,128]{1,0:T(8,128)S(1)}, u32[]{:S(2)}, u32[]{:S(2)}) collective-permute-start(f32[64,128]{1,0:T(8,128)S(1)} %get-tuple-element.48), channel_id=1, source_target_pairs={{0,1},{1,0},{2,3},{3,2},{4,5},{5,4},{6,7},{7,6},{8,9},{9,8},{10,11... | collective-permute-start | bytes 98312 | tf_op jit(solution)/shard_map/ppermute | solution.py:34

commit v22 on v18

--- a/solution.py
+++ b/solution.py
@@ -582,7 +582,7 @@
     poly = [f32(3, height, SUB, LANES)] * ITERS
     coef = f32(4, height, SUB, LANES)
     sol = f32(3, rows + 2, SUB, LANES)
-    result = f32(3, rows * SUB, LANES)
+    result = f32(3, (rows + 1) * SUB, LANES)
     state_of = (grid, coef, *poly)
     cost = pl.CostEstimate(
         flops=10 * ITERS * rows * SUB * LANES,

time: 16 us -> 16 us (level)
  no operation moved by 1% of the time
where the time goes in v22:
time: 16 us; the launch traced here: 15.9 us
  starting transfers between devices  9.4 us (59%)
  Pallas kernels  5.24 us (33%)
  waiting for transfers between devices  1.22 us (8%)
    ppermute x6, starting transfers between devices, swap(): return lax.ppermute(block, axis, pairs(lax.axis_size(axis), phase))  8.89 us
    pallas_call x1, Pallas kernels, shards(): pl.pallas_call(outer_kernel, out_shape=(f32(*state.shape), *kept), in_spe...  1.81 us
    ppermute x6, waiting for transfers between devices, swap(): return lax.ppermute(block, axis, pairs(lax.axis_size(axis), phase))  1.22 us
    pallas_call x1, Pallas kernels, shards(): pl.pallas_call(pack_columns_kernel, out_shape=(pltpu.VMEM((4, rows, colum...  1.07 us
    pallas_call x1, Pallas kernels, shards(): pl.pallas_call(mid_kernel, out_shape=state_of, in_specs=[vmem] * (2 + len...  0.85 us
    pallas_call x1, Pallas kernels, shards(): pl.pallas_call(inner_kernel, out_shape=state_of, in_specs=[vmem] * 3, out...  0.79 us
    pallas_call x1, Pallas kernels, shards(): pl.pallas_call(functools.partial(pole_sums_kernel, 4 * poles), out_shape=...  0.67 us
    ppermute x1, starting transfers between devices, shift(): lax.ppermute(block, axis, [(i, (i + step) % count) for i in range(count)])  0.51 us
  transfers between devices with their start and end apart: 7, of which 2 were waited for; matrix products, arithmetic and copies ran while one was open for 0% of the time, Pallas kernels for 15%

profile of v22, /device:TPU:0, one launch (start us, length us, event | category | flops | bytes accessed | tf_op | source)
XLA Modules:
  0.0 15.9 jit_solution(15707756430665393940)
XLA Ops:
  0.0 1.1 %pack_columns.1 = (f32[4,16,512]{2,1,0:T(8,128)S(1)}, f32[16,128]{1,0:T(8,128)S(1)}, f32[16,128]{1,0:T(8,128)S(1)}) custom-call(f32[3,16,512]{2,1,0:T(8,128)} %state.1, f32[16,512]{1,0:T(8,128)} %depth.1, f32[4]{0:T(128)} %real.1, f32[4]{0:T(128)} %imag.1, f32[2,4]{1,0:T(2,128)} %weight.1), custom_call_target="tpu_custom_call" | custom-call | tf_op jit(solution)/shard_map/pack_columns/pallas_call | solution.py:538
  1.1 4.0 %collective-permute-start.1 = (f32[16,128]{1,0:T(8,128)S(1)}, f32[16,128]{1,0:T(8,128)S(1)}, u32[]{:S(2)}, u32[]{:S(2)}) collective-permute-start(f32[16,128]{1,0:T(8,128)S(1)} %get-tuple-element.40.second), channel_id=1, source_target_pairs={{8,16},{16,8},{24,0},{0,24},{9,17},{17,9},{25,1},{1,25},{10,18},{1... | collective-permute-start | bytes 24584 | tf_op jit(solution)/shard_map/ppermute | solution.py:34
  5.0 0.5 %collective-permute-start.2 = (f32[16,128]{1,0:T(8,128)S(1)}, f32[16,128]{1,0:T(8,128)S(1)}, u32[]{:S(2)}, u32[]{:S(2)}) collective-permute-start(f32[16,128]{1,0:T(8,128)S(1)} %get-tuple-element.41.first), channel_id=1, source_target_pairs={{0,8},{8,0},{16,24},{24,16},{1,9},{9,1},{17,25},{25,17},{2,10},{10... | collective-permute-start | bytes 24584 | tf_op jit(solution)/shard_map/ppermute | solution.py:34
  5.6 2.5 %collective-permute-start = (f32[84,128]{1,0:T(8,128)S(1)}, f32[84,128]{1,0:T(8,128)S(1)}, u32[]{:S(2)}, u32[]{:S(2)}) collective-permute-start(f32[84,128]{1,0:T(8,128)S(1)} %get-tuple-element.42), channel_id=1, source_target_pairs={{1,2},{2,1},{3,4},{4,3},{5,6},{6,5},{7,0},{0,7},{9,10},{10,9},{11,... | collective-permute-start | bytes 129032 | tf_op jit(solution)/shard_map/ppermute | solution.py:34
  8.2 0.0 collective-permute-start.5
  8.2 0.5 %collective-permute-start.4 = (f32[72,128]{1,0:T(8,128)S(1)}, f32[72,128]{1,0:T(8,128)S(1)}, u32[]{:S(2)}, u32[]{:S(2)}) collective-permute-start(f32[72,128]{1,0:T(8,128)S(1)} %get-tuple-element.46.scalars), channel_id=1, source_target_pairs={{0,16},{8,24},{16,0},{24,8},{1,17},{9,25},{17,1},{25,9},{2,18},{10... | collective-permute-start | bytes 110600 | tf_op jit(solution)/shard_map/ppermute | solution.py:39
  8.7 0.0 collective-permute-done.1.second
  8.7 0.0 collective-permute-done.2.first
  8.7 1.8 %collective-permute-start.3 = (f32[72,128]{1,0:T(8,128)S(1)}, f32[72,128]{1,0:T(8,128)S(1)}, u32[]{:S(2)}, u32[]{:S(2)}) collective-permute-start(f32[72,128]{1,0:T(8,128)S(1)} %get-tuple-element.45), channel_id=1, source_target_pairs={{1,2},{2,1},{3,4},{4,3},{5,6},{6,5},{7,0},{0,7},{9,10},{10,9},{11,... | collective-permute-start | bytes 110600 | tf_op jit(solution)/shard_map/ppermute | solution.py:34
  10.6 0.0 collective-permute-start.6
  10.6 0.8 %inner.1 = (f32[1088,128]{1,0:T(8,128)S(1)}, f32[4,34,8,128]{3,2,1,0:T(8,128)S(1)}, f32[3,34,8,128]{3,2,1,0:T(8,128)S(1)}, f32[3,34,8,128]{3,2,1,0:T(8,128)S(1)}...) custom-call(f32[4,16,512]{2,1,0:T(8,128)S(1)} %get-tuple-element.39., ...), custom_call_target="tpu_custom_call" | custom-call | flops 1310720 | bytes 1441792 | tf_op jit(solution)/shard_map/inner/pallas_call | solution.py:592
  11.3 0.0 collective-permute-done.5.near_early
  11.4 0.4 %collective-permute-done.6.near = f32[64,128]{1,0:T(8,128)S(1)} collective-permute-done((f32[64,128]{1,0:T(8,128)S(1)}, f32[64,128]{1,0:T(8,128)S(1)}, u32[]{:S(2)}, u32[]{:S(2)}) %collective-permute-start.6) | collective-permute-done | bytes 32800 | tf_op jit(solution)/shard_map/ppermute | solution.py:34
  11.8 0.8 %mid.1 = (f32[1088,128]{1,0:T(8,128)S(1)}, f32[4,34,8,128]{3,2,1,0:T(8,128)S(1)}, f32[3,34,8,128]{3,2,1,0:T(8,128)S(1)}, f32[3,34,8,128]{3,2,1,0:T(8,128)S(1)}, ...) custom-call(f32[80,128]{1,0:T(8,128)S(1)} %collective-permute-done.5, ...), custom_call_target="tpu_custom_call", output_to_operand_aliasing={{0}: (2, {}), {1}: (3, {}), {2}: (4, {}), {3}: (5, {}), {4}... | custom-call | flops 1310720 | bytes 1441792 | tf_op jit(solution)/shard_map/mid/pallas_call | solution.py:601
  12.6 0.0 collective-permute-done.4
  12.6 0.7 %pole_sums.1 = (f32[74,8,128]{2,1,0:T(8,128)S(1)}, f32[3,18,8,128]{3,2,1,0:T(8,128)S(1)}, f32[3,136,128]{2,1,0:T(8,128)S(1)}) custom-call(f32[72,128]{1,0:T(8,128)S(1)} %get-tuple-element.46.scalars, f32[16,128]{1,0:T(8,128)S(1)} %collective-permute-done.2.first, f32[16,128]{1,0:T(8,128)S(1)} %collective-permute-done.1.second, f32[1,72,128]{2,1,0:T(8,128)S(1)} %bitcast.1, ...), custom_call_target="tpu_custom_call" | custom-call | tf_op jit(solution)/shard_map/pole_sums/pallas_call | solution.py:612
  13.3 0.0 collective-permute-done.far_early
  13.3 0.8 %collective-permute-done.3.far = f32[72,128]{1,0:T(8,128)S(1)} collective-permute-done((f32[72,128]{1,0:T(8,128)S(1)}, f32[72,128]{1,0:T(8,128)S(1)}, u32[]{:S(2)}, u32[]{:S(2)}) %collective-permute-start.3) | collective-permute-done | bytes 36896 | tf_op jit(solution)/shard_map/ppermute | solution.py:34
  14.1 1.8 %outer.1 = (f32[3,16,512]{2,1,0:T(8,128)}, f32[1088,128]{1,0:T(8,128)S(1)}, f32[4,34,8,128]{3,2,1,0:T(8,128)S(1)}, f32[3,18,8,128]{3,2,1,0:T(8,128)S(1)}, f32[3,...) custom-call(f32[84,128]{1,0:T(8,128)S(1)} %collective-permute-done.f, ...), custom_call_target="tpu_custom_call", output_to_operand_aliasing={{1}: (3, {}), {2}: (4, {}), {3}: (5, {}), {4}: (6, {}), {5}... | custom-call | tf_op jit(solution)/shard_map/outer/pallas_call | solution.py:621
  (2 shorter events, 0.0 us)
Async XLA Ops:
  1.1 7.6 %collective-permute-start.1 = (f32[16,128]{1,0:T(8,128)S(1)}, f32[16,128]{1,0:T(8,128)S(1)}, u32[]{:S(2)}, u32[]{:S(2)}) collective-permute-start(f32[16,128]{1,0:T(8,128)S(1)} %get-tuple-element.40.second), channel_id=1, source_target_pairs={{8,16},{16,8},{24,0},{0,24},{9,17},{17,9},{25,1},{1,25},{10,18},{1... | collective-permute-start | bytes 24584 | tf_op jit(solution)/shard_map/ppermute | solution.py:34
  5.0 3.7 %collective-permute-start.2 = (f32[16,128]{1,0:T(8,128)S(1)}, f32[16,128]{1,0:T(8,128)S(1)}, u32[]{:S(2)}, u32[]{:S(2)}) collective-permute-start(f32[16,128]{1,0:T(8,128)S(1)} %get-tuple-element.41.first), channel_id=1, source_target_pairs={{0,8},{8,0},{16,24},{24,16},{1,9},{9,1},{17,25},{25,17},{2,10},{10... | collective-permute-start | bytes 24584 | tf_op jit(solution)/shard_map/ppermute | solution.py:34
  5.6 7.7 %collective-permute-start = (f32[84,128]{1,0:T(8,128)S(1)}, f32[84,128]{1,0:T(8,128)S(1)}, u32[]{:S(2)}, u32[]{:S(2)}) collective-permute-start(f32[84,128]{1,0:T(8,128)S(1)} %get-tuple-element.42), channel_id=1, source_target_pairs={{1,2},{2,1},{3,4},{4,3},{5,6},{6,5},{7,0},{0,7},{9,10},{10,9},{11,... | collective-permute-start | bytes 129032 | tf_op jit(solution)/shard_map/ppermute | solution.py:34
  8.2 3.2 %collective-permute-start.5 = (f32[80,128]{1,0:T(8,128)S(1)}, f32[80,128]{1,0:T(8,128)S(1)}, u32[]{:S(2)}, u32[]{:S(2)}) collective-permute-start(f32[80,128]{1,0:T(8,128)S(1)} %get-tuple-element.47), channel_id=1, source_target_pairs={{0,1},{1,0},{2,3},{3,2},{4,5},{5,4},{6,7},{7,6},{8,9},{9,8},{10,11... | collective-permute-start | bytes 122888 | tf_op jit(solution)/shard_map/ppermute | solution.py:34
  8.2 4.4 %collective-permute-start.4 = (f32[72,128]{1,0:T(8,128)S(1)}, f32[72,128]{1,0:T(8,128)S(1)}, u32[]{:S(2)}, u32[]{:S(2)}) collective-permute-start(f32[72,128]{1,0:T(8,128)S(1)} %get-tuple-element.46.scalars), channel_id=1, source_target_pairs={{0,16},{8,24},{16,0},{24,8},{1,17},{9,25},{17,1},{25,9},{2,18},{10... | collective-permute-start | bytes 110600 | tf_op jit(solution)/shard_map/ppermute | solution.py:39
  8.7 5.4 %collective-permute-start.3 = (f32[72,128]{1,0:T(8,128)S(1)}, f32[72,128]{1,0:T(8,128)S(1)}, u32[]{:S(2)}, u32[]{:S(2)}) collective-permute-start(f32[72,128]{1,0:T(8,128)S(1)} %get-tuple-element.45), channel_id=1, source_target_pairs={{1,2},{2,1},{3,4},{4,3},{5,6},{6,5},{7,0},{0,7},{9,10},{10,9},{11,... | collective-permute-start | bytes 110600 | tf_op jit(solution)/shard_map/ppermute | solution.py:34
  10.6 1.2 %collective-permute-start.6 = (f32[64,128]{1,0:T(8,128)S(1)}, f32[64,128]{1,0:T(8,128)S(1)}, u32[]{:S(2)}, u32[]{:S(2)}) collective-permute-start(f32[64,128]{1,0:T(8,128)S(1)} %get-tuple-element.48), channel_id=1, source_target_pairs={{0,1},{1,0},{2,3},{3,2},{4,5},{5,4},{6,7},{7,6},{8,9},{9,8},{10,11... | collective-permute-start | bytes 98312 | tf_op jit(solution)/shard_map/ppermute | solution.py:34

commit v23 on v22

--- a/solution.py
+++ b/solution.py
@@ -501,8 +501,8 @@
         span = [r for r in whole + edges[:1] if REACH <= r < REACH + rows]
         finish(grid, sums, result, acc, span)
 
+    pl.when(jnp.logical_not(above))(lambda: far_rows(False))
     pl.when(above)(lambda: far_rows(True))
-    pl.when(jnp.logical_not(above))(lambda: far_rows(False))
 
     moves = []
     for k in range(3):

time: 16 us -> 16 us (level)
  no operation moved by 1% of the time
where the time goes in v23:
time: 16 us; the launch traced here: 15.9 us
  starting transfers between devices  9.4 us (59%)
  Pallas kernels  5.24 us (33%)
  waiting for transfers between devices  1.22 us (8%)
    ppermute x6, starting transfers between devices, swap(): return lax.ppermute(block, axis, pairs(lax.axis_size(axis), phase))  8.89 us
    pallas_call x1, Pallas kernels, shards(): pl.pallas_call(outer_kernel, out_shape=(f32(*state.shape), *kept), in_spe...  1.82 us
    ppermute x6, waiting for transfers between devices, swap(): return lax.ppermute(block, axis, pairs(lax.axis_size(axis), phase))  1.22 us
    pallas_call x1, Pallas kernels, shards(): pl.pallas_call(pack_columns_kernel, out_shape=(pltpu.VMEM((4, rows, colum...  1.07 us
    pallas_call x1, Pallas kernels, shards(): pl.pallas_call(mid_kernel, out_shape=state_of, in_specs=[vmem] * (2 + len...  0.85 us
    pallas_call x1, Pallas kernels, shards(): pl.pallas_call(inner_kernel, out_shape=state_of, in_specs=[vmem] * 3, out...  0.79 us
    pallas_call x1, Pallas kernels, shards(): pl.pallas_call(functools.partial(pole_sums_kernel, 4 * poles), out_shape=...  0.67 us
    ppermute x1, starting transfers between devices, shift(): lax.ppermute(block, axis, [(i, (i + step) % count) for i in range(count)])  0.51 us
  transfers between devices with their start and end apart: 7, of which 2 were waited for; matrix products, arithmetic and copies ran while one was open for 0% of the time, Pallas kernels for 15%

profile of v23, /device:TPU:0, one launch (start us, length us, event | category | flops | bytes accessed | tf_op | source)
XLA Modules:
  0.0 15.9 jit_solution(2384192755364636475)
XLA Ops:
  0.0 1.1 %pack_columns.1 = (f32[4,16,512]{2,1,0:T(8,128)S(1)}, f32[16,128]{1,0:T(8,128)S(1)}, f32[16,128]{1,0:T(8,128)S(1)}) custom-call(f32[3,16,512]{2,1,0:T(8,128)} %state.1, f32[16,512]{1,0:T(8,128)} %depth.1, f32[4]{0:T(128)} %real.1, f32[4]{0:T(128)} %imag.1, f32[2,4]{1,0:T(2,128)} %weight.1), custom_call_target="tpu_custom_call" | custom-call | tf_op jit(solution)/shard_map/pack_columns/pallas_call | solution.py:538
  1.1 4.0 %collective-permute-start.1 = (f32[16,128]{1,0:T(8,128)S(1)}, f32[16,128]{1,0:T(8,128)S(1)}, u32[]{:S(2)}, u32[]{:S(2)}) collective-permute-start(f32[16,128]{1,0:T(8,128)S(1)} %get-tuple-element.40.second), channel_id=1, source_target_pairs={{8,16},{16,8},{24,0},{0,24},{9,17},{17,9},{25,1},{1,25},{10,18},{1... | collective-permute-start | bytes 24584 | tf_op jit(solution)/shard_map/ppermute | solution.py:34
  5.0 0.5 %collective-permute-start.2 = (f32[16,128]{1,0:T(8,128)S(1)}, f32[16,128]{1,0:T(8,128)S(1)}, u32[]{:S(2)}, u32[]{:S(2)}) collective-permute-start(f32[16,128]{1,0:T(8,128)S(1)} %get-tuple-element.41.first), channel_id=1, source_target_pairs={{0,8},{8,0},{16,24},{24,16},{1,9},{9,1},{17,25},{25,17},{2,10},{10... | collective-permute-start | bytes 24584 | tf_op jit(solution)/shard_map/ppermute | solution.py:34
  5.6 2.5 %collective-permute-start = (f32[84,128]{1,0:T(8,128)S(1)}, f32[84,128]{1,0:T(8,128)S(1)}, u32[]{:S(2)}, u32[]{:S(2)}) collective-permute-start(f32[84,128]{1,0:T(8,128)S(1)} %get-tuple-element.42), channel_id=1, source_target_pairs={{1,2},{2,1},{3,4},{4,3},{5,6},{6,5},{7,0},{0,7},{9,10},{10,9},{11,... | collective-permute-start | bytes 129032 | tf_op jit(solution)/shard_map/ppermute | solution.py:34
  8.2 0.0 collective-permute-start.5
  8.2 0.5 %collective-permute-start.4 = (f32[72,128]{1,0:T(8,128)S(1)}, f32[72,128]{1,0:T(8,128)S(1)}, u32[]{:S(2)}, u32[]{:S(2)}) collective-permute-start(f32[72,128]{1,0:T(8,128)S(1)} %get-tuple-element.46.scalars), channel_id=1, source_target_pairs={{0,16},{8,24},{16,0},{24,8},{1,17},{9,25},{17,1},{25,9},{2,18},{10... | collective-permute-start | bytes 110600 | tf_op jit(solution)/shard_map/ppermute | solution.py:39
  8.7 0.0 collective-permute-done.1.second
  8.7 0.0 collective-permute-done.2.first
  8.7 1.8 %collective-permute-start.3 = (f32[72,128]{1,0:T(8,128)S(1)}, f32[72,128]{1,0:T(8,128)S(1)}, u32[]{:S(2)}, u32[]{:S(2)}) collective-permute-start(f32[72,128]{1,0:T(8,128)S(1)} %get-tuple-element.45), channel_id=1, source_target_pairs={{1,2},{2,1},{3,4},{4,3},{5,6},{6,5},{7,0},{0,7},{9,10},{10,9},{11,... | collective-permute-start | bytes 110600 | tf_op jit(solution)/shard_map/ppermute | solution.py:34
  10.6 0.0 collective-permute-start.6
  10.6 0.8 %inner.1 = (f32[1088,128]{1,0:T(8,128)S(1)}, f32[4,34,8,128]{3,2,1,0:T(8,128)S(1)}, f32[3,34,8,128]{3,2,1,0:T(8,128)S(1)}, f32[3,34,8,128]{3,2,1,0:T(8,128)S(1)}...) custom-call(f32[4,16,512]{2,1,0:T(8,128)S(1)} %get-tuple-element.39., ...), custom_call_target="tpu_custom_call" | custom-call | flops 1310720 | bytes 1441792 | tf_op jit(solution)/shard_map/inner/pallas_call | solution.py:592
  11.3 0.0 collective-permute-done.5.near_early
  11.4 0.4 %collective-permute-done.6.near = f32[64,128]{1,0:T(8,128)S(1)} collective-permute-done((f32[64,128]{1,0:T(8,128)S(1)}, f32[64,128]{1,0:T(8,128)S(1)}, u32[]{:S(2)}, u32[]{:S(2)}) %collective-permute-start.6) | collective-permute-done | bytes 32800 | tf_op jit(solution)/shard_map/ppermute | solution.py:34
  11.8 0.8 %mid.1 = (f32[1088,128]{1,0:T(8,128)S(1)}, f32[4,34,8,128]{3,2,1,0:T(8,128)S(1)}, f32[3,34,8,128]{3,2,1,0:T(8,128)S(1)}, f32[3,34,8,128]{3,2,1,0:T(8,128)S(1)}, ...) custom-call(f32[80,128]{1,0:T(8,128)S(1)} %collective-permute-done.5, ...), custom_call_target="tpu_custom_call", output_to_operand_aliasing={{0}: (2, {}), {1}: (3, {}), {2}: (4, {}), {3}: (5, {}), {4}... | custom-call | flops 1310720 | bytes 1441792 | tf_op jit(solution)/shard_map/mid/pallas_call | solution.py:601
  12.6 0.0 collective-permute-done.4
  12.6 0.7 %pole_sums.1 = (f32[74,8,128]{2,1,0:T(8,128)S(1)}, f32[3,18,8,128]{3,2,1,0:T(8,128)S(1)}, f32[3,136,128]{2,1,0:T(8,128)S(1)}) custom-call(f32[72,128]{1,0:T(8,128)S(1)} %get-tuple-element.46.scalars, f32[16,128]{1,0:T(8,128)S(1)} %collective-permute-done.2.first, f32[16,128]{1,0:T(8,128)S(1)} %collective-permute-done.1.second, f32[1,72,128]{2,1,0:T(8,128)S(1)} %bitcast.1, ...), custom_call_target="tpu_custom_call" | custom-call | tf_op jit(solution)/shard_map/pole_sums/pallas_call | solution.py:612
  13.3 0.0 collective-permute-done.far_early
  13.3 0.8 %collective-permute-done.3.far = f32[72,128]{1,0:T(8,128)S(1)} collective-permute-done((f32[72,128]{1,0:T(8,128)S(1)}, f32[72,128]{1,0:T(8,128)S(1)}, u32[]{:S(2)}, u32[]{:S(2)}) %collective-permute-start.3) | collective-permute-done | bytes 36896 | tf_op jit(solution)/shard_map/ppermute | solution.py:34
  14.1 1.8 %outer.1 = (f32[3,16,512]{2,1,0:T(8,128)}, f32[1088,128]{1,0:T(8,128)S(1)}, f32[4,34,8,128]{3,2,1,0:T(8,128)S(1)}, f32[3,18,8,128]{3,2,1,0:T(8,128)S(1)}, f32[3,...) custom-call(f32[84,128]{1,0:T(8,128)S(1)} %collective-permute-done.f, ...), custom_call_target="tpu_custom_call", output_to_operand_aliasing={{1}: (3, {}), {2}: (4, {}), {3}: (5, {}), {4}: (6, {}), {5}... | custom-call | tf_op jit(solution)/shard_map/outer/pallas_call | solution.py:621
  (2 shorter events, 0.0 us)
Async XLA Ops:
  1.1 7.6 %collective-permute-start.1 = (f32[16,128]{1,0:T(8,128)S(1)}, f32[16,128]{1,0:T(8,128)S(1)}, u32[]{:S(2)}, u32[]{:S(2)}) collective-permute-start(f32[16,128]{1,0:T(8,128)S(1)} %get-tuple-element.40.second), channel_id=1, source_target_pairs={{8,16},{16,8},{24,0},{0,24},{9,17},{17,9},{25,1},{1,25},{10,18},{1... | collective-permute-start | bytes 24584 | tf_op jit(solution)/shard_map/ppermute | solution.py:34
  5.0 3.7 %collective-permute-start.2 = (f32[16,128]{1,0:T(8,128)S(1)}, f32[16,128]{1,0:T(8,128)S(1)}, u32[]{:S(2)}, u32[]{:S(2)}) collective-permute-start(f32[16,128]{1,0:T(8,128)S(1)} %get-tuple-element.41.first), channel_id=1, source_target_pairs={{0,8},{8,0},{16,24},{24,16},{1,9},{9,1},{17,25},{25,17},{2,10},{10... | collective-permute-start | bytes 24584 | tf_op jit(solution)/shard_map/ppermute | solution.py:34
  5.6 7.7 %collective-permute-start = (f32[84,128]{1,0:T(8,128)S(1)}, f32[84,128]{1,0:T(8,128)S(1)}, u32[]{:S(2)}, u32[]{:S(2)}) collective-permute-start(f32[84,128]{1,0:T(8,128)S(1)} %get-tuple-element.42), channel_id=1, source_target_pairs={{1,2},{2,1},{3,4},{4,3},{5,6},{6,5},{7,0},{0,7},{9,10},{10,9},{11,... | collective-permute-start | bytes 129032 | tf_op jit(solution)/shard_map/ppermute | solution.py:34
  8.2 3.2 %collective-permute-start.5 = (f32[80,128]{1,0:T(8,128)S(1)}, f32[80,128]{1,0:T(8,128)S(1)}, u32[]{:S(2)}, u32[]{:S(2)}) collective-permute-start(f32[80,128]{1,0:T(8,128)S(1)} %get-tuple-element.47), channel_id=1, source_target_pairs={{0,1},{1,0},{2,3},{3,2},{4,5},{5,4},{6,7},{7,6},{8,9},{9,8},{10,11... | collective-permute-start | bytes 122888 | tf_op jit(solution)/shard_map/ppermute | solution.py:34
  8.2 4.4 %collective-permute-start.4 = (f32[72,128]{1,0:T(8,128)S(1)}, f32[72,128]{1,0:T(8,128)S(1)}, u32[]{:S(2)}, u32[]{:S(2)}) collective-permute-start(f32[72,128]{1,0:T(8,128)S(1)} %get-tuple-element.46.scalars), channel_id=1, source_target_pairs={{0,16},{8,24},{16,0},{24,8},{1,17},{9,25},{17,1},{25,9},{2,18},{10... | collective-permute-start | bytes 110600 | tf_op jit(solution)/shard_map/ppermute | solution.py:39
  8.7 5.4 %collective-permute-start.3 = (f32[72,128]{1,0:T(8,128)S(1)}, f32[72,128]{1,0:T(8,128)S(1)}, u32[]{:S(2)}, u32[]{:S(2)}) collective-permute-start(f32[72,128]{1,0:T(8,128)S(1)} %get-tuple-element.45), channel_id=1, source_target_pairs={{1,2},{2,1},{3,4},{4,3},{5,6},{6,5},{7,0},{0,7},{9,10},{10,9},{11,... | collective-permute-start | bytes 110600 | tf_op jit(solution)/shard_map/ppermute | solution.py:34
  10.6 1.2 %collective-permute-start.6 = (f32[64,128]{1,0:T(8,128)S(1)}, f32[64,128]{1,0:T(8,128)S(1)}, u32[]{:S(2)}, u32[]{:S(2)}) collective-permute-start(f32[64,128]{1,0:T(8,128)S(1)} %get-tuple-element.48), channel_id=1, source_target_pairs={{0,1},{1,0},{2,3},{3,2},{4,5},{5,4},{6,7},{7,6},{8,9},{9,8},{10,11... | collective-permute-start | bytes 98312 | tf_op jit(solution)/shard_map/ppermute | solution.py:34
